TPU v7x, 32 devices: a whole 2x2x4 slice. The times are simulated.
32 devices in a mesh: dp: 16 (over z, y, x), mp: 2 (over core).
Axes of the slice: x: 2, y: 2, z: 4, core: 2. Of those that a mesh axis runs over, the one named last changes fastest.
Arguments:
- tokens: bfloat16 [32768, 768], P(('dp', 'mp')), may hold values from -7.2 to 7.2
- cotangent: bfloat16 [32768, 768], P(('dp', 'mp')), may hold values from -6 to 6
- seg_lengths: int32 [64, 8], P('dp'), may hold values from 1 to 256, 480 in all within a row
- w_qkv: float32 [768, 3, 768], P('dp', None, 'mp'), may hold values from -0.21875 to 0.21875
- w_out: float32 [768, 768], P(('mp', 'dp')), may hold values from -0.625 to 0.625
- w_up: float32 [768, 3072], P('dp', 'mp'), may hold values from -0.21875 to 0.21875
- w_down: float32 [3072, 768], P(('mp', 'dp')), may hold values from -0.109375 to 0.109375
- head_bias: float32 [2, 768], P(None, ('mp', 'dp')), may hold values from -1 to 1
- ffn_bias: float32 [3072], P(('mp', 'dp')), may hold values from -1 to 1
- norm_bias: float32 [6, 768], P(None, ('dp', 'mp')), may hold values from -1 to 3
- qkv_rows: float32 [768], P('dp'), may hold values from 1474.56 to 23592.96
- qkv_cols: float32 [3, 768], P(None, 'mp'), may hold values from 2949.12 to 11796.48
- out_rows: float32 [768], P(('mp', 'dp')), may hold values from 1474.56 to 23592.96
- out_cols: float32 [768], replicated, may hold values from 2949.12 to 11796.48
- up_rows: float32 [768], P('dp'), may hold values from 1966.08 to 31457.28
- up_cols: float32 [3072], P('mp'), may hold values from 3932.16 to 15728.64
- down_rows: float32 [3072], P(('mp', 'dp')), may hold values from 5898.24 to 94371.84
- down_cols: float32 [768], replicated, may hold values from 11796.48 to 47185.92
- head_bias_sq: float32 [2, 768], P(None, ('mp', 'dp')), may hold values from 655.36 to 6553.6
- ffn_bias_sq: float32 [3072], P(('mp', 'dp')), may hold values from 2949.12 to 11796.48
- norm_sq: float32 [6, 768], P(None, ('dp', 'mp')), may hold values from 16384 to 131072
Outputs:
- layer_out: bfloat16 [32768, 768], P(('dp', 'mp'))
- pooled: float32 [64, 8, 768], P(('dp', 'mp'))
- input_grad: float32 [32768, 768], P(('dp', 'mp'))
- qkv_grad: float32 [768, 3, 768], P('dp', None, 'mp')
- out_grad: float32 [768, 768], P(('mp', 'dp'))
- up_grad: float32 [768, 3072], P('dp', 'mp')
- down_grad: float32 [3072, 768], P(('mp', 'dp'))
- head_bias_grad: float32 [2, 768], P(None, ('mp', 'dp'))
- ffn_bias_grad: float32 [3072], P(('mp', 'dp'))
- norm_grad: float32 [6, 768], P(None, ('dp', 'mp'))
- qkv_rows_new: float32 [768], P('dp')
- qkv_cols_new: float32 [3, 768], P(None, 'mp')
- out_rows_new: float32 [768], P(('mp', 'dp'))
- out_cols_new: float32 [768], replicated
- up_rows_new: float32 [768], P('dp')
- up_cols_new: float32 [3072], P('mp')
- down_rows_new: float32 [3072], P(('mp', 'dp'))
- down_cols_new: float32 [768], replicated
- head_bias_sq_new: float32 [2, 768], P(None, ('mp', 'dp'))
- ffn_bias_sq_new: float32 [3072], P(('mp', 'dp'))
- norm_sq_new: float32 [6, 768], P(None, ('dp', 'mp'))
- qkv_new: float32 [768, 3, 768], P('dp', None, 'mp')
- out_new: float32 [768, 768], P(('mp', 'dp'))
- up_new: float32 [768, 3072], P('dp', 'mp')
- down_new: float32 [3072, 768], P(('mp', 'dp'))
- head_bias_new: float32 [2, 768], P(None, ('mp', 'dp'))
- ffn_bias_new: float32 [3072], P(('mp', 'dp'))
- norm_new: float32 [6, 768], P(None, ('dp', 'mp'))
Inputs may be any that keep to these rules, and one draw needn't show every extreme that they name: `seg_lengths`: in each row the 8 lengths sum to 480 and the largest is exactly 256; the positions after them are padding.
All inputs are finite; a program needn't handle non-finite values.
Results may differ from a plain program's by a relative error of at most 0.015.
Values may be sent and summed in bfloat16 or wider, within the bound.
A program may use at most 192 MiB of HBM per device.

v0:
```python
import jax
import jax.numpy as jnp
from jax import lax
from jax.sharding import PartitionSpec as P

D = 768
HD = 64
FF = 3072
LEN = 512
SEGS = 8


EPS_NORM = 1e-12
EPS_SQUARE = 1e-30
DECAY = 0.5
RATE = 3.0
CLIP = 0.3
HIGHEST = lax.Precision.HIGHEST


def layer_norm(values, gain, shift):
    center = values - jnp.mean(values, axis=-1, keepdims=True)
    spread = jnp.mean(center * center, axis=-1, keepdims=True)
    return center * lax.rsqrt(spread + EPS_NORM) * gain + shift


def gelu_exact(values):
    return jax.nn.gelu(values, approximate=False)


def segment_ids(lengths, length):
    bounds = jnp.cumsum(lengths, axis=-1)
    places = jnp.arange(length, dtype=jnp.int32)
    return jnp.sum((places[None, :, None] >= bounds[:, None, :]).astype(jnp.int32), axis=-1)


def join_rows(values):
    return lax.all_gather(values, "mp", axis=0, tiled=True)


def split_sums(values):
    return lax.psum_scatter(values, "mp", scatter_dimension=0, tiled=True)


def row_scores(packed, row_ids):
    scores = jnp.einsum(
        "qhd,khd->hqk", packed[:, 0], packed[:, 1], preferred_element_type=jnp.float32
    ) * HD ** (-0.5)
    same = row_ids[:, None] == row_ids[None, :]
    return jnp.where(same[None], scores, -1e30)


def attend_row(packed, row_ids):
    scores = row_scores(packed, row_ids)
    peak = jnp.max(scores, axis=-1, keepdims=True)
    raised = jnp.exp(scores - peak)
    total = jnp.sum(raised, axis=-1, keepdims=True)
    probs = raised / total
    context = jnp.einsum(
        "hqk,khd->qhd", probs.astype(jnp.bfloat16), packed[:, 2], preferred_element_type=jnp.float32
    )
    return (
        context.astype(jnp.bfloat16).reshape(context.shape[0], -1),
        (peak + jnp.log(total))[..., 0],
    )


def attend_back(packed, grad_context, log_total, row_ids):
    scores = row_scores(packed, row_ids)
    probs = jnp.exp(scores - log_total[..., None])
    grad_values = jnp.einsum(
        "hqk,qhd->khd", probs.astype(jnp.bfloat16), grad_context, preferred_element_type=jnp.float32
    )
    grad_probs = jnp.einsum(
        "qhd,khd->hqk", grad_context, packed[:, 2], preferred_element_type=jnp.float32
    )
    inner_sum = jnp.sum(probs * grad_probs, axis=-1, keepdims=True)
    grad_scores = (probs * (grad_probs - inner_sum)).astype(jnp.bfloat16)
    grad_queries = jnp.einsum(
        "hqk,khd->qhd", grad_scores, packed[:, 1], preferred_element_type=jnp.float32
    ) * HD ** (-0.5)
    grad_keys = jnp.einsum(
        "hqk,qhd->khd", grad_scores, packed[:, 0], preferred_element_type=jnp.float32
    ) * HD ** (-0.5)
    return jnp.stack([grad_queries, grad_keys, grad_values], axis=1).astype(jnp.bfloat16)


def body(
    tokens,
    cotangent,
    seg_lengths,
    w_qkv,
    w_out,
    w_up,
    w_down,
    head_bias,
    ffn_bias,
    norm_bias,
    qkv_rows,
    qkv_cols,
    out_rows,
    out_cols,
    up_rows,
    up_cols,
    down_rows,
    down_cols,
    head_bias_sq,
    ffn_bias_sq,
    norm_sq,
):
    f32 = jnp.float32
    tensor_count = lax.axis_size("mp")
    data_count = lax.axis_size("dp")
    tensor_index = lax.axis_index("mp")
    gathered = (
        lax.all_gather(w_qkv.astype(jnp.bfloat16), "dp", axis=0, tiled=True),
        lax.all_gather(w_out.astype(jnp.bfloat16), "dp", axis=0, tiled=True),
        lax.all_gather(w_up.astype(jnp.bfloat16), "dp", axis=0, tiled=True),
        lax.all_gather(w_down.astype(jnp.bfloat16), "dp", axis=0, tiled=True),
        lax.all_gather(head_bias.astype(jnp.bfloat16), "dp", axis=1, tiled=True),
        lax.all_gather(ffn_bias.astype(jnp.bfloat16), "dp", axis=0, tiled=True),
    )
    norm_values = lax.all_gather(
        norm_bias.astype(jnp.bfloat16), ("dp", "mp"), axis=1, tiled=True
    ).astype(f32)
    width = D
    local_width = w_qkv.shape[2]
    own_tokens = tokens.shape[0]
    own_rows = own_tokens // LEN
    ids = segment_ids(seg_lengths, LEN)
    own_ids = lax.dynamic_slice_in_dim(ids, tensor_index * own_rows, own_rows, 0)
    own_lengths = lax.dynamic_slice_in_dim(seg_lengths, tensor_index * own_rows, own_rows, 0)
    qkv_weight, out_weight, up_weight, down_weight, head_offsets, ffn_offsets = gathered
    attn_width = qkv_weight.shape[2]
    heads_here = attn_width // HD
    group_rows = ids.shape[0]
    group_tokens = group_rows * LEN
    tokens_all = join_rows(tokens)
    qkv_flat = qkv_weight.reshape(width, 3 * attn_width)
    offsets = jnp.stack([head_offsets[0], jnp.zeros_like(head_offsets[0]), head_offsets[1]]).astype(
        f32
    )
    projected = (
        jnp.dot(tokens_all, qkv_flat, preferred_element_type=f32).reshape(
            group_tokens, 3, attn_width
        )
        + offsets
    )
    packed_rows = projected.astype(jnp.bfloat16).reshape(group_rows, LEN, 3, heads_here, HD)
    context_rows, log_totals = lax.map(
        lambda pair: attend_row(pair[0], pair[1]), (packed_rows, ids)
    )
    context = context_rows.reshape(group_tokens, attn_width)
    attended = split_sums(jnp.dot(context, out_weight, preferred_element_type=f32)) + norm_values[0]
    hidden, norm_one_back = jax.vjp(
        layer_norm, tokens.astype(f32) + attended, norm_values[2], norm_values[3]
    )
    hidden_all = join_rows(hidden.astype(jnp.bfloat16))
    inner = jnp.dot(hidden_all, up_weight, preferred_element_type=f32) + ffn_offsets.astype(f32)
    activated, gelu_back = jax.vjp(gelu_exact, inner)
    activated_b = activated.astype(jnp.bfloat16)
    branch = (
        split_sums(jnp.dot(activated_b, down_weight, preferred_element_type=f32)) + norm_values[1]
    )
    output, norm_two_back = jax.vjp(layer_norm, hidden + branch, norm_values[4], norm_values[5])
    member = (own_ids[:, None, :] == jnp.arange(SEGS, dtype=jnp.int32)[None, :, None]).astype(f32)
    pooled = jnp.einsum(
        "rsl,rld->rsd", member, output.reshape(own_rows, LEN, width), precision=HIGHEST
    )
    pooled = pooled / own_lengths[:, :, None].astype(f32)
    grad_res_two, grad_gain_two, grad_shift_two = norm_two_back(cotangent.astype(f32))
    grad_branch = grad_res_two.astype(jnp.bfloat16)
    grad_bias_down = jnp.sum(grad_branch.astype(f32), axis=0)
    branch_all = join_rows(grad_branch)
    grad_act = jnp.dot(branch_all, down_weight.T, preferred_element_type=f32)
    grad_down = jnp.dot(activated_b.T, branch_all, preferred_element_type=f32)
    grad_inner = gelu_back(grad_act)[0].astype(jnp.bfloat16)
    grad_bias_up = jnp.sum(grad_inner.astype(f32), axis=0)
    grad_up = jnp.dot(hidden_all.T, grad_inner, preferred_element_type=f32)
    grad_hidden = grad_res_two + split_sums(
        jnp.dot(grad_inner, up_weight.T, preferred_element_type=f32)
    )
    grad_res_one, grad_gain_one, grad_shift_one = norm_one_back(grad_hidden)
    grad_attended = grad_res_one.astype(jnp.bfloat16)
    grad_bias_out = jnp.sum(grad_attended.astype(f32), axis=0)
    attended_all = join_rows(grad_attended)
    grad_context = jnp.dot(attended_all, out_weight.T, preferred_element_type=f32).astype(
        jnp.bfloat16
    )
    grad_out = jnp.dot(context.T, attended_all, preferred_element_type=f32)
    grad_rows = lax.map(
        lambda item: attend_back(item[0], item[1], item[2], item[3]),
        (packed_rows, grad_context.reshape(group_rows, LEN, heads_here, HD), log_totals, ids),
    )
    grad_packed = grad_rows.reshape(group_tokens, 3, attn_width)
    grad_head = jnp.stack(
        [
            jnp.sum(grad_packed[:, 0].astype(f32), axis=0),
            jnp.sum(grad_packed[:, 2].astype(f32), axis=0),
        ]
    )
    grad_flat = grad_packed.reshape(group_tokens, 3 * attn_width)
    grad_qkv = jnp.dot(tokens_all.T, grad_flat, preferred_element_type=f32).reshape(
        width, 3, attn_width
    )
    input_grad = grad_res_one + split_sums(
        jnp.dot(grad_flat, qkv_flat.T, preferred_element_type=f32)
    )
    norm_terms = jnp.stack(
        [
            grad_bias_out,
            grad_bias_down,
            grad_gain_one,
            grad_shift_one,
            grad_gain_two,
            grad_shift_two,
        ]
    )
    norm_grad = lax.psum_scatter(norm_terms, ("dp", "mp"), scatter_dimension=1, tiled=True)
    red_qkv, red_out, red_up, red_down, red_head, red_ffn = (
        lax.psum_scatter(grad_qkv, "dp", scatter_dimension=0, tiled=True),
        lax.psum_scatter(grad_out, "dp", scatter_dimension=0, tiled=True),
        lax.psum_scatter(grad_up, "dp", scatter_dimension=0, tiled=True),
        lax.psum_scatter(grad_down, "dp", scatter_dimension=0, tiled=True),
        lax.psum_scatter(grad_head, "dp", scatter_dimension=1, tiled=True),
        lax.psum_scatter(grad_bias_up, "dp", scatter_dimension=0, tiled=True),
    )
    rows_qkv = width // data_count
    weights_flat = [w_qkv.reshape(rows_qkv, -1), w_out, w_up, w_down]
    grads_flat = [red_qkv.reshape(rows_qkv, -1), red_out, red_up, red_down]
    rows_old = [qkv_rows, out_rows, up_rows, down_rows]
    cols_old = [qkv_cols.reshape(-1), out_cols, up_cols, down_cols]
    col_count = [3 * width, width, FF, width]
    row_count = [width, width, width, FF]
    row_share = [tensor_count, 1, tensor_count, 1]
    squares = [grad * grad + EPS_SQUARE for grad in grads_flat]
    row_parts = [jnp.sum(square, axis=1) for square in squares]
    col_parts = [jnp.sum(square, axis=0) for square in squares]
    vec_weights = [head_bias, ffn_bias, norm_bias]
    vec_grads = [red_head, red_ffn, norm_grad]
    vec_old = [head_bias_sq, ffn_bias_sq, norm_sq]
    vec_counts = [2 * width, FF, 6 * width]
    vec_second = [
        DECAY * old + (1.0 - DECAY) * (grad * grad + EPS_SQUARE)
        for old, grad in zip(vec_old, vec_grads)
    ]
    vec_update = [grad * lax.rsqrt(second) for grad, second in zip(vec_grads, vec_second)]
    weight_parts = [jnp.sum(weight * weight) for weight in weights_flat + vec_weights]
    vec_parts = [jnp.sum(update * update) for update in vec_update]
    row_qkv, row_up = lax.psum((row_parts[0], row_parts[2]), "mp")
    col_qkv, col_up = lax.psum((col_parts[0], col_parts[2]), "dp")
    col_out, col_down = lax.psum((col_parts[1], col_parts[3]), ("dp", "mp"))
    row_sums = [row_qkv, row_parts[1], row_up, row_parts[3]]
    col_sums = [col_qkv, col_out, col_up, col_down]
    rows_new = [
        DECAY * rows_old[index] + (1.0 - DECAY) * row_sums[index] / col_count[index]
        for index in range(4)
    ]
    cols_new = [
        DECAY * cols_old[index] + (1.0 - DECAY) * col_sums[index] / row_count[index]
        for index in range(4)
    ]
    ratio_parts = [
        jnp.sum(
            grads_flat[index]
            * grads_flat[index]
            / (rows_new[index][:, None] * cols_new[index][None, :])
        )
        for index in range(4)
    ]
    extra_parts = (
        [jnp.sum(rows_new[index]) / row_share[index] for index in range(4)]
        + weight_parts
        + vec_parts
    )
    totals = lax.psum(jnp.stack(ratio_parts + extra_parts), ("dp", "mp"))
    row_means = [totals[4 + index] / row_count[index] for index in range(4)]
    weight_totals = [totals[8 + index] for index in range(7)]
    vec_totals = [totals[15 + index] for index in range(3)]
    new_mats = []
    for index in range(4):
        entries = row_count[index] * col_count[index]
        estimate = rows_new[index][:, None] * cols_new[index][None, :] / row_means[index]
        update = grads_flat[index] / jnp.sqrt(estimate)
        update_rms = jnp.sqrt(row_means[index] * totals[index] / entries)
        stride = (
            RATE * jnp.sqrt(weight_totals[index] / entries) / jnp.maximum(1.0, update_rms / CLIP)
        )
        new_mats.append(weights_flat[index] - stride * update)
    new_vecs = []
    for index in range(3):
        update_rms = jnp.sqrt(vec_totals[index] / vec_counts[index])
        stride = (
            RATE
            * jnp.sqrt(weight_totals[4 + index] / vec_counts[index])
            / jnp.maximum(1.0, update_rms / CLIP)
        )
        new_vecs.append(vec_weights[index] - stride * vec_update[index])
    return (
        output.astype(jnp.bfloat16),
        pooled,
        input_grad,
        red_qkv,
        red_out,
        red_up,
        red_down,
        red_head,
        red_ffn,
        norm_grad,
        rows_new[0],
        cols_new[0].reshape(3, local_width),
        rows_new[1],
        cols_new[1],
        rows_new[2],
        cols_new[2],
        rows_new[3],
        cols_new[3],
        vec_second[0],
        vec_second[1],
        vec_second[2],
        new_mats[0].reshape(rows_qkv, 3, local_width),
        new_mats[1],
        new_mats[2],
        new_mats[3],
        new_vecs[0],
        new_vecs[1],
        new_vecs[2],
    )


def solution(mesh):
    return jax.shard_map(
        body,
        mesh=mesh,
        in_specs=(
            P(("dp", "mp"), None),
            P(("dp", "mp"), None),
            P("dp", None),
            P("dp", None, "mp"),
            P(("mp", "dp"), None),
            P("dp", "mp"),
            P(("mp", "dp"), None),
            P(None, ("mp", "dp")),
            P(("mp", "dp")),
            P(None, ("dp", "mp")),
            P("dp"),
            P(None, "mp"),
            P(("mp", "dp")),
            P(),
            P("dp"),
            P("mp"),
            P(("mp", "dp")),
            P(),
            P(None, ("mp", "dp")),
            P(("mp", "dp")),
            P(None, ("dp", "mp")),
        ),
        out_specs=(
            P(("dp", "mp"), None),
            P(("dp", "mp"), None, None),
            P(("dp", "mp"), None),
            P("dp", None, "mp"),
            P(("mp", "dp"), None),
            P("dp", "mp"),
            P(("mp", "dp"), None),
            P(None, ("mp", "dp")),
            P(("mp", "dp")),
            P(None, ("dp", "mp")),
            P("dp"),
            P(None, "mp"),
            P(("mp", "dp")),
            P(),
            P("dp"),
            P("mp"),
            P(("mp", "dp")),
            P(),
            P(None, ("mp", "dp")),
            P(("mp", "dp")),
            P(None, ("dp", "mp")),
            P("dp", None, "mp"),
            P(("mp", "dp"), None),
            P("dp", "mp"),
            P(("mp", "dp"), None),
            P(None, ("mp", "dp")),
            P(("mp", "dp")),
            P(None, ("dp", "mp")),
        ),
        check_vma=False,
    )
```

profile of v0, /device:TPU:0, one launch (start us, length us, event | category | flops | bytes accessed | tf_op | source)
XLA Modules:
  0.0 1167.8 jit_solution(2269260173216503008)
XLA Ops:
  11.8 42.3 %all-gather = bf16[16,24,2]{1,2,0:T(2,128)(2,1)S(1)} all-gather(bf16[1,24,2]{1,2,0:T(2,128)(2,1)S(1)} %get-tuple-element.252), channel_id=1, replica_groups=mesh['dp'=16,'mp'=2] {'dp'}, dimensions={0}, use_global_device_ids=true | all-gather | bytes 1632 | tf_op jit(solution)/shard_map/all_gather | solution.py:120
  56.9 41.0 %all_gather.36 = bf16[384,768]{1,0:T(8,128)(2,1)S(1)} all-gather(bf16[24,768]{1,0:T(8,128)(2,1)S(1)} %get-tuple-element.246), channel_id=1, replica_groups=mesh['dp'=16,'mp'=2] {'dp'}, dimensions={0}, use_global_device_ids=true | all-gather | bytes 626688 | tf_op jit(solution)/shard_map/all_gather | solution.py:117
  116.6 8.9 reshape.414
  131.1 28.0 %while.22 = (s32[]{:T(128)}, bf16[4,512,384]{2,1,0:T(8,128)(2,1)S(1)}, f32[4,6,512]{2,1,0:T(8,128)}, bf16[4,512,3,6,64]{1,4,3,2,0:T(8,128)(2,1)}, s32[4,512]{1,0:T(4,128)S(1)}, /*index=5*/s32[]{:T(128)}) while((s32[]{:T(128)}, bf16[4,512,384]{2,1,0:T(8,128)(2,1)S(1)}, f32[4,6,512]{2,1,0:T(8,128)}, bf16[4,512,3,6,64]{1,4,3,2,0:T(8,128)(2,1)}, ...), condition=%wide.region_5.6_spmd, body=%wide.region_2.5_spmd.sunk | while | flops 421983232 | bytes 25545296 | solution.py:150
  166.7 37.9 %all-gather.1 = bf16[32,24,6]{1,2,0:T(8,128)(2,1)S(1)} all-gather(bf16[1,24,6]{1,2,0:T(8,128)(2,1)S(1)} %get-tuple-element.248), channel_id=1, replica_groups=mesh['dp'=16,'mp'=2] {'dp','mp'}, dimensions={0}, use_global_device_ids=true | all-gather | bytes 9504 | tf_op jit(solution)/shard_map/all_gather | solution.py:123
  214.2 37.9 %all-reduce = bf16[1536]{0:T(1024)(128)(2,1)S(1)} all-reduce(bf16[1536]{0:T(1024)(128)(2,1)S(1)} %dynamic-update-slice), channel_id=1, replica_groups=mesh['dp'=16,'mp'=2] {'dp'}, use_global_device_ids=true, to_apply=%add | all-reduce | flops 1536 | bytes 6144
  255.8 34.9 %multiply_convert_fusion.1 = (bf16[2048,1536]{1,0:T(8,128)(2,1)}, f32[2048,1536]{1,0:T(8,128)}, f32[2048,1536]{1,0:T(8,128)}) fusion(f32[1536]{0:T(1024)S(1)} %convert_element_type.124, bf16[2048,768]{1,0:T(8,128)(2,1)} %all-gather.14.cloned.1.call-done, bf16[768,1536]{1,0:T(8,128)(2,1)} %all-gather.16.cloned.1.call-done), kind=kOutput, calls=%fused_computation.54 | convolution fusion | flops 5039456256 | bytes 36968448 | tf_op jit(solution)/shard_map/dot_general | solution.py:159
  290.7 32.2 %all-gather.18.cloned.1.call-done = bf16[1536,768]{1,0:T(8,128)(2,1)} async-done(((bf16[96,768]{1,0:T(8,128)(2,1)}), bf16[1536,768]{1,0:T(8,128)(2,1)}) %all-gather.18.cloned.1.call-update) | async-done | bytes 2359312 | tf_op jit(solution)/shard_map/all_gather | solution.py:119
  322.9 9.6 fusion.81
  333.0 13.0 %reduce-scatter.13.cloned.1.call-done = f32[1024,768]{1,0:T(8,128)} async-done(((f32[2048,768]{1,0:T(8,128)}), f32[1024,768]{1,0:T(8,128)}) %reduce-scatter.13.cloned.1.call-update) | async-done | bytes 3145744 | tf_op jit(solution)/shard_map/reduce_scatter | solution.py:42
  359.1 13.4 %all-gather.20.cloned.1.call-done = bf16[2048,768]{1,0:T(8,128)(2,1)} async-done(((bf16[1024,768]{1,0:T(8,128)(2,1)}), bf16[2048,768]{1,0:T(8,128)(2,1)}) %all-gather.20.cloned.1.call-update) | async-done | bytes 3145744 | tf_op jit(solution)/shard_map/all_gather | solution.py:38
  372.5 19.4 %convert_reduce_fusion = (f32[1536]{0:T(1024)}, bf16[2048,1536]{1,0:T(8,128)(2,1)}) fusion(f32[2048,1536]{1,0:T(8,128)} %get-tuple-element.230, bf16[2048,768]{1,0:T(8,128)(2,1)} %all-gather.20.cloned.1.call-done, bf16[1536,768]{1,0:T(8,128)(2,1)} %all-gather.18.cloned.1.call-done, f32[2048,1536]{1,0:T(8,128)} %get-tuple-element.275, ...), kind=kOutput, calls=%fused_computation.52 | convolution fusion | flops 4885314048 | bytes 36974592 | tf_op jit(solution)/shard_map/dot_general | solution.py:175
  391.8 9.7 fusion.82
  401.6 15.8 %reduce-scatter.15.cloned.1.call-done = f32[1024,768]{1,0:T(8,128)} async-done(((f32[2048,768]{1,0:T(8,128)}), f32[1024,768]{1,0:T(8,128)}) %reduce-scatter.15.cloned.1.call-update) | async-done | bytes 3145744 | tf_op jit(solution)/shard_map/reduce_scatter | solution.py:42
  438.1 9.5 fusion.86
  460.0 55.6 %while.23 = (s32[]{:T(128)}, bf16[4,512,3,6,64]{1,4,3,2,0:T(8,128)(2,1)}, bf16[4,512,3,6,64]{1,4,3,2,0:T(8,128)(2,1)}, s32[4,512]{1,0:T(4,128)S(1)}, f32[4,6,512...) while((s32[]{:T(128)}, bf16[4,512,3,6,64]{1,4,3,2,0:T(8,128)(2,1)}, ...), condition=%wide.region_19.20_spmd, body=%wide.region_17.19_spmd.sunk | while | flops 1035006976 | bytes 69565592 | solution.py:191
  546.1 38.8 %reduce-scatter.25.cloned.1.call-done = f32[96,768]{1,0:T(8,128)} async-done(((f32[1536,768]{1,0:T(8,128)}), f32[96,768]{1,0:T(8,128)}) %reduce-scatter.25.cloned.1.call-update) | async-done | bytes 294928 | tf_op jit(solution)/shard_map/reduce_scatter | solution.py:224
  586.0 140.8 %reduce-scatter.23.cloned.1.call-done = f32[48,1536]{1,0:T(8,128)} async-done(((f32[768,1536]{1,0:T(8,128)}), f32[48,1536]{1,0:T(8,128)}) %reduce-scatter.23.cloned.1.call-update) | async-done | bytes 294928 | tf_op jit(solution)/shard_map/reduce_scatter | solution.py:223
  740.1 115.5 %reduce-scatter.21.cloned.1.call-done = f32[24,768]{1,0:T(8,128)} async-done(((f32[384,768]{1,0:T(8,128)}), f32[24,768]{1,0:T(8,128)}) %reduce-scatter.21.cloned.1.call-update) | async-done | bytes 73744 | tf_op jit(solution)/shard_map/reduce_scatter | solution.py:222
  856.7 40.7 %all-reduce.4 = (f32[6,768]{1,0:T(8,128)S(1)}, f32[768]{0:T(1024)S(1)}, f32[768]{0:T(1024)S(1)}) all-reduce(f32[6,768]{1,0:T(8,128)S(1)} %stack.100, f32[768]{0:T(1024)S(1)} %get-tuple-element.160, f32[768]{0:T(1024)S(1)} %get-tuple-element.154), channel_id=12, replica_groups=mesh['dp'=16,'mp'=2] {'dp','mp'}, use_global_device_ids=true, to_apply=%region_36.37.clone | all-reduce | flops 6144 | bytes 49152
  901.8 92.6 %reduce-scatter.19.cloned.1.call-done = f32[48,3,384]{2,0,1:T(8,128)} async-done(((f32[768,3,384]{2,0,1:T(8,128)}), f32[48,3,384]{2,0,1:T(8,128)}) %reduce-scatter.19.cloned.1.call-update) | async-done | bytes 221200 | tf_op jit(solution)/shard_map/reduce_scatter | solution.py:221
  995.5 75.0 %all-reduce.5 = (f32[2,384]{1,0:T(2,128)}, f32[1536]{0:T(1024)}, f32[1152]{0:T(1024)S(1)}, f32[1536]{0:T(1024)S(1)}) all-reduce(f32[2,384]{1,0:T(2,128)S(1)} %pad_maximum_fusion, f32[1536]{0:T(1024)S(1)} %copy-done.34, f32[1152]{0:T(1024)S(1)} %reduce_sum.468, ...), channel_id=10, replica_groups=mesh['dp'=16,'mp'=2] {'dp'}, use_global_device_ids=true, to_apply=%region_27.28.clone | all-reduce | flops 4992 | bytes 39936
  1081.4 10.8 stack.119
  1095.8 37.1 %psum.55 = f32[18]{0:T(128)S(1)} all-reduce(f32[18]{0:T(128)} %stack.119), channel_id=1, replica_groups=mesh['dp'=16,'mp'=2] {'dp','mp'}, use_global_device_ids=true, to_apply=%region_69.70 | all-reduce | flops 18 | bytes 144 | tf_op jit(solution)/shard_map/psum | solution.py:276
  (343 shorter events, 259.9 us)
Async XLA Ops:
  7.2 90.7 %all-gather.12.cloned.1.call-start = ((), (), s32[]{:S(2)}) async-start(), calls=%async_computation.9 | async-start | bytes 1880064 | tf_op jit(solution)/shard_map/all_gather | solution.py:116
  9.6 92.4 %all-gather.10.cloned.1.call-start = ((), (), s32[]{:S(2)}) async-start(), calls=%async_computation.8 | async-start | bytes 4718592 | tf_op jit(solution)/shard_map/all_gather | solution.py:38
  10.3 194.6 %reduce-scatter.11.cloned.1.call-start = ((), (), s32[]{:S(2)}) async-start(), calls=%async_computation.10 | async-start | bytes 9437184 | tf_op jit(solution)/shard_map/reduce_scatter | solution.py:42
  163.7 88.5 %all-gather.16.cloned.1.call-start = ((), (), s32[]{:S(2)}) async-start(), calls=%async_computation.12 | async-start | bytes 2506752 | tf_op jit(solution)/shard_map/all_gather | solution.py:118
  165.9 89.9 %all-gather.14.cloned.1.call-start = ((), (), s32[]{:S(2)}) async-start(), calls=%async_computation.11 | async-start | bytes 4718592 | tf_op jit(solution)/shard_map/all_gather | solution.py:38
  210.6 112.3 %all-gather.18.cloned.1.call-start = ((), (), s32[]{:S(2)}) async-start(), calls=%async_computation.13 | async-start | bytes 2506752 | tf_op jit(solution)/shard_map/all_gather | solution.py:119
  212.1 134.0 %reduce-scatter.13.cloned.1.call-start = ((), (), s32[]{:S(2)}) async-start(), calls=%async_computation.14 | async-start | bytes 9437184 | tf_op jit(solution)/shard_map/reduce_scatter | solution.py:42
  332.5 39.9 %all-gather.20.cloned.1.call-start = ((), (), s32[]{:S(2)}) async-start(), calls=%async_computation.15 | async-start | bytes 4718592 | tf_op jit(solution)/shard_map/all_gather | solution.py:38
  359.0 58.4 %reduce-scatter.15.cloned.1.call-start = ((), (), s32[]{:S(2)}) async-start(), calls=%async_computation.16 | async-start | bytes 9437184 | tf_op jit(solution)/shard_map/reduce_scatter | solution.py:42
  401.6 46.1 %all-gather.22.cloned.1.call-start = ((), (), s32[]{:S(2)}) async-start(), calls=%async_computation.17 | async-start | bytes 4718592 | tf_op jit(solution)/shard_map/all_gather | solution.py:38
  426.9 158.0 %reduce-scatter.25.cloned.1.call-start = ((), (), s32[]{:S(2)}) async-start(), calls=%async_computation.22 | async-start | bytes 5013504 | tf_op jit(solution)/shard_map/reduce_scatter | solution.py:224
  436.0 290.9 %reduce-scatter.23.cloned.1.call-start = ((), (), s32[]{:S(2)}) async-start(), calls=%async_computation.21 | async-start | bytes 5013504 | tf_op jit(solution)/shard_map/reduce_scatter | solution.py:223
  447.6 408.0 %reduce-scatter.21.cloned.1.call-start = ((), (), s32[]{:S(2)}) async-start(), calls=%async_computation.20 | async-start | bytes 1253376 | tf_op jit(solution)/shard_map/reduce_scatter | solution.py:222
  459.7 534.6 %reduce-scatter.19.cloned.1.call-start = ((), (), s32[]{:S(2)}) async-start(), calls=%async_computation.19 | async-start | bytes 3760128 | tf_op jit(solution)/shard_map/reduce_scatter | solution.py:221
  532.6 624.2 %reduce-scatter.17.cloned.1.call-start = ((), (), s32[]{:S(2)}) async-start(), calls=%async_computation.18 | async-start | bytes 9437184 | tf_op jit(solution)/shard_map/reduce_scatter | solution.py:42
  737.5 258.0 %copy-start.34 = (f32[1536]{0:T(1024)S(1)}, f32[1536]{0:T(1024)}, u32[]{:S(2)}) copy-start(f32[1536]{0:T(1024)} %get-tuple-element.276) | copy-start | bytes 18436
  737.5 335.5 %copy-start.48 = (f32[48]{0:T(128)S(1)}, f32[48]{0:T(128)}, u32[]{:S(2)}) copy-start(f32[48]{0:T(128)} %param.39) | copy-start | bytes 580
  737.5 335.5 %copy-start.49 = (f32[48]{0:T(128)S(1)}, f32[48]{0:T(128)}, u32[]{:S(2)}) copy-start(f32[48]{0:T(128)} %param.35) | copy-start | bytes 580
  737.5 339.1 %copy-start.33 = (f32[1536]{0:T(1024)S(1)}, f32[1536]{0:T(1024)}, u32[]{:S(2)}) copy-start(f32[1536]{0:T(1024)} %param.40) | copy-start | bytes 18436
  737.5 339.1 %copy-start.9 = (f32[48,1536]{1,0:T(8,128)S(1)}, f32[48,1536]{1,0:T(8,128)}, u32[]{:S(2)}) copy-start(f32[48,1536]{1,0:T(8,128)} %reduce-scatter.23.cloned.1.call-done) | copy-start | bytes 884740
  737.5 354.7 %copy-start.30 = (s32[2,512]{1,0:T(2,128)S(1)}, s32[2,512]{1,0:T(2,128)}, u32[]{:S(2)}) copy-start(s32[2,512]{1,0:T(2,128)} %constant_dynamic-slice_fusion.4) | copy-start | bytes 12292
  855.6 294.0 %copy-start.16 = (f32[24,768]{1,0:T(8,128)S(1)}, f32[24,768]{1,0:T(8,128)}, u32[]{:S(2)}) copy-start(f32[24,768]{1,0:T(8,128)} %reduce-scatter.21.cloned.1.call-done) | copy-start | bytes 221188
  898.0 256.9 %copy-start.21 = (f32[768]{0:T(1024)}, f32[768]{0:T(1024)S(1)}, u32[]{:S(2)}) copy-start(f32[768]{0:T(1024)S(1)} %get-tuple-element.280) | copy-start | bytes 9220
  898.0 256.9 %copy-start.24 = (f32[768]{0:T(1024)}, f32[768]{0:T(1024)S(1)}, u32[]{:S(2)}) copy-start(f32[768]{0:T(1024)S(1)} %get-tuple-element.281) | copy-start | bytes 9220
  (51 other events, 2423.9 us)
Sparse Core Ops, SparseCore 0:
  11.3 64.4 all-gather.11
  77.3 10.4 all-gather.9
  163.8 11.4 reduce-scatter.10
  178.9 63.6 all-gather.15
  244.7 11.1 all-gather.13
  259.4 63.4 all-gather.17
  332.7 13.3 reduce-scatter.12
  359.1 13.2 all-gather.19
  401.7 15.6 reduce-scatter.14
  427.0 13.2 all-gather.21
  446.9 137.9 reduce-scatter.24
  590.5 136.2 reduce-scatter.22
  732.9 122.6 reduce-scatter.20
  861.9 132.3 reduce-scatter.18
  996.6 13.6 reduce-scatter.16
where the time goes:
time: 1180 us; the launch traced here: 1170 us
  waiting for transfers between devices  467 us (40%)
  blocking collectives  314 us (27%)
  matrix products  173 us (15%)
  local copies, waits for them, and re-layouts  91.2 us (8%)
  other arithmetic  89.8 us (8%)
  between operations  30.7 us (3%)
    unnamed x3, blocking collectives  154 us
    reduce_scatter x1, waiting for transfers between devices, body(): lax.psum_scatter(grad_up, 'dp', scatter_dimension=0, tiled=True)  141 us
    reduce_scatter x1, waiting for transfers between devices, body(): lax.psum_scatter(grad_out, 'dp', scatter_dimension=0, tiled=True)  116 us
    reduce_scatter x1, waiting for transfers between devices, body(): lax.psum_scatter(grad_qkv, 'dp', scatter_dimension=0, tiled=True)  92.6 us
    all_gather x1, blocking collectives, body(): lax.all_gather(head_bias.astype(jnp.bfloat16), 'dp', axis=1, tiled=True)  42.3 us
    all_gather x1, blocking collectives, body(): lax.all_gather(w_out.astype(jnp.bfloat16), 'dp', axis=0, tiled=True)  41 us
    reduce_scatter x1, waiting for transfers between devices, body(): lax.psum_scatter(grad_down, 'dp', scatter_dimension=0, tiled=True)  38.8 us
    all_gather x1, blocking collectives, body(): lax.all_gather(norm_bias.astype(jnp.bfloat16), ('dp', 'mp'), axis=1, tile...  37.9 us
  transfers between devices with their start and end apart: 15, of which 9 were waited for; matrix products, arithmetic and copies ran while one was open for 19% of the time, Pallas kernels for 0%

commit v1 on v0

v1 whole, which is shorter than its diff:
```python
import functools

import jax
import jax.numpy as jnp
from jax import lax
from jax.experimental import pallas as pl
from jax.experimental.pallas import tpu as pltpu
from jax.sharding import PartitionSpec as P

D = 768
HD = 64
FF = 3072
LEN = 512
SEGS = 8

EPS_NORM = 1e-12
EPS_SQUARE = 1e-30
DECAY = 0.5
RATE = 3.0
CLIP = 0.3

MESH = pl.DeviceIdType.MESH
BF = jnp.bfloat16
F32 = jnp.float32
EVERY = slice(None)


class Place:
    def __init__(self):
        d = lax.axis_index("dp")
        self.m = lax.axis_index("mp")
        self.z, self.y, self.x = d // 4, (d // 2) % 2, d % 2

    def at(self, axis, step):
        size = 4 if axis == "z" else 2
        spot = {"z": self.z, "y": self.y, "x": self.x, "m": self.m}
        spot[axis] = (spot[axis] + step) % size
        return spot

    @staticmethod
    def device(spot):
        return (spot["z"] * 4 + spot["y"] * 2 + spot["x"], spot["m"])


def steps_of(axis):
    return (1, 2, 3) if axis == "z" else (1,)


def greet(place):
    barrier = pltpu.get_barrier_semaphore()
    count = 0
    for axis in "zyxm":
        for step in steps_of(axis):
            pl.semaphore_signal(
                barrier, inc=1, device_id=place.device(place.at(axis, step)), device_id_type=MESH
            )
            count += 1
    pl.semaphore_wait(barrier, count)


def column_parts(cols):
    tiles = cols // 128
    first = tiles // 3
    parts = [("yzx", 0, first * 128)] if first else []
    return parts + [("zxy", first * 128, cols - first * 128)]


class Gatherer:
    def __init__(self, place, shard, full, part, sems, base):
        order, start, width = part
        self.place, self.shard, self.full = place, shard, full
        self.cols = pl.ds(start, width)
        self.order = order + "m"
        self.sems, self.base = sems, base

    def view(self, spot):
        return self.full.at[spot["m"], spot["z"], spot["y"], spot["x"], :, self.cols]

    def copies(self, stage):
        place, axis = self.place, self.order[stage]
        out = []
        for step in steps_of(axis):
            spot = {"z": place.z, "y": place.y, "x": place.x, "m": place.m}
            for done in self.order[:stage]:
                spot[done] = EVERY
            target = place.at(axis, step)
            send, recv = self.sems
            slot = self.base + 4 * stage + step
            source = self.shard.at[:, self.cols] if stage == 0 else self.view(spot)
            sent = pltpu.make_async_remote_copy(
                source, self.view(spot), send.at[slot], recv.at[slot],
                device_id=place.device(target), device_id_type=MESH)
            spot = dict(spot)
            spot[axis] = place.at(axis, -step)[axis]
            arrives = pltpu.make_async_remote_copy(
                self.view(spot), self.view(spot), send.at[slot], recv.at[slot],
                device_id=place.device(target), device_id_type=MESH)
            out.append((sent, arrives))
        return out

    def start(self, stage):
        for sent, _ in self.copies(stage):
            sent.start()

    def arrived(self, stage):
        for _, arrives in self.copies(stage):
            arrives.wait_recv()

    def finish(self):
        for stage in range(4):
            for sent, _ in self.copies(stage):
                sent.wait_send()


def gather_kernel(count, *refs):
    shards, fulls = refs[:count], refs[count:2 * count]
    cast = refs[2 * count:3 * count]
    send, recv, local = refs[3 * count:]
    place = Place()
    greet(place)
    paths, base = [], 0
    locals_ = []
    for index in range(count):
        rows = shards[index].shape[0]
        held = cast[index].shape[0]
        value = shards[index][...]
        if held != rows:
            value = jnp.concatenate([value, jnp.zeros((held - rows, value.shape[1]), F32)], 0)
        cast[index][...] = value.astype(cast[index].dtype)
        own = pltpu.make_async_copy(
            cast[index], fulls[index].at[place.m, place.z, place.y, place.x], local.at[index])
        own.start()
        locals_.append(own)
        group = []
        for part in column_parts(cast[index].shape[1]):
            group.append(Gatherer(place, cast[index], fulls[index], part, (send, recv), base))
            base += 16
        for path in group:
            path.start(0)
        paths.append(group)
    for own in locals_:
        own.wait()
    for turn in range(count + 3):
        for index in range(count):
            stage = turn - index + 1
            if 1 <= stage <= 3:
                for path in paths[index]:
                    path.arrived(stage - 1)
                    path.start(stage)
    for group in paths:
        for path in group:
            path.arrived(3)
    for group in paths:
        for path in group:
            path.finish()


def gather(shards, kinds):
    held = [(s.shape[0] + (-s.shape[0]) % (16 if k == BF else 8), s.shape[1])
            for s, k in zip(shards, kinds)]
    count = len(shards)
    slots = 16 * sum(len(column_parts(h[1])) for h in held)
    outs = pl.pallas_call(
        functools.partial(gather_kernel, count),
        out_shape=[jax.ShapeDtypeStruct((2, 4, 2, 2) + h, k) for h, k in zip(held, kinds)],
        in_specs=[pl.BlockSpec(memory_space=pltpu.VMEM)] * count,
        out_specs=[pl.BlockSpec(memory_space=pl.ANY)] * count,
        scratch_shapes=[pltpu.VMEM(h, k) for h, k in zip(held, kinds)] + [
            pltpu.SemaphoreType.DMA((slots,)),
            pltpu.SemaphoreType.DMA((slots,)),
            pltpu.SemaphoreType.DMA((count,)),
        ],
        compiler_params=pltpu.CompilerParams(
            collective_id=0, has_side_effects=True, vmem_limit_bytes=48 << 20),
        name="gather_weights",
    )(*shards)
    return outs


class Scatterer:
    def __init__(self, place, held, part, slots, sems, base):
        order, start, width = part
        self.place, self.held = place, held
        self.order = order[::-1]
        self.start_col, self.width = start, width
        self.cols = pl.ds(start, width)
        self.slots = slots
        self.sems, self.base = sems, base

    def view(self, spot):
        return self.held.at[spot["z"], spot["y"], spot["x"], :, self.cols]

    def copies(self, stage):
        place, axis = self.place, self.order[stage]
        out = []
        for step in steps_of(axis):
            spot = {"z": EVERY, "y": EVERY, "x": EVERY}
            for done in self.order[:stage]:
                spot[done] = getattr(place, done)
            target = place.at(axis, step)
            spot[axis] = target[axis]
            send, recv = self.sems
            slot = self.base + 4 * stage + step
            land = self.slots[stage].at[step - 1]
            out.append(pltpu.make_async_remote_copy(
                self.view(spot), land, send.at[slot], recv.at[slot],
                device_id=place.device(target), device_id_type=MESH))
        return out

    def start(self, stage):
        for sent in self.copies(stage):
            sent.start()

    def add(self, stage, result=None):
        place, axis = self.place, self.order[stage]
        for sent in self.copies(stage):
            sent.wait_recv()
        left = [name for name in "zyx" if name not in self.order[:stage + 1]]
        sizes = [4 if name == "z" else 2 for name in left]
        total = 1
        for size in sizes:
            total *= size
        slots = self.slots[stage]
        arrivals = len(steps_of(axis))

        def one(index):
            spot = {name: getattr(place, name) for name in "zyx"}
            inner = []
            rest = index
            for name, size in reversed(list(zip(left, sizes))):
                spot[name] = rest % size
                inner.insert(0, rest % size)
                rest = rest // size
            where = (spot["z"], spot["y"], spot["x"], EVERY, self.cols)
            value = self.held[where].astype(F32)
            for arrival in range(arrivals):
                value = value + slots[tuple([arrival] + inner)].astype(F32)
            if result is None:
                self.held[where] = value.astype(self.held.dtype)
            else:
                result[:, self.cols] = value[:result.shape[0]]

        if total == 1:
            one(0)
        else:
            pl.loop(0, total)(one)

    def finish(self):
        for stage in range(3):
            for sent in self.copies(stage):
                sent.wait_send()


def slot_shapes(part, rows):
    order, _, width = part
    order = order[::-1]
    shapes = []
    for stage in range(3):
        left = [4 if name == "z" else 2 for name in "zyx" if name not in order[:stage + 1]]
        shapes.append((len(steps_of(order[stage])), *left, rows, width))
    return shapes


def scatter_kernel(count, parts, *refs):
    fulls, results = refs[:count], refs[count:2 * count]
    rest = list(refs[2 * count:])
    held = [rest.pop(0) for _ in range(count)]
    other = [rest.pop(0) for _ in range(count)]
    slots = [[[rest.pop(0) for _ in range(3)] for _ in parts[index]] for index in range(count)]
    send, recv, local = rest
    place = Place()
    greet(place)
    partner = place.device(place.at("m", 1))
    base = 0
    groups, swaps, owns = [], [], []
    for index in range(count):
        swap = pltpu.make_async_remote_copy(
            fulls[index].at[1 - place.m], other[index], send.at[base], recv.at[base],
            device_id=partner, device_id_type=MESH)
        swap.start()
        own = pltpu.make_async_copy(fulls[index].at[place.m], held[index], local.at[index])
        own.start()
        swaps.append(swap)
        owns.append(own)
        base += 1
        group = []
        for number, part in enumerate(parts[index]):
            group.append(Scatterer(place, held[index], part, slots[index][number], (send, recv), base))
            base += 12
        groups.append(group)
    for turn in range(count + 3):
        for index in range(count):
            stage = turn - index
            if stage == 0:
                owns[index].wait()
                swaps[index].wait_recv()

                @pl.loop(0, 16)
                def _(block):
                    where = (block // 4, (block // 2) % 2, block % 2)
                    held[index][where] = (
                        held[index][where].astype(F32) + other[index][where].astype(F32)
                    ).astype(held[index].dtype)

                for path in groups[index]:
                    path.start(0)
            elif 1 <= stage <= 3:
                for path in groups[index]:
                    path.add(stage - 1, results[index] if stage == 3 else None)
                    if stage < 3:
                        path.start(stage)
    for index in range(count):
        swaps[index].wait_send()
        for path in groups[index]:
            path.finish()


def scatter(fulls, rows):
    count = len(fulls)
    parts = [column_parts(f.shape[-1]) for f in fulls]
    slots = []
    for full, own in zip(fulls, parts):
        for part in own:
            slots += [pltpu.VMEM(s, full.dtype) for s in slot_shapes(part, full.shape[-2])]
    sems = sum(1 + 12 * len(own) for own in parts)
    return pl.pallas_call(
        functools.partial(scatter_kernel, count, parts),
        out_shape=[jax.ShapeDtypeStruct((r, f.shape[-1]), F32) for r, f in zip(rows, fulls)],
        in_specs=[pl.BlockSpec(memory_space=pl.ANY)] * count,
        out_specs=[pl.BlockSpec(memory_space=pltpu.VMEM)] * count,
        scratch_shapes=[pltpu.VMEM(f.shape[1:], f.dtype) for f in fulls] * 2 + slots + [
            pltpu.SemaphoreType.DMA((sems,)),
            pltpu.SemaphoreType.DMA((sems,)),
            pltpu.SemaphoreType.DMA((count,)),
        ],
        compiler_params=pltpu.CompilerParams(
            collective_id=1, has_side_effects=True, vmem_limit_bytes=56 << 20),
        name="scatter_grads",
    )(*fulls)


def layer_norm(values, gain, shift):
    center = values - jnp.mean(values, axis=-1, keepdims=True)
    spread = jnp.mean(center * center, axis=-1, keepdims=True)
    return center * lax.rsqrt(spread + EPS_NORM) * gain + shift


def gelu_exact(values):
    return jax.nn.gelu(values, approximate=False)


def segment_ids(lengths, length):
    bounds = jnp.cumsum(lengths, axis=-1)
    places = jnp.arange(length, dtype=jnp.int32)
    return jnp.sum((places[None, :, None] >= bounds[:, None, :]).astype(jnp.int32), axis=-1)


def row_scores(packed, row_ids):
    scores = jnp.einsum(
        "qhd,khd->hqk", packed[:, 0], packed[:, 1], preferred_element_type=F32
    ) * HD ** (-0.5)
    same = row_ids[:, None] == row_ids[None, :]
    return jnp.where(same[None], scores, -1e30)


def attend_row(packed, row_ids):
    scores = row_scores(packed, row_ids)
    peak = jnp.max(scores, axis=-1, keepdims=True)
    raised = jnp.exp(scores - peak)
    total = jnp.sum(raised, axis=-1, keepdims=True)
    probs = raised / total
    context = jnp.einsum(
        "hqk,khd->qhd", probs.astype(BF), packed[:, 2], preferred_element_type=F32
    )
    return (
        context.astype(BF).reshape(context.shape[0], -1),
        (peak + jnp.log(total))[..., 0],
    )


def attend_back(packed, grad_context, log_total, row_ids):
    scores = row_scores(packed, row_ids)
    probs = jnp.exp(scores - log_total[..., None])
    grad_values = jnp.einsum(
        "hqk,qhd->khd", probs.astype(BF), grad_context, preferred_element_type=F32
    )
    grad_probs = jnp.einsum(
        "qhd,khd->hqk", grad_context, packed[:, 2], preferred_element_type=F32
    )
    inner_sum = jnp.sum(probs * grad_probs, axis=-1, keepdims=True)
    grad_scores = (probs * (grad_probs - inner_sum)).astype(BF)
    grad_queries = jnp.einsum(
        "hqk,khd->qhd", grad_scores, packed[:, 1], preferred_element_type=F32
    ) * HD ** (-0.5)
    grad_keys = jnp.einsum(
        "hqk,qhd->khd", grad_scores, packed[:, 0], preferred_element_type=F32
    ) * HD ** (-0.5)
    return jnp.stack([grad_queries, grad_keys, grad_values], axis=1).astype(BF)


def fast_mesh():
    return lax.axis_size("dp") == 16 and lax.axis_size("mp") == 2


def gather_all(shards, kinds):
    if fast_mesh():
        full = gather(shards, kinds)
        return [f.reshape(2, 16, *f.shape[-2:])[:, :, :s.shape[0]] for f, s in zip(full, shards)]
    both = [lax.all_gather(s.astype(k), "dp", axis=0) for s, k in zip(shards, kinds)]
    return [lax.all_gather(s, "mp", axis=0) for s in both]


def scatter_all(fulls):
    if fast_mesh():
        rows = [f.shape[-2] for f in fulls]
        held = [r + (-r) % (16 if f.dtype == BF else 8) for r, f in zip(rows, fulls)]
        padded = [
            jnp.pad(f, ((0, 0), (0, 0), (0, h - r), (0, 0))).reshape(2, 4, 2, 2, h, f.shape[-1])
            for f, h, r in zip(fulls, held, rows)
        ]
        return scatter(padded, rows)
    out = []
    for full in fulls:
        own = lax.psum_scatter(full.astype(F32), "mp", scatter_dimension=0)
        out.append(lax.psum_scatter(own, "dp", scatter_dimension=0))
    return out


def pack_small(head, ffn, norm):
    flat = jnp.concatenate([head.reshape(-1), ffn.reshape(-1), norm.reshape(-1)])
    rows = -(-flat.shape[0] // 1024) * 8
    return jnp.pad(flat, (0, rows * 128 - flat.shape[0])).reshape(rows, 128)


def body(
    tokens, cotangent, seg_lengths, w_qkv, w_out, w_up, w_down, head_bias, ffn_bias, norm_bias,
    qkv_rows, qkv_cols, out_rows, out_cols, up_rows, up_cols, down_rows, down_cols,
    head_bias_sq, ffn_bias_sq, norm_sq,
):
    f32 = F32
    cores = lax.axis_size("mp")
    data = lax.axis_size("dp")
    core = lax.axis_index("mp")
    own_tokens = tokens.shape[0]
    own_rows = own_tokens // LEN
    ids = segment_ids(seg_lengths, LEN)
    own_ids = lax.dynamic_slice_in_dim(ids, core * own_rows, own_rows, 0)
    own_lengths = lax.dynamic_slice_in_dim(seg_lengths, core * own_rows, own_rows, 0)
    rows_qkv = w_qkv.shape[0]
    half = w_qkv.shape[2]
    n_head, n_ffn, n_norm = head_bias.size, ffn_bias.size, norm_bias.size
    small, qkv_g, out_g, up_g, down_g = gather_all(
        [pack_small(head_bias, ffn_bias, norm_bias), w_qkv.reshape(rows_qkv, -1), w_out, w_up, w_down],
        [f32, BF, BF, BF, BF],
    )
    small = small.reshape(cores, data, -1).astype(BF).astype(f32)
    head_full = small[:, :, :n_head].reshape(cores, data, 2, -1).transpose(2, 0, 1, 3).reshape(2, D)
    ffn_full = small[:, :, n_head:n_head + n_ffn].reshape(-1)
    norm_full = small[:, :, n_head + n_ffn:n_head + n_ffn + n_norm]
    norm_full = norm_full.reshape(cores, data, 6, -1).transpose(2, 1, 0, 3).reshape(6, D)
    qkv_weight = qkv_g.reshape(cores, D, 3, half).transpose(1, 2, 0, 3).reshape(D, 3 * D)
    out_weight = out_g.reshape(D, D)
    up_weight = up_g.reshape(cores, D, FF // cores).transpose(1, 0, 2).reshape(D, FF)
    down_weight = down_g.reshape(FF, D)
    heads = D // HD
    offsets = jnp.stack([head_full[0], jnp.zeros_like(head_full[0]), head_full[1]])
    projected = jnp.dot(tokens, qkv_weight, preferred_element_type=f32).reshape(-1, 3, D) + offsets
    packed_rows = projected.astype(BF).reshape(own_rows, LEN, 3, heads, HD)
    context_rows, log_totals = lax.map(
        lambda pair: attend_row(pair[0], pair[1]), (packed_rows, own_ids)
    )
    context = context_rows.reshape(own_tokens, D)
    attended = jnp.dot(context, out_weight, preferred_element_type=f32) + norm_full[0]
    hidden, norm_one_back = jax.vjp(
        layer_norm, tokens.astype(f32) + attended, norm_full[2], norm_full[3]
    )
    hidden_b = hidden.astype(BF)
    inner = jnp.dot(hidden_b, up_weight, preferred_element_type=f32) + ffn_full
    activated, gelu_back = jax.vjp(gelu_exact, inner)
    activated_b = activated.astype(BF)
    branch = jnp.dot(activated_b, down_weight, preferred_element_type=f32) + norm_full[1]
    output, norm_two_back = jax.vjp(layer_norm, hidden + branch, norm_full[4], norm_full[5])
    member = (own_ids[:, None, :] == jnp.arange(SEGS, dtype=jnp.int32)[None, :, None]).astype(f32)
    pooled = jnp.einsum(
        "rsl,rld->rsd", member, output.reshape(own_rows, LEN, D), precision=lax.Precision.HIGHEST
    )
    pooled = pooled / own_lengths[:, :, None].astype(f32)
    grad_res_two, grad_gain_two, grad_shift_two = norm_two_back(cotangent.astype(f32))
    grad_branch = grad_res_two.astype(BF)
    grad_bias_down = jnp.sum(grad_branch.astype(f32), axis=0)
    grad_act = jnp.dot(grad_branch, down_weight.T, preferred_element_type=f32)
    grad_down = jnp.dot(activated_b.T, grad_branch, preferred_element_type=f32)
    grad_inner = gelu_back(grad_act)[0].astype(BF)
    grad_bias_up = jnp.sum(grad_inner.astype(f32), axis=0)
    grad_up = jnp.dot(hidden_b.T, grad_inner, preferred_element_type=f32)
    grad_hidden = grad_res_two + jnp.dot(grad_inner, up_weight.T, preferred_element_type=f32)
    grad_res_one, grad_gain_one, grad_shift_one = norm_one_back(grad_hidden)
    grad_attended = grad_res_one.astype(BF)
    grad_bias_out = jnp.sum(grad_attended.astype(f32), axis=0)
    grad_context = jnp.dot(grad_attended, out_weight.T, preferred_element_type=f32).astype(BF)
    grad_out = jnp.dot(context.T, grad_attended, preferred_element_type=f32)
    grad_rows = lax.map(
        lambda item: attend_back(item[0], item[1], item[2], item[3]),
        (packed_rows, grad_context.reshape(own_rows, LEN, heads, HD), log_totals, own_ids),
    )
    grad_packed = grad_rows.reshape(own_tokens, 3, D)
    grad_head = jnp.stack(
        [
            jnp.sum(grad_packed[:, 0].astype(f32), axis=0),
            jnp.sum(grad_packed[:, 2].astype(f32), axis=0),
        ]
    )
    grad_flat = grad_packed.reshape(own_tokens, 3 * D)
    grad_qkv = jnp.dot(tokens.T, grad_flat, preferred_element_type=f32)
    input_grad = grad_res_one + jnp.dot(grad_flat, qkv_weight.T, preferred_element_type=f32)
    norm_terms = jnp.stack(
        [grad_bias_out, grad_bias_down, grad_gain_one, grad_shift_one, grad_gain_two, grad_shift_two]
    )
    small_grads = jnp.concatenate(
        [
            grad_head.reshape(2, cores, data, -1).transpose(1, 2, 0, 3).reshape(cores, data, -1),
            grad_bias_up.reshape(cores, data, -1),
            norm_terms.reshape(6, data, cores, -1).transpose(2, 1, 0, 3).reshape(cores, data, -1),
        ],
        axis=-1,
    )
    small_rows = -(-small_grads.shape[-1] // 1024) * 8
    small_grads = jnp.pad(
        small_grads, ((0, 0), (0, 0), (0, small_rows * 128 - small_grads.shape[-1]))
    ).reshape(cores, data, small_rows, 128)
    qkv_blocks = grad_qkv.astype(BF).reshape(data, rows_qkv, 3, cores, half)
    red_small, red_qkv, red_out, red_up, red_down = scatter_all(
        [
            small_grads,
            qkv_blocks.transpose(3, 0, 1, 2, 4).reshape(cores, data, rows_qkv, 3 * half),
            grad_out.astype(BF).reshape(cores, data, -1, D),
            grad_up.astype(BF).reshape(data, rows_qkv, cores, -1).transpose(2, 0, 1, 3),
            grad_down.astype(BF).reshape(cores, data, -1, D),
        ]
    )
    red_small = red_small.reshape(-1)
    red_head = red_small[:n_head].reshape(head_bias.shape)
    red_ffn = red_small[n_head:n_head + n_ffn]
    norm_grad = red_small[n_head + n_ffn:n_head + n_ffn + n_norm].reshape(norm_bias.shape)
    weights_flat = [w_qkv.reshape(rows_qkv, -1), w_out, w_up, w_down]
    grads_flat = [red_qkv, red_out, red_up, red_down]
    rows_old = [qkv_rows, out_rows, up_rows, down_rows]
    cols_old = [qkv_cols.reshape(-1), out_cols, up_cols, down_cols]
    col_count = [3 * D, D, FF, D]
    row_count = [D, D, D, FF]
    row_share = [cores, 1, cores, 1]
    squares = [grad * grad + EPS_SQUARE for grad in grads_flat]
    row_parts = [jnp.sum(square, axis=1) for square in squares]
    col_parts = [jnp.sum(square, axis=0) for square in squares]
    vec_weights = [head_bias, ffn_bias, norm_bias]
    vec_grads = [red_head, red_ffn, norm_grad]
    vec_old = [head_bias_sq, ffn_bias_sq, norm_sq]
    vec_counts = [2 * D, FF, 6 * D]
    vec_second = [
        DECAY * old + (1.0 - DECAY) * (grad * grad + EPS_SQUARE)
        for old, grad in zip(vec_old, vec_grads)
    ]
    vec_update = [grad * lax.rsqrt(second) for grad, second in zip(vec_grads, vec_second)]
    weight_parts = [jnp.sum(weight * weight) for weight in weights_flat + vec_weights]
    vec_parts = [jnp.sum(update * update) for update in vec_update]
    row_qkv, row_up = lax.psum((row_parts[0], row_parts[2]), "mp")
    col_qkv, col_up = lax.psum((col_parts[0], col_parts[2]), "dp")
    col_out, col_down = lax.psum((col_parts[1], col_parts[3]), ("dp", "mp"))
    row_sums = [row_qkv, row_parts[1], row_up, row_parts[3]]
    col_sums = [col_qkv, col_out, col_up, col_down]
    rows_new = [
        DECAY * rows_old[index] + (1.0 - DECAY) * row_sums[index] / col_count[index]
        for index in range(4)
    ]
    cols_new = [
        DECAY * cols_old[index] + (1.0 - DECAY) * col_sums[index] / row_count[index]
        for index in range(4)
    ]
    ratio_parts = [
        jnp.sum(
            grads_flat[index]
            * grads_flat[index]
            / (rows_new[index][:, None] * cols_new[index][None, :])
        )
        for index in range(4)
    ]
    extra_parts = (
        [jnp.sum(rows_new[index]) / row_share[index] for index in range(4)]
        + weight_parts
        + vec_parts
    )
    totals = lax.psum(jnp.stack(ratio_parts + extra_parts), ("dp", "mp"))
    row_means = [totals[4 + index] / row_count[index] for index in range(4)]
    weight_totals = [totals[8 + index] for index in range(7)]
    vec_totals = [totals[15 + index] for index in range(3)]
    new_mats = []
    for index in range(4):
        entries = row_count[index] * col_count[index]
        estimate = rows_new[index][:, None] * cols_new[index][None, :] / row_means[index]
        update = grads_flat[index] / jnp.sqrt(estimate)
        update_rms = jnp.sqrt(row_means[index] * totals[index] / entries)
        stride = (
            RATE * jnp.sqrt(weight_totals[index] / entries) / jnp.maximum(1.0, update_rms / CLIP)
        )
        new_mats.append(weights_flat[index] - stride * update)
    new_vecs = []
    for index in range(3):
        update_rms = jnp.sqrt(vec_totals[index] / vec_counts[index])
        stride = (
            RATE
            * jnp.sqrt(weight_totals[4 + index] / vec_counts[index])
            / jnp.maximum(1.0, update_rms / CLIP)
        )
        new_vecs.append(vec_weights[index] - stride * vec_update[index])
    return (
        output.astype(BF),
        pooled,
        input_grad,
        red_qkv.reshape(w_qkv.shape),
        red_out,
        red_up,
        red_down,
        red_head,
        red_ffn,
        norm_grad,
        rows_new[0],
        cols_new[0].reshape(qkv_cols.shape),
        rows_new[1],
        cols_new[1],
        rows_new[2],
        cols_new[2],
        rows_new[3],
        cols_new[3],
        vec_second[0],
        vec_second[1],
        vec_second[2],
        new_mats[0].reshape(w_qkv.shape),
        new_mats[1],
        new_mats[2],
        new_mats[3],
        new_vecs[0],
        new_vecs[1],
        new_vecs[2],
    )


def solution(mesh):
    return jax.shard_map(
        body,
        mesh=mesh,
        in_specs=(
            P(("dp", "mp"), None),
            P(("dp", "mp"), None),
            P("dp", None),
            P("dp", None, "mp"),
            P(("mp", "dp"), None),
            P("dp", "mp"),
            P(("mp", "dp"), None),
            P(None, ("mp", "dp")),
            P(("mp", "dp")),
            P(None, ("dp", "mp")),
            P("dp"),
            P(None, "mp"),
            P(("mp", "dp")),
            P(),
            P("dp"),
            P("mp"),
            P(("mp", "dp")),
            P(),
            P(None, ("mp", "dp")),
            P(("mp", "dp")),
            P(None, ("dp", "mp")),
        ),
        out_specs=(
            P(("dp", "mp"), None),
            P(("dp", "mp"), None, None),
            P(("dp", "mp"), None),
            P("dp", None, "mp"),
            P(("mp", "dp"), None),
            P("dp", "mp"),
            P(("mp", "dp"), None),
            P(None, ("mp", "dp")),
            P(("mp", "dp")),
            P(None, ("dp", "mp")),
            P("dp"),
            P(None, "mp"),
            P(("mp", "dp")),
            P(),
            P("dp"),
            P("mp"),
            P(("mp", "dp")),
            P(),
            P(None, ("mp", "dp")),
            P(("mp", "dp")),
            P(None, ("dp", "mp")),
            P("dp", None, "mp"),
            P(("mp", "dp"), None),
            P("dp", "mp"),
            P(("mp", "dp"), None),
            P(None, ("mp", "dp")),
            P(("mp", "dp")),
            P(None, ("dp", "mp")),
        ),
        check_vma=False,
    )
```

time: 1180 us -> 775 us (0.66)
  waiting for transfers between devices: 467 us -> 0 us
  Pallas kernels: 0 us -> 198 us
  blocking collectives: 314 us -> 154 us
  local copies, waits for them, and re-layouts: 91.2 us -> 155 us
  other arithmetic: 89.8 us -> 73.6 us
  between operations: 30.7 us -> 15.7 us
    reduce_scatter x8 -> x0, waiting for transfers between devices: 417 us -> none  [the longest x1 141 us: body(): lax.psum_scatter(grad_up, 'dp', scatter_dimension=0, tiled=True)]
    pallas_call x0 -> x2, Pallas kernels: none -> 198 us  [the longest x1 100 us: gather(): pl.pallas_call(functools.partial(gather_kernel, count), out_shape=[jax.Sh...]
    unnamed x3 -> x0, blocking collectives: 154 us -> none
    all_gather x3 -> x0, blocking collectives: 121 us -> none  [the longest x1 42.3 us: body(): lax.all_gather(head_bias.astype(jnp.bfloat16), 'dp', axis=1, tiled=True)]
    psum x0 -> x2, blocking collectives: none -> 115 us  [the longest x1 75.2 us: body(): col_qkv, col_up = lax.psum((col_parts[0], col_parts[2]), 'dp')]
    all_gather x7 -> x0, waiting for transfers between devices: 49.3 us -> none  [the longest x1 32.2 us: body(): lax.all_gather(w_down.astype(jnp.bfloat16), 'dp', axis=0, tiled=True)]
    reshape x9 -> x21, local copies, waits for them, and re-layouts: 22 us -> 62.4 us  [the longest x2 17.6 us: body(): grad_up.astype(BF).reshape(data, rows_qkv, cores, -1).transpose(2, 0, 1, 3)]
    another operation x1 -> x5, local copies, waits for them, and re-layouts: 0.07 us -> 14 us  [the longest x1 6.67 us: body(): up_g.reshape(cores, D, FF // cores).transpose(1, 0, 2).reshape(D, FF)]
  transfers between devices with their start and end apart: 15 -> 0, of which waited for: 9 -> 0; matrix products, arithmetic and copies ran while one was open for 19% -> 0% of each run, Pallas kernels for 0% -> 0%
where the time goes in v1:
time: 775 us; the launch traced here: 766 us
  Pallas kernels  198 us (26%)
  matrix products  169 us (22%)
  local copies, waits for them, and re-layouts  155 us (20%)
  blocking collectives  154 us (20%)
  other arithmetic  73.6 us (9%)
  between operations  15.7 us (2%)
    pallas_call x1, Pallas kernels, gather(): pl.pallas_call(functools.partial(gather_kernel, count), out_shape=[jax.Sh...  100 us
    pallas_call x1, Pallas kernels, scatter(): pl.pallas_call(functools.partial(scatter_kernel, count, parts), out_shape...  97.7 us
    psum x1, blocking collectives, body(): col_qkv, col_up = lax.psum((col_parts[0], col_parts[2]), 'dp')  75.2 us
    psum x1, blocking collectives, body(): col_out, col_down = lax.psum((col_parts[1], col_parts[3]), ('dp', 'mp'))  39.7 us
    psum x1, blocking collectives, body(): totals = lax.psum(jnp.stack(ratio_parts + extra_parts), ('dp', 'mp'))  37.1 us
    dot_general x1, matrix products, body(): inner = jnp.dot(hidden_b, up_weight, preferred_element_type=f32) + ffn_full  36.1 us
    unnamed x154, local copies, waits for them, and re-layouts  19.1 us
    dot_general x1, matrix products, body(): grad_act = jnp.dot(grad_branch, down_weight.T, preferred_element_type=f32)  18 us

profile of v1, /device:TPU:0, one launch (start us, length us, event | category | flops | bytes accessed | tf_op | source)
XLA Modules:
  0.0 766.2 jit_solution(867256911518117035)
XLA Ops:
  8.3 100.3 %gather_weights.1 = (f32[2,4,2,2,8,128]{5,4,3,2,1,0:T(8,128)S(1)}, bf16[2,4,2,2,48,1152]{5,4,3,2,1,0:T(8,128)(2,1)S(1)}, bf16[2,4,2,2,32,768]{5,4,3,2,1,0:T(8,12...) custom-call(f32[8,128]{1,0:T(8,128)S(1)} %fusion.63.refs_0_, ...), custom_call_target="tpu_custom_call" | custom-call | tf_op jit(solution)/shard_map/gather_weights/pallas_call | solution.py:163
  130.1 8.8 %convolution_bitcast_fusion = f32[1024,2304]{0,1:T(8,128)} fusion(bf16[768,2304]{0,1:T(8,128)(2,1)S(1)} %bitcast.243, bf16[1024,768]{1,0:T(8,128)(2,1)} %param.25), kind=kOutput, calls=%fused_computation.68 | convolution fusion | flops 3623878656 | bytes 14548992 | tf_op jit(solution)/shard_map/dot_general | solution.py:467
  138.9 13.3 %reshape.493 = f32[2,512,3,12,64]{1,0,4,3,2:T(2,128)} reshape(f32[1024,2304]{0,1:T(8,128)} %convolution_bitcast_fusion) | data formatting | bytes 18874368 | tf_op jit(solution)/shard_map/reshape | solution.py:467
  152.2 7.4 fusion.35
  159.9 25.8 %while.22 = (s32[]{:T(128)}, bf16[2,512,768]{2,1,0:T(8,128)(2,1)}, f32[2,12,512]{2,1,0:T(8,128)S(1)}, bf16[2,512,3,12,64]{1,4,3,2,0:T(8,128)(2,1)}, s32[2,512]{1,0:T(2,128)S(1)}, /*index=5*/s32[]{:T(128)}) while((s32[]{:T(128)}, bf16[2,512,768]{2,1,0:T(8,128)(2,1)}, f32[2,12,512]{2,1,0:T(8,128)S(1)}, bf16[2,512,3,12,64]{1,4,3,2,0:T(8,128)(2,1)}, ...), condition=%wide.region_5.6_spmd, body=%wide.region_2.5_spmd.sunk | while | flops 843704320 | bytes 59472492 | solution.py:469
  200.1 36.1 %multiply_convert_fusion.3 = (bf16[1024,3072]{1,0:T(8,128)(2,1)}, f32[1024,3072]{1,0:T(8,128)}, f32[1024,3072]{1,0:T(8,128)}) fusion(f32[3072]{0:T(1024)S(1)} %add.225, bf16[768,3072]{0,1:T(8,128)(2,1)} %bitcast.240, f32[1024,768]{1,0:T(8,128)S(1)} %get-tuple-element.317, f32[768]{0:T(1024)S(1)} %add.222, f32[768]{0:T(1024)S(1)} %mul.460, ...), kind=kOutput, calls=%fused_computation.52 | convolution fusion | flops 5043388416 | bytes 39348224 | tf_op jit(solution)/shard_map/dot_general | solution.py:478
  236.3 9.3 %fusion.81 = (f32[1024]{0:T(1024)S(1)}, f32[1024,768]{1,0:T(8,128)S(1)}) fusion(f32[768]{0:T(1024)S(1)} %add.228, bf16[1024,3072]{1,0:T(8,128)(2,1)} %get-tuple-element.282, bf16[3072,768]{1,0:T(8,128)(2,1)} %bitcast.262, f32[768]{0:T(1024)S(1)} %add.222, f32[768]{0:T(1024)S(1)} %mul.460, f32[1024]{0:T(1024)S(1)} %fusion.64, f32[1024,768]{1,0:T(8,128)} %copy-done.13, ...), kind=kOutput, calls=%fused_computation.213 | convolution fusion | flops 4837342208 | bytes 17323008 | tf_op jit(solution)/shard_map/dot_general | solution.py:481
  256.3 9.8 %convolution_convert_fusion = bf16[3072,768]{1,0:T(8,128)(2,1)} fusion(bf16[1024,3072]{1,0:T(8,128)(2,1)} %get-tuple-element.282, bf16[1024,768]{1,0:T(8,128)(2,1)S(1)} %get-tuple-element.273), kind=kOutput, calls=%fused_computation.69 | convolution fusion | flops 4834197504 | bytes 12582912 | tf_op jit(solution)/shard_map/dot_general | solution.py:492
  266.1 18.0 %convert_reduce_fusion = (f32[3072]{0:T(1024)}, bf16[1024,3072]{1,0:T(8,128)(2,1)}) fusion(f32[1024,3072]{1,0:T(8,128)} %get-tuple-element.283, bf16[1024,768]{1,0:T(8,128)(2,1)S(1)} %get-tuple-element.273, bf16[3072,768]{1,0:T(8,128)(2,1)} %bitcast.263, f32[1024,3072]{1,0:T(8,128)} %get-tuple-element.318, f32[3072]{0:T(1024)S(1)} %add.225), kind=kOutput, calls=%fused_computation.50 | convolution fusion | flops 4885312512 | bytes 37773312 | tf_op jit(solution)/shard_map/dot_general | solution.py:491
  284.1 9.8 %convolution_convert_fusion.1 = bf16[768,3072]{1,0:T(8,128)(2,1)} fusion(bf16[1024,3072]{1,0:T(8,128)(2,1)} %get-tuple-element.323, f32[1024,768]{1,0:T(8,128)S(1)} %copy-done.14, f32[768]{0:T(1024)S(1)} %add.222, f32[768]{0:T(1024)S(1)} %mul.460, f32[1024]{0:T(1024)S(1)} %fusion.64, f32[1024]{0:T(1024)S(1)} %broadcast_multiply_fusion.2), kind=kOutput, calls=%fused_computation.70 | convolution fusion | flops 4838129664 | bytes 14170112 | tf_op jit(solution)/shard_map/dot_general | solution.py:495
  293.9 11.8 %reshape.511 = bf16[16,48,2,1536]{3,2,1,0:T(2,128)(2,1)} reshape(bf16[768,3072]{1,0:T(8,128)(2,1)} %convolution_convert_fusion.1) | data formatting | bytes 9437184 | tf_op jit(solution)/shard_map/reshape | solution.py:537
  312.4 8.9 %multiply_reduce_fusion.1 = (f32[768]{0:T(1024)}, f32[1024]{0:T(1024)S(1)}, f32[768]{0:T(1024)}, f32[1024,768]{1,0:T(8,128)S(1)}) fusion(f32[1024,768]{1,0:T(8,128)S(1)} %copy-done.14, f32[1024]{0:T(1024)S(1)} %fusion.64, f32[1024]{0:T(1024)S(1)} %broadcast_multiply_fusion.2, f32[768]{0:T(1024)S(1)} %mul.460, bf16[1024,3072]{1,0:T(8,128)(2,1)S(1)} %copy-done.72, ...), kind=kOutput, calls=%fused_computation.82 | convolution fusion | flops 4839699456 | bytes 20472832 | tf_op jit(solution)/shard_map/dot_general | solution.py:496
  334.7 52.4 %while.23 = (s32[]{:T(128)}, bf16[2,512,3,12,64]{1,4,3,2,0:T(8,128)(2,1)}, bf16[2,512,3,12,64]{1,4,3,2,0:T(8,128)(2,1)}, s32[2,512]{1,0:T(2,128)S(1)}, f32[2,12,...) while((s32[]{:T(128)}, bf16[2,512,3,12,64]{1,4,3,2,0:T(8,128)(2,1)}, ...), condition=%wide.region_16.17_spmd, body=%wide.region_14.16_spmd.sunk | while | flops 2069751808 | bytes 112917088 | solution.py:502
  338.8 7.2 multiply_reduce_fusion.16
  364.8 7.2 multiply_reduce_fusion.16
  387.1 9.4 %copy.104 = bf16[2,512,3,12,64]{1,0,4,3,2:T(2,128)(2,1)} copy(bf16[2,512,3,12,64]{1,4,3,2,0:T(8,128)(2,1)} %get-tuple-element.105) | data formatting | bytes 9437184 | tf_op jit(solution)/shard_map/while | solution.py:502
  422.0 9.6 %reshape.508.refs_1_ = bf16[2,4,2,2,48,1152]{5,4,3,2,1,0:T(8,128)(2,1)} reshape(bf16[2,16,48,3,384]{4,3,2,1,0:T(4,128)(2,1)} %copy.108) | data formatting | bytes 7077888 | tf_op jit(solution)/shard_map/reshape | solution.py:418
  431.6 9.2 %reshape.502 = bf16[1024,3,768]{0,2,1:T(8,128)(2,1)} reshape(bf16[2,512,3,12,64]{1,0,4,3,2:T(2,128)(2,1)} %copy.104) | data formatting | bytes 9437184 | tf_op jit(solution)/shard_map/reshape | solution.py:506
  445.5 97.7 %scatter_grads.1 = (f32[8,128]{1,0:T(8,128)}, f32[48,1152]{1,0:T(8,128)}, f32[24,768]{1,0:T(8,128)}, f32[48,1536]{1,0:T(8,128)}, f32[96,768]{1,0:T(8,128)}) custom-call(f32[2,4,2,2,8,128]{5,4,3,2,1,0:T(8,128)} %bitcast.250, bf16[2,4,2,2,48,1152]{5,4,3,2,1,0:T(8,128)(2,1)} %reshape.508.refs_1_, bf16[2,4,2,2,32,768]{5,4,3,2,1,0:T(8,128)(2,1)} %bitcast.235, ...), custom_call_target="tpu_custom_call" | custom-call | tf_op jit(solution)/shard_map/scatter_grads/pallas_call | solution.py:326
  545.5 39.7 %all-reduce.3 = (f32[768]{0:T(1024)S(1)}, f32[768]{0:T(1024)S(1)}) all-reduce(f32[768]{0:T(1024)S(1)} %get-tuple-element.227, f32[768]{0:T(1024)S(1)} %get-tuple-element.221), channel_id=1, replica_groups=mesh['dp'=16,'mp'=2] {'dp','mp'}, use_global_device_ids=true, to_apply=%region_32.33 | all-reduce | flops 1536 | bytes 12288 | tf_op jit(solution)/shard_map/psum | solution.py:568
  590.5 75.2 %all-reduce.4 = (f32[1152]{0:T(1024)S(1)}, f32[1536]{0:T(1024)S(1)}) all-reduce(f32[1152]{0:T(1024)S(1)} %get-tuple-element.225, f32[1536]{0:T(1024)S(1)} %get-tuple-element.223), channel_id=1, replica_groups=mesh['dp'=16,'mp'=2] {'dp'}, use_global_device_ids=true, to_apply=%region_29.30 | all-reduce | flops 2688 | bytes 21504 | tf_op jit(solution)/shard_map/psum | solution.py:567
  683.2 10.3 %stack.137 = f32[18]{0:T(128)S(1)} concatenate(f32[1]{0:T(128)} %bitcast.46, f32[1]{0:T(128)} %bitcast.47, f32[1]{0:T(128)} %bitcast.48, f32[1]{0:T(128)} %bitcast.49, f32[1]{0:T(128)} %bitcast.50, f32[1]{0:T(128)} %bitcast.51, f32[1]{0:T(128)} %bitcast.52, f32[1]{0:T(128)} %bitcast.53, f32[1]{0:T(128)} %bitcast.54, f32[1]{0:T(128)} %bitcast.55, f32[1]{0:T(128)} %bitcast.56, ...), dimensions={0} | concatenate | bytes 144 | tf_op jit(solution)/shard_map/stack | solution.py:592
  693.5 37.1 %psum.55 = f32[18]{0:T(128)S(1)} all-reduce(f32[18]{0:T(128)S(1)} %stack.137), channel_id=1, replica_groups=mesh['dp'=16,'mp'=2] {'dp','mp'}, use_global_device_ids=true, to_apply=%region_58.59 | all-reduce | flops 18 | bytes 144 | tf_op jit(solution)/shard_map/psum | solution.py:592
  752.0 10.1 %add_add_fusion.4 = f32[1024,768]{1,0:T(8,128)} fusion(f32[1024,768]{1,0:T(8,128)} %copy-done.12, bf16[1024,2304]{0,1:T(8,128)(2,1)} %bitcast.238, bf16[768,2304]{0,1:T(8,128)(2,1)} %bitcast.244, f32[1024]{0:T(1024)S(1)} %copy-done.42), kind=kOutput, calls=%fused_computation.94 | convolution fusion | flops 3625451520 | bytes 14553088 | tf_op jit(solution)/shard_map/dot_general | solution.py:515
  (323 shorter events, 203.7 us)
Async XLA Ops:
  445.3 139.9 %copy-start.66 = (f32[96]{0:T(128)S(1)}, f32[96]{0:T(128)}, u32[]{:S(2)}) copy-start(f32[96]{0:T(128)} %param.41) | copy-start | bytes 1156
  445.3 220.4 %copy-start.45 = (f32[1536]{0:T(1024)S(1)}, f32[1536]{0:T(1024)}, u32[]{:S(2)}) copy-start(f32[1536]{0:T(1024)} %param.40) | copy-start | bytes 18436
  445.3 222.8 %copy-start.68 = (f32[48]{0:T(128)S(1)}, f32[48]{0:T(128)}, u32[]{:S(2)}) copy-start(f32[48]{0:T(128)} %param.39) | copy-start | bytes 580
  445.3 222.8 %copy-start.69 = (f32[48]{0:T(128)S(1)}, f32[48]{0:T(128)}, u32[]{:S(2)}) copy-start(f32[48]{0:T(128)} %param.35) | copy-start | bytes 580
  445.3 225.1 %copy-start.67 = (f32[24]{0:T(128)S(1)}, f32[24]{0:T(128)}, u32[]{:S(2)}) copy-start(f32[24]{0:T(128)} %param.37) | copy-start | bytes 292
  445.3 227.3 %copy-start.46 = (f32[3,384]{1,0:T(4,128)S(1)}, f32[3,384]{1,0:T(4,128)}, u32[]{:S(2)}) copy-start(f32[3,384]{1,0:T(4,128)} %param.36) | copy-start | bytes 13828
  445.4 231.1 %copy-start.53 = (f32[6,24]{1,0:T(8,128)S(1)}, f32[6,24]{1,0:T(8,128)}, u32[]{:S(2)}) copy-start(f32[6,24]{1,0:T(8,128)} %param.45) | copy-start | bytes 1732
  445.4 232.5 %copy-start.63 = (f32[2,24]{1,0:T(2,128)S(1)}, f32[2,24]{1,0:T(2,128)}, u32[]{:S(2)}) copy-start(f32[2,24]{1,0:T(2,128)} %param.43) | copy-start | bytes 580
  445.4 233.1 %copy-start.25 = (f32[48,3,384]{2,0,1:T(8,128)S(1)}, f32[48,3,384]{2,0,1:T(8,128)}, u32[]{:S(2)}) copy-start(f32[48,3,384]{2,0,1:T(8,128)} %param.28) | copy-start | bytes 663556
  445.4 233.8 %copy-start.9 = (f32[24,768]{1,0:T(8,128)S(1)}, f32[24,768]{1,0:T(8,128)}, u32[]{:S(2)}) copy-start(f32[24,768]{1,0:T(8,128)} %refs_2_.1) | copy-start | bytes 221188
  445.4 234.5 %copy-start.3 = (f32[48,1536]{1,0:T(8,128)S(1)}, f32[48,1536]{1,0:T(8,128)}, u32[]{:S(2)}) copy-start(f32[48,1536]{1,0:T(8,128)} %refs_3_.1) | copy-start | bytes 884740
  445.4 235.2 %copy-start.1 = (f32[96,768]{1,0:T(8,128)S(1)}, f32[96,768]{1,0:T(8,128)}, u32[]{:S(2)}) copy-start(f32[96,768]{1,0:T(8,128)} %refs_4_.1) | copy-start | bytes 884740
  445.4 235.8 %copy-start.64 = (f32[2,24]{1,0:T(2,128)S(1)}, f32[2,24]{1,0:T(2,128)}, u32[]{:S(2)}) copy-start(f32[2,24]{1,0:T(2,128)} %param.32) | copy-start | bytes 580
  445.4 236.4 %copy-start.60 = (f32[96]{0:T(128)S(1)}, f32[96]{0:T(128)}, u32[]{:S(2)}) copy-start(f32[96]{0:T(128)} %param.33) | copy-start | bytes 1156
  445.5 237.1 %copy-start.36 = (f32[6,24]{1,0:T(8,128)S(1)}, f32[6,24]{1,0:T(8,128)}, u32[]{:S(2)}) copy-start(f32[6,24]{1,0:T(8,128)} %param.34) | copy-start | bytes 1732
  543.2 203.8 %copy-start.22 = (f32[24,768]{1,0:T(8,128)S(1)}, f32[24,768]{1,0:T(8,128)}, u32[]{:S(2)}) copy-start(f32[24,768]{1,0:T(8,128)} %get-tuple-element.477) | copy-start | bytes 221188
  543.2 206.6 %copy-start.5 = (f32[3,6,8,384]{3,2,0,1:T(8,128)S(1)}, f32[3,6,8,384]{3,2,0,1:T(8,128)}, u32[]{:S(2)}) copy-start(f32[3,6,8,384]{3,2,0,1:T(8,128)} %copy.121) | copy-start | bytes 663556
  543.2 206.6 %copy-start.20 = (f32[48,1152]{1,0:T(8,128)S(1)}, f32[48,1152]{1,0:T(8,128)}, u32[]{:S(2)}) copy-start(f32[48,1152]{1,0:T(8,128)} %get-tuple-element.106) | copy-start | bytes 663556
  543.2 208.7 %copy-start.42 = (f32[1024]{0:T(1024)S(1)}, f32[1024]{0:T(1024)}, u32[]{:S(2)}) copy-start(f32[1024]{0:T(1024)} %copy-done.41) | copy-start | bytes 12292
  585.1 176.9 %copy-start.31 = (f32[768]{0:T(1024)}, f32[768]{0:T(1024)S(1)}, u32[]{:S(2)}) copy-start(f32[768]{0:T(1024)S(1)} %get-tuple-element.490) | copy-start | bytes 9220
  585.2 176.9 %copy-start.34 = (f32[768]{0:T(1024)}, f32[768]{0:T(1024)S(1)}, u32[]{:S(2)}) copy-start(f32[768]{0:T(1024)S(1)} %get-tuple-element.486) | copy-start | bytes 9220
  586.6 175.5 %copy-start.47 = (f32[96]{0:T(128)}, f32[96]{0:T(128)S(1)}, u32[]{:S(2)}) copy-start(f32[96]{0:T(128)S(1)} %get-tuple-element.489) | copy-start | bytes 1156
  586.6 175.5 %copy-start.61 = (f32[96]{0:T(128)}, f32[96]{0:T(128)S(1)}, u32[]{:S(2)}) copy-start(f32[96]{0:T(128)S(1)} %get-tuple-element.492) | copy-start | bytes 1156
  586.6 175.5 %copy-start.62 = (f32[96]{0:T(128)}, f32[96]{0:T(128)S(1)}, u32[]{:S(2)}) copy-start(f32[96]{0:T(128)S(1)} %get-tuple-element.481) | copy-start | bytes 1156
  (50 other events, 1414.4 us)

commit v2 on v1

--- a/solution.py
+++ b/solution.py
@@ -112,21 +112,42 @@
                 sent.wait_send()
 
 
-def gather_kernel(count, *refs):
-    shards, fulls = refs[:count], refs[count:2 * count]
-    cast = refs[2 * count:3 * count]
-    send, recv, local = refs[3 * count:]
+def weight_sums_of(weights, small):
+    parts = []
+    for weight in weights:
+        value = weight[...]
+        if value.ndim == 3:
+            parts.append(sum(all_sum(value[:, part] * value[:, part]) for part in range(3)))
+        else:
+            parts.append(all_sum(value * value))
+    return scalars([jnp.zeros((1, 1), F32)] * 11 + parts + small_sums(small))
+
+
+def gather_kernel(*refs):
+    refs = list(refs)
+    take = lambda number: [refs.pop(0) for _ in range(number)]
+    weights = take(4)
+    head, ffn, norm = take(3)
+    fulls = take(5)
+    sums = refs.pop(0)
+    cast = take(5)
+    send, recv, local = refs
+    count = 5
+    half = weights[0].shape[2]
+    place_small(cast[0], norm[...], head[...], ffn[...], 0.0)
+    for part in range(3):
+        cast[1][:, part * half:(part + 1) * half] = weights[0][:, part, :].astype(BF)
+    value = weights[1][...]
+    held = cast[2].shape[0]
+    cast[2][...] = jnp.concatenate(
+        [value, jnp.zeros((held - value.shape[0], value.shape[1]), F32)], 0).astype(BF)
+    cast[3][...] = weights[2][...].astype(BF)
+    cast[4][...] = weights[3][...].astype(BF)
     place = Place()
     greet(place)
     paths, base = [], 0
     locals_ = []
     for index in range(count):
-        rows = shards[index].shape[0]
-        held = cast[index].shape[0]
-        value = shards[index][...]
-        if held != rows:
-            value = jnp.concatenate([value, jnp.zeros((held - rows, value.shape[1]), F32)], 0)
-        cast[index][...] = value.astype(cast[index].dtype)
         own = pltpu.make_async_copy(
             cast[index], fulls[index].at[place.m, place.z, place.y, place.x], local.at[index])
         own.start()
@@ -140,6 +161,7 @@
         paths.append(group)
     for own in locals_:
         own.wait()
+    sums[...] = weight_sums_of(weights, cast[0][...])
     for turn in range(count + 3):
         for index in range(count):
             stage = turn - index + 1
@@ -155,26 +177,27 @@
             path.finish()
 
 
-def gather(shards, kinds):
-    held = [(s.shape[0] + (-s.shape[0]) % (16 if k == BF else 8), s.shape[1])
-            for s, k in zip(shards, kinds)]
-    count = len(shards)
+def gather(weights, vectors):
+    qkv, out, up, down = weights
+    held = [(16, 128), (qkv.shape[0], 3 * qkv.shape[2]), (32, out.shape[1]), up.shape, down.shape]
+    kinds = [F32, BF, BF, BF, BF]
     slots = 16 * sum(len(column_parts(h[1])) for h in held)
-    outs = pl.pallas_call(
-        functools.partial(gather_kernel, count),
-        out_shape=[jax.ShapeDtypeStruct((2, 4, 2, 2) + h, k) for h, k in zip(held, kinds)],
-        in_specs=[pl.BlockSpec(memory_space=pltpu.VMEM)] * count,
-        out_specs=[pl.BlockSpec(memory_space=pl.ANY)] * count,
+    vmem = pl.BlockSpec(memory_space=pltpu.VMEM)
+    return pl.pallas_call(
+        gather_kernel,
+        out_shape=[jax.ShapeDtypeStruct((2, 4, 2, 2) + h, k) for h, k in zip(held, kinds)]
+        + [jax.ShapeDtypeStruct((8, 128), F32)],
+        in_specs=[vmem] * 7,
+        out_specs=[pl.BlockSpec(memory_space=pl.ANY)] * 5 + [vmem],
         scratch_shapes=[pltpu.VMEM(h, k) for h, k in zip(held, kinds)] + [
             pltpu.SemaphoreType.DMA((slots,)),
             pltpu.SemaphoreType.DMA((slots,)),
-            pltpu.SemaphoreType.DMA((count,)),
+            pltpu.SemaphoreType.DMA((5,)),
         ],
         compiler_params=pltpu.CompilerParams(
             collective_id=0, has_side_effects=True, vmem_limit_bytes=48 << 20),
         name="gather_weights",
-    )(*shards)
-    return outs
+    )(*weights, *vectors)
 
 
 class Scatterer:
@@ -261,13 +284,152 @@
     return shapes
 
 
+def to_column(row):
+    count = row.shape[1]
+    here = lax.broadcasted_iota(jnp.int32, (count, count), 0)
+    there = lax.broadcasted_iota(jnp.int32, (count, count), 1)
+    return jnp.sum(jnp.where(here == there, row, 0.0), axis=1, keepdims=True)
+
+
+def to_row(column):
+    count = column.shape[0]
+    here = lax.broadcasted_iota(jnp.int32, (count, count), 0)
+    there = lax.broadcasted_iota(jnp.int32, (count, count), 1)
+    return jnp.sum(jnp.where(here == there, column, 0.0), axis=0, keepdims=True)
+
+
+def put_line(ref, line, row):
+    for tile in range(row.shape[1] // 128):
+        ref[line + tile:line + tile + 1, :] = row[:, tile * 128:(tile + 1) * 128]
+
+
+def get_line(ref, line, width):
+    tiles = width // 128
+    return jnp.concatenate([ref[line + t:line + t + 1, :] for t in range(tiles)], axis=1)
+
+
+def scalars(values):
+    lane = lax.broadcasted_iota(jnp.int32, (8, 128), 1)
+    out = jnp.zeros((8, 128), F32)
+    for index, value in enumerate(values):
+        out = jnp.where(lane == index, value, out)
+    return out
+
+
+def all_sum(values):
+    return jnp.sum(jnp.sum(values, axis=1, keepdims=True), axis=0, keepdims=True)
+
+
+class Exchange:
+    def __init__(self, place, mine, land, sems, base):
+        self.place, self.mine, self.land = place, mine, land
+        self.sems, self.base = sems, base
+        self.sent = []
+
+    def swap(self, stage, axis):
+        place = self.place
+        send, recv = self.sems
+        own = place.z if axis == "z" else 0
+        for step in steps_of(axis):
+            slot = self.base + 4 * stage + step
+            copy = pltpu.make_async_remote_copy(
+                self.mine.at[stage], self.land.at[stage, own], send.at[slot], recv.at[slot],
+                device_id=place.device(place.at(axis, step)), device_id_type=MESH)
+            copy.start()
+            self.sent.append(copy)
+        if axis == "z":
+            self.land[stage, place.z] = self.mine[stage]
+        for step in steps_of(axis):
+            slot = self.base + 4 * stage + step
+            spot = (place.z - step) % 4 if axis == "z" else 0
+            pltpu.make_async_remote_copy(
+                self.mine.at[stage], self.land.at[stage, spot], send.at[slot], recv.at[slot],
+                device_id=place.device(place.at(axis, step)), device_id_type=MESH).wait_recv()
+        if axis == "z":
+            land = self.land
+            return (land[stage, 0] + land[stage, 1]) + (land[stage, 2] + land[stage, 3])
+        return self.mine[stage] + self.land[stage, 0]
+
+    def finish(self):
+        for copy in self.sent:
+            copy.wait_send()
+
+
+def add_up(exchange, value, picked=None):
+    exchange.mine[0] = value
+    total = exchange.swap(0, "m")
+    if picked is not None:
+        total = jnp.where(picked, total, value)
+    for stage, axis in ((1, "x"), (2, "y"), (3, "z")):
+        exchange.mine[stage] = total
+        total = exchange.swap(stage, axis)
+    return total
+
+
+QKV_LINE, UP_LINE, OUT_LINE, DOWN_LINE, ROW_LINE = 0, 9, 21, 27, 33
+LINES = 40
+WIDTHS = (3 * D // 2, D, FF // 2, D)
+COL_LINES = (QKV_LINE, OUT_LINE, UP_LINE, DOWN_LINE)
+COL_COUNT = (3 * D, D, FF, D)
+ROW_COUNT = (D, D, D, FF)
+
+
+def new_rows_cols(grads, rows_old, cols_old, lines):
+    rows_new, cols_new = [], []
+    for index in range(4):
+        if index in (0, 2):
+            line = ROW_LINE + index // 2
+            count = rows_old[index].shape[1]
+            row_sum = to_column(lines[line:line + 1, :count])
+        else:
+            grad = grads[index][...]
+            row_sum = jnp.sum(grad * grad + EPS_SQUARE, axis=1, keepdims=True)
+        rows_new.append(
+            DECAY * to_column(rows_old[index][...]) + (1.0 - DECAY) * row_sum / COL_COUNT[index])
+        col_sum = get_line(lines, COL_LINES[index], WIDTHS[index])
+        if index == 0:
+            old = cols_old[0]
+            old = jnp.concatenate([old[0:1, :], old[1:2, :], old[2:3, :]], axis=1)
+        else:
+            old = cols_old[index][...]
+        cols_new.append(DECAY * old + (1.0 - DECAY) * col_sum / ROW_COUNT[index])
+    return rows_new, cols_new
+
+
+def place_small(ref, norm, head, ffn, fill):
+    ref[...] = jnp.full(ref.shape, fill, F32)
+    ref[0:6, 0:norm.shape[1]] = norm
+    ref[6:8, 0:head.shape[1]] = head
+    ref[8:9, 0:ffn.shape[1]] = ffn
+
+
+def small_update(grad, old):
+    second = DECAY * old + (1.0 - DECAY) * (grad * grad + EPS_SQUARE)
+    return second, grad * lax.rsqrt(second)
+
+
+def small_sums(values):
+    line = lax.broadcasted_iota(jnp.int32, values.shape, 0)
+    square = values * values
+    return [
+        all_sum(jnp.where((line >= 6) & (line < 8), square, 0.0)),
+        all_sum(jnp.where(line == 8, square, 0.0)),
+        all_sum(jnp.where(line < 6, square, 0.0)),
+    ]
+
+
 def scatter_kernel(count, parts, *refs):
-    fulls, results = refs[:count], refs[count:2 * count]
-    rest = list(refs[2 * count:])
-    held = [rest.pop(0) for _ in range(count)]
-    other = [rest.pop(0) for _ in range(count)]
-    slots = [[[rest.pop(0) for _ in range(3)] for _ in parts[index]] for index in range(count)]
-    send, recv, local = rest
+    refs = list(refs)
+    take = lambda number: [refs.pop(0) for _ in range(number)]
+    fulls = take(count)
+    rows_old, cols_old = take(4), take(4)
+    head_sq, ffn_sq, norm_sq, weight_sums = take(4)
+    results = take(count)
+    lines, totals = take(2)
+    held, other = take(count), take(count)
+    slots = [[take(3) for _ in parts[index]] for index in range(count)]
+    mine_one, land_one, mine_two, land_two, old_small = take(5)
+    send, recv, local = refs
     place = Place()
     greet(place)
     partner = place.device(place.at("m", 1))
@@ -309,26 +471,68 @@
                     path.add(stage - 1, results[index] if stage == 3 else None)
                     if stage < 3:
                         path.start(stage)
+    small, grads = results[0], results[1:]
+    lines[...] = jnp.zeros(lines.shape, F32)
+    for index in range(4):
+        grad = grads[index][...]
+        square = grad * grad + EPS_SQUARE
+        put_line(lines, COL_LINES[index], jnp.sum(square, axis=0, keepdims=True))
+        if index in (0, 2):
+            line = ROW_LINE + index // 2
+            lines[line:line + 1, 0:grad.shape[0]] = to_row(jnp.sum(square, axis=1, keepdims=True))
+    first = Exchange(place, mine_one, land_one, (send, recv), base)
+    line = lax.broadcasted_iota(jnp.int32, lines.shape, 0)
+    value = lines[...]
+    first.mine[0] = value
+    paired = jnp.where(line >= OUT_LINE, first.swap(0, "m"), value)
+    total = paired
+    for stage, axis in ((1, "x"), (2, "y"), (3, "z")):
+        first.mine[stage] = total
+        total = first.swap(stage, axis)
+    lines[...] = jnp.where(line >= ROW_LINE, paired, total)
+    rows_new, cols_new = new_rows_cols(grads, rows_old, cols_old, lines)
+    ratios, row_totals = [], []
+    for index in range(4):
+        grad = grads[index][...]
+        scaled = jnp.sum(grad * grad * (1.0 / cols_new[index]), axis=1, keepdims=True)
+        ratios.append(jnp.sum(scaled / rows_new[index], axis=0, keepdims=True))
+        share = 0.5 if index in (0, 2) else 1.0
+        row_totals.append(jnp.sum(rows_new[index], axis=0, keepdims=True) * share)
+    place_small(old_small, norm_sq[...], head_sq[...], ffn_sq[...], 1.0)
+    _, update = small_update(small[...], old_small[...])
+    second = Exchange(place, mine_two, land_two, (send, recv), base + 16)
+    totals[...] = add_up(
+        second, scalars(ratios + row_totals + small_sums(update)) + weight_sums[...])
     for index in range(count):
         swaps[index].wait_send()
         for path in groups[index]:
             path.finish()
-
-
-def scatter(fulls, rows):
+    first.finish()
+    second.finish()
+
+
+def scatter(fulls, rows, rows_old, cols_old, squares, weight_sums):
     count = len(fulls)
     parts = [column_parts(f.shape[-1]) for f in fulls]
     slots = []
     for full, own in zip(fulls, parts):
         for part in own:
             slots += [pltpu.VMEM(s, full.dtype) for s in slot_shapes(part, full.shape[-2])]
-    sems = sum(1 + 12 * len(own) for own in parts)
+    sems = sum(1 + 12 * len(own) for own in parts) + 32
+    vmem = pl.BlockSpec(memory_space=pltpu.VMEM)
+    outs = [jax.ShapeDtypeStruct((r, f.shape[-1]), F32) for r, f in zip(rows, fulls)]
+    outs += [jax.ShapeDtypeStruct((LINES, 128), F32), jax.ShapeDtypeStruct((8, 128), F32)]
     return pl.pallas_call(
         functools.partial(scatter_kernel, count, parts),
-        out_shape=[jax.ShapeDtypeStruct((r, f.shape[-1]), F32) for r, f in zip(rows, fulls)],
-        in_specs=[pl.BlockSpec(memory_space=pl.ANY)] * count,
-        out_specs=[pl.BlockSpec(memory_space=pltpu.VMEM)] * count,
+        out_shape=outs,
+        in_specs=[pl.BlockSpec(memory_space=pl.ANY)] * count + [vmem] * 12,
+        out_specs=[vmem] * len(outs),
         scratch_shapes=[pltpu.VMEM(f.shape[1:], f.dtype) for f in fulls] * 2 + slots + [
+            pltpu.VMEM((4, LINES, 128), F32),
+            pltpu.VMEM((4, 4, LINES, 128), F32),
+            pltpu.VMEM((4, 8, 128), F32),
+            pltpu.VMEM((4, 4, 8, 128), F32),
+            pltpu.VMEM((16, 128), F32),
             pltpu.SemaphoreType.DMA((sems,)),
             pltpu.SemaphoreType.DMA((sems,)),
             pltpu.SemaphoreType.DMA((count,)),
@@ -336,7 +540,91 @@
         compiler_params=pltpu.CompilerParams(
             collective_id=1, has_side_effects=True, vmem_limit_bytes=56 << 20),
         name="scatter_grads",
-    )(*fulls)
+    )(*fulls, *rows_old, *cols_old, *squares, weight_sums)
+
+
+def step_kernel(*refs):
+    refs = list(refs)
+    take = lambda number: [refs.pop(0) for _ in range(number)]
+    grads = take(4)
+    small, lines, totals = take(3)
+    weights, rows_old, cols_old = take(4), take(4), take(4)
+    head, ffn, norm, head_sq, ffn_sq, norm_sq = take(6)
+    grads_out = take(4)
+    head_grad, ffn_grad, norm_grad = take(3)
+    rows_out, cols_out = take(4), take(4)
+    head_second, ffn_second, norm_second = take(3)
+    weights_out = take(4)
+    head_new, ffn_new, norm_new = take(3)
+    old_small, weight_small = refs
+    half = D // 2
+    rows_new, cols_new = new_rows_cols(grads, rows_old, cols_old, lines)
+    total = lambda lane: totals[0:1, lane:lane + 1]
+    for index in range(4):
+        rows_out[index][...] = to_row(rows_new[index])
+        if index == 0:
+            for part in range(3):
+                cols_out[0][part:part + 1, :] = cols_new[0][:, part * half:(part + 1) * half]
+        else:
+            cols_out[index][...] = cols_new[index]
+        entries = ROW_COUNT[index] * COL_COUNT[index]
+        row_mean = total(4 + index) / ROW_COUNT[index]
+        update_rms = jnp.sqrt(row_mean * total(index) / entries)
+        stride = (
+            RATE * jnp.sqrt(total(11 + index) / entries) / jnp.maximum(1.0, update_rms / CLIP))
+        scale_rows = lax.rsqrt(rows_new[index] / row_mean) * stride
+        scale_cols = lax.rsqrt(cols_new[index])
+        if index == 0:
+            for part in range(3):
+                cut = slice(part * half, (part + 1) * half)
+                grad = grads[0][:, cut]
+                grads_out[0][:, part, :] = grad
+                weights_out[0][:, part, :] = (
+                    weights[0][:, part, :] - grad * scale_rows * scale_cols[:, cut])
+        else:
+            grad = grads[index][...]
+            grads_out[index][...] = grad
+            weights_out[index][...] = weights[index][...] - grad * scale_rows * scale_cols
+    place_small(old_small, norm_sq[...], head_sq[...], ffn_sq[...], 1.0)
+    place_small(weight_small, norm[...], head[...], ffn[...], 0.0)
+    grad = small[...]
+    second, update = small_update(grad, old_small[...])
+    line = lax.broadcasted_iota(jnp.int32, grad.shape, 0)
+    counts = (2 * D, FF, 6 * D)
+    strides = []
+    for index in range(3):
+        update_rms = jnp.sqrt(total(8 + index) / counts[index])
+        strides.append(
+            RATE * jnp.sqrt(total(15 + index) / counts[index])
+            / jnp.maximum(1.0, update_rms / CLIP))
+    stride = jnp.where(line < 6, strides[2], jnp.where(line < 8, strides[0], strides[1]))
+    fresh = weight_small[...] - stride * update
+    for values, (norm_ref, head_ref, ffn_ref) in (
+        (grad, (norm_grad, head_grad, ffn_grad)),
+        (second, (norm_second, head_second, ffn_second)),
+        (fresh, (norm_new, head_new, ffn_new)),
+    ):
+        norm_ref[...] = values[0:6, 0:norm_ref.shape[1]]
+        head_ref[...] = values[6:8, 0:head_ref.shape[1]]
+        ffn_ref[...] = values[8:9, 0:ffn_ref.shape[1]]
+
+
+def step(reduced, lines, totals, weights, rows_old, cols_old, vectors, squares):
+    vmem = pl.BlockSpec(memory_space=pltpu.VMEM)
+    small, grads = reduced[0], reduced[1:]
+    shapes = [w.shape for w in weights] + [v.shape for v in vectors]
+    shapes += [r.shape for r in rows_old] + [c.shape for c in cols_old]
+    shapes += [v.shape for v in vectors] + [w.shape for w in weights] + [v.shape for v in vectors]
+    operands = [*grads, small, lines, totals, *weights, *rows_old, *cols_old, *vectors, *squares]
+    return pl.pallas_call(
+        step_kernel,
+        out_shape=[jax.ShapeDtypeStruct(s, F32) for s in shapes],
+        in_specs=[vmem] * len(operands),
+        out_specs=[vmem] * len(shapes),
+        scratch_shapes=[pltpu.VMEM((16, 128), F32), pltpu.VMEM((16, 128), F32)],
+        compiler_params=pltpu.CompilerParams(vmem_limit_bytes=32 << 20),
+        name="adafactor_step",
+    )(*operands)
 
 
 def layer_norm(values, gain, shift):
@@ -402,34 +690,27 @@
     return lax.axis_size("dp") == 16 and lax.axis_size("mp") == 2
 
 
-def gather_all(shards, kinds):
-    if fast_mesh():
-        full = gather(shards, kinds)
-        return [f.reshape(2, 16, *f.shape[-2:])[:, :, :s.shape[0]] for f, s in zip(full, shards)]
-    both = [lax.all_gather(s.astype(k), "dp", axis=0) for s, k in zip(shards, kinds)]
-    return [lax.all_gather(s, "mp", axis=0) for s in both]
-
-
-def scatter_all(fulls):
-    if fast_mesh():
-        rows = [f.shape[-2] for f in fulls]
-        held = [r + (-r) % (16 if f.dtype == BF else 8) for r, f in zip(rows, fulls)]
-        padded = [
-            jnp.pad(f, ((0, 0), (0, 0), (0, h - r), (0, 0))).reshape(2, 4, 2, 2, h, f.shape[-1])
-            for f, h, r in zip(fulls, held, rows)
-        ]
-        return scatter(padded, rows)
+def small_block(norm, head, ffn):
+    wide = lambda v: jnp.pad(v, [(0, 0)] * (v.ndim - 1) + [(0, 128 - v.shape[-1])])
+    block = jnp.concatenate([wide(norm), wide(head), wide(ffn)], axis=-2)
+    return jnp.pad(block, [(0, 0)] * (block.ndim - 2) + [(0, 16 - block.shape[-2]), (0, 0)])
+
+
+def gather_plain(weights, vectors):
+    head, ffn, norm = vectors
+    qkv, out, up, down = (w.astype(BF) for w in weights)
+    full = []
+    for shard in (small_block(norm, head, ffn), qkv.reshape(qkv.shape[0], -1), out, up, down):
+        full.append(lax.all_gather(lax.all_gather(shard, "dp", axis=0), "mp", axis=0))
+    return full
+
+
+def scatter_plain(fulls):
     out = []
     for full in fulls:
         own = lax.psum_scatter(full.astype(F32), "mp", scatter_dimension=0)
         out.append(lax.psum_scatter(own, "dp", scatter_dimension=0))
     return out
-
-
-def pack_small(head, ffn, norm):
-    flat = jnp.concatenate([head.reshape(-1), ffn.reshape(-1), norm.reshape(-1)])
-    rows = -(-flat.shape[0] // 1024) * 8
-    return jnp.pad(flat, (0, rows * 128 - flat.shape[0])).reshape(rows, 128)
 
 
 def body(
@@ -448,16 +729,21 @@
     own_lengths = lax.dynamic_slice_in_dim(seg_lengths, core * own_rows, own_rows, 0)
     rows_qkv = w_qkv.shape[0]
     half = w_qkv.shape[2]
-    n_head, n_ffn, n_norm = head_bias.size, ffn_bias.size, norm_bias.size
-    small, qkv_g, out_g, up_g, down_g = gather_all(
-        [pack_small(head_bias, ffn_bias, norm_bias), w_qkv.reshape(rows_qkv, -1), w_out, w_up, w_down],
-        [f32, BF, BF, BF, BF],
-    )
-    small = small.reshape(cores, data, -1).astype(BF).astype(f32)
-    head_full = small[:, :, :n_head].reshape(cores, data, 2, -1).transpose(2, 0, 1, 3).reshape(2, D)
-    ffn_full = small[:, :, n_head:n_head + n_ffn].reshape(-1)
-    norm_full = small[:, :, n_head + n_ffn:n_head + n_ffn + n_norm]
-    norm_full = norm_full.reshape(cores, data, 6, -1).transpose(2, 1, 0, 3).reshape(6, D)
+    fast = data == 16 and cores == 2
+    weights = [w_qkv, w_out, w_up, w_down]
+    vectors = [head_bias, ffn_bias.reshape(1, -1), norm_bias]
+    if fast:
+        *gathered, weight_sums = gather(weights, vectors)
+        gathered = [g.reshape(cores, data, *g.shape[-2:]) for g in gathered]
+        gathered[2] = gathered[2][:, :, :w_out.shape[0]]
+    else:
+        gathered = gather_plain(weights, vectors)
+    small, qkv_g, out_g, up_g, down_g = gathered
+    small = small.astype(BF).astype(f32)
+    own_head, own_ffn, own_norm = head_bias.shape[1], ffn_bias.shape[0], norm_bias.shape[1]
+    norm_full = small[:, :, 0:6, :own_norm].transpose(2, 1, 0, 3).reshape(6, D)
+    head_full = small[:, :, 6:8, :own_head].transpose(2, 0, 1, 3).reshape(2, D)
+    ffn_full = small[:, :, 8, :own_ffn].reshape(-1)
     qkv_weight = qkv_g.reshape(cores, D, 3, half).transpose(1, 2, 0, 3).reshape(D, 3 * D)
     out_weight = out_g.reshape(D, D)
     up_weight = up_g.reshape(cores, D, FF // cores).transpose(1, 0, 2).reshape(D, FF)
@@ -516,32 +802,43 @@
     norm_terms = jnp.stack(
         [grad_bias_out, grad_bias_down, grad_gain_one, grad_shift_one, grad_gain_two, grad_shift_two]
     )
-    small_grads = jnp.concatenate(
-        [
-            grad_head.reshape(2, cores, data, -1).transpose(1, 2, 0, 3).reshape(cores, data, -1),
-            grad_bias_up.reshape(cores, data, -1),
-            norm_terms.reshape(6, data, cores, -1).transpose(2, 1, 0, 3).reshape(cores, data, -1),
-        ],
-        axis=-1,
-    )
-    small_rows = -(-small_grads.shape[-1] // 1024) * 8
-    small_grads = jnp.pad(
-        small_grads, ((0, 0), (0, 0), (0, small_rows * 128 - small_grads.shape[-1]))
-    ).reshape(cores, data, small_rows, 128)
+    small_grads = small_block(
+        norm_terms.reshape(6, data, cores, -1).transpose(2, 1, 0, 3),
+        grad_head.reshape(2, cores, data, -1).transpose(1, 2, 0, 3),
+        grad_bias_up.reshape(cores, data, 1, -1),
+    )
     qkv_blocks = grad_qkv.astype(BF).reshape(data, rows_qkv, 3, cores, half)
-    red_small, red_qkv, red_out, red_up, red_down = scatter_all(
-        [
-            small_grads,
-            qkv_blocks.transpose(3, 0, 1, 2, 4).reshape(cores, data, rows_qkv, 3 * half),
-            grad_out.astype(BF).reshape(cores, data, -1, D),
-            grad_up.astype(BF).reshape(data, rows_qkv, cores, -1).transpose(2, 0, 1, 3),
-            grad_down.astype(BF).reshape(cores, data, -1, D),
-        ]
-    )
-    red_small = red_small.reshape(-1)
-    red_head = red_small[:n_head].reshape(head_bias.shape)
-    red_ffn = red_small[n_head:n_head + n_ffn]
-    norm_grad = red_small[n_head + n_ffn:n_head + n_ffn + n_norm].reshape(norm_bias.shape)
+    fulls = [
+        small_grads,
+        qkv_blocks.transpose(3, 0, 1, 2, 4).reshape(cores, data, rows_qkv, 3 * half),
+        grad_out.astype(BF).reshape(cores, data, -1, D),
+        grad_up.astype(BF).reshape(data, rows_qkv, cores, -1).transpose(2, 0, 1, 3),
+        grad_down.astype(BF).reshape(cores, data, -1, D),
+    ]
+    if fast:
+        fulls[2] = jnp.pad(fulls[2], ((0, 0), (0, 0), (0, 32 - w_out.shape[0]), (0, 0)))
+        fulls = [f.reshape(2, 4, 2, 2, *f.shape[-2:]) for f in fulls]
+        rows_old = [v.reshape(1, -1) for v in (qkv_rows, out_rows, up_rows, down_rows)]
+        cols_old = [qkv_cols] + [v.reshape(1, -1) for v in (out_cols, up_cols, down_cols)]
+        old = [head_bias_sq, ffn_bias_sq.reshape(1, -1), norm_sq]
+        *reduced, lines, totals = scatter(
+            fulls, [16, rows_qkv, w_out.shape[0], rows_qkv, w_down.shape[0]],
+            rows_old, cols_old, old, weight_sums)
+        new = step(reduced, lines, totals, weights, rows_old, cols_old, vectors, old)
+        grads, (g_head, g_ffn, g_norm) = new[:4], new[4:7]
+        rows_new, cols_new = [r.reshape(-1) for r in new[7:11]], new[11:15]
+        cols_new = [cols_new[0]] + [c.reshape(-1) for c in cols_new[1:]]
+        (s_head, s_ffn, s_norm), mats = new[15:18], new[18:22]
+        n_head, n_ffn, n_norm = new[22:25]
+        stats = [v for pair in zip(rows_new, cols_new) for v in pair]
+        return (
+            output.astype(BF), pooled, input_grad, *grads, g_head, g_ffn.reshape(-1), g_norm, *stats,
+            s_head, s_ffn.reshape(-1), s_norm, *mats, n_head, n_ffn.reshape(-1), n_norm,
+        )
+    red_small, red_qkv, red_out, red_up, red_down = scatter_plain(fulls)
+    norm_grad = red_small[0:6, :own_norm]
+    red_head = red_small[6:8, :own_head]
+    red_ffn = red_small[8, :own_ffn]
     weights_flat = [w_qkv.reshape(rows_qkv, -1), w_out, w_up, w_down]
     grads_flat = [red_qkv, red_out, red_up, red_down]
     rows_old = [qkv_rows, out_rows, up_rows, down_rows]

time: 775 us -> 583 us (0.75)
  blocking collectives: 154 us -> 0 us
  other arithmetic: 73.6 us -> 46.9 us
  Pallas kernels: 198 us -> 215 us
  between operations: 15.7 us -> 1.89 us
  local copies, waits for them, and re-layouts: 155 us -> 143 us
    psum x4 -> x0, blocking collectives: 154 us -> none  [the longest x1 75.2 us: body(): col_qkv, col_up = lax.psum((col_parts[0], col_parts[2]), 'dp')]
    reduce_sum x20 -> x0, other arithmetic: 19.6 us -> none  [the longest x4 6.7 us: body(): jnp.sum(grads_flat[index] * grads_flat[index] / (rows_new[index][:, None]...]
    pallas_call x1, Pallas kernels: 97.7 us -> 113 us  [scatter(): pl.pallas_call(functools.partial(scatter_kernel, count, parts), out_shape...]
    reshape x15 -> x5, local copies, waits for them, and re-layouts: 16.7 us -> 1.84 us  [the longest x3 1.76 us: body(): v.reshape(1, -1)]
    unnamed x154 -> x150, local copies, waits for them, and re-layouts: 19.1 us -> 25.7 us
    pallas_call x1 -> x2, Pallas kernels: 100 us -> 102 us  [the longest x1 101 us: gather(): pl.pallas_call(gather_kernel, out_shape=[jax.ShapeDtypeStruct((2, 4, 2, 2...]
where the time goes in v2:
time: 583 us; the launch traced here: 575 us
  Pallas kernels  215 us (37%)
  matrix products  167 us (29%)
  local copies, waits for them, and re-layouts  143 us (25%)
  other arithmetic  46.9 us (8%)
    pallas_call x1, Pallas kernels, scatter(): pl.pallas_call(functools.partial(scatter_kernel, count, parts), out_shape...  113 us
    pallas_call x1, Pallas kernels, gather(): pl.pallas_call(gather_kernel, out_shape=[jax.ShapeDtypeStruct((2, 4, 2, 2...  101 us
    dot_general x1, matrix products, body(): inner = jnp.dot(hidden_b, up_weight, preferred_element_type=f32) + ffn_full  36.2 us
    unnamed x150, local copies, waits for them, and re-layouts  25.7 us
    dot_general x1, matrix products, body(): grad_act = jnp.dot(grad_branch, down_weight.T, preferred_element_type=f32)  18 us
    reshape x2, local copies, waits for them, and re-layouts, body(): grad_up.astype(BF).reshape(data, rows_qkv, cores, -1).transpose(2, 0, 1, 3)  17.6 us
    dot_general x2, matrix products, attend_back(): jnp.einsum('qhd,khd->hqk', grad_context, packed[:, 2], preferred_element_...  14.2 us
    convert_element_type x2, other arithmetic, attend_back(): grad_scores = (probs * (grad_probs - inner_sum)).astype(BF)  14 us

profile of v2, /device:TPU:0, one launch (start us, length us, event | category | flops | bytes accessed | tf_op | source)
XLA Modules:
  0.0 575.1 jit_solution(14053833183673268835)
XLA Ops:
  6.6 100.9 %gather_weights.1 = (f32[2,4,2,2,16,128]{5,4,3,2,1,0:T(8,128)S(1)}, bf16[2,4,2,2,48,1152]{5,4,3,2,1,0:T(8,128)(2,1)}, bf16[2,4,2,2,32,768]{5,4,3,2,1,0:T(8,128)(...) custom-call(f32[48,3,384]{2,1,0:T(4,128)S(1)} %copy.112.refs_0_.refs, ...), custom_call_target="tpu_custom_call" | custom-call | tf_op jit(solution)/shard_map/gather_weights/pallas_call | solution.py:186
  109.8 8.5 %reshape_reshape.18 = bf16[2,768,3,384]{3,2,1,0:T(4,128)(2,1)} reshape(bf16[2,4,2,2,48,1152]{5,4,3,2,1,0:T(8,128)(2,1)} %get-tuple-element.126) | data formatting | bytes 7077888 | tf_op jit(solution)/shard_map/reshape;reshape | solution.py:747
  118.3 8.1 %copy.113 = bf16[768,3,2,384]{0,3,2,1:T(8,128)(2,1)} copy(bf16[768,3,2,384]{3,1,0,2:T(4,128)(2,1)} %bitcast.208) | data formatting | bytes 7077888 | tf_op jit(solution)/shard_map/transpose | solution.py:747
  126.5 8.3 %convolution_bitcast_fusion = f32[1024,2304]{0,1:T(8,128)} fusion(bf16[768,2304]{0,1:T(8,128)(2,1)} %bitcast.218, bf16[1024,768]{1,0:T(8,128)(2,1)S(1)} %copy-done.66), kind=kOutput, calls=%fused_computation.68 | convolution fusion | flops 3623878656 | bytes 14548992 | tf_op jit(solution)/shard_map/dot_general | solution.py:753
  134.8 13.3 %reshape.418 = f32[2,512,3,12,64]{1,0,4,3,2:T(2,128)} reshape(f32[1024,2304]{0,1:T(8,128)} %convolution_bitcast_fusion) | data formatting | bytes 18874368 | tf_op jit(solution)/shard_map/reshape | solution.py:753
  148.0 7.3 %fusion.35 = bf16[2,512,3,12,64]{1,4,3,2,0:T(8,128)(2,1)} fusion(f32[2,512,3,12,64]{1,0,4,3,2:T(2,128)} %reshape.418, f32[3,12,64]{2,1,0:T(8,128)S(1)} %pad_maximum_fusion), kind=kLoop, calls=%fused_computation.67 | loop fusion | flops 4718592 | bytes 14164992 | tf_op jit(solution)/shard_map/convert_element_type | solution.py:754
  155.7 25.8 %while.22 = (s32[]{:T(128)}, bf16[2,512,768]{2,1,0:T(8,128)(2,1)}, f32[2,12,512]{2,1,0:T(8,128)S(1)}, bf16[2,512,3,12,64]{1,4,3,2,0:T(8,128)(2,1)}, s32[2,512]{1,0:T(2,128)S(1)}, /*index=5*/s32[]{:T(128)}) while((s32[]{:T(128)}, bf16[2,512,768]{2,1,0:T(8,128)(2,1)}, f32[2,12,512]{2,1,0:T(8,128)S(1)}, bf16[2,512,3,12,64]{1,4,3,2,0:T(8,128)(2,1)}, ...), condition=%wide.region_5.6_spmd, body=%wide.region_2.5_spmd.sunk | while | flops 843704320 | bytes 59472492 | solution.py:755
  193.4 36.2 %multiply_convert_fusion.3 = (bf16[1024,3072]{1,0:T(8,128)(2,1)}, f32[1024,3072]{1,0:T(8,128)}, f32[1024,3072]{1,0:T(8,128)}) fusion(f32[3072]{0:T(1024)S(1)} %add.137, bf16[768,3072]{0,1:T(8,128)(2,1)} %bitcast.215, f32[1024,768]{1,0:T(8,128)S(1)} %get-tuple-element.360, f32[768]{0:T(1024)S(1)} %add.134, f32[768]{0:T(1024)S(1)} %mul.172, ...), kind=kOutput, calls=%fused_computation.52 | convolution fusion | flops 5043388416 | bytes 39348224 | tf_op jit(solution)/shard_map/dot_general | solution.py:764
  229.7 9.3 %fusion.57 = (f32[1024]{0:T(1024)S(1)}, f32[1024,768]{1,0:T(8,128)S(1)}) fusion(f32[768]{0:T(1024)S(1)} %add.140, bf16[1024,3072]{1,0:T(8,128)(2,1)} %get-tuple-element.343, bf16[3072,768]{1,0:T(8,128)(2,1)} %bitcast.232, f32[768]{0:T(1024)S(1)} %add.134, f32[768]{0:T(1024)S(1)} %mul.172, f32[1024]{0:T(1024)S(1)} %fusion.45, f32[1024,768]{1,0:T(8,128)} %copy-done.37, ...), kind=kOutput, calls=%fused_computation.141 | convolution fusion | flops 4837342208 | bytes 17323008 | tf_op jit(solution)/shard_map/dot_general | solution.py:767
  249.7 9.7 %convolution_convert_fusion = bf16[3072,768]{1,0:T(8,128)(2,1)} fusion(bf16[1024,3072]{1,0:T(8,128)(2,1)} %get-tuple-element.343, bf16[1024,768]{1,0:T(8,128)(2,1)S(1)} %get-tuple-element.334), kind=kOutput, calls=%fused_computation.69 | convolution fusion | flops 4834197504 | bytes 12582912 | tf_op jit(solution)/shard_map/dot_general | solution.py:778
  259.5 18.0 %convert_reduce_fusion = (f32[3072]{0:T(1024)}, bf16[1024,3072]{1,0:T(8,128)(2,1)}) fusion(f32[1024,3072]{1,0:T(8,128)} %get-tuple-element.344, bf16[1024,768]{1,0:T(8,128)(2,1)S(1)} %get-tuple-element.334, bf16[3072,768]{1,0:T(8,128)(2,1)} %bitcast.233, f32[1024,3072]{1,0:T(8,128)} %get-tuple-element.361, f32[3072]{0:T(1024)S(1)} %add.137), kind=kOutput, calls=%fused_computation.50 | convolution fusion | flops 4885312512 | bytes 37773312 | tf_op jit(solution)/shard_map/dot_general | solution.py:777
  277.5 9.8 %convolution_convert_fusion.1 = bf16[768,3072]{1,0:T(8,128)(2,1)} fusion(bf16[1024,3072]{1,0:T(8,128)(2,1)} %get-tuple-element.366, f32[1024,768]{1,0:T(8,128)S(1)} %copy-done.38, f32[768]{0:T(1024)S(1)} %add.134, f32[768]{0:T(1024)S(1)} %mul.172, f32[1024]{0:T(1024)S(1)} %fusion.45, f32[1024]{0:T(1024)S(1)} %broadcast_multiply_fusion.1), kind=kOutput, calls=%fused_computation.70 | convolution fusion | flops 4838129664 | bytes 14170112 | tf_op jit(solution)/shard_map/dot_general | solution.py:781
  287.3 11.8 %reshape.431 = bf16[16,48,2,1536]{3,2,1,0:T(2,128)(2,1)} reshape(bf16[768,3072]{1,0:T(8,128)(2,1)} %convolution_convert_fusion.1) | data formatting | bytes 9437184 | tf_op jit(solution)/shard_map/reshape | solution.py:815
  305.9 8.9 %multiply_reduce_fusion.1 = (f32[768]{0:T(1024)}, f32[1024]{0:T(1024)S(1)}, f32[768]{0:T(1024)}, f32[1024,768]{1,0:T(8,128)S(1)}) fusion(f32[1024,768]{1,0:T(8,128)S(1)} %copy-done.38, f32[1024]{0:T(1024)S(1)} %fusion.45, f32[1024]{0:T(1024)S(1)} %broadcast_multiply_fusion.1, f32[768]{0:T(1024)S(1)} %mul.172, bf16[1024,3072]{1,0:T(8,128)(2,1)S(1)} %copy-done.69, ...), kind=kOutput, calls=%fused_computation.84 | convolution fusion | flops 4839699456 | bytes 20472832 | tf_op jit(solution)/shard_map/dot_general | solution.py:782
  328.0 52.5 %while.23 = (s32[]{:T(128)}, bf16[2,512,3,12,64]{1,4,3,2,0:T(8,128)(2,1)}, bf16[2,512,3,12,64]{1,4,3,2,0:T(8,128)(2,1)}, s32[2,512]{1,0:T(2,128)S(1)}, f32[2,12,...) while((s32[]{:T(128)}, bf16[2,512,3,12,64]{1,4,3,2,0:T(8,128)(2,1)}, ...), condition=%wide.region_16.17_spmd, body=%wide.region_14.16_spmd.sunk | while | flops 2069751808 | bytes 112917088 | solution.py:788
  332.2 7.1 %multiply_reduce_fusion.6 = (f32[12,512]{1,0:T(8,128)S(1)}, f32[12,512,512]{1,2,0:T(8,128)}) fusion(f32[12,512,512]{1,2,0:T(8,128)S(1)} %fusion.101, f32[12,512]{1,0:T(8,128)S(1)} %dynamic-slice_bitcast_fusion.8, pred[512,512]{0,1:T(8,128)(4,1)S(1)} %broadcast_compare_fusion.5, bf16[512,3,12,64]{0,3,2,1:T(8,128)(2,1)S(1)} %dynamic-slice_bitcast_fusion.7, ...), kind=kOutput, calls=%fused_computation.19.clone.1 | convolution fusion | flops 418375680 | bytes 27058180 | tf_op jit(solution)/shard_map/while/body/eval_jaxpr/qhd,khd->hqk/dot_general | solution.py:675
  339.3 7.0 %multiply_convert_fusion.5 = bf16[12,512,512]{1,2,0:T(8,128)(2,1)S(1)} fusion(f32[12,512,512]{1,2,0:T(8,128)} %get-tuple-element.441, f32[12,512,512]{1,2,0:T(8,128)S(1)} %fusion.101, f32[12,512]{1,0:T(8,128)S(1)} %get-tuple-element.442, f32[12,512]{1,0:T(8,128)S(1)} %dynamic-slice_bitcast_fusion.8, pred[512,512]{0,1:T(8,128)(4,1)S(1)} %broadcast_compare_fusion.5), kind=kLoop, calls=%fused_computation.18.clone.1 | loop fusion | flops 18874368 | bytes 31768576 | tf_op jit(solution)/shard_map/while/body/eval_jaxpr/convert_element_type | solution.py:679
  358.1 7.1 %multiply_reduce_fusion.6 = (f32[12,512]{1,0:T(8,128)S(1)}, f32[12,512,512]{1,2,0:T(8,128)}) fusion(f32[12,512,512]{1,2,0:T(8,128)S(1)} %fusion.101, f32[12,512]{1,0:T(8,128)S(1)} %dynamic-slice_bitcast_fusion.8, pred[512,512]{0,1:T(8,128)(4,1)S(1)} %broadcast_compare_fusion.5, bf16[512,3,12,64]{0,3,2,1:T(8,128)(2,1)S(1)} %dynamic-slice_bitcast_fusion.7, ...), kind=kOutput, calls=%fused_computation.19.clone.1 | convolution fusion | flops 418375680 | bytes 27058180 | tf_op jit(solution)/shard_map/while/body/eval_jaxpr/qhd,khd->hqk/dot_general | solution.py:675
  365.2 7.0 %multiply_convert_fusion.5 = bf16[12,512,512]{1,2,0:T(8,128)(2,1)S(1)} fusion(f32[12,512,512]{1,2,0:T(8,128)} %get-tuple-element.441, f32[12,512,512]{1,2,0:T(8,128)S(1)} %fusion.101, f32[12,512]{1,0:T(8,128)S(1)} %get-tuple-element.442, f32[12,512]{1,0:T(8,128)S(1)} %dynamic-slice_bitcast_fusion.8, pred[512,512]{0,1:T(8,128)(4,1)S(1)} %broadcast_compare_fusion.5), kind=kLoop, calls=%fused_computation.18.clone.1 | loop fusion | flops 18874368 | bytes 31768576 | tf_op jit(solution)/shard_map/while/body/eval_jaxpr/convert_element_type | solution.py:679
  380.5 9.4 %copy.121 = bf16[2,512,3,12,64]{1,0,4,3,2:T(2,128)(2,1)} copy(bf16[2,512,3,12,64]{1,4,3,2,0:T(8,128)(2,1)} %get-tuple-element.133) | data formatting | bytes 9437184 | tf_op jit(solution)/shard_map/while | solution.py:788
  415.5 9.6 %reshape_reshape.22.refs_1_ = bf16[2,4,2,2,48,1152]{5,4,3,2,1,0:T(8,128)(2,1)} reshape(bf16[2,16,48,3,384]{4,3,2,1,0:T(4,128)(2,1)} %copy.128) | data formatting | bytes 7077888 | tf_op jit(solution)/shard_map/reshape;reshape | solution.py:820
  425.9 8.9 %reshape.425 = bf16[1024,3,768]{0,2,1:T(8,128)(2,1)} reshape(bf16[2,512,3,12,64]{1,0,4,3,2:T(2,128)(2,1)} %copy.121) | data formatting | bytes 9437184 | tf_op jit(solution)/shard_map/reshape | solution.py:792
  440.3 113.0 %scatter_grads.1 = (f32[16,128]{1,0:T(8,128)}, f32[48,1152]{1,0:T(8,128)}, f32[24,768]{1,0:T(8,128)}, f32[48,1536]{1,0:T(8,128)}, f32[96,768]{1,0:T(8,128)}, /*index=5*/f32[40,128]{1,0:T(8,128)}, f32[8,128]{1,0:T(8,128)}) custom-call(f32[2,4,2,2,16,128]{5,4,3,2,1,0:T(8,128)} %bitcast.226, bf16[2,4,2,2,48,1152]{5,4,3,2,1,0:T(8,128)(2,1)} %reshape_reshape.22.refs_1_, ...), custom_call_target="tpu_custom_call" | custom-call | tf_op jit(solution)/shard_map/scatter_grads/pallas_call | solution.py:525
  564.0 9.2 %add_add_fusion.4 = f32[1024,768]{1,0:T(8,128)} fusion(f32[1024,768]{1,0:T(8,128)S(1)} %copy-done.36, bf16[1024,2304]{0,1:T(8,128)(2,1)} %bitcast.214, bf16[768,2304]{0,1:T(8,128)(2,1)} %bitcast.219, f32[1024]{0:T(1024)S(1)} %copy-done.57), kind=kOutput, calls=%fused_computation.94 | convolution fusion | flops 3625451520 | bytes 14553088 | tf_op jit(solution)/shard_map/dot_general | solution.py:801
  (269 shorter events, 143.6 us)
Async XLA Ops:
  155.7 25.8 %copy-start.43 = (bf16[2,4,2,2,16,128]{5,4,3,2,1,0:T(8,128)(2,1)S(1)}, bf16[2,4,2,2,16,128]{5,4,3,2,1,0:T(8,128)(2,1)}, u32[]{:S(2)}) copy-start(bf16[2,4,2,2,16,128]{5,4,3,2,1,0:T(8,128)(2,1)} %copy-done.42) | copy-start | bytes 393220
  259.5 18.0 %copy-start.38 = (f32[1024,768]{1,0:T(8,128)S(1)}, f32[1024,768]{1,0:T(8,128)}, u32[]{:S(2)}) copy-start(f32[1024,768]{1,0:T(8,128)} %copy-done.37) | copy-start | bytes 9437188
  425.9 13.1 %copy-start.64 = (f32[768]{0:T(1024)S(1)}, f32[768]{0:T(1024)}, u32[]{:S(2)}) copy-start(f32[768]{0:T(1024)} %param.38) | copy-start | bytes 9220
  425.9 13.7 %copy-start.65 = (f32[768]{0:T(1024)S(1)}, f32[768]{0:T(1024)}, u32[]{:S(2)}) copy-start(f32[768]{0:T(1024)} %param.42) | copy-start | bytes 9220
  440.1 113.2 %copy-start.1 = (f32[48,3,384]{2,1,0:T(4,128)S(1)}, f32[48,3,384]{2,1,0:T(4,128)}, u32[]{:S(2)}) copy-start(f32[48,3,384]{2,1,0:T(4,128)} %copy-done) | copy-start | bytes 663556
  440.1 113.2 %copy-start.3 = (f32[48,1536]{1,0:T(8,128)S(1)}, f32[48,1536]{1,0:T(8,128)}, u32[]{:S(2)}) copy-start(f32[48,1536]{1,0:T(8,128)} %refs_9_.3) | copy-start | bytes 884740
  440.1 113.2 %copy-start.5 = (f32[96,768]{1,0:T(8,128)S(1)}, f32[96,768]{1,0:T(8,128)}, u32[]{:S(2)}) copy-start(f32[96,768]{1,0:T(8,128)} %refs_10_.1) | copy-start | bytes 884740
  440.1 113.2 %copy-start.7 = (f32[24,768]{1,0:T(8,128)S(1)}, f32[24,768]{1,0:T(8,128)}, u32[]{:S(2)}) copy-start(f32[24,768]{1,0:T(8,128)} %refs_8_.1) | copy-start | bytes 221188
  440.1 113.2 %copy-start.12 = (f32[1,1536]{1,0:T(1,128)S(1)}, f32[1,1536]{1,0:T(1,128)}, u32[]{:S(2)}) copy-start(f32[1,1536]{1,0:T(1,128)} %reshape.438.refs_11_.refs_17_) | copy-start | bytes 18436
  440.1 113.2 %copy-start.13 = (f32[1,768]{1,0:T(1,128)S(1)}, f32[1,768]{1,0:T(1,128)}, u32[]{:S(2)}) copy-start(f32[1,768]{1,0:T(1,128)} %reshape.437.refs_10_.refs_16_) | copy-start | bytes 9220
  440.2 113.2 %copy-start.14 = (f32[1,768]{1,0:T(1,128)S(1)}, f32[1,768]{1,0:T(1,128)}, u32[]{:S(2)}) copy-start(f32[1,768]{1,0:T(1,128)} %reshape.439.refs_12_.refs_18_) | copy-start | bytes 9220
  440.2 113.2 %copy-start.15 = (f32[3,384]{1,0:T(4,128)S(1)}, f32[3,384]{1,0:T(4,128)}, u32[]{:S(2)}) copy-start(f32[3,384]{1,0:T(4,128)} %refs_15_.3) | copy-start | bytes 13828
  440.2 113.2 %copy-start.18 = (f32[6,24]{1,0:T(8,128)S(1)}, f32[6,24]{1,0:T(8,128)}, u32[]{:S(2)}) copy-start(f32[6,24]{1,0:T(8,128)} %refs_21_.1) | copy-start | bytes 1732
  440.2 113.2 %copy-start.19 = (f32[6,24]{1,0:T(8,128)S(1)}, f32[6,24]{1,0:T(8,128)}, u32[]{:S(2)}) copy-start(f32[6,24]{1,0:T(8,128)} %refs_24_.1) | copy-start | bytes 1732
  440.2 113.2 %copy-start.22 = (f32[2,24]{1,0:T(2,128)S(1)}, f32[2,24]{1,0:T(2,128)}, u32[]{:S(2)}) copy-start(f32[2,24]{1,0:T(2,128)} %refs_22_.1) | copy-start | bytes 580
  440.2 113.2 %copy-start.24 = (f32[2,24]{1,0:T(2,128)S(1)}, f32[2,24]{1,0:T(2,128)}, u32[]{:S(2)}) copy-start(f32[2,24]{1,0:T(2,128)} %refs_19_.1) | copy-start | bytes 580
  440.2 113.2 %copy-start.27 = (f32[96]{0:T(128)S(1)}, f32[96]{0:T(128)}, u32[]{:S(2)}) copy-start(f32[96]{0:T(128)} %param.33) | copy-start | bytes 1156
  440.2 113.2 %copy-start.28 = (f32[48]{0:T(128)S(1)}, f32[48]{0:T(128)}, u32[]{:S(2)}) copy-start(f32[48]{0:T(128)} %param.35) | copy-start | bytes 580
  440.3 113.2 %copy-start.29 = (f32[24]{0:T(128)S(1)}, f32[24]{0:T(128)}, u32[]{:S(2)}) copy-start(f32[24]{0:T(128)} %param.37) | copy-start | bytes 292
  440.3 113.2 %copy-start.30 = (f32[48]{0:T(128)S(1)}, f32[48]{0:T(128)}, u32[]{:S(2)}) copy-start(f32[48]{0:T(128)} %param.39) | copy-start | bytes 580
  440.3 113.2 %copy-start.31 = (f32[96]{0:T(128)S(1)}, f32[96]{0:T(128)}, u32[]{:S(2)}) copy-start(f32[96]{0:T(128)} %param.41) | copy-start | bytes 1156
  440.3 113.2 %copy-start.32 = (f32[96]{0:T(128)S(1)}, f32[96]{0:T(128)}, u32[]{:S(2)}) copy-start(f32[96]{0:T(128)} %param.44) | copy-start | bytes 1156
  440.3 123.7 %copy-start.36 = (f32[1024,768]{1,0:T(8,128)S(1)}, f32[1024,768]{1,0:T(8,128)}, u32[]{:S(2)}) copy-start(f32[1024,768]{1,0:T(8,128)} %copy-done.35) | copy-start | bytes 9437188
  440.3 123.6 %copy-start.57 = (f32[1024]{0:T(1024)S(1)}, f32[1024]{0:T(1024)}, u32[]{:S(2)}) copy-start(f32[1024]{0:T(1024)} %copy-done.56) | copy-start | bytes 12292
  (47 other events, 216.5 us)

commit v3 on v2

--- a/solution.py
+++ b/solution.py
@@ -627,67 +627,353 @@
     )(*operands)
 
 
-def layer_norm(values, gain, shift):
+HALF = D // 2
+QKV_HALF = 3 * HALF
+VMEM = pl.BlockSpec(memory_space=pltpu.VMEM)
+SMEM = pl.BlockSpec(memory_space=pltpu.SMEM)
+
+
+def dot(a, b):
+    return jnp.dot(a, b, preferred_element_type=F32)
+
+
+def dot_last(a, b):
+    return lax.dot_general(a, b, (((1,), (1,)), ((), ())), preferred_element_type=F32)
+
+
+def dot_first(a, b):
+    return lax.dot_general(a, b, (((0,), (0,)), ((), ())), preferred_element_type=F32)
+
+
+def ids_at(lengths, row, places):
+    bound = jnp.int32(0)
+    ids = jnp.zeros(places.shape, jnp.int32)
+    for segment in range(SEGS):
+        bound = bound + lengths[row, segment]
+        ids = ids + (places >= bound).astype(jnp.int32)
+    return ids
+
+
+def set_bias(bias, lengths, row):
+    down = ids_at(lengths, row, lax.broadcasted_iota(jnp.int32, (LEN, 1), 0))
+    across = ids_at(lengths, row, lax.broadcasted_iota(jnp.int32, (1, LEN), 1))
+    bias[...] = jnp.where(down == across, 0.0, -1e30)
+
+
+def half_masks():
+    lane = lax.broadcasted_iota(jnp.int32, (1, 128), 1)
+    return [((lane // HD) == half).astype(F32).astype(BF) for half in range(2)]
+
+
+def slab(ref, core, row, part, pair):
+    return ref[core, pl.ds(pl.multiple_of(row * LEN, LEN), LEN),
+               pl.ds(pl.multiple_of(part * HALF + pair * 128, 128), 128)]
+
+
+def project(tokens, weight, offsets, qkv, row):
+    rows = pl.ds(pl.multiple_of(row * LEN, LEN), LEN)
+    values = tokens[rows, :]
+    for core in range(2):
+        for part in range(3):
+            cut = slice(part * HALF, (part + 1) * HALF)
+            out = (dot(values, weight[core, :, cut]) + offsets[core, :, cut]).astype(BF)
+            if part == 0:
+                out = out * jnp.asarray(HD ** -0.5, BF)
+            qkv[core, rows, cut] = out
+
+
+def attend(qkv, bias, context, lse, held, row):
+    rows = pl.ds(pl.multiple_of(row * LEN, LEN), LEN)
+    lane = lax.broadcasted_iota(jnp.int32, (LEN, 128), 1)
+    held[...] = jnp.zeros(held.shape, F32)
+
+    @pl.loop(0, 6)
+    def _(item):
+        core, pair = item // 3, item % 3
+        queries, keys, values = (slab(qkv, core, row, part, pair) for part in range(3))
+        wide = jnp.concatenate([values, jnp.ones_like(values)], axis=1)
+        outs = []
+        logs = held[...]
+        for half, mask in enumerate(half_masks()):
+            scores = dot_last(queries * mask, keys) + bias[...]
+            peak = jnp.max(scores, axis=1, keepdims=True)
+            raised = jnp.exp(scores - peak).astype(BF)
+            both = dot(raised, wide)
+            total = both[:, 128:]
+            outs.append(both[:, :128] / total)
+            logs = jnp.where(lane == item * 2 + half, peak + jnp.log(total), logs)
+        held[...] = logs
+        context[rows, pl.ds(pl.multiple_of(item * 128, 128), 128)] = jnp.where(
+            lane < HD, outs[0], outs[1]).astype(BF)
+
+    lse[row] = held[...].T[0:16, :]
+
+
+def forward_kernel(tokens, weight, offsets, lengths, qkv, context, lse, bias, held):
+    core = lax.axis_index("mp")
+
+    @pl.loop(0, 2)
+    def _(row):
+        set_bias(bias, lengths, core * 2 + row)
+        project(tokens, weight, offsets, qkv, row)
+        attend(qkv, bias, context, lse, held, row)
+
+
+def forward(tokens, weight, offsets, lengths):
+    count = tokens.shape[0]
+    return pl.pallas_call(
+        forward_kernel,
+        out_shape=[
+            jax.ShapeDtypeStruct((2, count, QKV_HALF), BF),
+            jax.ShapeDtypeStruct((count, D), BF),
+            jax.ShapeDtypeStruct((count // LEN, 16, LEN), F32),
+        ],
+        in_specs=[VMEM, VMEM, VMEM, SMEM],
+        out_specs=[VMEM] * 3,
+        scratch_shapes=[pltpu.VMEM((LEN, LEN), F32), pltpu.VMEM((LEN, 128), F32)],
+        compiler_params=pltpu.CompilerParams(vmem_limit_bytes=56 << 20),
+        name="project_attend",
+    )(tokens, weight, offsets, lengths)
+
+
+def gelu_both(inner):
+    cdf = 0.5 * (1.0 + lax.erf(inner * 0.7071067811865476))
+    density = 0.3989422804014327 * jnp.exp(-0.5 * inner * inner)
+    return inner * cdf, cdf + inner * density
+
+
+def norm_parts(values):
     center = values - jnp.mean(values, axis=-1, keepdims=True)
-    spread = jnp.mean(center * center, axis=-1, keepdims=True)
-    return center * lax.rsqrt(spread + EPS_NORM) * gain + shift
-
-
-def gelu_exact(values):
-    return jax.nn.gelu(values, approximate=False)
-
-
-def segment_ids(lengths, length):
-    bounds = jnp.cumsum(lengths, axis=-1)
-    places = jnp.arange(length, dtype=jnp.int32)
-    return jnp.sum((places[None, :, None] >= bounds[:, None, :]).astype(jnp.int32), axis=-1)
-
-
-def row_scores(packed, row_ids):
-    scores = jnp.einsum(
-        "qhd,khd->hqk", packed[:, 0], packed[:, 1], preferred_element_type=F32
-    ) * HD ** (-0.5)
-    same = row_ids[:, None] == row_ids[None, :]
-    return jnp.where(same[None], scores, -1e30)
-
-
-def attend_row(packed, row_ids):
-    scores = row_scores(packed, row_ids)
-    peak = jnp.max(scores, axis=-1, keepdims=True)
-    raised = jnp.exp(scores - peak)
-    total = jnp.sum(raised, axis=-1, keepdims=True)
-    probs = raised / total
-    context = jnp.einsum(
-        "hqk,khd->qhd", probs.astype(BF), packed[:, 2], preferred_element_type=F32
+    scale = lax.rsqrt(jnp.mean(center * center, axis=-1, keepdims=True) + EPS_NORM)
+    return center * scale, scale
+
+
+def norm_back(grad, normed, scale, gain):
+    scaled = grad * gain
+    mean = jnp.mean(scaled, axis=-1, keepdims=True)
+    along = jnp.mean(scaled * normed, axis=-1, keepdims=True)
+    return (
+        (scaled - mean - normed * along) * scale,
+        jnp.sum(grad * normed, axis=0, keepdims=True),
+        jnp.sum(grad, axis=0, keepdims=True),
     )
-    return (
-        context.astype(BF).reshape(context.shape[0], -1),
-        (peak + jnp.log(total))[..., 0],
-    )
-
-
-def attend_back(packed, grad_context, log_total, row_ids):
-    scores = row_scores(packed, row_ids)
-    probs = jnp.exp(scores - log_total[..., None])
-    grad_values = jnp.einsum(
-        "hqk,qhd->khd", probs.astype(BF), grad_context, preferred_element_type=F32
-    )
-    grad_probs = jnp.einsum(
-        "qhd,khd->hqk", grad_context, packed[:, 2], preferred_element_type=F32
-    )
-    inner_sum = jnp.sum(probs * grad_probs, axis=-1, keepdims=True)
-    grad_scores = (probs * (grad_probs - inner_sum)).astype(BF)
-    grad_queries = jnp.einsum(
-        "hqk,khd->qhd", grad_scores, packed[:, 1], preferred_element_type=F32
-    ) * HD ** (-0.5)
-    grad_keys = jnp.einsum(
-        "hqk,qhd->khd", grad_scores, packed[:, 0], preferred_element_type=F32
-    ) * HD ** (-0.5)
-    return jnp.stack([grad_queries, grad_keys, grad_values], axis=1).astype(BF)
-
-
-def fast_mesh():
-    return lax.axis_size("dp") == 16 and lax.axis_size("mp") == 2
+
+
+CHUNK = 512
+
+
+def middle(row, core, tokens, context, cotangent, lengths, w_out, w_up, w_down, ffn, norm, layer_out,
+           pooled, hidden_b, act, grad_branch, grad_inner, grad_attended, grad_context,
+           grad_one, delta, norm_sums, ffn_sums, slope, branch, hidden, normed_one, grad_two):
+    rows = pl.ds(pl.multiple_of(row * LEN, LEN), LEN)
+    attended = dot(context[rows, :], w_out[...]) + norm[0:1, :]
+    normed, scale_one = norm_parts(tokens[rows, :].astype(F32) + attended)
+    normed_one[...] = normed
+    value = normed * norm[2:3, :] + norm[3:4, :]
+    hidden[...] = value
+    hidden_b[rows, :] = value.astype(BF)
+    branch[...] = jnp.zeros(branch.shape, F32)
+    for chunk in range(FF // CHUNK):
+        core_of, start = chunk * CHUNK // (FF // 2), chunk * CHUNK % (FF // 2)
+        cols = slice(chunk * CHUNK, (chunk + 1) * CHUNK)
+        up = w_up[core_of, :, start:start + CHUNK]
+        value, slope_value = gelu_both(dot(hidden_b[rows, :], up) + ffn[:, cols])
+        value = value.astype(BF)
+        act[rows, cols] = value
+        slope[:, cols] = slope_value.astype(BF)
+        branch[...] += dot(value, w_down[cols, :])
+    normed, scale = norm_parts(hidden[...] + branch[...] + norm[1:2, :])
+    output = normed * norm[4:5, :] + norm[5:6, :]
+    high = output.astype(BF)
+    layer_out[rows, :] = high
+    low = (output - high.astype(F32)).astype(BF)
+    place = lax.broadcasted_iota(jnp.int32, (SEGS, LEN), 1)
+    segment = lax.broadcasted_iota(jnp.int32, (SEGS, 1), 0)
+    ids = ids_at(lengths, core * 2 + row, place)
+    member = (ids == segment).astype(F32)
+    sizes = jnp.sum(member, axis=1, keepdims=True)
+    member = member.astype(BF)
+    pooled[row] = (dot(member, high) + dot(member, low)) / sizes
+    back, gain, shift = norm_back(cotangent[rows, :].astype(F32), normed, scale, norm[4:5, :])
+    norm_sums[4:5, :] += gain
+    norm_sums[5:6, :] += shift
+    grad_two[...] = back
+    back = back.astype(BF)
+    grad_branch[rows, :] = back
+    norm_sums[1:2, :] += jnp.sum(back.astype(F32), axis=0, keepdims=True)
+    for chunk in range(FF // CHUNK):
+        core_of, start = chunk * CHUNK // (FF // 2), chunk * CHUNK % (FF // 2)
+        cols = slice(chunk * CHUNK, (chunk + 1) * CHUNK)
+        value = dot_last(grad_branch[rows, :], w_down[cols, :])
+        value = (value * slope[:, cols].astype(F32)).astype(BF)
+        grad_inner[rows, cols] = value
+        ffn_sums[:, cols] += jnp.sum(value.astype(F32), axis=0, keepdims=True)
+        grad_two[...] += dot_last(value, w_up[core_of, :, start:start + CHUNK])
+    back, gain, shift = norm_back(grad_two[...], normed_one[...], scale_one, norm[2:3, :])
+    norm_sums[2:3, :] += gain
+    norm_sums[3:4, :] += shift
+    grad_one[rows, :] = back
+    back = back.astype(BF)
+    grad_attended[rows, :] = back
+    norm_sums[0:1, :] += jnp.sum(back.astype(F32), axis=0, keepdims=True)
+    back = dot_last(back, w_out[...]).astype(BF)
+    grad_context[rows, :] = back
+    product = back.astype(F32) * context[rows, :].astype(F32)
+    high = product.astype(BF)
+    low = (product - high.astype(F32)).astype(BF)
+    head = lax.broadcasted_iota(jnp.int32, (16, D), 0)
+    member = (lax.broadcasted_iota(jnp.int32, (16, D), 1) // HD == head).astype(F32).astype(BF)
+    delta[row] = dot_last(member, high) + dot_last(member, low)
+
+
+def middle_kernel(*refs):
+    core = lax.axis_index("mp")
+    norm_sums, ffn_sums = refs[19], refs[20]
+    norm_sums[...] = jnp.zeros(norm_sums.shape, F32)
+    ffn_sums[...] = jnp.zeros(ffn_sums.shape, F32)
+
+    @pl.loop(0, 2)
+    def _(row):
+        middle(row, core, *refs)
+
+
+def middle_call(tokens, context, cotangent, lengths, w_out, w_up, w_down, ffn, norm):
+    count = tokens.shape[0]
+    shape = jax.ShapeDtypeStruct
+    return pl.pallas_call(
+        middle_kernel,
+        out_shape=[
+            shape((count, D), BF),
+            shape((count // LEN, SEGS, D), F32),
+            shape((count, D), BF),
+            shape((count, FF), BF),
+            shape((count, D), BF),
+            shape((count, FF), BF),
+            shape((count, D), BF),
+            shape((count, D), BF),
+            shape((count, D), F32),
+            shape((count // LEN, 16, LEN), F32),
+            shape((8, D), F32),
+            shape((1, FF), F32),
+        ],
+        in_specs=[VMEM] * 3 + [SMEM] + [VMEM] * 5,
+        out_specs=[VMEM] * 12,
+        scratch_shapes=[
+            pltpu.VMEM((LEN, FF), BF),
+            pltpu.VMEM((LEN, D), F32),
+            pltpu.VMEM((LEN, D), F32),
+            pltpu.VMEM((LEN, D), F32),
+            pltpu.VMEM((LEN, D), F32),
+        ],
+        compiler_params=pltpu.CompilerParams(vmem_limit_bytes=60 << 20),
+        name="feed_forward",
+    )(tokens, context, cotangent, lengths, w_out, w_up, w_down, ffn, norm)
+
+
+def weight_grads_kernel(context, hidden_b, act, grad_branch, grad_inner, grad_attended,
+                        out_grad, up_grad, down_grad, flipped):
+    flipped[...] = hidden_b[...].T
+
+    @pl.loop(0, FF // CHUNK)
+    def _(chunk):
+        half_chunks = FF // 2 // CHUNK
+        cols = pl.ds(pl.multiple_of(chunk * CHUNK, CHUNK), CHUNK)
+        local = pl.ds(pl.multiple_of((chunk % half_chunks) * CHUNK, CHUNK), CHUNK)
+        up_grad[chunk // half_chunks, :, local] = dot(flipped[...], grad_inner[:, cols]).astype(BF)
+        down_grad[cols, :] = dot_first(act[:, cols], grad_branch[...]).astype(BF)
+
+    flipped[...] = context[...].T
+    value = dot(flipped[...], grad_attended[...])
+    rows, held = D // out_grad.shape[0], out_grad.shape[1]
+    for block in range(out_grad.shape[0]):
+        piece = value[block * rows:(block + 1) * rows, :]
+        if held > rows:
+            piece = jnp.concatenate([piece, jnp.zeros((held - rows, D), F32)], axis=0)
+        out_grad[block] = piece.astype(BF)
+
+
+def weight_grads(context, hidden_b, act, grad_branch, grad_inner, grad_attended, blocks, held):
+    shape = jax.ShapeDtypeStruct
+    return pl.pallas_call(
+        weight_grads_kernel,
+        out_shape=[shape((blocks, held, D), BF), shape((2, D, FF // 2), BF), shape((FF, D), BF)],
+        in_specs=[VMEM] * 6,
+        out_specs=[VMEM] * 3,
+        scratch_shapes=[pltpu.VMEM((D, context.shape[0]), BF)],
+        compiler_params=pltpu.CompilerParams(vmem_limit_bytes=60 << 20),
+        name="weight_grads",
+    )(context, hidden_b, act, grad_branch, grad_inner, grad_attended)
+
+
+def attend_back(qkv, grad_context, lse, delta, bias, grad_qkv, grad_head, row):
+    rows = pl.ds(pl.multiple_of(row * LEN, LEN), LEN)
+    lane = lax.broadcasted_iota(jnp.int32, (LEN, 128), 1)
+
+    @pl.loop(0, 6)
+    def _(item):
+        core, pair = item // 3, item % 3
+        queries, keys, values = (slab(qkv, core, row, part, pair) for part in range(3))
+        wide = pl.ds(pl.multiple_of(item * 128, 128), 128)
+        grad = grad_context[rows, wide]
+        flipped = keys.T
+        grads_k, grads_v, grads_q = [], [], []
+        for half, mask in enumerate(half_masks()):
+            head = item * 2 + half
+            scores = dot_last(keys * mask, queries) + bias[...] - lse[row, pl.ds(head, 1), :]
+            probs = jnp.exp(scores)
+            grad_probs = dot_last(values * mask, grad)
+            grad_scores = (probs * (grad_probs - delta[row, pl.ds(head, 1), :])).astype(BF)
+            grads_v.append(dot(probs.astype(BF), grad))
+            grads_k.append(dot(grad_scores, queries))
+            grads_q.append(dot(flipped[half * HD:(half + 1) * HD, :], grad_scores))
+        grad_q = (jnp.concatenate(grads_q, axis=0).T * HD ** -0.5).astype(BF)
+        grad_k = jnp.where(lane < HD, grads_k[0], grads_k[1]).astype(BF)
+        grad_v = jnp.where(lane < HD, grads_v[0], grads_v[1]).astype(BF)
+        for part, value in enumerate((grad_q, grad_k, grad_v)):
+            grad_qkv[core, rows, pl.ds(pl.multiple_of(part * HALF + pair * 128, 128), 128)] = value
+        grad_head[0:1, wide] += jnp.sum(grad_q.astype(F32), axis=0, keepdims=True)
+        grad_head[1:2, wide] += jnp.sum(grad_v.astype(F32), axis=0, keepdims=True)
+
+
+def backward_kernel(tokens, qkv, grad_context, lse, delta, lengths, weight, grad_one,
+                    qkv_grad, input_grad, grad_head, grad_qkv, bias, flipped):
+    core = lax.axis_index("mp")
+    grad_head[...] = jnp.zeros(grad_head.shape, F32)
+
+    @pl.loop(0, 2)
+    def _(row):
+        set_bias(bias, lengths, core * 2 + row)
+        attend_back(qkv, grad_context, lse, delta, bias, grad_qkv, grad_head, row)
+        rows = pl.ds(pl.multiple_of(row * LEN, LEN), LEN)
+        input_grad[rows, :] = (
+            grad_one[rows, :]
+            + dot_last(grad_qkv[0, rows, :], weight[0])
+            + dot_last(grad_qkv[1, rows, :], weight[1])
+        )
+
+    flipped[...] = tokens[...].T
+    for core_of in range(2):
+        for part in range(3):
+            cut = slice(part * HALF, (part + 1) * HALF)
+            qkv_grad[core_of, :, cut] = dot(flipped[...], grad_qkv[core_of, :, cut]).astype(BF)
+
+
+def backward(tokens, qkv, grad_context, lse, delta, lengths, weight, grad_one):
+    count = tokens.shape[0]
+    shape = jax.ShapeDtypeStruct
+    return pl.pallas_call(
+        backward_kernel,
+        out_shape=[shape((2, D, QKV_HALF), BF), shape((count, D), F32), shape((2, D), F32)],
+        in_specs=[VMEM] * 5 + [SMEM] + [VMEM] * 2,
+        out_specs=[VMEM] * 3,
+        scratch_shapes=[
+            pltpu.VMEM((2, count, QKV_HALF), BF),
+            pltpu.VMEM((LEN, LEN), F32),
+            pltpu.VMEM((D, count), BF),
+        ],
+        compiler_params=pltpu.CompilerParams(vmem_limit_bytes=60 << 20),
+        name="attend_back",
+    )(tokens, qkv, grad_context, lse, delta, lengths, weight, grad_one)
 
 
 def small_block(norm, head, ffn):
@@ -718,17 +1004,9 @@
     qkv_rows, qkv_cols, out_rows, out_cols, up_rows, up_cols, down_rows, down_cols,
     head_bias_sq, ffn_bias_sq, norm_sq,
 ):
-    f32 = F32
     cores = lax.axis_size("mp")
     data = lax.axis_size("dp")
-    core = lax.axis_index("mp")
-    own_tokens = tokens.shape[0]
-    own_rows = own_tokens // LEN
-    ids = segment_ids(seg_lengths, LEN)
-    own_ids = lax.dynamic_slice_in_dim(ids, core * own_rows, own_rows, 0)
-    own_lengths = lax.dynamic_slice_in_dim(seg_lengths, core * own_rows, own_rows, 0)
     rows_qkv = w_qkv.shape[0]
-    half = w_qkv.shape[2]
     fast = data == 16 and cores == 2
     weights = [w_qkv, w_out, w_up, w_down]
     vectors = [head_bias, ffn_bias.reshape(1, -1), norm_bias]
@@ -739,90 +1017,46 @@
     else:
         gathered = gather_plain(weights, vectors)
     small, qkv_g, out_g, up_g, down_g = gathered
-    small = small.astype(BF).astype(f32)
+    small = small.astype(BF).astype(F32)
     own_head, own_ffn, own_norm = head_bias.shape[1], ffn_bias.shape[0], norm_bias.shape[1]
     norm_full = small[:, :, 0:6, :own_norm].transpose(2, 1, 0, 3).reshape(6, D)
-    head_full = small[:, :, 6:8, :own_head].transpose(2, 0, 1, 3).reshape(2, D)
-    ffn_full = small[:, :, 8, :own_ffn].reshape(-1)
-    qkv_weight = qkv_g.reshape(cores, D, 3, half).transpose(1, 2, 0, 3).reshape(D, 3 * D)
-    out_weight = out_g.reshape(D, D)
-    up_weight = up_g.reshape(cores, D, FF // cores).transpose(1, 0, 2).reshape(D, FF)
-    down_weight = down_g.reshape(FF, D)
-    heads = D // HD
-    offsets = jnp.stack([head_full[0], jnp.zeros_like(head_full[0]), head_full[1]])
-    projected = jnp.dot(tokens, qkv_weight, preferred_element_type=f32).reshape(-1, 3, D) + offsets
-    packed_rows = projected.astype(BF).reshape(own_rows, LEN, 3, heads, HD)
-    context_rows, log_totals = lax.map(
-        lambda pair: attend_row(pair[0], pair[1]), (packed_rows, own_ids)
+    head_full = small[:, :, 6:8, :own_head].transpose(2, 0, 1, 3).reshape(2, 2, 1, HALF)
+    ffn_full = small[:, :, 8, :own_ffn].reshape(1, FF)
+    offsets = jnp.concatenate([head_full[0], jnp.zeros_like(head_full[0]), head_full[1]], axis=-1)
+    qkv_full = qkv_g.reshape(2, D, QKV_HALF)
+    up_full = up_g.reshape(2, D, FF // 2)
+    down_full = down_g.reshape(FF, D)
+    out_full = out_g.reshape(D, D)
+    norm_full = jnp.pad(norm_full, ((0, 2), (0, 0)))
+    qkv, context, lse = forward(tokens, qkv_full, offsets, seg_lengths)
+    (layer_out, pooled, hidden_b, act, grad_branch, grad_inner, grad_attended, grad_context,
+     grad_one, delta, norm_sums, ffn_sums) = middle_call(
+        tokens, context, cotangent, seg_lengths, out_full, up_full, down_full, ffn_full, norm_full)
+    rows_out = w_out.shape[0]
+    held = 32 if fast else rows_out
+    grad_out, grad_up, grad_down = weight_grads(
+        context, hidden_b, act, grad_branch, grad_inner, grad_attended, cores * data, held)
+    grad_qkv, input_grad, grad_head = backward(
+        tokens, qkv, grad_context, lse, delta, seg_lengths, qkv_full, grad_one)
+    small_grads = small_block(
+        norm_sums[:6].reshape(6, data, cores, -1).transpose(2, 1, 0, 3),
+        grad_head.reshape(2, cores, data, -1).transpose(1, 2, 0, 3),
+        ffn_sums.reshape(cores, data, 1, -1),
     )
-    context = context_rows.reshape(own_tokens, D)
-    attended = jnp.dot(context, out_weight, preferred_element_type=f32) + norm_full[0]
-    hidden, norm_one_back = jax.vjp(
-        layer_norm, tokens.astype(f32) + attended, norm_full[2], norm_full[3]
-    )
-    hidden_b = hidden.astype(BF)
-    inner = jnp.dot(hidden_b, up_weight, preferred_element_type=f32) + ffn_full
-    activated, gelu_back = jax.vjp(gelu_exact, inner)
-    activated_b = activated.astype(BF)
-    branch = jnp.dot(activated_b, down_weight, preferred_element_type=f32) + norm_full[1]
-    output, norm_two_back = jax.vjp(layer_norm, hidden + branch, norm_full[4], norm_full[5])
-    member = (own_ids[:, None, :] == jnp.arange(SEGS, dtype=jnp.int32)[None, :, None]).astype(f32)
-    pooled = jnp.einsum(
-        "rsl,rld->rsd", member, output.reshape(own_rows, LEN, D), precision=lax.Precision.HIGHEST
-    )
-    pooled = pooled / own_lengths[:, :, None].astype(f32)
-    grad_res_two, grad_gain_two, grad_shift_two = norm_two_back(cotangent.astype(f32))
-    grad_branch = grad_res_two.astype(BF)
-    grad_bias_down = jnp.sum(grad_branch.astype(f32), axis=0)
-    grad_act = jnp.dot(grad_branch, down_weight.T, preferred_element_type=f32)
-    grad_down = jnp.dot(activated_b.T, grad_branch, preferred_element_type=f32)
-    grad_inner = gelu_back(grad_act)[0].astype(BF)
-    grad_bias_up = jnp.sum(grad_inner.astype(f32), axis=0)
-    grad_up = jnp.dot(hidden_b.T, grad_inner, preferred_element_type=f32)
-    grad_hidden = grad_res_two + jnp.dot(grad_inner, up_weight.T, preferred_element_type=f32)
-    grad_res_one, grad_gain_one, grad_shift_one = norm_one_back(grad_hidden)
-    grad_attended = grad_res_one.astype(BF)
-    grad_bias_out = jnp.sum(grad_attended.astype(f32), axis=0)
-    grad_context = jnp.dot(grad_attended, out_weight.T, preferred_element_type=f32).astype(BF)
-    grad_out = jnp.dot(context.T, grad_attended, preferred_element_type=f32)
-    grad_rows = lax.map(
-        lambda item: attend_back(item[0], item[1], item[2], item[3]),
-        (packed_rows, grad_context.reshape(own_rows, LEN, heads, HD), log_totals, own_ids),
-    )
-    grad_packed = grad_rows.reshape(own_tokens, 3, D)
-    grad_head = jnp.stack(
-        [
-            jnp.sum(grad_packed[:, 0].astype(f32), axis=0),
-            jnp.sum(grad_packed[:, 2].astype(f32), axis=0),
-        ]
-    )
-    grad_flat = grad_packed.reshape(own_tokens, 3 * D)
-    grad_qkv = jnp.dot(tokens.T, grad_flat, preferred_element_type=f32)
-    input_grad = grad_res_one + jnp.dot(grad_flat, qkv_weight.T, preferred_element_type=f32)
-    norm_terms = jnp.stack(
-        [grad_bias_out, grad_bias_down, grad_gain_one, grad_shift_one, grad_gain_two, grad_shift_two]
-    )
-    small_grads = small_block(
-        norm_terms.reshape(6, data, cores, -1).transpose(2, 1, 0, 3),
-        grad_head.reshape(2, cores, data, -1).transpose(1, 2, 0, 3),
-        grad_bias_up.reshape(cores, data, 1, -1),
-    )
-    qkv_blocks = grad_qkv.astype(BF).reshape(data, rows_qkv, 3, cores, half)
     fulls = [
         small_grads,
-        qkv_blocks.transpose(3, 0, 1, 2, 4).reshape(cores, data, rows_qkv, 3 * half),
-        grad_out.astype(BF).reshape(cores, data, -1, D),
-        grad_up.astype(BF).reshape(data, rows_qkv, cores, -1).transpose(2, 0, 1, 3),
-        grad_down.astype(BF).reshape(cores, data, -1, D),
+        grad_qkv.reshape(cores, data, rows_qkv, QKV_HALF),
+        grad_out.reshape(cores, data, held, D),
+        grad_up.reshape(cores, data, rows_qkv, FF // 2),
+        grad_down.reshape(cores, data, -1, D),
     ]
     if fast:
-        fulls[2] = jnp.pad(fulls[2], ((0, 0), (0, 0), (0, 32 - w_out.shape[0]), (0, 0)))
         fulls = [f.reshape(2, 4, 2, 2, *f.shape[-2:]) for f in fulls]
         rows_old = [v.reshape(1, -1) for v in (qkv_rows, out_rows, up_rows, down_rows)]
         cols_old = [qkv_cols] + [v.reshape(1, -1) for v in (out_cols, up_cols, down_cols)]
         old = [head_bias_sq, ffn_bias_sq.reshape(1, -1), norm_sq]
         *reduced, lines, totals = scatter(
-            fulls, [16, rows_qkv, w_out.shape[0], rows_qkv, w_down.shape[0]],
+            fulls, [16, rows_qkv, rows_out, rows_qkv, w_down.shape[0]],
             rows_old, cols_old, old, weight_sums)
         new = step(reduced, lines, totals, weights, rows_old, cols_old, vectors, old)
         grads, (g_head, g_ffn, g_norm) = new[:4], new[4:7]
@@ -832,7 +1066,7 @@
         n_head, n_ffn, n_norm = new[22:25]
         stats = [v for pair in zip(rows_new, cols_new) for v in pair]
         return (
-            output.astype(BF), pooled, input_grad, *grads, g_head, g_ffn.reshape(-1), g_norm, *stats,
+            layer_out, pooled, input_grad, *grads, g_head, g_ffn.reshape(-1), g_norm, *stats,
             s_head, s_ffn.reshape(-1), s_norm, *mats, n_head, n_ffn.reshape(-1), n_norm,
         )
     red_small, red_qkv, red_out, red_up, red_down = scatter_plain(fulls)
@@ -910,7 +1144,7 @@
         )
         new_vecs.append(vec_weights[index] - stride * vec_update[index])
     return (
-        output.astype(BF),
+        layer_out,
         pooled,
         input_grad,
         red_qkv.reshape(w_qkv.shape),

time: 583 us -> 368 us (0.63); the launches traced: 575 us -> 367 us
  matrix products: 167 us -> 0 us
  Pallas kernels: 215 us -> 342 us
  local copies, waits for them, and re-layouts: 143 us -> 20.8 us
  other arithmetic: 46.9 us -> 3.19 us
    dot_general x27 -> x0, matrix products: 167 us -> none  [the longest x1 36.2 us: body(): inner = jnp.dot(hidden_b, up_weight, preferred_element_type=f32) + ffn_full]
    pallas_call x0 -> x4, Pallas kernels: none -> 127 us  [the longest x1 44.8 us: middle_call(): pl.pallas_call(middle_kernel, out_shape=[shape((count, D), BF), shape((co...]
    reshape x8 -> x6, local copies, waits for them, and re-layouts: 45.4 us -> 1.31 us  [the longest x2 0.8 us: body(): grad_head.reshape(2, cores, data, -1).transpose(1, 2, 0, 3)]
    another operation x17 -> x1, local copies, waits for them, and re-layouts: 26 us -> 0.68 us  [body(): ffn_full = small[:, :, 8, :own_ffn].reshape(1, FF)]
    convert_element_type x6 -> x1, other arithmetic: 21.3 us -> 0.02 us  [body(): small = small.astype(BF).astype(F32)]
    reduce_sum x11 -> x0, other arithmetic: 19.2 us -> none  [the longest x2 5.63 us: layer_norm(): center = values - jnp.mean(values, axis=-1, keepdims=True)]
    transpose x2 -> x0, local copies, waits for them, and re-layouts: 14.8 us -> none  [the longest x1 8.14 us: body(): qkv_g.reshape(cores, D, 3, half).transpose(1, 2, 0, 3).reshape(D, 3 * D)]
    unnamed x150 -> x77, local copies, waits for them, and re-layouts: 25.7 us -> 13.9 us
where the time goes in v3:
time: 368 us; the launch traced here: 367 us
  Pallas kernels  342 us (93%)
  local copies, waits for them, and re-layouts  20.8 us (6%)
    pallas_call x1, Pallas kernels, scatter(): pl.pallas_call(functools.partial(scatter_kernel, count, parts), out_shape...  113 us
    pallas_call x1, Pallas kernels, gather(): pl.pallas_call(gather_kernel, out_shape=[jax.ShapeDtypeStruct((2, 4, 2, 2...  101 us
    pallas_call x1, Pallas kernels, middle_call(): pl.pallas_call(middle_kernel, out_shape=[shape((count, D), BF), shape((co...  44.8 us
    pallas_call x1, Pallas kernels, backward(): pl.pallas_call(backward_kernel, out_shape=[shape((2, D, QKV_HALF), BF), s...  36.6 us
    pallas_call x1, Pallas kernels, forward(): pl.pallas_call(forward_kernel, out_shape=[jax.ShapeDtypeStruct((2, count,...  24.4 us
    pallas_call x1, Pallas kernels, weight_grads(): pl.pallas_call(weight_grads_kernel, out_shape=[shape((blocks, held, D), B...  21.4 us
    unnamed x77, local copies, waits for them, and re-layouts  13.9 us

profile of v3, /device:TPU:0, one launch (start us, length us, event | category | flops | bytes accessed | tf_op | source)
XLA Modules:
  0.0 367.3 jit_solution(14803032796756058570)
XLA Ops:
  0.7 1.1 copy.49.refs_0_.refs_7_
  1.7 1.0 copy-done
  2.7 1.0 copy-done.2
  3.7 0.9 copy-done.4
  4.5 0.7 copy-done.15
  6.6 100.9 %gather_weights.1 = (f32[2,4,2,2,16,128]{5,4,3,2,1,0:T(8,128)S(1)}, bf16[2,4,2,2,48,1152]{5,4,3,2,1,0:T(8,128)(2,1)}, bf16[2,4,2,2,32,768]{5,4,3,2,1,0:T(8,128)(...) custom-call(f32[48,3,384]{2,1,0:T(4,128)S(1)} %copy.49.refs_0_.refs_, ...), custom_call_target="tpu_custom_call" | custom-call | tf_op jit(solution)/shard_map/gather_weights/pallas_call | solution.py:186
  108.9 24.4 %project_attend.1 = (bf16[2,1024,1152]{2,1,0:T(8,128)(2,1)}, bf16[1024,768]{1,0:T(8,128)(2,1)}, f32[2,16,512]{2,1,0:T(8,128)}) custom-call(bf16[1024,768]{1,0:T(8,128)(2,1)} %tokens.3, bf16[2,768,1152]{2,1,0:T(8,128)(2,1)} %bitcast.61, f32[2,1,1152]{2,1,0:T(1,128)} %pad_maximum_fusion.offsets, s32[4,8]{1,0:T(4,128)} %lengths.3), custom_call_target="tpu_custom_call" | custom-call | tf_op jit(solution)/shard_map/project_attend/pallas_call | solution.py:724
  133.3 1.1 slice.33
  134.4 0.7 reshape_squeeze.3.refs_7_
  136.0 44.8 %feed_forward.1 = (bf16[1024,768]{1,0:T(8,128)(2,1)}, f32[2,8,768]{2,1,0:T(8,128)}, bf16[1024,768]{1,0:T(8,128)(2,1)}, bf16[1024,3072]{1,0:T(8,128)(2,1)}, bf16[...) custom-call(bf16[1024,768]{1,0:T(8,128)(2,1)} %tokens.3, ...), custom_call_target="tpu_custom_call" | custom-call | tf_op jit(solution)/shard_map/feed_forward/pallas_call | solution.py:843
  180.8 36.6 %attend_back.1 = (bf16[2,768,1152]{2,1,0:T(8,128)(2,1)}, f32[1024,768]{1,0:T(8,128)}, f32[2,768]{1,0:T(2,128)}) custom-call(bf16[1024,768]{1,0:T(8,128)(2,1)} %tokens.3, bf16[2,1024,1152]{2,1,0:T(8,128)(2,1)} %get-tuple-element.95.qkv, bf16[1024,768]{1,0:T(8,128)(2,1)} %get-tuple-element.96.grad_context, f32[2,16,512]{2,1,0:T(8,128)} %get-tuple-element.97.lse, ...), custom_call_target="tpu_custom_call" | custom-call | tf_op jit(solution)/shard_map/attend_back/pallas_call | solution.py:964
  218.7 0.8 reshape.148
  219.8 0.7 pad.24
  220.6 21.4 %weight_grads.1 = (bf16[32,32,768]{2,1,0:T(8,128)(2,1)}, bf16[2,768,1536]{2,1,0:T(8,128)(2,1)}, bf16[3072,768]{1,0:T(8,128)(2,1)}) custom-call(bf16[1024,768]{1,0:T(8,128)(2,1)} %get-tuple-element.89.refs_1_.context, bf16[1024,768]{1,0:T(8,128)(2,1)} %get-tuple-element.105.hidden_b, bf16[1024,3072]{1,0:T(8,128)(2,1)} %get-tuple-element.106.act, ...), custom_call_target="tpu_custom_call" | custom-call | tf_op jit(solution)/shard_map/weight_grads/pallas_call | solution.py:897
  243.9 112.8 %scatter_grads.1 = (f32[16,128]{1,0:T(8,128)}, f32[48,1152]{1,0:T(8,128)}, f32[24,768]{1,0:T(8,128)}, f32[48,1536]{1,0:T(8,128)}, f32[96,768]{1,0:T(8,128)}, /*index=5*/f32[40,128]{1,0:T(8,128)}, f32[8,128]{1,0:T(8,128)}) custom-call(f32[2,4,2,2,16,128]{5,4,3,2,1,0:T(8,128)} %bitcast.70, bf16[2,4,2,2,48,1152]{5,4,3,2,1,0:T(8,128)(2,1)} %bitcast.68, ...), custom_call_target="tpu_custom_call" | custom-call | tf_op jit(solution)/shard_map/scatter_grads/pallas_call | solution.py:525
  356.8 1.0 copy-done.6
  357.8 1.0 copy-done.7
  358.8 0.9 copy-done.8
  359.7 0.9 copy-done.9
  360.6 0.7 copy-done.14
  361.3 0.7 copy-done.18
  362.7 1.4 adafactor_step.1
  364.1 0.7 copy.57
  366.6 0.7 copy.58
  (89 shorter events, 9.6 us)
Async XLA Ops:
  1.7 1.0 copy-start
  180.8 37.1 %copy-start.32 = (f32[1,3072]{1,0:T(1,128)S(1)}, f32[1,3072]{1,0:T(1,128)}, u32[]{:S(2)}) copy-start(f32[1,3072]{1,0:T(1,128)} %get-tuple-element.103) | copy-start | bytes 36868
  180.8 38.7 %copy-start.31 = (f32[8,768]{1,0:T(8,128)S(1)}, f32[8,768]{1,0:T(8,128)}, u32[]{:S(2)}) copy-start(f32[8,768]{1,0:T(8,128)} %get-tuple-element.101) | copy-start | bytes 73732
  220.5 21.4 %copy-start.34 = (f32[768]{0:T(1024)S(1)}, f32[768]{0:T(1024)}, u32[]{:S(2)}) copy-start(f32[768]{0:T(1024)} %param.34) | copy-start | bytes 9220
  220.5 22.0 %copy-start.33 = (f32[1536]{0:T(1024)S(1)}, f32[1536]{0:T(1024)}, u32[]{:S(2)}) copy-start(f32[1536]{0:T(1024)} %param.36) | copy-start | bytes 18436
  220.6 22.6 %copy-start.35 = (f32[768]{0:T(1024)S(1)}, f32[768]{0:T(1024)}, u32[]{:S(2)}) copy-start(f32[768]{0:T(1024)} %param.38) | copy-start | bytes 9220
  243.7 112.9 %copy-start.1 = (f32[48,1536]{1,0:T(8,128)S(1)}, f32[48,1536]{1,0:T(8,128)}, u32[]{:S(2)}) copy-start(f32[48,1536]{1,0:T(8,128)} %refs_9_.3) | copy-start | bytes 884740
  243.7 112.9 %copy-start.3 = (f32[96,768]{1,0:T(8,128)S(1)}, f32[96,768]{1,0:T(8,128)}, u32[]{:S(2)}) copy-start(f32[96,768]{1,0:T(8,128)} %refs_10_.1) | copy-start | bytes 884740
  243.7 113.0 %copy-start.5 = (f32[24,768]{1,0:T(8,128)S(1)}, f32[24,768]{1,0:T(8,128)}, u32[]{:S(2)}) copy-start(f32[24,768]{1,0:T(8,128)} %refs_8_.1) | copy-start | bytes 221188
  243.7 113.0 %copy-start.10 = (f32[1,1536]{1,0:T(1,128)S(1)}, f32[1,1536]{1,0:T(1,128)}, u32[]{:S(2)}) copy-start(f32[1,1536]{1,0:T(1,128)} %reshape.156.refs_11_.refs_17_) | copy-start | bytes 18436
  243.7 113.0 %copy-start.11 = (f32[1,768]{1,0:T(1,128)S(1)}, f32[1,768]{1,0:T(1,128)}, u32[]{:S(2)}) copy-start(f32[1,768]{1,0:T(1,128)} %reshape.155.refs_10_.refs_16_) | copy-start | bytes 9220
  243.7 113.0 %copy-start.12 = (f32[1,768]{1,0:T(1,128)S(1)}, f32[1,768]{1,0:T(1,128)}, u32[]{:S(2)}) copy-start(f32[1,768]{1,0:T(1,128)} %reshape.157.refs_12_.refs_18_) | copy-start | bytes 9220
  243.8 113.0 %copy-start.13 = (f32[3,384]{1,0:T(4,128)S(1)}, f32[3,384]{1,0:T(4,128)}, u32[]{:S(2)}) copy-start(f32[3,384]{1,0:T(4,128)} %refs_15_.3) | copy-start | bytes 13828
  243.8 113.0 %copy-start.16 = (f32[6,24]{1,0:T(8,128)S(1)}, f32[6,24]{1,0:T(8,128)}, u32[]{:S(2)}) copy-start(f32[6,24]{1,0:T(8,128)} %refs_21_.1) | copy-start | bytes 1732
  243.8 113.0 %copy-start.17 = (f32[6,24]{1,0:T(8,128)S(1)}, f32[6,24]{1,0:T(8,128)}, u32[]{:S(2)}) copy-start(f32[6,24]{1,0:T(8,128)} %refs_24_.1) | copy-start | bytes 1732
  243.8 113.0 %copy-start.20 = (f32[2,24]{1,0:T(2,128)S(1)}, f32[2,24]{1,0:T(2,128)}, u32[]{:S(2)}) copy-start(f32[2,24]{1,0:T(2,128)} %refs_22_.1) | copy-start | bytes 580
  243.8 113.0 %copy-start.22 = (f32[2,24]{1,0:T(2,128)S(1)}, f32[2,24]{1,0:T(2,128)}, u32[]{:S(2)}) copy-start(f32[2,24]{1,0:T(2,128)} %refs_19_.1) | copy-start | bytes 580
  243.8 113.0 %copy-start.25 = (f32[96]{0:T(128)S(1)}, f32[96]{0:T(128)}, u32[]{:S(2)}) copy-start(f32[96]{0:T(128)} %param.29) | copy-start | bytes 1156
  243.8 113.0 %copy-start.26 = (f32[48]{0:T(128)S(1)}, f32[48]{0:T(128)}, u32[]{:S(2)}) copy-start(f32[48]{0:T(128)} %param.31) | copy-start | bytes 580
  243.8 113.0 %copy-start.27 = (f32[24]{0:T(128)S(1)}, f32[24]{0:T(128)}, u32[]{:S(2)}) copy-start(f32[24]{0:T(128)} %param.33) | copy-start | bytes 292
  243.8 112.9 %copy-start.28 = (f32[48]{0:T(128)S(1)}, f32[48]{0:T(128)}, u32[]{:S(2)}) copy-start(f32[48]{0:T(128)} %param.35) | copy-start | bytes 580
  243.9 112.9 %copy-start.29 = (f32[96]{0:T(128)S(1)}, f32[96]{0:T(128)}, u32[]{:S(2)}) copy-start(f32[96]{0:T(128)} %param.37) | copy-start | bytes 1156
  243.9 112.9 %copy-start.30 = (f32[96]{0:T(128)S(1)}, f32[96]{0:T(128)}, u32[]{:S(2)}) copy-start(f32[96]{0:T(128)} %param.40) | copy-start | bytes 1156
  356.8 1.0 copy-start.6
  (12 other events, 9.3 us)

commit v4 on v3

--- a/solution.py
+++ b/solution.py
@@ -65,53 +65,6 @@
     return parts + [("zxy", first * 128, cols - first * 128)]
 
 
-class Gatherer:
-    def __init__(self, place, shard, full, part, sems, base):
-        order, start, width = part
-        self.place, self.shard, self.full = place, shard, full
-        self.cols = pl.ds(start, width)
-        self.order = order + "m"
-        self.sems, self.base = sems, base
-
-    def view(self, spot):
-        return self.full.at[spot["m"], spot["z"], spot["y"], spot["x"], :, self.cols]
-
-    def copies(self, stage):
-        place, axis = self.place, self.order[stage]
-        out = []
-        for step in steps_of(axis):
-            spot = {"z": place.z, "y": place.y, "x": place.x, "m": place.m}
-            for done in self.order[:stage]:
-                spot[done] = EVERY
-            target = place.at(axis, step)
-            send, recv = self.sems
-            slot = self.base + 4 * stage + step
-            source = self.shard.at[:, self.cols] if stage == 0 else self.view(spot)
-            sent = pltpu.make_async_remote_copy(
-                source, self.view(spot), send.at[slot], recv.at[slot],
-                device_id=place.device(target), device_id_type=MESH)
-            spot = dict(spot)
-            spot[axis] = place.at(axis, -step)[axis]
-            arrives = pltpu.make_async_remote_copy(
-                self.view(spot), self.view(spot), send.at[slot], recv.at[slot],
-                device_id=place.device(target), device_id_type=MESH)
-            out.append((sent, arrives))
-        return out
-
-    def start(self, stage):
-        for sent, _ in self.copies(stage):
-            sent.start()
-
-    def arrived(self, stage):
-        for _, arrives in self.copies(stage):
-            arrives.wait_recv()
-
-    def finish(self):
-        for stage in range(4):
-            for sent, _ in self.copies(stage):
-                sent.wait_send()
-
-
 def weight_sums_of(weights, small):
     parts = []
     for weight in weights:
@@ -121,83 +74,6 @@
         else:
             parts.append(all_sum(value * value))
     return scalars([jnp.zeros((1, 1), F32)] * 11 + parts + small_sums(small))
-
-
-def gather_kernel(*refs):
-    refs = list(refs)
-    take = lambda number: [refs.pop(0) for _ in range(number)]
-    weights = take(4)
-    head, ffn, norm = take(3)
-    fulls = take(5)
-    sums = refs.pop(0)
-    cast = take(5)
-    send, recv, local = refs
-    count = 5
-    half = weights[0].shape[2]
-    place_small(cast[0], norm[...], head[...], ffn[...], 0.0)
-    for part in range(3):
-        cast[1][:, part * half:(part + 1) * half] = weights[0][:, part, :].astype(BF)
-    value = weights[1][...]
-    held = cast[2].shape[0]
-    cast[2][...] = jnp.concatenate(
-        [value, jnp.zeros((held - value.shape[0], value.shape[1]), F32)], 0).astype(BF)
-    cast[3][...] = weights[2][...].astype(BF)
-    cast[4][...] = weights[3][...].astype(BF)
-    place = Place()
-    greet(place)
-    paths, base = [], 0
-    locals_ = []
-    for index in range(count):
-        own = pltpu.make_async_copy(
-            cast[index], fulls[index].at[place.m, place.z, place.y, place.x], local.at[index])
-        own.start()
-        locals_.append(own)
-        group = []
-        for part in column_parts(cast[index].shape[1]):
-            group.append(Gatherer(place, cast[index], fulls[index], part, (send, recv), base))
-            base += 16
-        for path in group:
-            path.start(0)
-        paths.append(group)
-    for own in locals_:
-        own.wait()
-    sums[...] = weight_sums_of(weights, cast[0][...])
-    for turn in range(count + 3):
-        for index in range(count):
-            stage = turn - index + 1
-            if 1 <= stage <= 3:
-                for path in paths[index]:
-                    path.arrived(stage - 1)
-                    path.start(stage)
-    for group in paths:
-        for path in group:
-            path.arrived(3)
-    for group in paths:
-        for path in group:
-            path.finish()
-
-
-def gather(weights, vectors):
-    qkv, out, up, down = weights
-    held = [(16, 128), (qkv.shape[0], 3 * qkv.shape[2]), (32, out.shape[1]), up.shape, down.shape]
-    kinds = [F32, BF, BF, BF, BF]
-    slots = 16 * sum(len(column_parts(h[1])) for h in held)
-    vmem = pl.BlockSpec(memory_space=pltpu.VMEM)
-    return pl.pallas_call(
-        gather_kernel,
-        out_shape=[jax.ShapeDtypeStruct((2, 4, 2, 2) + h, k) for h, k in zip(held, kinds)]
-        + [jax.ShapeDtypeStruct((8, 128), F32)],
-        in_specs=[vmem] * 7,
-        out_specs=[pl.BlockSpec(memory_space=pl.ANY)] * 5 + [vmem],
-        scratch_shapes=[pltpu.VMEM(h, k) for h, k in zip(held, kinds)] + [
-            pltpu.SemaphoreType.DMA((slots,)),
-            pltpu.SemaphoreType.DMA((slots,)),
-            pltpu.SemaphoreType.DMA((5,)),
-        ],
-        compiler_params=pltpu.CompilerParams(
-            collective_id=0, has_side_effects=True, vmem_limit_bytes=48 << 20),
-        name="gather_weights",
-    )(*weights, *vectors)
 
 
 class Scatterer:
@@ -374,6 +250,16 @@
 ROW_COUNT = (D, D, D, FF)
 
 
+def pair_cuts():
+    out = []
+    for pair in range(3):
+        for part in range(3):
+            start = (pair * 3 + part) * 128
+            out.append(((slice(part, part + 1), slice(pair * 128, (pair + 1) * 128)),
+                        slice(start, start + 128)))
+    return out
+
+
 def new_rows_cols(grads, rows_old, cols_old, lines):
     rows_new, cols_new = [], []
     for index in range(4):
@@ -388,8 +274,7 @@
             DECAY * to_column(rows_old[index][...]) + (1.0 - DECAY) * row_sum / COL_COUNT[index])
         col_sum = get_line(lines, COL_LINES[index], WIDTHS[index])
         if index == 0:
-            old = cols_old[0]
-            old = jnp.concatenate([old[0:1, :], old[1:2, :], old[2:3, :]], axis=1)
+            old = jnp.concatenate([cols_old[0][at] for at, _ in pair_cuts()], axis=1)
         else:
             old = cols_old[index][...]
         cols_new.append(DECAY * old + (1.0 - DECAY) * col_sum / ROW_COUNT[index])
@@ -557,14 +442,13 @@
     weights_out = take(4)
     head_new, ffn_new, norm_new = take(3)
     old_small, weight_small = refs
-    half = D // 2
     rows_new, cols_new = new_rows_cols(grads, rows_old, cols_old, lines)
     total = lambda lane: totals[0:1, lane:lane + 1]
     for index in range(4):
         rows_out[index][...] = to_row(rows_new[index])
         if index == 0:
-            for part in range(3):
-                cols_out[0][part:part + 1, :] = cols_new[0][:, part * half:(part + 1) * half]
+            for at, cut in pair_cuts():
+                cols_out[0][at] = cols_new[0][:, cut]
         else:
             cols_out[index][...] = cols_new[index]
         entries = ROW_COUNT[index] * COL_COUNT[index]
@@ -575,12 +459,11 @@
         scale_rows = lax.rsqrt(rows_new[index] / row_mean) * stride
         scale_cols = lax.rsqrt(cols_new[index])
         if index == 0:
-            for part in range(3):
-                cut = slice(part * half, (part + 1) * half)
+            for (part, cols), cut in pair_cuts():
+                at = (EVERY, part.start, cols)
                 grad = grads[0][:, cut]
-                grads_out[0][:, part, :] = grad
-                weights_out[0][:, part, :] = (
-                    weights[0][:, part, :] - grad * scale_rows * scale_cols[:, cut])
+                grads_out[0][at] = grad
+                weights_out[0][at] = weights[0][at] - grad * scale_rows * scale_cols[:, cut]
         else:
             grad = grads[index][...]
             grads_out[index][...] = grad
@@ -665,21 +548,24 @@
     return [((lane // HD) == half).astype(F32).astype(BF) for half in range(2)]
 
 
+PAIR = 3 * 128
+
+
 def slab(ref, core, row, part, pair):
     return ref[core, pl.ds(pl.multiple_of(row * LEN, LEN), LEN),
-               pl.ds(pl.multiple_of(part * HALF + pair * 128, 128), 128)]
+               pl.ds(pl.multiple_of(pair * PAIR + part * 128, 128), 128)]
 
 
 def project(tokens, weight, offsets, qkv, row):
     rows = pl.ds(pl.multiple_of(row * LEN, LEN), LEN)
     values = tokens[rows, :]
     for core in range(2):
-        for part in range(3):
-            cut = slice(part * HALF, (part + 1) * HALF)
+        for pair in range(3):
+            cut = slice(pair * PAIR, (pair + 1) * PAIR)
             out = (dot(values, weight[core, :, cut]) + offsets[core, :, cut]).astype(BF)
-            if part == 0:
-                out = out * jnp.asarray(HD ** -0.5, BF)
-            qkv[core, rows, cut] = out
+            scale = jnp.where(
+                lax.broadcasted_iota(jnp.int32, (1, PAIR), 1) < 128, HD ** -0.5, 1.0).astype(BF)
+            qkv[core, rows, cut] = out * scale
 
 
 def attend(qkv, bias, context, lse, held, row):
@@ -871,19 +757,17 @@
 
 
 def weight_grads_kernel(context, hidden_b, act, grad_branch, grad_inner, grad_attended,
-                        out_grad, up_grad, down_grad, flipped):
-    flipped[...] = hidden_b[...].T
+                        out_grad, up_grad, down_grad):
 
     @pl.loop(0, FF // CHUNK)
     def _(chunk):
         half_chunks = FF // 2 // CHUNK
         cols = pl.ds(pl.multiple_of(chunk * CHUNK, CHUNK), CHUNK)
         local = pl.ds(pl.multiple_of((chunk % half_chunks) * CHUNK, CHUNK), CHUNK)
-        up_grad[chunk // half_chunks, :, local] = dot(flipped[...], grad_inner[:, cols]).astype(BF)
-        down_grad[cols, :] = dot_first(act[:, cols], grad_branch[...]).astype(BF)
-
-    flipped[...] = context[...].T
-    value = dot(flipped[...], grad_attended[...])
+        up_grad[chunk // half_chunks, :, local] = dot(hidden_b[...], grad_inner[:, cols]).astype(BF)
+        down_grad[cols, :] = dot(act[cols, :], grad_branch[...]).astype(BF)
+
+    value = dot(context[...], grad_attended[...])
     rows, held = D // out_grad.shape[0], out_grad.shape[1]
     for block in range(out_grad.shape[0]):
         piece = value[block * rows:(block + 1) * rows, :]
@@ -899,7 +783,6 @@
         out_shape=[shape((blocks, held, D), BF), shape((2, D, FF // 2), BF), shape((FF, D), BF)],
         in_specs=[VMEM] * 6,
         out_specs=[VMEM] * 3,
-        scratch_shapes=[pltpu.VMEM((D, context.shape[0]), BF)],
         compiler_params=pltpu.CompilerParams(vmem_limit_bytes=60 << 20),
         name="weight_grads",
     )(context, hidden_b, act, grad_branch, grad_inner, grad_attended)
@@ -930,13 +813,13 @@
         grad_k = jnp.where(lane < HD, grads_k[0], grads_k[1]).astype(BF)
         grad_v = jnp.where(lane < HD, grads_v[0], grads_v[1]).astype(BF)
         for part, value in enumerate((grad_q, grad_k, grad_v)):
-            grad_qkv[core, rows, pl.ds(pl.multiple_of(part * HALF + pair * 128, 128), 128)] = value
+            grad_qkv[core, rows, pl.ds(pl.multiple_of(pair * PAIR + part * 128, 128), 128)] = value
         grad_head[0:1, wide] += jnp.sum(grad_q.astype(F32), axis=0, keepdims=True)
         grad_head[1:2, wide] += jnp.sum(grad_v.astype(F32), axis=0, keepdims=True)
 
 
 def backward_kernel(tokens, qkv, grad_context, lse, delta, lengths, weight, grad_one,
-                    qkv_grad, input_grad, grad_head, grad_qkv, bias, flipped):
+                    qkv_grad, input_grad, grad_head, grad_qkv, bias):
     core = lax.axis_index("mp")
     grad_head[...] = jnp.zeros(grad_head.shape, F32)
 
@@ -951,15 +834,14 @@
             + dot_last(grad_qkv[1, rows, :], weight[1])
         )
 
-    flipped[...] = tokens[...].T
     for core_of in range(2):
         for part in range(3):
             cut = slice(part * HALF, (part + 1) * HALF)
-            qkv_grad[core_of, :, cut] = dot(flipped[...], grad_qkv[core_of, :, cut]).astype(BF)
+            qkv_grad[core_of, :, cut] = dot(tokens[...], grad_qkv[core_of, :, cut]).astype(BF)
 
 
 def backward(tokens, qkv, grad_context, lse, delta, lengths, weight, grad_one):
-    count = tokens.shape[0]
+    count = tokens.shape[1]
     shape = jax.ShapeDtypeStruct
     return pl.pallas_call(
         backward_kernel,
@@ -969,24 +851,511 @@
         scratch_shapes=[
             pltpu.VMEM((2, count, QKV_HALF), BF),
             pltpu.VMEM((LEN, LEN), F32),
-            pltpu.VMEM((D, count), BF),
         ],
         compiler_params=pltpu.CompilerParams(vmem_limit_bytes=60 << 20),
         name="attend_back",
     )(tokens, qkv, grad_context, lse, delta, lengths, weight, grad_one)
 
 
+UP_CHUNK = 512
+DOWN_CHUNK = 256
+
+
+class Spread:
+    COUNT = 8
+
+    def __init__(self, place, full, start, width, flip, sems, base, shard=None):
+        self.place, self.full, self.shard = place, full, shard
+        self.cols = pl.ds(start, width)
+        tiles = width // 128
+        cut = (tiles // 2 if flip else tiles - tiles // 2) * 128
+        self.halves = [("xy", pl.ds(start, cut))]
+        if cut < width:
+            self.halves.append(("yx", pl.ds(start + cut, width - cut)))
+        self.sems, self.base = sems, base
+
+    def view(self, spot, cols):
+        return self.full.at[spot["m"], spot["z"], spot["y"], spot["x"], :, cols]
+
+    def copy(self, slot, axis, step, spot, cols, source=None):
+        place = self.place
+        send, recv = self.sems
+        send, recv = send.at[self.base + slot], recv.at[self.base + slot]
+        device = place.device(place.at(axis, step))
+        view = self.view(spot, cols)
+        sent = pltpu.make_async_remote_copy(
+            view if source is None else source, view, send, recv,
+            device_id=device, device_id_type=MESH)
+        land = dict(spot)
+        land[axis] = place.at(axis, -step)[axis]
+        land = self.view(land, cols)
+        arrives = pltpu.make_async_remote_copy(
+            land, land, send, recv, device_id=device, device_id_type=MESH)
+        return sent, arrives
+
+    def copies(self, stage):
+        place = self.place
+        here = {"z": place.z, "y": place.y, "x": place.x, "m": place.m}
+        if stage == 0:
+            source = None if self.shard is None else self.shard.at[:, self.cols]
+            return [self.copy(step - 1, "z", step, here, self.cols, source) for step in (1, 2, 3)]
+        here["z"] = EVERY
+        if stage == 3:
+            here["y"] = here["x"] = EVERY
+            return [self.copy(7, "m", 1, here, self.cols)]
+        out = []
+        for number, (order, cols) in enumerate(self.halves):
+            spot = dict(here)
+            if stage == 2:
+                spot[order[0]] = EVERY
+            out.append(self.copy(1 + 2 * stage + number, order[stage - 1], 1, spot, cols))
+        return out
+
+    def start(self, stage):
+        for sent, _ in self.copies(stage):
+            sent.start()
+
+    def arrived(self, stage):
+        for _, arrives in self.copies(stage):
+            arrives.wait_recv()
+
+    def finish(self):
+        for stage in range(4):
+            for sent, _ in self.copies(stage):
+                sent.wait_send()
+
+
+def spread_tick(groups, tick):
+    for stage in range(4):
+        index = tick + 2 if stage == 0 else tick - stage + 1
+        if 0 <= index < len(groups):
+            for chunk in groups[index]:
+                if stage:
+                    chunk.arrived(stage - 1)
+                chunk.start(stage)
+
+
+def unpack_small(small, norm_out, offsets, ffn_out):
+    iota = lambda shape, axis: lax.broadcasted_iota(jnp.int32, shape, axis)
+    pick = ((iota((128, D), 1) % 24 == iota((128, D), 0))).astype(F32).astype(BF)
+    pick_ffn = ((iota((128, FF), 1) % 96 == iota((128, FF), 0))).astype(F32).astype(BF)
+    total = jnp.zeros((16, D), F32)
+    ffn = jnp.zeros((1, FF), F32)
+    line, col = iota((256, D), 0), iota((256, D), 1) // 24
+    device, kind = line // 16, line % 16
+    for core in range(2):
+        block = small[core].reshape(256, 128).astype(BF)
+        wide = dot(block, pick)
+        right = jnp.where(kind < 6, 2 * device + core, 16 * core + device)
+        wide = jnp.where((col == right) & (kind < 8), wide, 0.0)
+        total = total + jnp.sum(wide.reshape(16, 16, D), axis=0)
+        wide = dot(small[core, :, :, :, 8, :].reshape(16, 128).astype(BF), pick_ffn)
+        right = iota((16, FF), 1) // 96 == iota((16, FF), 0) + 16 * core
+        ffn = ffn + jnp.sum(jnp.where(right, wide, 0.0), axis=0, keepdims=True)
+    norm_out[0:6, :] = total[0:6, :]
+    norm_out[6:8, :] = jnp.zeros((2, D), F32)
+    ffn_out[...] = ffn
+    offsets[...] = jnp.zeros(offsets.shape, F32)
+    for core in range(2):
+        for pair in range(3):
+            source = core * HALF + pair * 128
+            for part, row in ((0, 6), (2, 7)):
+                start = pair * PAIR + part * 128
+                offsets[core, :, start:start + 128] = total[row:row + 1, source:source + 128]
+
+
+def project_pair(tokens, weight, offsets, qkv, pair):
+    cols = pl.ds(pl.multiple_of(pair * PAIR, PAIR), PAIR)
+    scale = jnp.where(
+        lax.broadcasted_iota(jnp.int32, (1, PAIR), 1) < 128, HD ** -0.5, 1.0).astype(BF)
+    for core in range(2):
+        piece = weight[core, :, :, :, :, cols].reshape(D, PAIR)
+        out = dot(tokens[...], piece) + offsets[core, :, cols]
+        qkv[core, :, cols] = out.astype(BF) * scale
+
+
+def attend_pair(qkv, bias, context, logs_ref, core, row, pair):
+    rows = pl.ds(pl.multiple_of(row * LEN, LEN), LEN)
+    lane = lax.broadcasted_iota(jnp.int32, (LEN, 128), 1)
+    item = core * 3 + pair
+    queries, keys, values = (slab(qkv, core, row, part, pair) for part in range(3))
+    wide = jnp.concatenate([values, jnp.ones_like(values)], axis=1)
+    outs = []
+    logs = logs_ref[row]
+    for half, mask in enumerate(half_masks()):
+        scores = dot_last(queries * mask, keys) + bias[row]
+        peak = jnp.max(scores, axis=1, keepdims=True)
+        raised = jnp.exp(scores - peak).astype(BF)
+        both = dot(raised, wide)
+        total = both[:, 128:]
+        outs.append(both[:, :128] / total)
+        logs = jnp.where(lane == item * 2 + half, peak + jnp.log(total), logs)
+    logs_ref[row] = logs
+    context[rows, pl.ds(pl.multiple_of(item * 128, 128), 128)] = jnp.where(
+        lane < HD, outs[0], outs[1]).astype(BF)
+
+
+def forward_gather_kernel(*refs):
+    refs = list(refs)
+    take = lambda number: [refs.pop(0) for _ in range(number)]
+    w_qkv, w_out, w_up, w_down, head, ffn, norm, tokens, lengths = take(9)
+    (sums, norm_out, ffn_out, lse, hidden_scale, out_full) = take(6)
+    (qkv_full, up_full, down_full, qkv_out, context_flip, token_flip, hidden_flip, normed_out,
+     context_out, act_out, act_flip, slope_out) = take(12)
+    (g_small, g_qkv, g_out, g_up, cast_down, qkv, context, flip_context, flip_token, flip_hidden,
+     hidden_b, normed_one, act, slope, flip_act, bias, logs, offsets) = take(18)
+    send, recv, local = refs
+    place = Place()
+    here = (place.m, place.z, place.y, place.x)
+    half = w_qkv.shape[2]
+    place_small(g_small.at[here], norm[...], head[...], ffn[...], 0.0)
+    for part in range(3):
+        for pair in range(3):
+            start = pair * PAIR + part * 128
+            g_qkv[here + (EVERY, slice(start, start + 128))] = w_qkv[
+                :, part, pair * 128:(pair + 1) * 128].astype(BF)
+    value = w_out[...]
+    spare = g_out.shape[4] - value.shape[0]
+    g_out[here] = jnp.concatenate([value, jnp.zeros((spare, D), F32)], axis=0).astype(BF)
+    g_up[here] = w_up[...].astype(BF)
+    cast_down[...] = w_down[...].astype(BF)
+    copies, used = [], [0]
+
+    def keep(source, target):
+        copy = pltpu.make_async_copy(source, target, local.at[used[0]])
+        used[0] += 1
+        copy.start()
+        copies.append(copy)
+        return copy
+
+    down_own = keep(cast_down, down_full.at[here])
+    sems, base = (send, recv), [0]
+
+    def chunk(full, start, width, flip, shard=None):
+        made = Spread(place, full, start, width, flip, sems, base[0], shard)
+        base[0] += Spread.COUNT
+        return made
+
+    groups = [[chunk(g_small, 0, 128, False), chunk(g_qkv, 0, PAIR, False)]]
+    groups += [[chunk(g_qkv, pair * PAIR, PAIR, pair == 1)] for pair in (1, 2)]
+    groups += [[chunk(g_out, 0, D, False)]]
+    groups += [[chunk(g_up, at, UP_CHUNK, False)] for at in range(0, FF // 2, UP_CHUNK)]
+    groups += [[chunk(down_full, at, DOWN_CHUNK, False, cast_down)]
+               for at in range(0, D, DOWN_CHUNK)]
+
+    def ready(index):
+        for made in groups[index]:
+            made.arrived(3)
+
+    greet(place)
+    for index in (0, 1):
+        for made in groups[index]:
+            made.start(0)
+    sums[...] = weight_sums_of([w_qkv, w_out, w_up, w_down], g_small[here])
+    down_own.wait()
+    spread_tick(groups, 0)
+    for row in range(2):
+        set_bias(bias.at[row], lengths, place.m * 2 + row)
+    spread_tick(groups, 1)
+    flip_token[...] = tokens[...].T
+    keep(flip_token, token_flip)
+    spread_tick(groups, 2)
+    logs[...] = jnp.zeros(logs.shape, F32)
+    ready(0)
+    unpack_small(g_small, norm_out, offsets, ffn_out)
+
+    @pl.loop(0, 12)
+    def _(item):
+        pair, row, core = item // 4, (item % 4) // 2, item % 2
+        for number, at in enumerate((2, 4, 6, 8, 10)):
+            @pl.when(item == at)
+            def _():
+                spread_tick(groups, 3 + number)
+                if at in (4, 8):
+                    ready(at // 4)
+
+        @pl.when(item % 4 == 0)
+        def _():
+            project_pair(tokens, g_qkv, offsets, qkv, pair)
+
+        attend_pair(qkv, bias, context, logs, core, row, pair)
+
+    for core in range(2):
+        keep(g_qkv.at[core], qkv_full.at[core])
+    keep(qkv, qkv_out)
+    keep(context, context_out)
+    for row in range(2):
+        lse[row] = logs[row].T[0:16, :]
+    flip_context[...] = context[...].T
+    keep(flip_context, context_flip)
+    ready(3)
+    rows_out = w_out.shape[0]
+    for core in range(2):
+        value = g_out[core].reshape(16, g_out.shape[4], D).astype(F32)[:, :rows_out]
+        out_full[core * HALF:(core + 1) * HALF, :] = value.reshape(HALF, D).astype(BF)
+    for row in range(2):
+        rows = slice(row * LEN, (row + 1) * LEN)
+        attended = dot(context[rows, :], out_full[...]) + norm_out[0:1, :]
+        normed, scale = norm_parts(tokens[rows, :].astype(F32) + attended)
+        normed_one[rows, :] = normed
+        hidden_scale[rows, :] = jnp.broadcast_to(scale, (LEN, 128))
+        hidden_b[rows, :] = (normed * norm_out[2:3, :] + norm_out[3:4, :]).astype(BF)
+    keep(normed_one, normed_out)
+    flip_hidden[...] = hidden_b[...].T
+    keep(flip_hidden, hidden_flip)
+    spread_tick(groups, 8)
+    waiting = [[], []]
+    for third in range(3):
+        ready(4 + third)
+        for core in range(2):
+            for copy in waiting[core]:
+                copy.wait()
+            local_cols = slice(third * UP_CHUNK, (third + 1) * UP_CHUNK)
+            start = core * (FF // 2) + third * UP_CHUNK
+            cols = pl.ds(start, UP_CHUNK)
+            up = g_up[core, :, :, :, :, local_cols].reshape(D, UP_CHUNK)
+
+            @pl.loop(0, 2)
+            def _(row):
+                rows = pl.ds(pl.multiple_of(row * LEN, LEN), LEN)
+                value, slope_value = gelu_both(
+                    dot(hidden_b[rows, :], up) + ffn_out[:, start:start + UP_CHUNK])
+                act[core, rows, :] = value.astype(BF)
+                slope[core, rows, :] = slope_value.astype(BF)
+
+            flip_act[core] = act[core].T
+            slot = 16 + 3 * core
+            waiting[core] = [
+                pltpu.make_async_copy(act.at[core], act_out.at[:, cols], local.at[slot]),
+                pltpu.make_async_copy(slope.at[core], slope_out.at[:, cols], local.at[slot + 1]),
+                pltpu.make_async_copy(flip_act.at[core], act_flip.at[cols, :], local.at[slot + 2]),
+            ]
+            for copy in waiting[core]:
+                copy.start()
+        spread_tick(groups, 9 + third)
+    for core in range(2):
+        keep(g_up.at[core], up_full.at[core])
+    for index in (7, 8, 9):
+        ready(index)
+    for copy in copies[1:] + waiting[0] + waiting[1]:
+        copy.wait()
+    for group in groups:
+        for made in group:
+            made.finish()
+
+
+def forward_gather(weights, vectors, tokens, lengths):
+    qkv, out, up, down = weights
+    count = tokens.shape[0]
+    shape = jax.ShapeDtypeStruct
+    grid = (2, 4, 2, 2)
+    held_out = 32
+    flipped = shape((D, count), BF)
+    small_outs = [
+        shape((8, 128), F32), shape((8, D), F32), shape((1, FF), F32),
+        shape((count // LEN, 16, LEN), F32), shape((count, 128), F32), shape((D, D), BF),
+    ]
+    large_outs = [
+        shape(grid + (qkv.shape[0], QKV_HALF), BF), shape(grid + up.shape, BF),
+        shape(grid + down.shape, BF), shape((2, count, QKV_HALF), BF), flipped, flipped, flipped,
+        shape((count, D), F32), shape((count, D), BF), shape((count, FF), BF),
+        shape((FF, count), BF), shape((count, FF), BF),
+    ]
+    slots = 11 * Spread.COUNT
+    return pl.pallas_call(
+        forward_gather_kernel,
+        out_shape=small_outs + large_outs,
+        in_specs=[VMEM] * 8 + [SMEM],
+        out_specs=[VMEM] * len(small_outs) + [pl.BlockSpec(memory_space=pl.ANY)] * len(large_outs),
+        scratch_shapes=[
+            pltpu.VMEM(grid + (16, 128), F32),
+            pltpu.VMEM(grid + (qkv.shape[0], QKV_HALF), BF),
+            pltpu.VMEM(grid + (held_out, D), BF),
+            pltpu.VMEM(grid + up.shape, BF),
+            pltpu.VMEM(down.shape, BF),
+            pltpu.VMEM((2, count, QKV_HALF), BF),
+            pltpu.VMEM((count, D), BF),
+            pltpu.VMEM((D, count), BF),
+            pltpu.VMEM((D, count), BF),
+            pltpu.VMEM((D, count), BF),
+            pltpu.VMEM((count, D), BF),
+            pltpu.VMEM((count, D), F32),
+            pltpu.VMEM((2, count, UP_CHUNK), BF),
+            pltpu.VMEM((2, count, UP_CHUNK), BF),
+            pltpu.VMEM((2, UP_CHUNK, count), BF),
+            pltpu.VMEM((2, LEN, LEN), F32),
+            pltpu.VMEM((2, LEN, 128), F32),
+            pltpu.VMEM((2, 1, QKV_HALF), F32),
+            pltpu.SemaphoreType.DMA((slots,)),
+            pltpu.SemaphoreType.DMA((slots,)),
+            pltpu.SemaphoreType.DMA((24,)),
+        ],
+        compiler_params=pltpu.CompilerParams(
+            collective_id=0, has_side_effects=True, vmem_limit_bytes=60 << 20),
+        name="forward_gather",
+    )(*weights, *vectors, tokens, lengths)
+
+
+def finish_kernel(*refs):
+    refs = list(refs)
+    take = lambda number: [refs.pop(0) for _ in range(number)]
+    lengths, norm, scale_one, w_out = take(4)
+    (down_any, up_any, act_any, slope_any, normed_any, context_any, cotangent_any) = take(7)
+    pooled, delta, norm_sums, ffn_sums = take(4)
+    (layer_any, branch_any, inner_any, attended_any, grad_context_any, one_any) = take(6)
+    (w_down, w_up, act, slope, normed_one, context, cotangent, layer_out, grad_branch,
+     grad_attended, grad_context, hidden) = take(12)
+    loads, stores = refs
+    core = lax.axis_index("mp")
+    started = []
+
+    def load(source, target):
+        copy = pltpu.make_async_copy(source, target, loads.at[len(started)])
+        copy.start()
+        started.append(copy)
+        return copy
+
+    halves = [pl.ds(row * LEN, LEN) for row in range(2)]
+    pair = lambda source, target: [load(source.at[rows], target.at[rows]) for rows in halves]
+    down_loaded = load(down_any, w_down)
+    act_loaded, normed_loaded = [], []
+    for rows in halves:
+        act_loaded.append(load(act_any.at[rows], act.at[rows]))
+        normed_loaded.append(load(normed_any.at[rows], normed_one.at[rows]))
+    cotangent_loaded = pair(cotangent_any, cotangent)
+    slope_loaded = pair(slope_any, slope)
+    up_loaded = load(up_any, w_up)
+    context_loaded = pair(context_any, context)
+    norm_sums[...] = jnp.zeros(norm_sums.shape, F32)
+    ffn_sums[...] = jnp.zeros(ffn_sums.shape, F32)
+    kept = []
+
+    def keep(source, target):
+        copy = pltpu.make_async_copy(source, target, stores.at[len(kept)])
+        copy.start()
+        kept.append(copy)
+
+    down_loaded.wait()
+    for row, rows in enumerate(halves):
+        act_loaded[row].wait()
+        normed_loaded[row].wait()
+        hidden[...] = normed_one[rows, :] * norm[2:3, :] + norm[3:4, :]
+        branch = dot(act[rows, :], w_down[...])
+        normed, scale = norm_parts(hidden[...] + branch + norm[1:2, :])
+        output = normed * norm[4:5, :] + norm[5:6, :]
+        high = output.astype(BF)
+        layer_out[rows, :] = high
+        keep(layer_out.at[rows], layer_any.at[rows])
+        low = (output - high.astype(F32)).astype(BF)
+        place = lax.broadcasted_iota(jnp.int32, (SEGS, LEN), 1)
+        segment = lax.broadcasted_iota(jnp.int32, (SEGS, 1), 0)
+        ids = ids_at(lengths, core * 2 + row, place)
+        member = (ids == segment).astype(F32)
+        sizes = jnp.sum(member, axis=1, keepdims=True)
+        member = member.astype(BF)
+        pooled[row] = (dot(member, high) + dot(member, low)) / sizes
+        cotangent_loaded[row].wait()
+        back, gain, shift = norm_back(cotangent[rows, :].astype(F32), normed, scale, norm[4:5, :])
+        norm_sums[4:5, :] += gain
+        norm_sums[5:6, :] += shift
+        hidden[...] = back
+        back = back.astype(BF)
+        grad_branch[rows, :] = back
+        keep(grad_branch.at[rows], branch_any.at[rows])
+        norm_sums[1:2, :] += jnp.sum(back.astype(F32), axis=0, keepdims=True)
+        slope_loaded[row].wait()
+        for start in range(0, FF, FF // 4):
+            cols = slice(start, start + FF // 4)
+            value = dot_last(grad_branch[rows, :], w_down[cols, :])
+            value = (value * slope[rows, cols].astype(F32)).astype(BF)
+            slope[rows, cols] = value
+            ffn_sums[:, cols] += jnp.sum(value.astype(F32), axis=0, keepdims=True)
+        keep(slope.at[rows], inner_any.at[rows])
+        if row == 0:
+            up_loaded.wait()
+        for half in range(2):
+            cols = slice(half * FF // 2, (half + 1) * FF // 2)
+            hidden[...] += dot_last(slope[rows, cols], w_up[half])
+        normed = normed_one[rows, :]
+        scale = scale_one[rows, 0:1]
+        back, gain, shift = norm_back(hidden[...], normed, scale, norm[2:3, :])
+        norm_sums[2:3, :] += gain
+        norm_sums[3:4, :] += shift
+        normed_one[rows, :] = back
+        keep(normed_one.at[rows], one_any.at[rows])
+        back = back.astype(BF)
+        grad_attended[rows, :] = back
+        keep(grad_attended.at[rows], attended_any.at[rows])
+        norm_sums[0:1, :] += jnp.sum(back.astype(F32), axis=0, keepdims=True)
+        back = dot_last(back, w_out[...]).astype(BF)
+        grad_context[rows, :] = back
+        keep(grad_context.at[rows], grad_context_any.at[rows])
+        context_loaded[row].wait()
+        product = back.astype(F32) * context[rows, :].astype(F32)
+        high = product.astype(BF)
+        low = (product - high.astype(F32)).astype(BF)
+        head = lax.broadcasted_iota(jnp.int32, (16, D), 0)
+        member = (lax.broadcasted_iota(jnp.int32, (16, D), 1) // HD == head).astype(F32).astype(BF)
+        delta[row] = dot_last(member, high) + dot_last(member, low)
+    for copy in kept:
+        copy.wait()
+
+
+def finish_forward(lengths, norm, scale_one, w_out, w_down, w_up, act, slope, normed, context,
+                   cotangent):
+    count = act.shape[0]
+    shape = jax.ShapeDtypeStruct
+    outs = [
+        shape((count // LEN, SEGS, D), F32), shape((count // LEN, 16, LEN), F32),
+        shape((8, D), F32), shape((1, FF), F32),
+    ]
+    large = [
+        shape((count, D), BF), shape((count, D), BF), shape((count, FF), BF),
+        shape((count, D), BF), shape((count, D), BF), shape((count, D), F32),
+    ]
+    some = pl.BlockSpec(memory_space=pl.ANY)
+    return pl.pallas_call(
+        finish_kernel,
+        out_shape=outs + large,
+        in_specs=[SMEM] + [VMEM] * 3 + [some] * 7,
+        out_specs=[VMEM] * 4 + [some] * 6,
+        scratch_shapes=[
+            pltpu.VMEM((FF, D), BF),
+            pltpu.VMEM((2, D, FF // 2), BF),
+            pltpu.VMEM((count, FF), BF),
+            pltpu.VMEM((count, FF), BF),
+            pltpu.VMEM((count, D), F32),
+            pltpu.VMEM((count, D), BF),
+            pltpu.VMEM((count, D), BF),
+            pltpu.VMEM((count, D), BF),
+            pltpu.VMEM((count, D), BF),
+            pltpu.VMEM((count, D), BF),
+            pltpu.VMEM((count, D), BF),
+            pltpu.VMEM((LEN, D), F32),
+            pltpu.SemaphoreType.DMA((16,)),
+            pltpu.SemaphoreType.DMA((16,)),
+        ],
+        compiler_params=pltpu.CompilerParams(vmem_limit_bytes=60 << 20),
+        name="finish_forward",
+    )(lengths, norm, scale_one, w_out, w_down, w_up, act, slope, normed, context, cotangent)
+
+
 def small_block(norm, head, ffn):
     wide = lambda v: jnp.pad(v, [(0, 0)] * (v.ndim - 1) + [(0, 128 - v.shape[-1])])
     block = jnp.concatenate([wide(norm), wide(head), wide(ffn)], axis=-2)
     return jnp.pad(block, [(0, 0)] * (block.ndim - 2) + [(0, 16 - block.shape[-2]), (0, 0)])
 
 
+def pair_major(weight):
+    count = weight.shape[0]
+    return weight.reshape(count, 3, 3, 128).transpose(0, 2, 1, 3).reshape(count, QKV_HALF)
+
+
 def gather_plain(weights, vectors):
     head, ffn, norm = vectors
     qkv, out, up, down = (w.astype(BF) for w in weights)
     full = []
-    for shard in (small_block(norm, head, ffn), qkv.reshape(qkv.shape[0], -1), out, up, down):
+    for shard in (small_block(norm, head, ffn), pair_major(qkv), out, up, down):
         full.append(lax.all_gather(lax.all_gather(shard, "dp", axis=0), "mp", axis=0))
     return full
 
@@ -1010,34 +1379,47 @@
     fast = data == 16 and cores == 2
     weights = [w_qkv, w_out, w_up, w_down]
     vectors = [head_bias, ffn_bias.reshape(1, -1), norm_bias]
-    if fast:
-        *gathered, weight_sums = gather(weights, vectors)
-        gathered = [g.reshape(cores, data, *g.shape[-2:]) for g in gathered]
-        gathered[2] = gathered[2][:, :, :w_out.shape[0]]
-    else:
-        gathered = gather_plain(weights, vectors)
-    small, qkv_g, out_g, up_g, down_g = gathered
-    small = small.astype(BF).astype(F32)
-    own_head, own_ffn, own_norm = head_bias.shape[1], ffn_bias.shape[0], norm_bias.shape[1]
-    norm_full = small[:, :, 0:6, :own_norm].transpose(2, 1, 0, 3).reshape(6, D)
-    head_full = small[:, :, 6:8, :own_head].transpose(2, 0, 1, 3).reshape(2, 2, 1, HALF)
-    ffn_full = small[:, :, 8, :own_ffn].reshape(1, FF)
-    offsets = jnp.concatenate([head_full[0], jnp.zeros_like(head_full[0]), head_full[1]], axis=-1)
-    qkv_full = qkv_g.reshape(2, D, QKV_HALF)
-    up_full = up_g.reshape(2, D, FF // 2)
-    down_full = down_g.reshape(FF, D)
-    out_full = out_g.reshape(D, D)
-    norm_full = jnp.pad(norm_full, ((0, 2), (0, 0)))
-    qkv, context, lse = forward(tokens, qkv_full, offsets, seg_lengths)
-    (layer_out, pooled, hidden_b, act, grad_branch, grad_inner, grad_attended, grad_context,
-     grad_one, delta, norm_sums, ffn_sums) = middle_call(
-        tokens, context, cotangent, seg_lengths, out_full, up_full, down_full, ffn_full, norm_full)
     rows_out = w_out.shape[0]
     held = 32 if fast else rows_out
-    grad_out, grad_up, grad_down = weight_grads(
-        context, hidden_b, act, grad_branch, grad_inner, grad_attended, cores * data, held)
+    if fast:
+        (weight_sums, norm_full, ffn_full, lse, scale_one, out_full, qkv_full, up_full, down_full,
+         qkv, context_flip, token_flip, hidden_flip, normed_one, context, act, act_flip, slope
+         ) = forward_gather(weights, vectors, tokens, seg_lengths)
+        qkv_full = qkv_full.reshape(2, D, QKV_HALF)
+        up_full = up_full.reshape(2, D, FF // 2)
+        down_full = down_full.reshape(FF, D)
+        (pooled, delta, norm_sums, ffn_sums, layer_out, grad_branch, grad_inner, grad_attended,
+         grad_context, grad_one) = finish_forward(
+            seg_lengths, norm_full, scale_one, out_full, down_full, up_full, act, slope,
+            normed_one, context, cotangent)
+        grad_out, grad_up, grad_down = weight_grads(
+            context_flip, hidden_flip, act_flip, grad_branch, grad_inner, grad_attended,
+            cores * data, held)
+    else:
+        small, qkv_g, out_g, up_g, down_g = gather_plain(weights, vectors)
+        small = small.astype(BF).astype(F32)
+        own_head, own_ffn, own_norm = head_bias.shape[1], ffn_bias.shape[0], norm_bias.shape[1]
+        norm_full = small[:, :, 0:6, :own_norm].transpose(2, 1, 0, 3).reshape(6, D)
+        head_full = small[:, :, 6:8, :own_head].transpose(2, 0, 1, 3).reshape(2, 2, 3, 1, 128)
+        ffn_full = small[:, :, 8, :own_ffn].reshape(1, FF)
+        offsets = jnp.concatenate([head_full[0], jnp.zeros_like(head_full[0]), head_full[1]], axis=2)
+        offsets = offsets.reshape(2, 1, QKV_HALF)
+        qkv_full = qkv_g.reshape(2, D, QKV_HALF)
+        up_full = up_g.reshape(2, D, FF // 2)
+        down_full = down_g.reshape(FF, D)
+        out_full = out_g.reshape(D, D)
+        norm_full = jnp.pad(norm_full, ((0, 2), (0, 0)))
+        qkv, context, lse = forward(tokens, qkv_full, offsets, seg_lengths)
+        (layer_out, pooled, hidden_b, act, grad_branch, grad_inner, grad_attended, grad_context,
+         grad_one, delta, norm_sums, ffn_sums) = middle_call(
+            tokens, context, cotangent, seg_lengths, out_full, up_full, down_full, ffn_full,
+            norm_full)
+        grad_out, grad_up, grad_down = weight_grads(
+            context.T, hidden_b.T, act.T, grad_branch, grad_inner, grad_attended,
+            cores * data, held)
+        token_flip = tokens.T
     grad_qkv, input_grad, grad_head = backward(
-        tokens, qkv, grad_context, lse, delta, seg_lengths, qkv_full, grad_one)
+        token_flip, qkv, grad_context, lse, delta, seg_lengths, qkv_full, grad_one)
     small_grads = small_block(
         norm_sums[:6].reshape(6, data, cores, -1).transpose(2, 1, 0, 3),
         grad_head.reshape(2, cores, data, -1).transpose(1, 2, 0, 3),
@@ -1071,6 +1453,7 @@
         )
     red_small, red_qkv, red_out, red_up, red_down = scatter_plain(fulls)
     norm_grad = red_small[0:6, :own_norm]
+    red_qkv = pair_major(red_qkv)
     red_head = red_small[6:8, :own_head]
     red_ffn = red_small[8, :own_ffn]
     weights_flat = [w_qkv.reshape(rows_qkv, -1), w_out, w_up, w_down]

time: 368 us -> 315 us (0.86)
  Pallas kernels: 342 us -> 295 us
  local copies, waits for them, and re-layouts: 20.8 us -> 13.3 us
    pallas_call x3 -> x2, Pallas kernels: 170 us -> 123 us  [the longest x1 88.9 us: forward_gather(): pl.pallas_call(forward_gather_kernel, out_shape=small_outs + large_outs,...]
    unnamed x77 -> x63, local copies, waits for them, and re-layouts: 13.9 us -> 9.12 us
where the time goes in v4:
time: 315 us; the launch traced here: 312 us
  Pallas kernels  295 us (94%)
  local copies, waits for them, and re-layouts  13.3 us (4%)
    pallas_call x1, Pallas kernels, scatter(): pl.pallas_call(functools.partial(scatter_kernel, count, parts), out_shape...  113 us
    pallas_call x1, Pallas kernels, forward_gather(): pl.pallas_call(forward_gather_kernel, out_shape=small_outs + large_outs,...  88.9 us
    pallas_call x1, Pallas kernels, backward(): pl.pallas_call(backward_kernel, out_shape=[shape((2, D, QKV_HALF), BF), s...  36.7 us
    pallas_call x1, Pallas kernels, finish_forward(): pl.pallas_call(finish_kernel, out_shape=outs + large, in_specs=[SMEM] + [...  34.5 us
    pallas_call x1, Pallas kernels, weight_grads(): pl.pallas_call(weight_grads_kernel, out_shape=[shape((blocks, held, D), B...  20.8 us
    unnamed x63, local copies, waits for them, and re-layouts  9.12 us

profile of v4, /device:TPU:0, one launch (start us, length us, event | category | flops | bytes accessed | tf_op | source)
XLA Modules:
  0.0 312.4 jit_solution(6247904383267632997)
XLA Ops:
  0.7 1.8 copy.49.refs_0_.refs_7_
  2.4 88.9 %forward_gather.1 = (f32[8,128]{1,0:T(8,128)}, f32[8,768]{1,0:T(8,128)}, f32[1,3072]{1,0:T(1,128)}, f32[2,16,512]{2,1,0:T(8,128)}, f32[1024,128]{1,0:T(8,128)}, ...) custom-call(f32[48,3,384]{2,1,0:T(4,128)} %copy.49.refs_0_.refs_7_, ...), custom_call_target="tpu_custom_call" | custom-call | tf_op jit(solution)/shard_map/forward_gather/pallas_call | solution.py:1165
  91.3 34.5 %finish_forward.1 = (f32[2,8,768]{2,1,0:T(8,128)}, f32[2,16,512]{2,1,0:T(8,128)}, f32[8,768]{1,0:T(8,128)}, f32[1,3072]{1,0:T(1,128)}, bf16[1024,768]{1,0:T(8,12...) custom-call(s32[4,8]{1,0:T(4,128)} %lengths.1, ...), custom_call_target="tpu_custom_call" | custom-call | tf_op jit(solution)/shard_map/finish_forward/pallas_call | solution.py:1317
  125.8 20.8 %weight_grads.1 = (bf16[32,32,768]{2,1,0:T(8,128)(2,1)}, bf16[2,768,1536]{2,1,0:T(8,128)(2,1)}, bf16[3072,768]{1,0:T(8,128)(2,1)}) custom-call(bf16[768,1024]{1,0:T(8,128)(2,1)} %get-tuple-element.116.context, bf16[768,1024]{1,0:T(8,128)(2,1)} %get-tuple-element.117.hidden_b, bf16[3072,1024]{1,0:T(8,128)(2,1)} %get-tuple-element.118.act, ...), custom_call_target="tpu_custom_call" | custom-call | tf_op jit(solution)/shard_map/weight_grads/pallas_call | solution.py:781
  146.6 36.7 %attend_back.1 = (bf16[2,768,1152]{2,1,0:T(8,128)(2,1)}, f32[1024,768]{1,0:T(8,128)}, f32[2,768]{1,0:T(2,128)}) custom-call(bf16[768,1024]{1,0:T(8,128)(2,1)} %get-tuple-element.104.tokens, bf16[2,1024,1152]{2,1,0:T(8,128)(2,1)} %get-tuple-element.105.qkv, bf16[1024,768]{1,0:T(8,128)(2,1)} %get-tuple-element.106.grad_context, ...), custom_call_target="tpu_custom_call" | custom-call | tf_op jit(solution)/shard_map/attend_back/pallas_call | solution.py:846
  183.3 0.8 reshape.139
  184.9 0.7 reduce.6
  185.7 0.7 pad.19
  186.4 0.6 reshape.147.refs_11_.refs_17_
  187.0 0.6 reshape.146.refs_10_.refs_16_
  188.4 112.8 %scatter_grads.1 = (f32[16,128]{1,0:T(8,128)}, f32[48,1152]{1,0:T(8,128)}, f32[24,768]{1,0:T(8,128)}, f32[48,1536]{1,0:T(8,128)}, f32[96,768]{1,0:T(8,128)}, /*index=5*/f32[40,128]{1,0:T(8,128)}, f32[8,128]{1,0:T(8,128)}) custom-call(f32[2,4,2,2,16,128]{5,4,3,2,1,0:T(8,128)} %bitcast.48, bf16[2,4,2,2,48,1152]{5,4,3,2,1,0:T(8,128)(2,1)} %bitcast.45, ...), custom_call_target="tpu_custom_call" | custom-call | tf_op jit(solution)/shard_map/scatter_grads/pallas_call | solution.py:410
  301.4 1.0 copy-done.4
  302.4 1.0 copy-done.5
  303.3 0.9 copy-done.6
  304.3 0.9 copy-done.7
  305.1 0.7 copy-done.12
  305.9 0.7 copy-done.15
  306.6 0.7 copy-done.16
  307.2 1.7 adafactor_step.1
  309.0 0.7 copy.54
  309.7 0.7 copy.55
  310.4 0.6 reduce.2
  311.0 0.6 reduce.1
  311.6 0.6 reduce.3
  (60 shorter events, 1.6 us)
Async XLA Ops:
  146.6 37.5 %copy-start.25 = (f32[8,768]{1,0:T(8,128)S(1)}, f32[8,768]{1,0:T(8,128)}, u32[]{:S(2)}) copy-start(f32[8,768]{1,0:T(8,128)} %get-tuple-element.112) | copy-start | bytes 73732
  146.6 38.3 %copy-start.26 = (f32[1,3072]{1,0:T(1,128)S(1)}, f32[1,3072]{1,0:T(1,128)}, u32[]{:S(2)}) copy-start(f32[1,3072]{1,0:T(1,128)} %get-tuple-element.114) | copy-start | bytes 36868
  146.6 39.9 %copy-start.27 = (f32[1536]{0:T(1024)S(1)}, f32[1536]{0:T(1024)}, u32[]{:S(2)}) copy-start(f32[1536]{0:T(1024)} %param.36) | copy-start | bytes 18436
  146.6 40.5 %copy-start.28 = (f32[768]{0:T(1024)S(1)}, f32[768]{0:T(1024)}, u32[]{:S(2)}) copy-start(f32[768]{0:T(1024)} %param.34) | copy-start | bytes 9220
  146.6 41.0 %copy-start.29 = (f32[768]{0:T(1024)S(1)}, f32[768]{0:T(1024)}, u32[]{:S(2)}) copy-start(f32[768]{0:T(1024)} %param.38) | copy-start | bytes 9220
  188.2 113.0 %copy-start = (f32[48,3,384]{2,1,0:T(4,128)S(1)}, f32[48,3,384]{2,1,0:T(4,128)}, u32[]{:S(2)}) copy-start(f32[48,3,384]{2,1,0:T(4,128)} %copy.49.refs_0_.refs_7_) | copy-start | bytes 663556
  188.2 113.0 %copy-start.1 = (f32[48,1536]{1,0:T(8,128)S(1)}, f32[48,1536]{1,0:T(8,128)}, u32[]{:S(2)}) copy-start(f32[48,1536]{1,0:T(8,128)} %refs_9_.3) | copy-start | bytes 884740
  188.2 113.0 %copy-start.2 = (f32[96,768]{1,0:T(8,128)S(1)}, f32[96,768]{1,0:T(8,128)}, u32[]{:S(2)}) copy-start(f32[96,768]{1,0:T(8,128)} %refs_10_.3) | copy-start | bytes 884740
  188.2 113.0 %copy-start.3 = (f32[24,768]{1,0:T(8,128)S(1)}, f32[24,768]{1,0:T(8,128)}, u32[]{:S(2)}) copy-start(f32[24,768]{1,0:T(8,128)} %refs_8_.3) | copy-start | bytes 221188
  188.2 113.0 %copy-start.8 = (f32[1,1536]{1,0:T(1,128)S(1)}, f32[1,1536]{1,0:T(1,128)}, u32[]{:S(2)}) copy-start(f32[1,1536]{1,0:T(1,128)} %reshape.147.refs_11_.refs_17_) | copy-start | bytes 18436
  188.2 113.0 %copy-start.9 = (f32[1,768]{1,0:T(1,128)S(1)}, f32[1,768]{1,0:T(1,128)}, u32[]{:S(2)}) copy-start(f32[1,768]{1,0:T(1,128)} %reshape.146.refs_10_.refs_16_) | copy-start | bytes 9220
  188.2 113.0 %copy-start.10 = (f32[1,768]{1,0:T(1,128)S(1)}, f32[1,768]{1,0:T(1,128)}, u32[]{:S(2)}) copy-start(f32[1,768]{1,0:T(1,128)} %reshape.148.refs_12_.refs_18_) | copy-start | bytes 9220
  188.3 113.0 %copy-start.11 = (f32[3,384]{1,0:T(4,128)S(1)}, f32[3,384]{1,0:T(4,128)}, u32[]{:S(2)}) copy-start(f32[3,384]{1,0:T(4,128)} %refs_15_.3) | copy-start | bytes 13828
  188.3 113.0 %copy-start.13 = (f32[6,24]{1,0:T(8,128)S(1)}, f32[6,24]{1,0:T(8,128)}, u32[]{:S(2)}) copy-start(f32[6,24]{1,0:T(8,128)} %refs_21_.1) | copy-start | bytes 1732
  188.3 113.0 %copy-start.14 = (f32[6,24]{1,0:T(8,128)S(1)}, f32[6,24]{1,0:T(8,128)}, u32[]{:S(2)}) copy-start(f32[6,24]{1,0:T(8,128)} %refs_24_.1) | copy-start | bytes 1732
  188.3 113.0 %copy-start.17 = (f32[2,24]{1,0:T(2,128)S(1)}, f32[2,24]{1,0:T(2,128)}, u32[]{:S(2)}) copy-start(f32[2,24]{1,0:T(2,128)} %refs_19_.1) | copy-start | bytes 580
  188.3 113.0 %copy-start.18 = (f32[2,24]{1,0:T(2,128)S(1)}, f32[2,24]{1,0:T(2,128)}, u32[]{:S(2)}) copy-start(f32[2,24]{1,0:T(2,128)} %refs_22_.1) | copy-start | bytes 580
  188.3 113.0 %copy-start.19 = (f32[96]{0:T(128)S(1)}, f32[96]{0:T(128)}, u32[]{:S(2)}) copy-start(f32[96]{0:T(128)} %param.29) | copy-start | bytes 1156
  188.3 113.0 %copy-start.20 = (f32[48]{0:T(128)S(1)}, f32[48]{0:T(128)}, u32[]{:S(2)}) copy-start(f32[48]{0:T(128)} %param.31) | copy-start | bytes 580
  188.3 113.0 %copy-start.21 = (f32[24]{0:T(128)S(1)}, f32[24]{0:T(128)}, u32[]{:S(2)}) copy-start(f32[24]{0:T(128)} %param.33) | copy-start | bytes 292
  188.4 113.0 %copy-start.22 = (f32[48]{0:T(128)S(1)}, f32[48]{0:T(128)}, u32[]{:S(2)}) copy-start(f32[48]{0:T(128)} %param.35) | copy-start | bytes 580
  188.4 113.0 %copy-start.23 = (f32[96]{0:T(128)S(1)}, f32[96]{0:T(128)}, u32[]{:S(2)}) copy-start(f32[96]{0:T(128)} %param.37) | copy-start | bytes 1156
  188.4 113.0 %copy-start.24 = (f32[96]{0:T(128)S(1)}, f32[96]{0:T(128)}, u32[]{:S(2)}) copy-start(f32[96]{0:T(128)} %param.40) | copy-start | bytes 1156
  301.4 1.0 copy-start.4
  (6 other events, 4.9 us)

commit v5 on v4

--- a/solution.py
+++ b/solution.py
@@ -58,13 +58,6 @@
     pl.semaphore_wait(barrier, count)
 
 
-def column_parts(cols):
-    tiles = cols // 128
-    first = tiles // 3
-    parts = [("yzx", 0, first * 128)] if first else []
-    return parts + [("zxy", first * 128, cols - first * 128)]
-
-
 def weight_sums_of(weights, small):
     parts = []
     for weight in weights:
@@ -74,90 +67,6 @@
         else:
             parts.append(all_sum(value * value))
     return scalars([jnp.zeros((1, 1), F32)] * 11 + parts + small_sums(small))
-
-
-class Scatterer:
-    def __init__(self, place, held, part, slots, sems, base):
-        order, start, width = part
-        self.place, self.held = place, held
-        self.order = order[::-1]
-        self.start_col, self.width = start, width
-        self.cols = pl.ds(start, width)
-        self.slots = slots
-        self.sems, self.base = sems, base
-
-    def view(self, spot):
-        return self.held.at[spot["z"], spot["y"], spot["x"], :, self.cols]
-
-    def copies(self, stage):
-        place, axis = self.place, self.order[stage]
-        out = []
-        for step in steps_of(axis):
-            spot = {"z": EVERY, "y": EVERY, "x": EVERY}
-            for done in self.order[:stage]:
-                spot[done] = getattr(place, done)
-            target = place.at(axis, step)
-            spot[axis] = target[axis]
-            send, recv = self.sems
-            slot = self.base + 4 * stage + step
-            land = self.slots[stage].at[step - 1]
-            out.append(pltpu.make_async_remote_copy(
-                self.view(spot), land, send.at[slot], recv.at[slot],
-                device_id=place.device(target), device_id_type=MESH))
-        return out
-
-    def start(self, stage):
-        for sent in self.copies(stage):
-            sent.start()
-
-    def add(self, stage, result=None):
-        place, axis = self.place, self.order[stage]
-        for sent in self.copies(stage):
-            sent.wait_recv()
-        left = [name for name in "zyx" if name not in self.order[:stage + 1]]
-        sizes = [4 if name == "z" else 2 for name in left]
-        total = 1
-        for size in sizes:
-            total *= size
-        slots = self.slots[stage]
-        arrivals = len(steps_of(axis))
-
-        def one(index):
-            spot = {name: getattr(place, name) for name in "zyx"}
-            inner = []
-            rest = index
-            for name, size in reversed(list(zip(left, sizes))):
-                spot[name] = rest % size
-                inner.insert(0, rest % size)
-                rest = rest // size
-            where = (spot["z"], spot["y"], spot["x"], EVERY, self.cols)
-            value = self.held[where].astype(F32)
-            for arrival in range(arrivals):
-                value = value + slots[tuple([arrival] + inner)].astype(F32)
-            if result is None:
-                self.held[where] = value.astype(self.held.dtype)
-            else:
-                result[:, self.cols] = value[:result.shape[0]]
-
-        if total == 1:
-            one(0)
-        else:
-            pl.loop(0, total)(one)
-
-    def finish(self):
-        for stage in range(3):
-            for sent in self.copies(stage):
-                sent.wait_send()
-
-
-def slot_shapes(part, rows):
-    order, _, width = part
-    order = order[::-1]
-    shapes = []
-    for stage in range(3):
-        left = [4 if name == "z" else 2 for name in "zyx" if name not in order[:stage + 1]]
-        shapes.append((len(steps_of(order[stage])), *left, rows, width))
-    return shapes
 
 
 def to_column(row):
@@ -301,131 +210,6 @@
         all_sum(jnp.where(line == 8, square, 0.0)),
         all_sum(jnp.where(line < 6, square, 0.0)),
     ]
-
-
-def scatter_kernel(count, parts, *refs):
-    refs = list(refs)
-    take = lambda number: [refs.pop(0) for _ in range(number)]
-    fulls = take(count)
-    rows_old, cols_old = take(4), take(4)
-    head_sq, ffn_sq, norm_sq, weight_sums = take(4)
-    results = take(count)
-    lines, totals = take(2)
-    held, other = take(count), take(count)
-    slots = [[take(3) for _ in parts[index]] for index in range(count)]
-    mine_one, land_one, mine_two, land_two, old_small = take(5)
-    send, recv, local = refs
-    place = Place()
-    greet(place)
-    partner = place.device(place.at("m", 1))
-    base = 0
-    groups, swaps, owns = [], [], []
-    for index in range(count):
-        swap = pltpu.make_async_remote_copy(
-            fulls[index].at[1 - place.m], other[index], send.at[base], recv.at[base],
-            device_id=partner, device_id_type=MESH)
-        swap.start()
-        own = pltpu.make_async_copy(fulls[index].at[place.m], held[index], local.at[index])
-        own.start()
-        swaps.append(swap)
-        owns.append(own)
-        base += 1
-        group = []
-        for number, part in enumerate(parts[index]):
-            group.append(Scatterer(place, held[index], part, slots[index][number], (send, recv), base))
-            base += 12
-        groups.append(group)
-    for turn in range(count + 3):
-        for index in range(count):
-            stage = turn - index
-            if stage == 0:
-                owns[index].wait()
-                swaps[index].wait_recv()
-
-                @pl.loop(0, 16)
-                def _(block):
-                    where = (block // 4, (block // 2) % 2, block % 2)
-                    held[index][where] = (
-                        held[index][where].astype(F32) + other[index][where].astype(F32)
-                    ).astype(held[index].dtype)
-
-                for path in groups[index]:
-                    path.start(0)
-            elif 1 <= stage <= 3:
-                for path in groups[index]:
-                    path.add(stage - 1, results[index] if stage == 3 else None)
-                    if stage < 3:
-                        path.start(stage)
-    small, grads = results[0], results[1:]
-    lines[...] = jnp.zeros(lines.shape, F32)
-    for index in range(4):
-        grad = grads[index][...]
-        square = grad * grad + EPS_SQUARE
-        put_line(lines, COL_LINES[index], jnp.sum(square, axis=0, keepdims=True))
-        if index in (0, 2):
-            line = ROW_LINE + index // 2
-            lines[line:line + 1, 0:grad.shape[0]] = to_row(jnp.sum(square, axis=1, keepdims=True))
-    first = Exchange(place, mine_one, land_one, (send, recv), base)
-    line = lax.broadcasted_iota(jnp.int32, lines.shape, 0)
-    value = lines[...]
-    first.mine[0] = value
-    paired = jnp.where(line >= OUT_LINE, first.swap(0, "m"), value)
-    total = paired
-    for stage, axis in ((1, "x"), (2, "y"), (3, "z")):
-        first.mine[stage] = total
-        total = first.swap(stage, axis)
-    lines[...] = jnp.where(line >= ROW_LINE, paired, total)
-    rows_new, cols_new = new_rows_cols(grads, rows_old, cols_old, lines)
-    ratios, row_totals = [], []
-    for index in range(4):
-        grad = grads[index][...]
-        scaled = jnp.sum(grad * grad * (1.0 / cols_new[index]), axis=1, keepdims=True)
-        ratios.append(jnp.sum(scaled / rows_new[index], axis=0, keepdims=True))
-        share = 0.5 if index in (0, 2) else 1.0
-        row_totals.append(jnp.sum(rows_new[index], axis=0, keepdims=True) * share)
-    place_small(old_small, norm_sq[...], head_sq[...], ffn_sq[...], 1.0)
-    _, update = small_update(small[...], old_small[...])
-    second = Exchange(place, mine_two, land_two, (send, recv), base + 16)
-    totals[...] = add_up(
-        second, scalars(ratios + row_totals + small_sums(update)) + weight_sums[...])
-    for index in range(count):
-        swaps[index].wait_send()
-        for path in groups[index]:
-            path.finish()
-    first.finish()
-    second.finish()
-
-
-def scatter(fulls, rows, rows_old, cols_old, squares, weight_sums):
-    count = len(fulls)
-    parts = [column_parts(f.shape[-1]) for f in fulls]
-    slots = []
-    for full, own in zip(fulls, parts):
-        for part in own:
-            slots += [pltpu.VMEM(s, full.dtype) for s in slot_shapes(part, full.shape[-2])]
-    sems = sum(1 + 12 * len(own) for own in parts) + 32
-    vmem = pl.BlockSpec(memory_space=pltpu.VMEM)
-    outs = [jax.ShapeDtypeStruct((r, f.shape[-1]), F32) for r, f in zip(rows, fulls)]
-    outs += [jax.ShapeDtypeStruct((LINES, 128), F32), jax.ShapeDtypeStruct((8, 128), F32)]
-    return pl.pallas_call(
-        functools.partial(scatter_kernel, count, parts),
-        out_shape=outs,
-        in_specs=[pl.BlockSpec(memory_space=pl.ANY)] * count + [vmem] * 12,
-        out_specs=[vmem] * len(outs),
-        scratch_shapes=[pltpu.VMEM(f.shape[1:], f.dtype) for f in fulls] * 2 + slots + [
-            pltpu.VMEM((4, LINES, 128), F32),
-            pltpu.VMEM((4, 4, LINES, 128), F32),
-            pltpu.VMEM((4, 8, 128), F32),
-            pltpu.VMEM((4, 4, 8, 128), F32),
-            pltpu.VMEM((16, 128), F32),
-            pltpu.SemaphoreType.DMA((sems,)),
-            pltpu.SemaphoreType.DMA((sems,)),
-            pltpu.SemaphoreType.DMA((count,)),
-        ],
-        compiler_params=pltpu.CompilerParams(
-            collective_id=1, has_side_effects=True, vmem_limit_bytes=56 << 20),
-        name="scatter_grads",
-    )(*fulls, *rows_old, *cols_old, *squares, weight_sums)
 
 
 def step_kernel(*refs):
@@ -1340,6 +1124,442 @@
     )(lengths, norm, scale_one, w_out, w_down, w_up, act, slope, normed, context, cotangent)
 
 
+class Collect:
+    COUNT = 8
+
+    def __init__(self, place, held, slots, result, start, width, flip, sems, base):
+        self.place, self.held, self.slots, self.result = place, held, slots, result
+        self.cols = pl.ds(start, width)
+        tiles = width // 128
+        cut = (tiles // 2 if flip else tiles - tiles // 2) * 128
+        self.halves = [("xy", pl.ds(start, cut))]
+        if cut < width:
+            self.halves.append(("yx", pl.ds(start + cut, width - cut)))
+        self.sems, self.base = sems, base
+
+    def copy(self, slot, axis, step, source, target):
+        send, recv = self.sems
+        return pltpu.make_async_remote_copy(
+            source, target, send.at[self.base + slot], recv.at[self.base + slot],
+            device_id=self.place.device(self.place.at(axis, step)), device_id_type=MESH)
+
+    def copies(self, stage):
+        place = self.place
+        if stage == 2:
+            out = []
+            for step in (1, 2, 3):
+                source = self.held.at[place.at("z", step)["z"], place.y, place.x, :, self.cols]
+                out.append(self.copy(
+                    step - 1, "z", step, source, self.slots[2].at[step - 1, :, self.cols]))
+            return out
+        out = []
+        for number, (order, cols) in enumerate(self.halves):
+            axis = order[stage]
+            spot = {"y": EVERY, "x": EVERY}
+            if stage == 1:
+                spot[order[0]] = getattr(place, order[0])
+            spot[axis] = place.at(axis, 1)[axis]
+            land = (EVERY,) * (2 - stage) + (EVERY, cols)
+            out.append(self.copy(
+                3 + 2 * stage + number, axis, 1, self.held.at[:, spot["y"], spot["x"], :, cols],
+                self.slots[stage].at[land]))
+        return out
+
+    def start(self, stage):
+        for sent in self.copies(stage):
+            sent.start()
+
+    def add(self, stage):
+        place, held, slots = self.place, self.held, self.slots[stage]
+        for sent in self.copies(stage):
+            sent.wait_recv()
+        if stage == 2:
+            value = held[place.z, place.y, place.x, :, self.cols].astype(F32)
+            for step in range(3):
+                value = value + slots[step, :, self.cols].astype(F32)
+            self.result[:, self.cols] = value[:self.result.shape[0]]
+            return
+        for order, cols in self.halves:
+
+            @pl.loop(0, 8 if stage == 0 else 4)
+            def _(index):
+                spot = {"y": place.y, "x": place.x}
+                if stage == 0:
+                    layer = index // 2
+                    spot[order[1]] = index % 2
+                    arrived = slots[layer, index % 2, :, cols]
+                else:
+                    layer = index
+                    arrived = slots[layer, :, cols]
+                at = (layer, spot["y"], spot["x"], EVERY, cols)
+                held[at] = (held[at].astype(F32) + arrived.astype(F32)).astype(held.dtype)
+
+    def finish(self):
+        for stage in range(3):
+            for sent in self.copies(stage):
+                sent.wait_send()
+
+
+def collect_tick(groups, tick):
+    for stage in range(4):
+        if 0 <= tick - stage < len(groups):
+            for chunk in groups[tick - stage]:
+                if stage:
+                    chunk.add(stage - 1)
+                if stage < 3:
+                    chunk.start(stage)
+
+
+def pack_small(target, core, norm_sums, grad_head, ffn_sums):
+    iota = lambda shape, axis: lax.broadcasted_iota(jnp.int32, shape, axis)
+    pick = (iota((D, 128), 0) % 24 == iota((D, 128), 1)).astype(F32).astype(BF)
+    pick_ffn = (iota((FF, 128), 0) % 96 == iota((FF, 128), 1)).astype(F32).astype(BF)
+
+    def split_dot(value, other):
+        high = value.astype(BF)
+        return dot(high, other) + dot((value - high.astype(F32)).astype(BF), other)
+
+    rows = jnp.concatenate(
+        [norm_sums[0:6, :], grad_head[0:2, :], jnp.zeros((8, D), F32)], axis=0)
+    rows = jnp.broadcast_to(rows[None], (16, 16, D)).reshape(256, D)
+    line = iota((256, D), 0)
+    device, kind = line // 16, line % 16
+    right = jnp.where(kind < 6, 2 * device + core, 16 * core + device)
+    rows = jnp.where(iota((256, D), 1) // 24 == right, rows, 0.0)
+    target[...] = split_dot(rows, pick).reshape(4, 2, 2, 16, 128)
+    right = iota((16, FF), 1) // 96 == iota((16, FF), 0) + 16 * core
+    ffn = split_dot(jnp.where(right, ffn_sums[...], 0.0), pick_ffn)
+    target[:, :, :, 8, :] = ffn.reshape(4, 2, 2, 128)
+
+
+def attend_back_pair(qkv, grad_context, lse, delta, bias, grad_head, core, row, pair):
+    lane = lax.broadcasted_iota(jnp.int32, (LEN, 128), 1)
+    item = core * 3 + pair
+    queries, keys, values = (slab(qkv, core, row, part, pair) for part in range(3))
+    rows = pl.ds(pl.multiple_of(row * LEN, LEN), LEN)
+    wide = pl.ds(pl.multiple_of(item * 128, 128), 128)
+    grad = grad_context[rows, wide]
+    flipped = keys.T
+    grads_k, grads_v, grads_q = [], [], []
+    for half, mask in enumerate(half_masks()):
+        head = item * 2 + half
+        scores = dot_last(keys * mask, queries) + bias[row] - lse[row, pl.ds(head, 1), :]
+        probs = jnp.exp(scores)
+        grad_probs = dot_last(values * mask, grad)
+        grad_scores = (probs * (grad_probs - delta[row, pl.ds(head, 1), :])).astype(BF)
+        grads_v.append(dot(probs.astype(BF), grad))
+        grads_k.append(dot(grad_scores, queries))
+        grads_q.append(dot(flipped[half * HD:(half + 1) * HD, :], grad_scores))
+    grad_q = (jnp.concatenate(grads_q, axis=0).T * HD ** -0.5).astype(BF)
+    grad_k = jnp.where(lane < HD, grads_k[0], grads_k[1]).astype(BF)
+    grad_v = jnp.where(lane < HD, grads_v[0], grads_v[1]).astype(BF)
+    for part, value in enumerate((grad_q, grad_k, grad_v)):
+        qkv[core, rows, pl.ds(pl.multiple_of(pair * PAIR + part * 128, 128), 128)] = value
+    grad_head[0:1, wide] += jnp.sum(grad_q.astype(F32), axis=0, keepdims=True)
+    grad_head[1:2, wide] += jnp.sum(grad_v.astype(F32), axis=0, keepdims=True)
+
+
+def backward_scatter_kernel(*refs):
+    refs = list(refs)
+    take = lambda number: [refs.pop(0) for _ in range(number)]
+    lengths, lse, delta, norm_sums, ffn_sums = take(5)
+    rows_old, cols_old = take(4), take(4)
+    head_sq, ffn_sq, norm_sq, weight_sums = take(4)
+    (act_any, inner_any, branch_any, hidden_any, context_any, attended_any, token_any, qkv_any,
+     grad_context_any, weight_any, one_any) = take(11)
+    results = take(5)
+    lines, totals, input_any = take(3)
+    held, other = take(5), take(5)
+    slots = [take(3) for _ in range(5)]
+    (wide, flip, flip_context, attended, qkv, weight, one, act, inner, bias, grad_head) = take(11)
+    mine_one, land_one, mine_two, land_two, old_small = take(5)
+    send, recv, local = refs
+    place = Place()
+    sems = (send, recv)
+    partner = place.device(place.at("m", 1))
+    mine, theirs = place.m, 1 - place.m
+    loaded = {}
+
+    def load(name, source, target):
+        copy = pltpu.make_async_copy(source, target, local.at[len(loaded)])
+        copy.start()
+        loaded[name] = copy
+
+    tile_rows = FF // 2 // 4
+    act_slots, inner_slots = 12, 14
+
+    def act_load(index):
+        core = jnp.where(index < 4, theirs, mine)
+        start = pl.multiple_of(core * (FF // 2) + (index % 4) * tile_rows, tile_rows)
+        return pltpu.make_async_copy(
+            act_any.at[pl.ds(start, tile_rows)], act.at[index % 2], local.at[act_slots + index % 2])
+
+    def inner_load(index):
+        core = jnp.where(index < 3, theirs, mine)
+        start = pl.multiple_of(core * (FF // 2) + (index % 3) * UP_CHUNK, UP_CHUNK)
+        return pltpu.make_async_copy(
+            inner_any.at[:, pl.ds(start, UP_CHUNK)], inner.at[index % 2],
+            local.at[inner_slots + index % 2])
+
+    load("branch", branch_any, wide)
+    for index in range(2):
+        act_load(index).start()
+    load("hidden", hidden_any, flip)
+    for index in range(2):
+        inner_load(index).start()
+    load("attended", attended_any, attended)
+    load("context", context_any, flip_context)
+    load("qkv", qkv_any, qkv)
+    load("weight", weight_any, weight)
+    load("one", one_any, one)
+
+    small, qkv_held, out_held, up_held, down_held = held
+    small_other, qkv_other, out_other, up_other, down_other = other
+    base = 12
+
+    def swap(slot, source, target):
+        return pltpu.make_async_remote_copy(
+            source, target, send.at[slot], recv.at[slot],
+            device_id=partner, device_id_type=MESH)
+
+    def down_swap(layer):
+        return swap(layer, down_held.at[layer], down_other.at[layer])
+
+    def up_swap(third):
+        cols = pl.ds(pl.multiple_of(third * UP_CHUNK, UP_CHUNK), UP_CHUNK)
+        at = (EVERY, EVERY, EVERY, EVERY, cols)
+        return swap(4 + third, up_held.at[at], up_other.at[at])
+
+    def qkv_swap(pair):
+        at = (EVERY, EVERY, EVERY, EVERY, pl.ds(pl.multiple_of(pair * PAIR, PAIR), PAIR))
+        return swap(8 + pair, qkv_held.at[at], qkv_other.at[at])
+
+    out_swap = swap(7, out_held, out_other)
+    small_swap = swap(11, small, small_other)
+    widths = (128, PAIR, D, UP_CHUNK, DOWN_CHUNK)
+    chunks = [[] for _ in range(5)]
+    for index in (4, 3, 2, 1, 0):
+        for start in range(0, held[index].shape[4], widths[index]):
+            chunks[index].append(Collect(
+                place, held[index], slots[index], results[index], start, widths[index],
+                index == 1 and start == PAIR, sems, base))
+            base += Collect.COUNT
+    groups = [[c] for index in (4, 3, 2, 1) for c in chunks[index]]
+    groups[-1] += chunks[0]
+
+    greet(place)
+    loaded["branch"].wait()
+
+    @pl.loop(0, 4)
+    def _(layer):
+        act_load(layer).wait()
+        value = dot(act[layer % 2], wide[...])
+        down_held[layer] = value.reshape(2, 2, tile_rows // 4, D).astype(BF)
+        down_swap(layer).start()
+        act_load(layer + 2).start()
+
+    @pl.loop(0, 4)
+    def _(layer):
+        act_load(layer + 4).wait()
+        value = dot(act[layer % 2], wide[...]).reshape(2, 2, tile_rows // 4, D)
+        down_swap(layer).wait()
+        down_held[layer] = (value + down_other[layer].astype(F32)).astype(BF)
+
+        @pl.when(layer < 2)
+        def _():
+            act_load(layer + 6).start()
+
+    load("grad_context", grad_context_any, wide)
+    collect_tick(groups, 0)
+    loaded["hidden"].wait()
+
+    @pl.loop(0, 3)
+    def _(third):
+        inner_load(third).wait()
+        cols = pl.ds(pl.multiple_of(third * UP_CHUNK, UP_CHUNK), UP_CHUNK)
+        value = dot(flip[...], inner[third % 2])
+        up_held[:, :, :, :, cols] = value.reshape(4, 2, 2, D // 16, UP_CHUNK).astype(BF)
+        up_swap(third).start()
+        inner_load(third + 2).start()
+
+    @pl.loop(0, 3)
+    def _(third):
+        inner_load(third + 3).wait()
+        at = (EVERY, EVERY, EVERY, EVERY,
+              pl.ds(pl.multiple_of(third * UP_CHUNK, UP_CHUNK), UP_CHUNK))
+        value = dot(flip[...], inner[(third + 3) % 2]).reshape(4, 2, 2, D // 16, UP_CHUNK)
+        up_swap(third).wait()
+        up_held[at] = (value + up_other[at].astype(F32)).astype(BF)
+
+        @pl.when(third == 0)
+        def _():
+            inner_load(5).start()
+            collect_tick(groups, 1)
+
+    load("token", token_any, flip)
+    loaded["attended"].wait()
+    loaded["context"].wait()
+    spare = out_held.shape[3] - D // 32
+
+    def out_half(core):
+        rows = pl.ds(pl.multiple_of(core * HALF, HALF), HALF)
+        value = dot(flip_context[rows, :], attended[...]).reshape(16, D // 32, D)
+        value = jnp.concatenate([value, jnp.zeros((16, spare, D), F32)], axis=1)
+        return value.reshape(4, 2, 2, D // 32 + spare, D)
+
+    out_held[...] = out_half(theirs).astype(BF)
+    out_swap.start()
+    value = out_half(mine)
+    out_swap.wait()
+    out_held[...] = (value + out_other[...].astype(F32)).astype(BF)
+    collect_tick(groups, 2)
+    for row in range(2):
+        set_bias(bias.at[row], lengths, place.m * 2 + row)
+    grad_head[...] = jnp.zeros(grad_head.shape, F32)
+    for name in ("qkv", "grad_context", "token"):
+        loaded[name].wait()
+
+    def qkv_theirs(pair):
+        cols = pl.ds(pl.multiple_of(pair * PAIR, PAIR), PAIR)
+        value = dot(flip[...], qkv[theirs, :, cols])
+        qkv_held[:, :, :, :, cols] = value.reshape(4, 2, 2, D // 16, PAIR).astype(BF)
+        qkv_swap(pair).start()
+
+    def qkv_mine(pair):
+        cols = pl.ds(pl.multiple_of(pair * PAIR, PAIR), PAIR)
+        at = (EVERY, EVERY, EVERY, EVERY, cols)
+        value = dot(flip[...], qkv[mine, :, cols]).reshape(4, 2, 2, D // 16, PAIR)
+        qkv_swap(pair).wait()
+        qkv_held[at] = (value + qkv_other[at].astype(F32)).astype(BF)
+
+    @pl.loop(0, 12)
+    def _(item):
+        pair, row, core = item // 4, (item % 4) // 2, item % 2
+
+        @pl.when((item == 4) | (item == 8))
+        def _():
+            qkv_theirs(pair - 1)
+
+        @pl.when((item == 5) | (item == 9))
+        def _():
+            qkv_mine(pair - 1)
+
+        for number, at in enumerate((1, 3, 5, 7, 9, 11)):
+            @pl.when(item == at)
+            def _():
+                collect_tick(groups, 3 + number)
+
+        attend_back_pair(qkv, wide, lse, delta, bias, grad_head, core, row, pair)
+
+    qkv_theirs(2)
+    pack_small(small, theirs, norm_sums, grad_head, ffn_sums)
+    small_swap.start()
+    loaded["weight"].wait()
+    loaded["one"].wait()
+
+    def input_rows(row):
+        rows = pl.ds(pl.multiple_of(row * LEN, LEN), LEN)
+        one[rows, :] += dot_last(qkv[0, rows, :], weight[0]) + dot_last(qkv[1, rows, :], weight[1])
+
+    qkv_mine(2)
+    small_swap.wait()
+    pack_small(small, mine, norm_sums, grad_head, ffn_sums)
+    small[...] += small_other[...]
+    collect_tick(groups, 9)
+    input_rows(0)
+    collect_tick(groups, 10)
+    input_rows(1)
+    input_done = pltpu.make_async_copy(one, input_any, local.at[16])
+    input_done.start()
+    collect_tick(groups, 11)
+    collect_tick(groups, 12)
+    small_sum, grads = results[0], results[1:]
+    lines[...] = jnp.zeros(lines.shape, F32)
+    for index in range(4):
+        grad = grads[index][...]
+        square = grad * grad + EPS_SQUARE
+        put_line(lines, COL_LINES[index], jnp.sum(square, axis=0, keepdims=True))
+        if index in (0, 2):
+            line = ROW_LINE + index // 2
+            lines[line:line + 1, 0:grad.shape[0]] = to_row(jnp.sum(square, axis=1, keepdims=True))
+    first = Exchange(place, mine_one, land_one, sems, base)
+    line = lax.broadcasted_iota(jnp.int32, lines.shape, 0)
+    value = lines[...]
+    first.mine[0] = value
+    paired = jnp.where(line >= OUT_LINE, first.swap(0, "m"), value)
+    total = paired
+    for stage, axis in ((1, "x"), (2, "y"), (3, "z")):
+        first.mine[stage] = total
+        total = first.swap(stage, axis)
+    lines[...] = jnp.where(line >= ROW_LINE, paired, total)
+    rows_new, cols_new = new_rows_cols(grads, rows_old, cols_old, lines)
+    ratios, row_totals = [], []
+    for index in range(4):
+        grad = grads[index][...]
+        scaled = jnp.sum(grad * grad * (1.0 / cols_new[index]), axis=1, keepdims=True)
+        ratios.append(jnp.sum(scaled / rows_new[index], axis=0, keepdims=True))
+        share = 0.5 if index in (0, 2) else 1.0
+        row_totals.append(jnp.sum(rows_new[index], axis=0, keepdims=True) * share)
+    place_small(old_small, norm_sq[...], head_sq[...], ffn_sq[...], 1.0)
+    _, update = small_update(small_sum[...], old_small[...])
+    second = Exchange(place, mine_two, land_two, sems, base + 16)
+    totals[...] = add_up(
+        second, scalars(ratios + row_totals + small_sums(update)) + weight_sums[...])
+    input_done.wait()
+    for group in groups:
+        for chunk in group:
+            chunk.finish()
+    first.finish()
+    second.finish()
+
+
+def backward_scatter(lengths, lse, delta, norm_sums, ffn_sums, rows_old, cols_old, squares,
+                     weight_sums, large, rows, widths):
+    count = large[2].shape[0]
+    shape = jax.ShapeDtypeStruct
+    some = pl.BlockSpec(memory_space=pl.ANY)
+    kinds = [F32, BF, BF, BF, BF]
+    padded = [16, rows[1], 32, rows[3], rows[4]]
+    held = [pltpu.VMEM((4, 2, 2, r, w), k) for r, w, k in zip(padded, widths, kinds)]
+    slots = []
+    for r, w, k in zip(padded, widths, kinds):
+        slots += [pltpu.VMEM((4, 2, r, w), k), pltpu.VMEM((4, r, w), k), pltpu.VMEM((3, r, w), k)]
+    sems = 12 + 11 * Collect.COUNT + 32
+    outs = [shape((r, w), F32) for r, w in zip(rows, widths)]
+    outs += [shape((LINES, 128), F32), shape((8, 128), F32), shape((count, D), F32)]
+    small = [lse, delta, norm_sums, ffn_sums, *rows_old, *cols_old, *squares, weight_sums]
+    return pl.pallas_call(
+        backward_scatter_kernel,
+        out_shape=outs,
+        in_specs=[SMEM] + [VMEM] * len(small) + [some] * len(large),
+        out_specs=[VMEM] * 7 + [some],
+        scratch_shapes=held + held + slots + [
+            pltpu.VMEM((count, D), BF),
+            pltpu.VMEM((D, count), BF),
+            pltpu.VMEM((D, count), BF),
+            pltpu.VMEM((count, D), BF),
+            pltpu.VMEM((2, count, QKV_HALF), BF),
+            pltpu.VMEM((2, D, QKV_HALF), BF),
+            pltpu.VMEM((count, D), F32),
+            pltpu.VMEM((2, FF // 8, count), BF),
+            pltpu.VMEM((2, count, UP_CHUNK), BF),
+            pltpu.VMEM((2, LEN, LEN), F32),
+            pltpu.VMEM((8, D), F32),
+            pltpu.VMEM((4, LINES, 128), F32),
+            pltpu.VMEM((4, 4, LINES, 128), F32),
+            pltpu.VMEM((4, 8, 128), F32),
+            pltpu.VMEM((4, 4, 8, 128), F32),
+            pltpu.VMEM((16, 128), F32),
+            pltpu.SemaphoreType.DMA((sems,)),
+            pltpu.SemaphoreType.DMA((sems,)),
+            pltpu.SemaphoreType.DMA((18,)),
+        ],
+        compiler_params=pltpu.CompilerParams(
+            collective_id=1, has_side_effects=True, vmem_limit_bytes=62 << 20),
+        name="backward_scatter",
+    )(lengths, *small, *large)
+
+
 def small_block(norm, head, ffn):
     wide = lambda v: jnp.pad(v, [(0, 0)] * (v.ndim - 1) + [(0, 128 - v.shape[-1])])
     block = jnp.concatenate([wide(norm), wide(head), wide(ffn)], axis=-2)
@@ -1380,7 +1600,6 @@
     weights = [w_qkv, w_out, w_up, w_down]
     vectors = [head_bias, ffn_bias.reshape(1, -1), norm_bias]
     rows_out = w_out.shape[0]
-    held = 32 if fast else rows_out
     if fast:
         (weight_sums, norm_full, ffn_full, lse, scale_one, out_full, qkv_full, up_full, down_full,
          qkv, context_flip, token_flip, hidden_flip, normed_one, context, act, act_flip, slope
@@ -1392,54 +1611,15 @@
          grad_context, grad_one) = finish_forward(
             seg_lengths, norm_full, scale_one, out_full, down_full, up_full, act, slope,
             normed_one, context, cotangent)
-        grad_out, grad_up, grad_down = weight_grads(
-            context_flip, hidden_flip, act_flip, grad_branch, grad_inner, grad_attended,
-            cores * data, held)
-    else:
-        small, qkv_g, out_g, up_g, down_g = gather_plain(weights, vectors)
-        small = small.astype(BF).astype(F32)
-        own_head, own_ffn, own_norm = head_bias.shape[1], ffn_bias.shape[0], norm_bias.shape[1]
-        norm_full = small[:, :, 0:6, :own_norm].transpose(2, 1, 0, 3).reshape(6, D)
-        head_full = small[:, :, 6:8, :own_head].transpose(2, 0, 1, 3).reshape(2, 2, 3, 1, 128)
-        ffn_full = small[:, :, 8, :own_ffn].reshape(1, FF)
-        offsets = jnp.concatenate([head_full[0], jnp.zeros_like(head_full[0]), head_full[1]], axis=2)
-        offsets = offsets.reshape(2, 1, QKV_HALF)
-        qkv_full = qkv_g.reshape(2, D, QKV_HALF)
-        up_full = up_g.reshape(2, D, FF // 2)
-        down_full = down_g.reshape(FF, D)
-        out_full = out_g.reshape(D, D)
-        norm_full = jnp.pad(norm_full, ((0, 2), (0, 0)))
-        qkv, context, lse = forward(tokens, qkv_full, offsets, seg_lengths)
-        (layer_out, pooled, hidden_b, act, grad_branch, grad_inner, grad_attended, grad_context,
-         grad_one, delta, norm_sums, ffn_sums) = middle_call(
-            tokens, context, cotangent, seg_lengths, out_full, up_full, down_full, ffn_full,
-            norm_full)
-        grad_out, grad_up, grad_down = weight_grads(
-            context.T, hidden_b.T, act.T, grad_branch, grad_inner, grad_attended,
-            cores * data, held)
-        token_flip = tokens.T
-    grad_qkv, input_grad, grad_head = backward(
-        token_flip, qkv, grad_context, lse, delta, seg_lengths, qkv_full, grad_one)
-    small_grads = small_block(
-        norm_sums[:6].reshape(6, data, cores, -1).transpose(2, 1, 0, 3),
-        grad_head.reshape(2, cores, data, -1).transpose(1, 2, 0, 3),
-        ffn_sums.reshape(cores, data, 1, -1),
-    )
-    fulls = [
-        small_grads,
-        grad_qkv.reshape(cores, data, rows_qkv, QKV_HALF),
-        grad_out.reshape(cores, data, held, D),
-        grad_up.reshape(cores, data, rows_qkv, FF // 2),
-        grad_down.reshape(cores, data, -1, D),
-    ]
-    if fast:
-        fulls = [f.reshape(2, 4, 2, 2, *f.shape[-2:]) for f in fulls]
         rows_old = [v.reshape(1, -1) for v in (qkv_rows, out_rows, up_rows, down_rows)]
         cols_old = [qkv_cols] + [v.reshape(1, -1) for v in (out_cols, up_cols, down_cols)]
         old = [head_bias_sq, ffn_bias_sq.reshape(1, -1), norm_sq]
-        *reduced, lines, totals = scatter(
-            fulls, [16, rows_qkv, rows_out, rows_qkv, w_down.shape[0]],
-            rows_old, cols_old, old, weight_sums)
+        *reduced, lines, totals, input_grad = backward_scatter(
+            seg_lengths, lse, delta, norm_sums, ffn_sums, rows_old, cols_old, old, weight_sums,
+            [act_flip, grad_inner, grad_branch, hidden_flip, context_flip, grad_attended,
+             token_flip, qkv, grad_context, qkv_full, grad_one],
+            [16, rows_qkv, rows_out, rows_qkv, w_down.shape[0]],
+            [128, QKV_HALF, D, w_up.shape[1], D])
         new = step(reduced, lines, totals, weights, rows_old, cols_old, vectors, old)
         grads, (g_head, g_ffn, g_norm) = new[:4], new[4:7]
         rows_new, cols_new = [r.reshape(-1) for r in new[7:11]], new[11:15]
@@ -1451,6 +1631,42 @@
             layer_out, pooled, input_grad, *grads, g_head, g_ffn.reshape(-1), g_norm, *stats,
             s_head, s_ffn.reshape(-1), s_norm, *mats, n_head, n_ffn.reshape(-1), n_norm,
         )
+    small, qkv_g, out_g, up_g, down_g = gather_plain(weights, vectors)
+    small = small.astype(BF).astype(F32)
+    own_head, own_ffn, own_norm = head_bias.shape[1], ffn_bias.shape[0], norm_bias.shape[1]
+    norm_full = small[:, :, 0:6, :own_norm].transpose(2, 1, 0, 3).reshape(6, D)
+    head_full = small[:, :, 6:8, :own_head].transpose(2, 0, 1, 3).reshape(2, 2, 3, 1, 128)
+    ffn_full = small[:, :, 8, :own_ffn].reshape(1, FF)
+    offsets = jnp.concatenate([head_full[0], jnp.zeros_like(head_full[0]), head_full[1]], axis=2)
+    offsets = offsets.reshape(2, 1, QKV_HALF)
+    qkv_full = qkv_g.reshape(2, D, QKV_HALF)
+    up_full = up_g.reshape(2, D, FF // 2)
+    down_full = down_g.reshape(FF, D)
+    out_full = out_g.reshape(D, D)
+    norm_full = jnp.pad(norm_full, ((0, 2), (0, 0)))
+    qkv, context, lse = forward(tokens, qkv_full, offsets, seg_lengths)
+    (layer_out, pooled, hidden_b, act, grad_branch, grad_inner, grad_attended, grad_context,
+     grad_one, delta, norm_sums, ffn_sums) = middle_call(
+        tokens, context, cotangent, seg_lengths, out_full, up_full, down_full, ffn_full,
+        norm_full)
+    grad_out, grad_up, grad_down = weight_grads(
+        context.T, hidden_b.T, act.T, grad_branch, grad_inner, grad_attended,
+        cores * data, rows_out)
+    token_flip = tokens.T
+    grad_qkv, input_grad, grad_head = backward(
+        token_flip, qkv, grad_context, lse, delta, seg_lengths, qkv_full, grad_one)
+    small_grads = small_block(
+        norm_sums[:6].reshape(6, data, cores, -1).transpose(2, 1, 0, 3),
+        grad_head.reshape(2, cores, data, -1).transpose(1, 2, 0, 3),
+        ffn_sums.reshape(cores, data, 1, -1),
+    )
+    fulls = [
+        small_grads,
+        grad_qkv.reshape(cores, data, rows_qkv, QKV_HALF),
+        grad_out.reshape(cores, data, rows_out, D),
+        grad_up.reshape(cores, data, rows_qkv, FF // 2),
+        grad_down.reshape(cores, data, -1, D),
+    ]
     red_small, red_qkv, red_out, red_up, red_down = scatter_plain(fulls)
     norm_grad = red_small[0:6, :own_norm]
     red_qkv = pair_major(red_qkv)

time: 315 us -> 266 us (0.84)
  Pallas kernels: 295 us -> 245 us
    pallas_call x3 -> x1, Pallas kernels: 170 us -> 120 us  [backward_scatter(): pl.pallas_call(backward_scatter_kernel, out_shape=outs, in_specs=[SMEM] +...]
    unnamed x63 -> x60, local copies, waits for them, and re-layouts: 9.12 us -> 12.9 us
where the time goes in v5:
time: 266 us; the launch traced here: 263 us
  Pallas kernels  245 us (92%)
  local copies, waits for them, and re-layouts  14.6 us (5%)
    pallas_call x1, Pallas kernels, backward_scatter(): pl.pallas_call(backward_scatter_kernel, out_shape=outs, in_specs=[SMEM] +...  120 us
    pallas_call x1, Pallas kernels, forward_gather(): pl.pallas_call(forward_gather_kernel, out_shape=small_outs + large_outs,...  89 us
    pallas_call x1, Pallas kernels, finish_forward(): pl.pallas_call(finish_kernel, out_shape=outs + large, in_specs=[SMEM] + [...  34.5 us
    unnamed x60, local copies, waits for them, and re-layouts  12.9 us

profile of v5, /device:TPU:0, one launch (start us, length us, event | category | flops | bytes accessed | tf_op | source)
XLA Modules:
  0.0 262.6 jit_solution(127386650820014229)
XLA Ops:
  0.7 1.8 copy.49.refs_0_.refs_7_
  2.4 89.0 %forward_gather.1 = (f32[8,128]{1,0:T(8,128)}, f32[8,768]{1,0:T(8,128)}, f32[1,3072]{1,0:T(1,128)}, f32[2,16,512]{2,1,0:T(8,128)}, f32[1024,128]{1,0:T(8,128)}, ...) custom-call(f32[48,3,384]{2,1,0:T(4,128)} %copy.49.refs_0_.refs_7_, ...), custom_call_target="tpu_custom_call" | custom-call | tf_op jit(solution)/shard_map/forward_gather/pallas_call | solution.py:949
  91.4 0.0 copy-start.26
  91.4 0.0 copy-start.27
  91.4 34.5 %finish_forward.1 = (f32[2,8,768]{2,1,0:T(8,128)}, f32[2,16,512]{2,1,0:T(8,128)}, f32[8,768]{1,0:T(8,128)}, f32[1,3072]{1,0:T(1,128)}, bf16[1024,768]{1,0:T(8,12...) custom-call(s32[4,8]{1,0:T(4,128)} %refs_0_.4, ...), custom_call_target="tpu_custom_call" | custom-call | tf_op jit(solution)/shard_map/finish_forward/pallas_call | solution.py:1101
  126.0 0.6 reshape.130.refs_11_.refs_17_
  126.6 0.6 reshape.129.refs_10_.refs_16_
  127.2 0.6 reshape.131.refs_12_.refs_18_
  127.7 0.0 copy-start.8
  127.9 119.8 %backward_scatter.1 = (f32[16,128]{1,0:T(8,128)}, f32[48,1152]{1,0:T(8,128)}, f32[24,768]{1,0:T(8,128)}, f32[48,1536]{1,0:T(8,128)}, f32[96,768]{1,0:T(8,128)}, ...) custom-call(s32[4,8]{1,0:T(4,128)} %refs_0_.4, f32[2,16,512]{2,1,0:T(8,128)} %get-tuple-element.99.refs_1_, ...), custom_call_target="tpu_custom_call" | custom-call | tf_op jit(solution)/shard_map/backward_scatter/pallas_call | solution.py:1531
  247.9 1.0 copy-done.4
  248.8 1.0 copy-done.5
  249.8 0.9 copy-done.6
  250.7 0.9 copy-done.7
  251.6 0.7 copy-done.12
  252.3 0.7 copy-done.15
  253.0 0.7 copy-done.16
  253.7 1.7 adafactor_step.1
  255.4 0.7 copy.51
  256.1 0.7 copy.52
  256.8 0.6 reduce.1
  257.5 0.6 reduce
  258.1 0.6 reduce.2
  258.7 3.8 %copy.54 = f32[1024,768]{1,0:T(8,128)} copy(f32[1024,768]{1,0:T(8,128)} %get-tuple-element.206) | data formatting | bytes 6291456
  (46 shorter events, 0.1 us)
Async XLA Ops:
  91.4 34.6 %copy-start.25 = (f32[1536]{0:T(1024)S(1)}, f32[1536]{0:T(1024)}, u32[]{:S(2)}) copy-start(f32[1536]{0:T(1024)} %param.36) | copy-start | bytes 18436
  91.4 35.2 %copy-start.26 = (f32[768]{0:T(1024)S(1)}, f32[768]{0:T(1024)}, u32[]{:S(2)}) copy-start(f32[768]{0:T(1024)} %param.34) | copy-start | bytes 9220
  91.4 35.7 %copy-start.27 = (f32[768]{0:T(1024)S(1)}, f32[768]{0:T(1024)}, u32[]{:S(2)}) copy-start(f32[768]{0:T(1024)} %param.38) | copy-start | bytes 9220
  127.7 120.0 %copy-start = (f32[48,3,384]{2,1,0:T(4,128)S(1)}, f32[48,3,384]{2,1,0:T(4,128)}, u32[]{:S(2)}) copy-start(f32[48,3,384]{2,1,0:T(4,128)} %copy.49.refs_0_.refs_7_) | copy-start | bytes 663556
  127.7 120.0 %copy-start.1 = (f32[48,1536]{1,0:T(8,128)S(1)}, f32[48,1536]{1,0:T(8,128)}, u32[]{:S(2)}) copy-start(f32[48,1536]{1,0:T(8,128)} %refs_9_.3) | copy-start | bytes 884740
  127.7 120.0 %copy-start.2 = (f32[96,768]{1,0:T(8,128)S(1)}, f32[96,768]{1,0:T(8,128)}, u32[]{:S(2)}) copy-start(f32[96,768]{1,0:T(8,128)} %refs_10_.3) | copy-start | bytes 884740
  127.7 120.0 %copy-start.3 = (f32[24,768]{1,0:T(8,128)S(1)}, f32[24,768]{1,0:T(8,128)}, u32[]{:S(2)}) copy-start(f32[24,768]{1,0:T(8,128)} %refs_8_.3) | copy-start | bytes 221188
  127.7 120.0 %copy-start.8 = (f32[1,1536]{1,0:T(1,128)S(1)}, f32[1,1536]{1,0:T(1,128)}, u32[]{:S(2)}) copy-start(f32[1,1536]{1,0:T(1,128)} %reshape.130.refs_11_.refs_17_) | copy-start | bytes 18436
  127.8 120.0 %copy-start.9 = (f32[1,768]{1,0:T(1,128)S(1)}, f32[1,768]{1,0:T(1,128)}, u32[]{:S(2)}) copy-start(f32[1,768]{1,0:T(1,128)} %reshape.129.refs_10_.refs_16_) | copy-start | bytes 9220
  127.8 120.0 %copy-start.10 = (f32[1,768]{1,0:T(1,128)S(1)}, f32[1,768]{1,0:T(1,128)}, u32[]{:S(2)}) copy-start(f32[1,768]{1,0:T(1,128)} %reshape.131.refs_12_.refs_18_) | copy-start | bytes 9220
  127.8 120.0 %copy-start.11 = (f32[3,384]{1,0:T(4,128)S(1)}, f32[3,384]{1,0:T(4,128)}, u32[]{:S(2)}) copy-start(f32[3,384]{1,0:T(4,128)} %refs_15_.3) | copy-start | bytes 13828
  127.8 120.0 %copy-start.13 = (f32[6,24]{1,0:T(8,128)S(1)}, f32[6,24]{1,0:T(8,128)}, u32[]{:S(2)}) copy-start(f32[6,24]{1,0:T(8,128)} %refs_21_.1) | copy-start | bytes 1732
  127.8 120.0 %copy-start.14 = (f32[6,24]{1,0:T(8,128)S(1)}, f32[6,24]{1,0:T(8,128)}, u32[]{:S(2)}) copy-start(f32[6,24]{1,0:T(8,128)} %refs_24_.1) | copy-start | bytes 1732
  127.8 120.0 %copy-start.17 = (f32[2,24]{1,0:T(2,128)S(1)}, f32[2,24]{1,0:T(2,128)}, u32[]{:S(2)}) copy-start(f32[2,24]{1,0:T(2,128)} %refs_19_.1) | copy-start | bytes 580
  127.8 120.0 %copy-start.18 = (f32[2,24]{1,0:T(2,128)S(1)}, f32[2,24]{1,0:T(2,128)}, u32[]{:S(2)}) copy-start(f32[2,24]{1,0:T(2,128)} %refs_22_.1) | copy-start | bytes 580
  127.8 120.0 %copy-start.19 = (f32[96]{0:T(128)S(1)}, f32[96]{0:T(128)}, u32[]{:S(2)}) copy-start(f32[96]{0:T(128)} %param.29) | copy-start | bytes 1156
  127.9 120.0 %copy-start.20 = (f32[48]{0:T(128)S(1)}, f32[48]{0:T(128)}, u32[]{:S(2)}) copy-start(f32[48]{0:T(128)} %param.31) | copy-start | bytes 580
  127.9 120.0 %copy-start.21 = (f32[24]{0:T(128)S(1)}, f32[24]{0:T(128)}, u32[]{:S(2)}) copy-start(f32[24]{0:T(128)} %param.33) | copy-start | bytes 292
  127.9 120.0 %copy-start.22 = (f32[48]{0:T(128)S(1)}, f32[48]{0:T(128)}, u32[]{:S(2)}) copy-start(f32[48]{0:T(128)} %param.35) | copy-start | bytes 580
  127.9 120.0 %copy-start.23 = (f32[96]{0:T(128)S(1)}, f32[96]{0:T(128)}, u32[]{:S(2)}) copy-start(f32[96]{0:T(128)} %param.37) | copy-start | bytes 1156
  127.9 120.0 %copy-start.24 = (f32[96]{0:T(128)S(1)}, f32[96]{0:T(128)}, u32[]{:S(2)}) copy-start(f32[96]{0:T(128)} %param.40) | copy-start | bytes 1156
  247.9 1.0 copy-start.4
  248.8 1.0 copy-start.5
  249.8 0.9 copy-start.6
  (4 other events, 3.0 us)

commit v6 on v5

--- a/solution.py
+++ b/solution.py
@@ -63,10 +63,15 @@
     for weight in weights:
         value = weight[...]
         if value.ndim == 3:
-            parts.append(sum(all_sum(value[:, part] * value[:, part]) for part in range(3)))
+            parts.append(sum(all_sum(value[part] * value[part]) for part in range(3)))
         else:
             parts.append(all_sum(value * value))
     return scalars([jnp.zeros((1, 1), F32)] * 11 + parts + small_sums(small))
+
+
+def as_row(ref):
+    value = ref[...]
+    return value.reshape(1, value.shape[0]) if value.ndim == 1 else value
 
 
 def to_column(row):
@@ -174,18 +179,18 @@
     for index in range(4):
         if index in (0, 2):
             line = ROW_LINE + index // 2
-            count = rows_old[index].shape[1]
+            count = rows_old[index].shape[0]
             row_sum = to_column(lines[line:line + 1, :count])
         else:
             grad = grads[index][...]
             row_sum = jnp.sum(grad * grad + EPS_SQUARE, axis=1, keepdims=True)
         rows_new.append(
-            DECAY * to_column(rows_old[index][...]) + (1.0 - DECAY) * row_sum / COL_COUNT[index])
+            DECAY * to_column(as_row(rows_old[index])) + (1.0 - DECAY) * row_sum / COL_COUNT[index])
         col_sum = get_line(lines, COL_LINES[index], WIDTHS[index])
         if index == 0:
             old = jnp.concatenate([cols_old[0][at] for at, _ in pair_cuts()], axis=1)
         else:
-            old = cols_old[index][...]
+            old = as_row(cols_old[index])
         cols_new.append(DECAY * old + (1.0 - DECAY) * col_sum / ROW_COUNT[index])
     return rows_new, cols_new
 
@@ -215,9 +220,10 @@
 def step_kernel(*refs):
     refs = list(refs)
     take = lambda number: [refs.pop(0) for _ in range(number)]
-    grads = take(4)
+    grads_any, weights_any = take(4), take(4)
+    passed = take(3)
     small, lines, totals = take(3)
-    weights, rows_old, cols_old = take(4), take(4), take(4)
+    rows_old, cols_old = take(4), take(4)
     head, ffn, norm, head_sq, ffn_sq, norm_sq = take(6)
     grads_out = take(4)
     head_grad, ffn_grad, norm_grad = take(3)
@@ -225,16 +231,28 @@
     head_second, ffn_second, norm_second = take(3)
     weights_out = take(4)
     head_new, ffn_new, norm_new = take(3)
-    old_small, weight_small = refs
+    passed_out = take(3)
+    grads, weights = take(4), take(4)
+    old_small, weight_small, sems = refs
+    loads = []
+    for number, (source, target) in enumerate(
+            zip(grads_any + weights_any + passed, grads + weights + passed_out)):
+        copy = pltpu.make_async_copy(source, target, sems.at[number])
+        copy.start()
+        loads.append(copy)
+    place_small(old_small, norm_sq[...], head_sq[...], as_row(ffn_sq), 1.0)
+    place_small(weight_small, norm[...], head[...], as_row(ffn), 0.0)
+    for copy in loads[:4]:
+        copy.wait()
     rows_new, cols_new = new_rows_cols(grads, rows_old, cols_old, lines)
     total = lambda lane: totals[0:1, lane:lane + 1]
     for index in range(4):
-        rows_out[index][...] = to_row(rows_new[index])
+        rows_out[index][...] = to_row(rows_new[index]).reshape(rows_out[index].shape)
         if index == 0:
             for at, cut in pair_cuts():
                 cols_out[0][at] = cols_new[0][:, cut]
         else:
-            cols_out[index][...] = cols_new[index]
+            cols_out[index][...] = cols_new[index].reshape(cols_out[index].shape)
         entries = ROW_COUNT[index] * COL_COUNT[index]
         row_mean = total(4 + index) / ROW_COUNT[index]
         update_rms = jnp.sqrt(row_mean * total(index) / entries)
@@ -242,9 +260,10 @@
             RATE * jnp.sqrt(total(11 + index) / entries) / jnp.maximum(1.0, update_rms / CLIP))
         scale_rows = lax.rsqrt(rows_new[index] / row_mean) * stride
         scale_cols = lax.rsqrt(cols_new[index])
+        loads[4 + index].wait()
         if index == 0:
             for (part, cols), cut in pair_cuts():
-                at = (EVERY, part.start, cols)
+                at = (part.start, EVERY, cols)
                 grad = grads[0][:, cut]
                 grads_out[0][at] = grad
                 weights_out[0][at] = weights[0][at] - grad * scale_rows * scale_cols[:, cut]
@@ -252,8 +271,6 @@
             grad = grads[index][...]
             grads_out[index][...] = grad
             weights_out[index][...] = weights[index][...] - grad * scale_rows * scale_cols
-    place_small(old_small, norm_sq[...], head_sq[...], ffn_sq[...], 1.0)
-    place_small(weight_small, norm[...], head[...], ffn[...], 0.0)
     grad = small[...]
     second, update = small_update(grad, old_small[...])
     line = lax.broadcasted_iota(jnp.int32, grad.shape, 0)
@@ -273,25 +290,32 @@
     ):
         norm_ref[...] = values[0:6, 0:norm_ref.shape[1]]
         head_ref[...] = values[6:8, 0:head_ref.shape[1]]
-        ffn_ref[...] = values[8:9, 0:ffn_ref.shape[1]]
-
-
-def step(reduced, lines, totals, weights, rows_old, cols_old, vectors, squares):
-    vmem = pl.BlockSpec(memory_space=pltpu.VMEM)
+        ffn_ref[...] = values[8:9, 0:ffn_ref.shape[0]].reshape(ffn_ref.shape)
+    for copy in loads[8:]:
+        copy.wait()
+
+
+def step(reduced, lines, totals, weights, rows_old, cols_old, vectors, squares, passed):
+    vmem, some = pl.BlockSpec(memory_space=pltpu.VMEM), pl.BlockSpec(memory_space=pl.ANY)
     small, grads = reduced[0], reduced[1:]
     shapes = [w.shape for w in weights] + [v.shape for v in vectors]
     shapes += [r.shape for r in rows_old] + [c.shape for c in cols_old]
     shapes += [v.shape for v in vectors] + [w.shape for w in weights] + [v.shape for v in vectors]
-    operands = [*grads, small, lines, totals, *weights, *rows_old, *cols_old, *vectors, *squares]
+    outs = [jax.ShapeDtypeStruct(s, F32) for s in shapes]
+    large = [*grads, *weights, *passed]
+    operands = [small, lines, totals, *rows_old, *cols_old, *vectors, *squares]
     return pl.pallas_call(
         step_kernel,
-        out_shape=[jax.ShapeDtypeStruct(s, F32) for s in shapes],
-        in_specs=[vmem] * len(operands),
-        out_specs=[vmem] * len(shapes),
-        scratch_shapes=[pltpu.VMEM((16, 128), F32), pltpu.VMEM((16, 128), F32)],
-        compiler_params=pltpu.CompilerParams(vmem_limit_bytes=32 << 20),
+        out_shape=outs + [jax.ShapeDtypeStruct(v.shape, v.dtype) for v in passed],
+        in_specs=[some] * len(large) + [vmem] * len(operands),
+        out_specs=[vmem] * (len(shapes) + len(passed)),
+        scratch_shapes=[pltpu.VMEM(v.shape, F32) for v in [*grads, *weights]] + [
+            pltpu.VMEM((16, 128), F32), pltpu.VMEM((16, 128), F32),
+            pltpu.SemaphoreType.DMA((11,)),
+        ],
+        compiler_params=pltpu.CompilerParams(vmem_limit_bytes=60 << 20),
         name="adafactor_step",
-    )(*operands)
+    )(*large, *operands)
 
 
 HALF = D // 2
@@ -748,6 +772,14 @@
                 offsets[core, :, start:start + 128] = total[row:row + 1, source:source + 128]
 
 
+def place_of(core, part, width):
+    return pl.ds(pl.multiple_of(core * PAIR + part * 128, 128), width)
+
+
+def trio(ref, core, row, part, pair):
+    return ref[pair, pl.ds(pl.multiple_of(row * LEN, LEN), LEN), place_of(core, part, 128)]
+
+
 def project_pair(tokens, weight, offsets, qkv, pair):
     cols = pl.ds(pl.multiple_of(pair * PAIR, PAIR), PAIR)
     scale = jnp.where(
@@ -755,14 +787,14 @@
     for core in range(2):
         piece = weight[core, :, :, :, :, cols].reshape(D, PAIR)
         out = dot(tokens[...], piece) + offsets[core, :, cols]
-        qkv[core, :, cols] = out.astype(BF) * scale
+        qkv[pair, :, place_of(core, 0, PAIR)] = out.astype(BF) * scale
 
 
 def attend_pair(qkv, bias, context, logs_ref, core, row, pair):
     rows = pl.ds(pl.multiple_of(row * LEN, LEN), LEN)
     lane = lax.broadcasted_iota(jnp.int32, (LEN, 128), 1)
     item = core * 3 + pair
-    queries, keys, values = (slab(qkv, core, row, part, pair) for part in range(3))
+    queries, keys, values = (trio(qkv, core, row, part, pair) for part in range(3))
     wide = jnp.concatenate([values, jnp.ones_like(values)], axis=1)
     outs = []
     logs = logs_ref[row]
@@ -782,50 +814,54 @@
 def forward_gather_kernel(*refs):
     refs = list(refs)
     take = lambda number: [refs.pop(0) for _ in range(number)]
-    w_qkv, w_out, w_up, w_down, head, ffn, norm, tokens, lengths = take(9)
-    (sums, norm_out, ffn_out, lse, hidden_scale, out_full) = take(6)
+    w_qkv, w_out, w_up, w_down, head, ffn, norm, lengths = take(8)
+    tokens_any, cotangent_any = take(2)
+    (sums, norm_out, ffn_out, lse, hidden_scale, out_full, pooled, norm_sums) = take(8)
     (qkv_full, up_full, down_full, qkv_out, context_flip, token_flip, hidden_flip, normed_out,
-     context_out, act_out, act_flip, slope_out) = take(12)
-    (g_small, g_qkv, g_out, g_up, cast_down, qkv, context, flip_context, flip_token, flip_hidden,
-     hidden_b, normed_one, act, slope, flip_act, bias, logs, offsets) = take(18)
+     context_out, act_flip, slope_out, layer_out, branch_out, grad_two_out) = take(14)
+    (g_small, g_qkv, g_out, g_up, g_down, tokens, qkv, context, flip,
+     hidden_b, normed_one, act, slope, flip_act, bias, logs, offsets, branch) = take(18)
     send, recv, local = refs
     place = Place()
     here = (place.m, place.z, place.y, place.x)
-    half = w_qkv.shape[2]
-    place_small(g_small.at[here], norm[...], head[...], ffn[...], 0.0)
+    used = [0]
+    unwaited = []
+
+    def keep(source, target):
+        copy = pltpu.make_async_copy(source, target, local.at[used[0]])
+        used[0] += 1
+        copy.start()
+        unwaited.append(copy)
+        return copy
+
+    def done(copy):
+        copy.wait()
+        unwaited[:] = [other for other in unwaited if other is not copy]
+
+    tokens_loaded = keep(tokens_any, tokens)
+    place_small(g_small.at[here], norm[...], head[...], as_row(ffn), 0.0)
     for part in range(3):
         for pair in range(3):
             start = pair * PAIR + part * 128
             g_qkv[here + (EVERY, slice(start, start + 128))] = w_qkv[
-                :, part, pair * 128:(pair + 1) * 128].astype(BF)
+                part, :, pair * 128:(pair + 1) * 128].astype(BF)
     value = w_out[...]
     spare = g_out.shape[4] - value.shape[0]
     g_out[here] = jnp.concatenate([value, jnp.zeros((spare, D), F32)], axis=0).astype(BF)
     g_up[here] = w_up[...].astype(BF)
-    cast_down[...] = w_down[...].astype(BF)
-    copies, used = [], [0]
-
-    def keep(source, target):
-        copy = pltpu.make_async_copy(source, target, local.at[used[0]])
-        used[0] += 1
-        copy.start()
-        copies.append(copy)
-        return copy
-
-    down_own = keep(cast_down, down_full.at[here])
+    g_down[here] = w_down[...].astype(BF)
     sems, base = (send, recv), [0]
 
-    def chunk(full, start, width, flip, shard=None):
-        made = Spread(place, full, start, width, flip, sems, base[0], shard)
+    def chunk(full, start, width, flip=False):
+        made = Spread(place, full, start, width, flip, sems, base[0])
         base[0] += Spread.COUNT
         return made
 
-    groups = [[chunk(g_small, 0, 128, False), chunk(g_qkv, 0, PAIR, False)]]
+    groups = [[chunk(g_small, 0, 128), chunk(g_qkv, 0, PAIR)]]
     groups += [[chunk(g_qkv, pair * PAIR, PAIR, pair == 1)] for pair in (1, 2)]
-    groups += [[chunk(g_out, 0, D, False)]]
-    groups += [[chunk(g_up, at, UP_CHUNK, False)] for at in range(0, FF // 2, UP_CHUNK)]
-    groups += [[chunk(down_full, at, DOWN_CHUNK, False, cast_down)]
-               for at in range(0, D, DOWN_CHUNK)]
+    groups += [[chunk(g_out, 0, D)]]
+    groups += [[chunk(g_up, at, UP_CHUNK)] for at in range(0, FF // 2, UP_CHUNK)]
+    groups += [[chunk(g_down, at, DOWN_CHUNK)] for at in range(0, D, DOWN_CHUNK)]
 
     def ready(index):
         for made in groups[index]:
@@ -836,13 +872,13 @@
         for made in groups[index]:
             made.start(0)
     sums[...] = weight_sums_of([w_qkv, w_out, w_up, w_down], g_small[here])
-    down_own.wait()
     spread_tick(groups, 0)
     for row in range(2):
         set_bias(bias.at[row], lengths, place.m * 2 + row)
     spread_tick(groups, 1)
-    flip_token[...] = tokens[...].T
-    keep(flip_token, token_flip)
+    done(tokens_loaded)
+    flip[...] = tokens[...].T
+    flip_kept = keep(flip, token_flip)
     spread_tick(groups, 2)
     logs[...] = jnp.zeros(logs.shape, F32)
     ready(0)
@@ -865,28 +901,31 @@
         attend_pair(qkv, bias, context, logs, core, row, pair)
 
     for core in range(2):
-        keep(g_qkv.at[core], qkv_full.at[core])
+        for pair in range(3):
+            cols = slice(pair * PAIR, (pair + 1) * PAIR)
+            keep(g_qkv.at[core, :, :, :, :, cols],
+                 qkv_full.at[pair, :, :, :, :, core * PAIR:(core + 1) * PAIR])
     keep(qkv, qkv_out)
-    keep(context, context_out)
+    context_kept = keep(context, context_out)
     for row in range(2):
         lse[row] = logs[row].T[0:16, :]
-    flip_context[...] = context[...].T
-    keep(flip_context, context_flip)
+    done(flip_kept)
+    flip[...] = context[...].T
+    flip_kept = keep(flip, context_flip)
     ready(3)
     rows_out = w_out.shape[0]
     for core in range(2):
         value = g_out[core].reshape(16, g_out.shape[4], D).astype(F32)[:, :rows_out]
         out_full[core * HALF:(core + 1) * HALF, :] = value.reshape(HALF, D).astype(BF)
-    for row in range(2):
-        rows = slice(row * LEN, (row + 1) * LEN)
+    halves = [slice(row * LEN, (row + 1) * LEN) for row in range(2)]
+    for rows in halves:
         attended = dot(context[rows, :], out_full[...]) + norm_out[0:1, :]
         normed, scale = norm_parts(tokens[rows, :].astype(F32) + attended)
         normed_one[rows, :] = normed
         hidden_scale[rows, :] = jnp.broadcast_to(scale, (LEN, 128))
         hidden_b[rows, :] = (normed * norm_out[2:3, :] + norm_out[3:4, :]).astype(BF)
+    cotangent_loaded = keep(cotangent_any, tokens)
     keep(normed_one, normed_out)
-    flip_hidden[...] = hidden_b[...].T
-    keep(flip_hidden, hidden_flip)
     spread_tick(groups, 8)
     waiting = [[], []]
     for third in range(3):
@@ -904,224 +943,115 @@
                 rows = pl.ds(pl.multiple_of(row * LEN, LEN), LEN)
                 value, slope_value = gelu_both(
                     dot(hidden_b[rows, :], up) + ffn_out[:, start:start + UP_CHUNK])
-                act[core, rows, :] = value.astype(BF)
+                act[rows, cols] = value.astype(BF)
                 slope[core, rows, :] = slope_value.astype(BF)
 
-            flip_act[core] = act[core].T
-            slot = 16 + 3 * core
+            flip_act[core] = act[:, cols].T
+            slot = 24 + 2 * core
             waiting[core] = [
-                pltpu.make_async_copy(act.at[core], act_out.at[:, cols], local.at[slot]),
-                pltpu.make_async_copy(slope.at[core], slope_out.at[:, cols], local.at[slot + 1]),
-                pltpu.make_async_copy(flip_act.at[core], act_flip.at[cols, :], local.at[slot + 2]),
+                pltpu.make_async_copy(slope.at[core], slope_out.at[:, cols], local.at[slot]),
+                pltpu.make_async_copy(flip_act.at[core], act_flip.at[cols, :], local.at[slot + 1]),
             ]
             for copy in waiting[core]:
                 copy.start()
         spread_tick(groups, 9 + third)
+    done(flip_kept)
+    flip[...] = hidden_b[...].T
+    keep(flip, hidden_flip)
     for core in range(2):
         keep(g_up.at[core], up_full.at[core])
-    for index in (7, 8, 9):
-        ready(index)
-    for copy in copies[1:] + waiting[0] + waiting[1]:
+    for third in range(3):
+        ready(7 + third)
+        cols = slice(third * DOWN_CHUNK, (third + 1) * DOWN_CHUNK)
+        down = g_down[:, :, :, :, :, cols].reshape(FF, DOWN_CHUNK)
+        for rows in halves:
+            branch[rows, cols] = dot(act[rows, :], down)
+    for core in range(2):
+        keep(g_down.at[core], down_full.at[core])
+    norm_sums[...] = jnp.zeros(norm_sums.shape, F32)
+    done(cotangent_loaded)
+    done(context_kept)
+    for row, rows in enumerate(halves):
+        hidden = normed_one[rows, :] * norm_out[2:3, :] + norm_out[3:4, :]
+        normed, scale = norm_parts(hidden + branch[rows, :] + norm_out[1:2, :])
+        output = normed * norm_out[4:5, :] + norm_out[5:6, :]
+        high = output.astype(BF)
+        context[rows, :] = high
+        keep(context.at[rows], layer_out.at[rows])
+        low = (output - high.astype(F32)).astype(BF)
+        spots = lax.broadcasted_iota(jnp.int32, (SEGS, LEN), 1)
+        segment = lax.broadcasted_iota(jnp.int32, (SEGS, 1), 0)
+        member = (ids_at(lengths, place.m * 2 + row, spots) == segment).astype(F32)
+        sizes = jnp.sum(member, axis=1, keepdims=True)
+        member = member.astype(BF)
+        pooled[row] = (dot(member, high) + dot(member, low)) / sizes
+        back, gain, shift = norm_back(tokens[rows, :].astype(F32), normed, scale, norm_out[4:5, :])
+        norm_sums[4:5, :] += gain
+        norm_sums[5:6, :] += shift
+        branch[rows, :] = back
+        keep(branch.at[rows], grad_two_out.at[rows])
+        back = back.astype(BF)
+        hidden_b[rows, :] = back
+        keep(hidden_b.at[rows], branch_out.at[rows])
+        norm_sums[1:2, :] += jnp.sum(back.astype(F32), axis=0, keepdims=True)
+    for copy in unwaited + waiting[0] + waiting[1]:
         copy.wait()
     for group in groups:
         for made in group:
             made.finish()
 
 
-def forward_gather(weights, vectors, tokens, lengths):
+def forward_gather(weights, vectors, lengths, tokens, cotangent):
     qkv, out, up, down = weights
     count = tokens.shape[0]
     shape = jax.ShapeDtypeStruct
     grid = (2, 4, 2, 2)
-    held_out = 32
+    rows = count // LEN
     flipped = shape((D, count), BF)
     small_outs = [
-        shape((8, 128), F32), shape((8, D), F32), shape((1, FF), F32),
-        shape((count // LEN, 16, LEN), F32), shape((count, 128), F32), shape((D, D), BF),
+        shape((8, 128), F32), shape((8, D), F32), shape((1, FF), F32), shape((rows, 16, LEN), F32),
+        shape((count, 128), F32), shape((D, D), BF), shape((rows, SEGS, D), F32), shape((8, D), F32),
     ]
     large_outs = [
-        shape(grid + (qkv.shape[0], QKV_HALF), BF), shape(grid + up.shape, BF),
-        shape(grid + down.shape, BF), shape((2, count, QKV_HALF), BF), flipped, flipped, flipped,
-        shape((count, D), F32), shape((count, D), BF), shape((count, FF), BF),
-        shape((FF, count), BF), shape((count, FF), BF),
+        shape((3,) + grid[1:] + (qkv.shape[1], D), BF), shape(grid + up.shape, BF),
+        shape(grid + down.shape, BF), shape((3, count, D), BF), flipped, flipped, flipped,
+        shape((count, D), F32), shape((count, D), BF), shape((FF, count), BF),
+        shape((count, FF), BF), shape((count, D), BF), shape((count, D), BF), shape((count, D), F32),
     ]
     slots = 11 * Spread.COUNT
+    some = pl.BlockSpec(memory_space=pl.ANY)
     return pl.pallas_call(
         forward_gather_kernel,
         out_shape=small_outs + large_outs,
-        in_specs=[VMEM] * 8 + [SMEM],
-        out_specs=[VMEM] * len(small_outs) + [pl.BlockSpec(memory_space=pl.ANY)] * len(large_outs),
+        in_specs=[VMEM] * 7 + [SMEM] + [some] * 2,
+        out_specs=[VMEM] * len(small_outs) + [some] * len(large_outs),
         scratch_shapes=[
             pltpu.VMEM(grid + (16, 128), F32),
-            pltpu.VMEM(grid + (qkv.shape[0], QKV_HALF), BF),
-            pltpu.VMEM(grid + (held_out, D), BF),
+            pltpu.VMEM(grid + (qkv.shape[1], QKV_HALF), BF),
+            pltpu.VMEM(grid + (32, D), BF),
             pltpu.VMEM(grid + up.shape, BF),
-            pltpu.VMEM(down.shape, BF),
-            pltpu.VMEM((2, count, QKV_HALF), BF),
+            pltpu.VMEM(grid + down.shape, BF),
             pltpu.VMEM((count, D), BF),
-            pltpu.VMEM((D, count), BF),
-            pltpu.VMEM((D, count), BF),
+            pltpu.VMEM((3, count, D), BF),
+            pltpu.VMEM((count, D), BF),
             pltpu.VMEM((D, count), BF),
             pltpu.VMEM((count, D), BF),
             pltpu.VMEM((count, D), F32),
-            pltpu.VMEM((2, count, UP_CHUNK), BF),
+            pltpu.VMEM((count, FF), BF),
             pltpu.VMEM((2, count, UP_CHUNK), BF),
             pltpu.VMEM((2, UP_CHUNK, count), BF),
             pltpu.VMEM((2, LEN, LEN), F32),
             pltpu.VMEM((2, LEN, 128), F32),
             pltpu.VMEM((2, 1, QKV_HALF), F32),
+            pltpu.VMEM((count, D), F32),
             pltpu.SemaphoreType.DMA((slots,)),
             pltpu.SemaphoreType.DMA((slots,)),
-            pltpu.SemaphoreType.DMA((24,)),
+            pltpu.SemaphoreType.DMA((30,)),
         ],
         compiler_params=pltpu.CompilerParams(
-            collective_id=0, has_side_effects=True, vmem_limit_bytes=60 << 20),
+            collective_id=0, has_side_effects=True, vmem_limit_bytes=61 << 20),
         name="forward_gather",
-    )(*weights, *vectors, tokens, lengths)
-
-
-def finish_kernel(*refs):
-    refs = list(refs)
-    take = lambda number: [refs.pop(0) for _ in range(number)]
-    lengths, norm, scale_one, w_out = take(4)
-    (down_any, up_any, act_any, slope_any, normed_any, context_any, cotangent_any) = take(7)
-    pooled, delta, norm_sums, ffn_sums = take(4)
-    (layer_any, branch_any, inner_any, attended_any, grad_context_any, one_any) = take(6)
-    (w_down, w_up, act, slope, normed_one, context, cotangent, layer_out, grad_branch,
-     grad_attended, grad_context, hidden) = take(12)
-    loads, stores = refs
-    core = lax.axis_index("mp")
-    started = []
-
-    def load(source, target):
-        copy = pltpu.make_async_copy(source, target, loads.at[len(started)])
-        copy.start()
-        started.append(copy)
-        return copy
-
-    halves = [pl.ds(row * LEN, LEN) for row in range(2)]
-    pair = lambda source, target: [load(source.at[rows], target.at[rows]) for rows in halves]
-    down_loaded = load(down_any, w_down)
-    act_loaded, normed_loaded = [], []
-    for rows in halves:
-        act_loaded.append(load(act_any.at[rows], act.at[rows]))
-        normed_loaded.append(load(normed_any.at[rows], normed_one.at[rows]))
-    cotangent_loaded = pair(cotangent_any, cotangent)
-    slope_loaded = pair(slope_any, slope)
-    up_loaded = load(up_any, w_up)
-    context_loaded = pair(context_any, context)
-    norm_sums[...] = jnp.zeros(norm_sums.shape, F32)
-    ffn_sums[...] = jnp.zeros(ffn_sums.shape, F32)
-    kept = []
-
-    def keep(source, target):
-        copy = pltpu.make_async_copy(source, target, stores.at[len(kept)])
-        copy.start()
-        kept.append(copy)
-
-    down_loaded.wait()
-    for row, rows in enumerate(halves):
-        act_loaded[row].wait()
-        normed_loaded[row].wait()
-        hidden[...] = normed_one[rows, :] * norm[2:3, :] + norm[3:4, :]
-        branch = dot(act[rows, :], w_down[...])
-        normed, scale = norm_parts(hidden[...] + branch + norm[1:2, :])
-        output = normed * norm[4:5, :] + norm[5:6, :]
-        high = output.astype(BF)
-        layer_out[rows, :] = high
-        keep(layer_out.at[rows], layer_any.at[rows])
-        low = (output - high.astype(F32)).astype(BF)
-        place = lax.broadcasted_iota(jnp.int32, (SEGS, LEN), 1)
-        segment = lax.broadcasted_iota(jnp.int32, (SEGS, 1), 0)
-        ids = ids_at(lengths, core * 2 + row, place)
-        member = (ids == segment).astype(F32)
-        sizes = jnp.sum(member, axis=1, keepdims=True)
-        member = member.astype(BF)
-        pooled[row] = (dot(member, high) + dot(member, low)) / sizes
-        cotangent_loaded[row].wait()
-        back, gain, shift = norm_back(cotangent[rows, :].astype(F32), normed, scale, norm[4:5, :])
-        norm_sums[4:5, :] += gain
-        norm_sums[5:6, :] += shift
-        hidden[...] = back
-        back = back.astype(BF)
-        grad_branch[rows, :] = back
-        keep(grad_branch.at[rows], branch_any.at[rows])
-        norm_sums[1:2, :] += jnp.sum(back.astype(F32), axis=0, keepdims=True)
-        slope_loaded[row].wait()
-        for start in range(0, FF, FF // 4):
-            cols = slice(start, start + FF // 4)
-            value = dot_last(grad_branch[rows, :], w_down[cols, :])
-            value = (value * slope[rows, cols].astype(F32)).astype(BF)
-            slope[rows, cols] = value
-            ffn_sums[:, cols] += jnp.sum(value.astype(F32), axis=0, keepdims=True)
-        keep(slope.at[rows], inner_any.at[rows])
-        if row == 0:
-            up_loaded.wait()
-        for half in range(2):
-            cols = slice(half * FF // 2, (half + 1) * FF // 2)
-            hidden[...] += dot_last(slope[rows, cols], w_up[half])
-        normed = normed_one[rows, :]
-        scale = scale_one[rows, 0:1]
-        back, gain, shift = norm_back(hidden[...], normed, scale, norm[2:3, :])
-        norm_sums[2:3, :] += gain
-        norm_sums[3:4, :] += shift
-        normed_one[rows, :] = back
-        keep(normed_one.at[rows], one_any.at[rows])
-        back = back.astype(BF)
-        grad_attended[rows, :] = back
-        keep(grad_attended.at[rows], attended_any.at[rows])
-        norm_sums[0:1, :] += jnp.sum(back.astype(F32), axis=0, keepdims=True)
-        back = dot_last(back, w_out[...]).astype(BF)
-        grad_context[rows, :] = back
-        keep(grad_context.at[rows], grad_context_any.at[rows])
-        context_loaded[row].wait()
-        product = back.astype(F32) * context[rows, :].astype(F32)
-        high = product.astype(BF)
-        low = (product - high.astype(F32)).astype(BF)
-        head = lax.broadcasted_iota(jnp.int32, (16, D), 0)
-        member = (lax.broadcasted_iota(jnp.int32, (16, D), 1) // HD == head).astype(F32).astype(BF)
-        delta[row] = dot_last(member, high) + dot_last(member, low)
-    for copy in kept:
-        copy.wait()
-
-
-def finish_forward(lengths, norm, scale_one, w_out, w_down, w_up, act, slope, normed, context,
-                   cotangent):
-    count = act.shape[0]
-    shape = jax.ShapeDtypeStruct
-    outs = [
-        shape((count // LEN, SEGS, D), F32), shape((count // LEN, 16, LEN), F32),
-        shape((8, D), F32), shape((1, FF), F32),
-    ]
-    large = [
-        shape((count, D), BF), shape((count, D), BF), shape((count, FF), BF),
-        shape((count, D), BF), shape((count, D), BF), shape((count, D), F32),
-    ]
-    some = pl.BlockSpec(memory_space=pl.ANY)
-    return pl.pallas_call(
-        finish_kernel,
-        out_shape=outs + large,
-        in_specs=[SMEM] + [VMEM] * 3 + [some] * 7,
-        out_specs=[VMEM] * 4 + [some] * 6,
-        scratch_shapes=[
-            pltpu.VMEM((FF, D), BF),
-            pltpu.VMEM((2, D, FF // 2), BF),
-            pltpu.VMEM((count, FF), BF),
-            pltpu.VMEM((count, FF), BF),
-            pltpu.VMEM((count, D), F32),
-            pltpu.VMEM((count, D), BF),
-            pltpu.VMEM((count, D), BF),
-            pltpu.VMEM((count, D), BF),
-            pltpu.VMEM((count, D), BF),
-            pltpu.VMEM((count, D), BF),
-            pltpu.VMEM((count, D), BF),
-            pltpu.VMEM((LEN, D), F32),
-            pltpu.SemaphoreType.DMA((16,)),
-            pltpu.SemaphoreType.DMA((16,)),
-        ],
-        compiler_params=pltpu.CompilerParams(vmem_limit_bytes=60 << 20),
-        name="finish_forward",
-    )(lengths, norm, scale_one, w_out, w_down, w_up, act, slope, normed, context, cotangent)
+    )(*weights, *vectors, lengths, tokens, cotangent)
 
 
 class Collect:
@@ -1235,7 +1165,7 @@
 def attend_back_pair(qkv, grad_context, lse, delta, bias, grad_head, core, row, pair):
     lane = lax.broadcasted_iota(jnp.int32, (LEN, 128), 1)
     item = core * 3 + pair
-    queries, keys, values = (slab(qkv, core, row, part, pair) for part in range(3))
+    queries, keys, values = (trio(qkv, core, row, part, pair) for part in range(3))
     rows = pl.ds(pl.multiple_of(row * LEN, LEN), LEN)
     wide = pl.ds(pl.multiple_of(item * 128, 128), 128)
     grad = grad_context[rows, wide]
@@ -1254,7 +1184,7 @@
     grad_k = jnp.where(lane < HD, grads_k[0], grads_k[1]).astype(BF)
     grad_v = jnp.where(lane < HD, grads_v[0], grads_v[1]).astype(BF)
     for part, value in enumerate((grad_q, grad_k, grad_v)):
-        qkv[core, rows, pl.ds(pl.multiple_of(pair * PAIR + part * 128, 128), 128)] = value
+        qkv[pair, rows, place_of(core, part, 128)] = value
     grad_head[0:1, wide] += jnp.sum(grad_q.astype(F32), axis=0, keepdims=True)
     grad_head[1:2, wide] += jnp.sum(grad_v.astype(F32), axis=0, keepdims=True)
 
@@ -1262,16 +1192,17 @@
 def backward_scatter_kernel(*refs):
     refs = list(refs)
     take = lambda number: [refs.pop(0) for _ in range(number)]
-    lengths, lse, delta, norm_sums, ffn_sums = take(5)
+    lengths, lse, norm_given, norm, scale_one, w_out = take(6)
     rows_old, cols_old = take(4), take(4)
     head_sq, ffn_sq, norm_sq, weight_sums = take(4)
-    (act_any, inner_any, branch_any, hidden_any, context_any, attended_any, token_any, qkv_any,
-     grad_context_any, weight_any, one_any) = take(11)
+    (act_any, branch_any, down_any, slope_any, up_any, two_any, normed_any, hidden_any, context_any,
+     flip_any, token_any, qkv_any, weight_any) = take(13)
     results = take(5)
     lines, totals, input_any = take(3)
     held, other = take(5), take(5)
     slots = [take(3) for _ in range(5)]
-    (wide, flip, flip_context, attended, qkv, weight, one, act, inner, bias, grad_head) = take(11)
+    (wide, flip, flip_context, context, attended, qkv, weight, one, two, act, inner, bias, delta,
+     grad_head, norm_sums, ffn_sums) = take(16)
     mine_one, land_one, mine_two, land_two, old_small = take(5)
     send, recv, local = refs
     place = Place()
@@ -1286,7 +1217,7 @@
         loaded[name] = copy
 
     tile_rows = FF // 2 // 4
-    act_slots, inner_slots = 12, 14
+    act_slots, chunk_slots = 16, 18
 
     def act_load(index):
         core = jnp.where(index < 4, theirs, mine)
@@ -1294,24 +1225,38 @@
         return pltpu.make_async_copy(
             act_any.at[pl.ds(start, tile_rows)], act.at[index % 2], local.at[act_slots + index % 2])
 
-    def inner_load(index):
+    def down_tile(index):
+        return qkv.at[0, pl.ds(pl.multiple_of(index % 2 * UP_CHUNK, UP_CHUNK), UP_CHUNK)]
+
+    def slope_tile(index):
+        return qkv.at[1 + index % 2, :, pl.ds(0, UP_CHUNK)]
+
+    def up_tile(index):
+        return weight.at[index % 2, :, pl.ds(0, UP_CHUNK)]
+
+    def chunk_loads(index):
         core = jnp.where(index < 3, theirs, mine)
-        start = pl.multiple_of(core * (FF // 2) + (index % 3) * UP_CHUNK, UP_CHUNK)
-        return pltpu.make_async_copy(
-            inner_any.at[:, pl.ds(start, UP_CHUNK)], inner.at[index % 2],
-            local.at[inner_slots + index % 2])
+        inside = pl.ds(pl.multiple_of(index % 3 * UP_CHUNK, UP_CHUNK), UP_CHUNK)
+        whole = pl.ds(
+            pl.multiple_of(core * (FF // 2) + index % 3 * UP_CHUNK, UP_CHUNK), UP_CHUNK)
+        slot = chunk_slots + 3 * (index % 2)
+        return [
+            pltpu.make_async_copy(down_any.at[whole], down_tile(index), local.at[slot]),
+            pltpu.make_async_copy(slope_any.at[:, whole], slope_tile(index), local.at[slot + 1]),
+            pltpu.make_async_copy(up_any.at[core, :, inside], up_tile(index), local.at[slot + 2]),
+        ]
 
     load("branch", branch_any, wide)
     for index in range(2):
         act_load(index).start()
     load("hidden", hidden_any, flip)
+    load("two", two_any, two)
     for index in range(2):
-        inner_load(index).start()
-    load("attended", attended_any, attended)
-    load("context", context_any, flip_context)
-    load("qkv", qkv_any, qkv)
-    load("weight", weight_any, weight)
-    load("one", one_any, one)
+        for copy in chunk_loads(index):
+            copy.start()
+    load("normed", normed_any, one)
+    load("context", context_any, context)
+    load("flip", flip_any, flip_context)
 
     small, qkv_held, out_held, up_held, down_held = held
     small_other, qkv_other, out_other, up_other, down_other = other
@@ -1348,6 +1293,7 @@
     groups[-1] += chunks[0]
 
     greet(place)
+    norm_sums[...] = norm_given[...]
     loaded["branch"].wait()
 
     @pl.loop(0, 4)
@@ -1369,36 +1315,74 @@
         def _():
             act_load(layer + 6).start()
 
-    load("grad_context", grad_context_any, wide)
     collect_tick(groups, 0)
     loaded["hidden"].wait()
+    loaded["two"].wait()
+
+    def feed_back(index):
+        for copy in chunk_loads(index):
+            copy.wait()
+        core = jnp.where(index < 3, theirs, mine)
+        whole = pl.ds(
+            pl.multiple_of(core * (FF // 2) + index % 3 * UP_CHUNK, UP_CHUNK), UP_CHUNK)
+        value = dot_last(wide[...], down_tile(index)[...])
+        value = (value * slope_tile(index)[...].astype(F32)).astype(BF)
+        inner[...] = value
+        ffn_sums[:, whole] = jnp.sum(value.astype(F32), axis=0, keepdims=True)
+        two[...] += dot_last(inner[...], up_tile(index)[...])
+        return dot(flip[...], inner[...]).reshape(4, 2, 2, D // 16, UP_CHUNK)
 
     @pl.loop(0, 3)
     def _(third):
-        inner_load(third).wait()
         cols = pl.ds(pl.multiple_of(third * UP_CHUNK, UP_CHUNK), UP_CHUNK)
-        value = dot(flip[...], inner[third % 2])
-        up_held[:, :, :, :, cols] = value.reshape(4, 2, 2, D // 16, UP_CHUNK).astype(BF)
+        up_held[:, :, :, :, cols] = feed_back(third).astype(BF)
         up_swap(third).start()
-        inner_load(third + 2).start()
+        for copy in chunk_loads(third + 2):
+            copy.start()
+
+        @pl.when(third == 1)
+        def _():
+            collect_tick(groups, 1)
 
     @pl.loop(0, 3)
     def _(third):
-        inner_load(third + 3).wait()
         at = (EVERY, EVERY, EVERY, EVERY,
               pl.ds(pl.multiple_of(third * UP_CHUNK, UP_CHUNK), UP_CHUNK))
-        value = dot(flip[...], inner[(third + 3) % 2]).reshape(4, 2, 2, D // 16, UP_CHUNK)
+        value = feed_back(third + 3)
         up_swap(third).wait()
         up_held[at] = (value + up_other[at].astype(F32)).astype(BF)
 
         @pl.when(third == 0)
         def _():
-            inner_load(5).start()
-            collect_tick(groups, 1)
+            for copy in chunk_loads(5):
+                copy.start()
+            collect_tick(groups, 2)
 
     load("token", token_any, flip)
-    loaded["attended"].wait()
+    load("qkv", qkv_any, qkv)
+    load("weight", weight_any, weight)
+    loaded["normed"].wait()
     loaded["context"].wait()
+    collect_tick(groups, 3)
+    for row in range(2):
+        rows = slice(row * LEN, (row + 1) * LEN)
+        back, gain, shift = norm_back(
+            two[rows, :], one[rows, :], scale_one[rows, 0:1], norm[2:3, :])
+        norm_sums[2:3, :] += gain
+        norm_sums[3:4, :] += shift
+        one[rows, :] = back
+        back = back.astype(BF)
+        attended[rows, :] = back
+        norm_sums[0:1, :] += jnp.sum(back.astype(F32), axis=0, keepdims=True)
+        back = dot_last(back, w_out[...]).astype(BF)
+        wide[rows, :] = back
+        product = back.astype(F32) * context[rows, :].astype(F32)
+        high = product.astype(BF)
+        low = (product - high.astype(F32)).astype(BF)
+        head = lax.broadcasted_iota(jnp.int32, (16, D), 0)
+        member = (lax.broadcasted_iota(jnp.int32, (16, D), 1) // HD == head).astype(F32).astype(BF)
+        delta[row] = dot_last(member, high) + dot_last(member, low)
+    loaded["flip"].wait()
     spare = out_held.shape[3] - D // 32
 
     def out_half(core):
@@ -1412,23 +1396,23 @@
     value = out_half(mine)
     out_swap.wait()
     out_held[...] = (value + out_other[...].astype(F32)).astype(BF)
-    collect_tick(groups, 2)
+    collect_tick(groups, 4)
     for row in range(2):
         set_bias(bias.at[row], lengths, place.m * 2 + row)
     grad_head[...] = jnp.zeros(grad_head.shape, F32)
-    for name in ("qkv", "grad_context", "token"):
+    for name in ("qkv", "token"):
         loaded[name].wait()
 
     def qkv_theirs(pair):
         cols = pl.ds(pl.multiple_of(pair * PAIR, PAIR), PAIR)
-        value = dot(flip[...], qkv[theirs, :, cols])
+        value = dot(flip[...], qkv[pair, :, place_of(theirs, 0, PAIR)])
         qkv_held[:, :, :, :, cols] = value.reshape(4, 2, 2, D // 16, PAIR).astype(BF)
         qkv_swap(pair).start()
 
     def qkv_mine(pair):
         cols = pl.ds(pl.multiple_of(pair * PAIR, PAIR), PAIR)
         at = (EVERY, EVERY, EVERY, EVERY, cols)
-        value = dot(flip[...], qkv[mine, :, cols]).reshape(4, 2, 2, D // 16, PAIR)
+        value = dot(flip[...], qkv[pair, :, place_of(mine, 0, PAIR)]).reshape(4, 2, 2, D // 16, PAIR)
         qkv_swap(pair).wait()
         qkv_held[at] = (value + qkv_other[at].astype(F32)).astype(BF)
 
@@ -1444,10 +1428,10 @@
         def _():
             qkv_mine(pair - 1)
 
-        for number, at in enumerate((1, 3, 5, 7, 9, 11)):
+        for number, at in enumerate((1, 4, 7, 10)):
             @pl.when(item == at)
             def _():
-                collect_tick(groups, 3 + number)
+                collect_tick(groups, 5 + number)
 
         attend_back_pair(qkv, wide, lse, delta, bias, grad_head, core, row, pair)
 
@@ -1455,11 +1439,11 @@
     pack_small(small, theirs, norm_sums, grad_head, ffn_sums)
     small_swap.start()
     loaded["weight"].wait()
-    loaded["one"].wait()
 
     def input_rows(row):
         rows = pl.ds(pl.multiple_of(row * LEN, LEN), LEN)
-        one[rows, :] += dot_last(qkv[0, rows, :], weight[0]) + dot_last(qkv[1, rows, :], weight[1])
+        one[rows, :] += (dot_last(qkv[0, rows, :], weight[0]) + dot_last(qkv[1, rows, :], weight[1])
+                         + dot_last(qkv[2, rows, :], weight[2]))
 
     qkv_mine(2)
     small_swap.wait()
@@ -1469,7 +1453,7 @@
     input_rows(0)
     collect_tick(groups, 10)
     input_rows(1)
-    input_done = pltpu.make_async_copy(one, input_any, local.at[16])
+    input_done = pltpu.make_async_copy(one, input_any, local.at[12])
     input_done.start()
     collect_tick(groups, 11)
     collect_tick(groups, 12)
@@ -1500,7 +1484,7 @@
         ratios.append(jnp.sum(scaled / rows_new[index], axis=0, keepdims=True))
         share = 0.5 if index in (0, 2) else 1.0
         row_totals.append(jnp.sum(rows_new[index], axis=0, keepdims=True) * share)
-    place_small(old_small, norm_sq[...], head_sq[...], ffn_sq[...], 1.0)
+    place_small(old_small, norm_sq[...], head_sq[...], as_row(ffn_sq), 1.0)
     _, update = small_update(small_sum[...], old_small[...])
     second = Exchange(place, mine_two, land_two, sems, base + 16)
     totals[...] = add_up(
@@ -1513,9 +1497,9 @@
     second.finish()
 
 
-def backward_scatter(lengths, lse, delta, norm_sums, ffn_sums, rows_old, cols_old, squares,
+def backward_scatter(lengths, lse, norm_sums, norm, scale_one, w_out, rows_old, cols_old, squares,
                      weight_sums, large, rows, widths):
-    count = large[2].shape[0]
+    count = scale_one.shape[0]
     shape = jax.ShapeDtypeStruct
     some = pl.BlockSpec(memory_space=pl.ANY)
     kinds = [F32, BF, BF, BF, BF]
@@ -1527,7 +1511,7 @@
     sems = 12 + 11 * Collect.COUNT + 32
     outs = [shape((r, w), F32) for r, w in zip(rows, widths)]
     outs += [shape((LINES, 128), F32), shape((8, 128), F32), shape((count, D), F32)]
-    small = [lse, delta, norm_sums, ffn_sums, *rows_old, *cols_old, *squares, weight_sums]
+    small = [lse, norm_sums, norm, scale_one, w_out, *rows_old, *cols_old, *squares, weight_sums]
     return pl.pallas_call(
         backward_scatter_kernel,
         out_shape=outs,
@@ -1538,13 +1522,18 @@
             pltpu.VMEM((D, count), BF),
             pltpu.VMEM((D, count), BF),
             pltpu.VMEM((count, D), BF),
-            pltpu.VMEM((2, count, QKV_HALF), BF),
-            pltpu.VMEM((2, D, QKV_HALF), BF),
+            pltpu.VMEM((count, D), BF),
+            pltpu.VMEM((3, count, D), BF),
+            pltpu.VMEM((3, D, D), BF),
+            pltpu.VMEM((count, D), F32),
             pltpu.VMEM((count, D), F32),
             pltpu.VMEM((2, FF // 8, count), BF),
-            pltpu.VMEM((2, count, UP_CHUNK), BF),
+            pltpu.VMEM((count, UP_CHUNK), BF),
             pltpu.VMEM((2, LEN, LEN), F32),
+            pltpu.VMEM((2, 16, LEN), F32),
             pltpu.VMEM((8, D), F32),
+            pltpu.VMEM((8, D), F32),
+            pltpu.VMEM((1, FF), F32),
             pltpu.VMEM((4, LINES, 128), F32),
             pltpu.VMEM((4, 4, LINES, 128), F32),
             pltpu.VMEM((4, 8, 128), F32),
@@ -1552,7 +1541,7 @@
             pltpu.VMEM((16, 128), F32),
             pltpu.SemaphoreType.DMA((sems,)),
             pltpu.SemaphoreType.DMA((sems,)),
-            pltpu.SemaphoreType.DMA((18,)),
+            pltpu.SemaphoreType.DMA((24,)),
         ],
         compiler_params=pltpu.CompilerParams(
             collective_id=1, has_side_effects=True, vmem_limit_bytes=62 << 20),
@@ -1597,40 +1586,33 @@
     data = lax.axis_size("dp")
     rows_qkv = w_qkv.shape[0]
     fast = data == 16 and cores == 2
-    weights = [w_qkv, w_out, w_up, w_down]
-    vectors = [head_bias, ffn_bias.reshape(1, -1), norm_bias]
+    weights = [w_qkv.transpose(1, 0, 2) if fast else w_qkv, w_out, w_up, w_down]
+    vectors = [head_bias, ffn_bias if fast else ffn_bias.reshape(1, -1), norm_bias]
     rows_out = w_out.shape[0]
     if fast:
-        (weight_sums, norm_full, ffn_full, lse, scale_one, out_full, qkv_full, up_full, down_full,
-         qkv, context_flip, token_flip, hidden_flip, normed_one, context, act, act_flip, slope
-         ) = forward_gather(weights, vectors, tokens, seg_lengths)
-        qkv_full = qkv_full.reshape(2, D, QKV_HALF)
-        up_full = up_full.reshape(2, D, FF // 2)
-        down_full = down_full.reshape(FF, D)
-        (pooled, delta, norm_sums, ffn_sums, layer_out, grad_branch, grad_inner, grad_attended,
-         grad_context, grad_one) = finish_forward(
-            seg_lengths, norm_full, scale_one, out_full, down_full, up_full, act, slope,
-            normed_one, context, cotangent)
-        rows_old = [v.reshape(1, -1) for v in (qkv_rows, out_rows, up_rows, down_rows)]
-        cols_old = [qkv_cols] + [v.reshape(1, -1) for v in (out_cols, up_cols, down_cols)]
-        old = [head_bias_sq, ffn_bias_sq.reshape(1, -1), norm_sq]
+        (weight_sums, norm_full, ffn_full, lse, scale_one, out_full, pooled, norm_sums, qkv_full,
+         up_full, down_full, qkv, context_flip, token_flip, hidden_flip, normed_one, context,
+         act_flip, slope, layer_out, grad_branch, grad_two
+         ) = forward_gather(weights, vectors, seg_lengths, tokens, cotangent)
+        rows_old = [qkv_rows, out_rows, up_rows, down_rows]
+        cols_old = [qkv_cols, out_cols, up_cols, down_cols]
+        old = [head_bias_sq, ffn_bias_sq, norm_sq]
         *reduced, lines, totals, input_grad = backward_scatter(
-            seg_lengths, lse, delta, norm_sums, ffn_sums, rows_old, cols_old, old, weight_sums,
-            [act_flip, grad_inner, grad_branch, hidden_flip, context_flip, grad_attended,
-             token_flip, qkv, grad_context, qkv_full, grad_one],
+            seg_lengths, lse, norm_sums, norm_full, scale_one, out_full, rows_old, cols_old, old,
+            weight_sums,
+            [act_flip, grad_branch, down_full.reshape(FF, D), slope,
+             up_full.reshape(2, D, FF // 2), grad_two, normed_one, hidden_flip, context,
+             context_flip, token_flip, qkv, qkv_full.reshape(3, D, D)],
             [16, rows_qkv, rows_out, rows_qkv, w_down.shape[0]],
             [128, QKV_HALF, D, w_up.shape[1], D])
-        new = step(reduced, lines, totals, weights, rows_old, cols_old, vectors, old)
-        grads, (g_head, g_ffn, g_norm) = new[:4], new[4:7]
-        rows_new, cols_new = [r.reshape(-1) for r in new[7:11]], new[11:15]
-        cols_new = [cols_new[0]] + [c.reshape(-1) for c in cols_new[1:]]
-        (s_head, s_ffn, s_norm), mats = new[15:18], new[18:22]
-        n_head, n_ffn, n_norm = new[22:25]
+        new = step(reduced, lines, totals, weights, rows_old, cols_old, vectors, old,
+                   [layer_out, pooled, input_grad])
+        new = list(new)
+        grads, small_grads, rows_new, cols_new = new[:4], new[4:7], new[7:11], new[11:15]
+        seconds, mats, fresh, passed = new[15:18], new[18:22], new[22:25], new[25:]
+        grads[0], mats[0] = grads[0].transpose(1, 0, 2), mats[0].transpose(1, 0, 2)
         stats = [v for pair in zip(rows_new, cols_new) for v in pair]
-        return (
-            layer_out, pooled, input_grad, *grads, g_head, g_ffn.reshape(-1), g_norm, *stats,
-            s_head, s_ffn.reshape(-1), s_norm, *mats, n_head, n_ffn.reshape(-1), n_norm,
-        )
+        return (*passed, *grads, *small_grads, *stats, *seconds, *mats, *fresh)
     small, qkv_g, out_g, up_g, down_g = gather_plain(weights, vectors)
     small = small.astype(BF).astype(F32)
     own_head, own_ffn, own_norm = head_bias.shape[1], ffn_bias.shape[0], norm_bias.shape[1]

time: 266 us -> 231 us (0.87)
  Pallas kernels: 245 us -> 227 us
  local copies, waits for them, and re-layouts: 14.6 us -> 0 us
    pallas_call x2 -> x1, Pallas kernels: 36.2 us -> 6.94 us  [step(): pl.pallas_call(step_kernel, out_shape=outs + [jax.ShapeDtypeStruct(v.shap...]
    unnamed x60 -> x0, local copies, waits for them, and re-layouts: 12.9 us -> none
    pallas_call x1, Pallas kernels: 89 us -> 95.4 us  [forward_gather(): pl.pallas_call(forward_gather_kernel, out_shape=small_outs + large_outs,...]
    pallas_call x1, Pallas kernels: 120 us -> 124 us  [backward_scatter(): pl.pallas_call(backward_scatter_kernel, out_shape=outs, in_specs=[SMEM] +...]
where the time goes in v6:
time: 231 us; the launch traced here: 228 us
  Pallas kernels  227 us (98%)
    pallas_call x1, Pallas kernels, backward_scatter(): pl.pallas_call(backward_scatter_kernel, out_shape=outs, in_specs=[SMEM] +...  124 us
    pallas_call x1, Pallas kernels, forward_gather(): pl.pallas_call(forward_gather_kernel, out_shape=small_outs + large_outs,...  95.4 us
    pallas_call x1, Pallas kernels, step(): pl.pallas_call(step_kernel, out_shape=outs + [jax.ShapeDtypeStruct(v.shap...  6.94 us

profile of v6, /device:TPU:0, one launch (start us, length us, event | category | flops | bytes accessed | tf_op | source)
XLA Modules:
  0.0 227.7 jit_solution(1965801615839397819)
XLA Ops:
  0.7 95.4 %forward_gather.1 = (f32[8,128]{1,0:T(8,128)}, f32[8,768]{1,0:T(8,128)}, f32[1,3072]{1,0:T(1,128)}, f32[2,16,512]{2,1,0:T(8,128)}, f32[1024,128]{1,0:T(8,128)}, ...) custom-call(f32[3,48,384]{2,1,0:T(8,128)} %bitcast.9, ...), custom_call_target="tpu_custom_call" | custom-call | tf_op jit(solution)/shard_map/forward_gather/pallas_call | solution.py:1023
  96.1 124.4 %backward_scatter.1 = (f32[16,128]{1,0:T(8,128)}, f32[48,1152]{1,0:T(8,128)}, f32[24,768]{1,0:T(8,128)}, f32[48,1536]{1,0:T(8,128)}, f32[96,768]{1,0:T(8,128)}, ...) custom-call(s32[4,8]{1,0:T(4,128)} %refs_0_.1, f32[2,16,512]{2,1,0:T(8,128)} %get-tuple-element.85.refs_1_, ...), custom_call_target="tpu_custom_call" | custom-call | tf_op jit(solution)/shard_map/backward_scatter/pallas_call | solution.py:1515
  220.5 6.9 %adafactor_step.1 = (f32[3,48,384]{2,1,0:T(8,128)}, f32[24,768]{1,0:T(8,128)}, f32[48,1536]{1,0:T(8,128)}, f32[96,768]{1,0:T(8,128)}, f32[2,24]{1,0:T(2,128)}, /...) custom-call(f32[48,1152]{1,0:T(8,128)} %get-tuple-element.104.refs_0, ...), custom_call_target="tpu_custom_call" | custom-call | tf_op jit(solution)/shard_map/adafactor_step/pallas_call | solution.py:307

commit v7 on v6

--- a/solution.py
+++ b/solution.py
@@ -25,6 +25,9 @@
 EVERY = slice(None)
 
 
+PLANE = [(m, y, x) for m in range(2) for y in range(2) for x in range(2)][1:]
+
+
 class Place:
     def __init__(self):
         d = lax.axis_index("dp")
@@ -37,6 +40,10 @@
         spot[axis] = (spot[axis] + step) % size
         return spot
 
+    def across(self, steps):
+        m, y, x = steps
+        return {"z": self.z, "m": (self.m + m) % 2, "y": (self.y + y) % 2, "x": (self.x + x) % 2}
+
     @staticmethod
     def device(spot):
         return (spot["z"] * 4 + spot["y"] * 2 + spot["x"], spot["m"])
@@ -46,16 +53,22 @@
     return (1, 2, 3) if axis == "z" else (1,)
 
 
-def greet(place):
+def near(place, wide):
+    spots = [place.at("z", step) for step in (1, 2, 3)]
+    for steps in PLANE:
+        if wide or sum(steps) == 1:
+            spots.append(place.across(steps))
+    return [place.device(spot) for spot in spots]
+
+
+def greet(place, wide=False):
     barrier = pltpu.get_barrier_semaphore()
-    count = 0
-    for axis in "zyxm":
-        for step in steps_of(axis):
-            pl.semaphore_signal(
-                barrier, inc=1, device_id=place.device(place.at(axis, step)), device_id_type=MESH
-            )
-            count += 1
-    pl.semaphore_wait(barrier, count)
+    for device in near(place, wide):
+        pl.semaphore_signal(barrier, inc=1, device_id=device, device_id_type=MESH)
+
+
+def meet(place, wide=False):
+    pl.semaphore_wait(pltpu.get_barrier_semaphore(), len(near(place, wide)))
 
 
 def weight_sums_of(weights, small):
@@ -111,53 +124,76 @@
 
 
 class Exchange:
-    def __init__(self, place, mine, land, sems, base):
-        self.place, self.mine, self.land = place, mine, land
+    COUNT = 10
+
+    def __init__(self, place, mine, plane, line, sems, base):
+        self.place, self.mine, self.plane, self.line = place, mine, plane, line
         self.sems, self.base = sems, base
-        self.sent = []
-
-    def swap(self, stage, axis):
+
+    def plane_copies(self):
         place = self.place
         send, recv = self.sems
-        own = place.z if axis == "z" else 0
-        for step in steps_of(axis):
-            slot = self.base + 4 * stage + step
-            copy = pltpu.make_async_remote_copy(
-                self.mine.at[stage], self.land.at[stage, own], send.at[slot], recv.at[slot],
-                device_id=place.device(place.at(axis, step)), device_id_type=MESH)
-            copy.start()
-            self.sent.append(copy)
-        if axis == "z":
-            self.land[stage, place.z] = self.mine[stage]
-        for step in steps_of(axis):
-            slot = self.base + 4 * stage + step
-            spot = (place.z - step) % 4 if axis == "z" else 0
-            pltpu.make_async_remote_copy(
-                self.mine.at[stage], self.land.at[stage, spot], send.at[slot], recv.at[slot],
-                device_id=place.device(place.at(axis, step)), device_id_type=MESH).wait_recv()
-        if axis == "z":
-            land = self.land
-            return (land[stage, 0] + land[stage, 1]) + (land[stage, 2] + land[stage, 3])
-        return self.mine[stage] + self.land[stage, 0]
+        out = []
+        for number, steps in enumerate(PLANE):
+            spot = place.across(steps)
+            slot = self.base + number
+            device = place.device(spot)
+            sent, arrives = (
+                pltpu.make_async_remote_copy(
+                    self.mine.at[0], self.plane.at[at["m"], at["y"], at["x"]],
+                    send.at[slot], recv.at[slot], device_id=device, device_id_type=MESH)
+                for at in ({"m": place.m, "y": place.y, "x": place.x}, spot))
+            out.append((sent, arrives))
+        return out
+
+    def line_copies(self):
+        place = self.place
+        send, recv = self.sems
+        out = []
+        for step in (1, 2, 3):
+            slot = self.base + 6 + step
+            device = place.device(place.at("z", step))
+            sent, arrives = (
+                pltpu.make_async_remote_copy(
+                    self.mine.at[1], self.line.at[layer], send.at[slot], recv.at[slot],
+                    device_id=device, device_id_type=MESH)
+                for layer in (place.z, place.at("z", -step)["z"]))
+            out.append((sent, arrives))
+        return out
+
+    def start_plane(self, value):
+        place = self.place
+        self.mine[0] = value
+        for sent, _ in self.plane_copies():
+            sent.start()
+        self.plane[place.m, place.y, place.x] = value
+
+    def end_plane(self):
+        plane, core = self.plane, self.place.m
+        for _, arrives in self.plane_copies():
+            arrives.wait_recv()
+        return [(plane[c, 0, 0] + plane[c, 0, 1]) + (plane[c, 1, 0] + plane[c, 1, 1])
+                for c in (core, 1 - core)]
+
+    def start_line(self, value):
+        self.mine[1] = value
+        for sent, _ in self.line_copies():
+            sent.start()
+        self.line[self.place.z] = value
+
+    def end_line(self):
+        line = self.line
+        for _, arrives in self.line_copies():
+            arrives.wait_recv()
+        return (line[0] + line[1]) + (line[2] + line[3])
 
     def finish(self):
-        for copy in self.sent:
-            copy.wait_send()
-
-
-def add_up(exchange, value, picked=None):
-    exchange.mine[0] = value
-    total = exchange.swap(0, "m")
-    if picked is not None:
-        total = jnp.where(picked, total, value)
-    for stage, axis in ((1, "x"), (2, "y"), (3, "z")):
-        exchange.mine[stage] = total
-        total = exchange.swap(stage, axis)
-    return total
-
-
-QKV_LINE, UP_LINE, OUT_LINE, DOWN_LINE, ROW_LINE = 0, 9, 21, 27, 33
-LINES = 40
+        for sent, _ in self.plane_copies() + self.line_copies():
+            sent.wait_send()
+
+
+QKV_LINE, QKV_ROWS, UP_LINE, OUT_LINE, DOWN_LINE, UP_ROWS = 0, 9, 16, 28, 34, 40
+LATE, LINES = 16, 48
 WIDTHS = (3 * D // 2, D, FF // 2, D)
 COL_LINES = (QKV_LINE, OUT_LINE, UP_LINE, DOWN_LINE)
 COL_COUNT = (3 * D, D, FF, D)
@@ -174,11 +210,11 @@
     return out
 
 
-def new_rows_cols(grads, rows_old, cols_old, lines):
+def new_rows_cols(grads, rows_old, cols_old, lines, which=range(4)):
     rows_new, cols_new = [], []
-    for index in range(4):
+    for index in which:
         if index in (0, 2):
-            line = ROW_LINE + index // 2
+            line = UP_ROWS if index else QKV_ROWS
             count = rows_old[index].shape[0]
             row_sum = to_column(lines[line:line + 1, :count])
         else:
@@ -670,30 +706,29 @@
 
 
 class Spread:
-    COUNT = 8
-
-    def __init__(self, place, full, start, width, flip, sems, base, shard=None):
-        self.place, self.full, self.shard = place, full, shard
+    def __init__(self, place, full, start, width, flip, orders, sems, base):
+        self.place, self.full = place, full
         self.cols = pl.ds(start, width)
         tiles = width // 128
         cut = (tiles // 2 if flip else tiles - tiles // 2) * 128
-        self.halves = [("xy", pl.ds(start, cut))]
+        self.halves = [(orders[0], pl.ds(start, cut))]
         if cut < width:
-            self.halves.append(("yx", pl.ds(start + cut, width - cut)))
-        self.sems, self.base = sems, base
+            self.halves.append((orders[1], pl.ds(start + cut, width - cut)))
+        self.sems, self.base, self.slots = sems, base, {}
+        self.count = sum(len(self.copies(stage)) for stage in range(4))
 
     def view(self, spot, cols):
         return self.full.at[spot["m"], spot["z"], spot["y"], spot["x"], :, cols]
 
-    def copy(self, slot, axis, step, spot, cols, source=None):
+    def copy(self, key, axis, step, spot, cols):
         place = self.place
+        slot = self.base + self.slots.setdefault(key, len(self.slots))
         send, recv = self.sems
-        send, recv = send.at[self.base + slot], recv.at[self.base + slot]
+        send, recv = send.at[slot], recv.at[slot]
         device = place.device(place.at(axis, step))
         view = self.view(spot, cols)
         sent = pltpu.make_async_remote_copy(
-            view if source is None else source, view, send, recv,
-            device_id=device, device_id_type=MESH)
+            view, view, send, recv, device_id=device, device_id_type=MESH)
         land = dict(spot)
         land[axis] = place.at(axis, -step)[axis]
         land = self.view(land, cols)
@@ -704,19 +739,19 @@
     def copies(self, stage):
         place = self.place
         here = {"z": place.z, "y": place.y, "x": place.x, "m": place.m}
-        if stage == 0:
-            source = None if self.shard is None else self.shard.at[:, self.cols]
-            return [self.copy(step - 1, "z", step, here, self.cols, source) for step in (1, 2, 3)]
-        here["z"] = EVERY
         if stage == 3:
-            here["y"] = here["x"] = EVERY
-            return [self.copy(7, "m", 1, here, self.cols)]
+            here["z"] = here["y"] = here["x"] = EVERY
+            return [self.copy((3, 0, 1), "m", 1, here, self.cols)]
+        halves = self.halves
+        if stage == 0 and halves[0][0][0] == "z":
+            halves = [(halves[0][0], self.cols)]
         out = []
-        for number, (order, cols) in enumerate(self.halves):
+        for number, (order, cols) in enumerate(halves):
             spot = dict(here)
-            if stage == 2:
-                spot[order[0]] = EVERY
-            out.append(self.copy(1 + 2 * stage + number, order[stage - 1], 1, spot, cols))
+            for axis in order[:stage]:
+                spot[axis] = EVERY
+            for step in steps_of(order[stage]):
+                out.append(self.copy((stage, number, step), order[stage], step, spot, cols))
         return out
 
     def start(self, stage):
@@ -733,14 +768,12 @@
                 sent.wait_send()
 
 
-def spread_tick(groups, tick):
-    for stage in range(4):
-        index = tick + 2 if stage == 0 else tick - stage + 1
-        if 0 <= index < len(groups):
-            for chunk in groups[index]:
-                if stage:
-                    chunk.arrived(stage - 1)
-                chunk.start(stage)
+def spread(groups, *moves):
+    for group, stage in moves:
+        for chunk in groups[group]:
+            if stage:
+                chunk.arrived(stage - 1)
+            chunk.start(stage)
 
 
 def unpack_small(small, norm_out, offsets, ffn_out):
@@ -790,25 +823,23 @@
         qkv[pair, :, place_of(core, 0, PAIR)] = out.astype(BF) * scale
 
 
-def attend_pair(qkv, bias, context, logs_ref, core, row, pair):
-    rows = pl.ds(pl.multiple_of(row * LEN, LEN), LEN)
-    lane = lax.broadcasted_iota(jnp.int32, (LEN, 128), 1)
+def attend_pair(qkv, bias, probs, flip, core, row, pair):
     item = core * 3 + pair
     queries, keys, values = (trio(qkv, core, row, part, pair) for part in range(3))
-    wide = jnp.concatenate([values, jnp.ones_like(values)], axis=1)
-    outs = []
-    logs = logs_ref[row]
+    flipped = values.T
+    cols = pl.ds(pl.multiple_of(row * LEN, LEN), LEN)
     for half, mask in enumerate(half_masks()):
-        scores = dot_last(queries * mask, keys) + bias[row]
-        peak = jnp.max(scores, axis=1, keepdims=True)
-        raised = jnp.exp(scores - peak).astype(BF)
-        both = dot(raised, wide)
-        total = both[:, 128:]
-        outs.append(both[:, :128] / total)
-        logs = jnp.where(lane == item * 2 + half, peak + jnp.log(total), logs)
-    logs_ref[row] = logs
-    context[rows, pl.ds(pl.multiple_of(item * 128, 128), 128)] = jnp.where(
-        lane < HD, outs[0], outs[1]).astype(BF)
+        scores = dot_last(keys * mask, queries) + bias[row]
+        raised = jnp.exp(scores - jnp.max(scores, axis=0, keepdims=True))
+        share = (raised * (1.0 / jnp.sum(raised, axis=0, keepdims=True))).astype(BF)
+        probs[half] = share
+        lines = pl.ds(pl.multiple_of(item * 128 + half * HD, HD), HD)
+        flip[lines, cols] = dot(flipped[half * HD:(half + 1) * HD, :], share).astype(BF)
+
+
+FEED_MOVES = (
+    ((8, 2),), ((9, 2),), (), ((6, 3),), ((7, 3),), ((8, 3),),
+)
 
 
 def forward_gather_kernel(*refs):
@@ -816,13 +847,14 @@
     take = lambda number: [refs.pop(0) for _ in range(number)]
     w_qkv, w_out, w_up, w_down, head, ffn, norm, lengths = take(8)
     tokens_any, cotangent_any = take(2)
-    (sums, norm_out, ffn_out, lse, hidden_scale, out_full, pooled, norm_sums) = take(8)
+    (sums, norm_out, ffn_out, hidden_scale, out_full, pooled, norm_sums) = take(7)
     (qkv_full, up_full, down_full, qkv_out, context_flip, token_flip, hidden_flip, normed_out,
-     context_out, act_flip, slope_out, layer_out, branch_out, grad_two_out) = take(14)
+     context_out, act_flip, slope_out, layer_out, branch_out, grad_two_out, probs_out) = take(15)
     (g_small, g_qkv, g_out, g_up, g_down, tokens, qkv, context, flip,
-     hidden_b, normed_one, act, slope, flip_act, bias, logs, offsets, branch) = take(18)
+     hidden_b, normed_one, act, slope, flip_act, bias, probs, offsets, branch, flip_context) = take(19)
     send, recv, local = refs
     place = Place()
+    greet(place)
     here = (place.m, place.z, place.y, place.x)
     used = [0]
     unwaited = []
@@ -852,9 +884,9 @@
     g_down[here] = w_down[...].astype(BF)
     sems, base = (send, recv), [0]
 
-    def chunk(full, start, width, flip=False):
-        made = Spread(place, full, start, width, flip, sems, base[0])
-        base[0] += Spread.COUNT
+    def chunk(full, start, width, flip=False, orders=("zxy", "zyx")):
+        made = Spread(place, full, start, width, flip, orders, sems, base[0])
+        base[0] += made.count
         return made
 
     groups = [[chunk(g_small, 0, 128), chunk(g_qkv, 0, PAIR)]]
@@ -867,66 +899,95 @@
         for made in groups[index]:
             made.arrived(3)
 
-    greet(place)
-    for index in (0, 1):
-        for made in groups[index]:
-            made.start(0)
+    meet(place)
+    spread(groups, (0, 0), (1, 0))
     sums[...] = weight_sums_of([w_qkv, w_out, w_up, w_down], g_small[here])
-    spread_tick(groups, 0)
     for row in range(2):
         set_bias(bias.at[row], lengths, place.m * 2 + row)
-    spread_tick(groups, 1)
     done(tokens_loaded)
     flip[...] = tokens[...].T
     flip_kept = keep(flip, token_flip)
-    spread_tick(groups, 2)
-    logs[...] = jnp.zeros(logs.shape, F32)
+    spread(groups, (0, 1), (2, 0))
+    spread(groups, (1, 1), (3, 0))
+    spread(groups, (0, 2))
+    spread(groups, (2, 1), (4, 0))
+    spread(groups, (1, 2))
+    spread(groups, (0, 3), (3, 1), (5, 0))
     ready(0)
     unpack_small(g_small, norm_out, offsets, ffn_out)
 
     @pl.loop(0, 12)
     def _(item):
         pair, row, core = item // 4, (item % 4) // 2, item % 2
-        for number, at in enumerate((2, 4, 6, 8, 10)):
+        for at, moves in (
+            (1, ((3, 2), (5, 1), (7, 0))),
+            (4, ((2, 3),)),
+            (6, ((7, 1), (9, 0))),
+            (7, ((3, 3),)),
+            (10, ((4, 3), (9, 1))),
+            (11, ((6, 2),)),
+        ):
             @pl.when(item == at)
             def _():
-                spread_tick(groups, 3 + number)
-                if at in (4, 8):
-                    ready(at // 4)
+                spread(groups, *moves)
+
+        for at in (4, 8):
+            @pl.when(item == at)
+            def _():
+                ready(at // 4)
 
         @pl.when(item % 4 == 0)
         def _():
             project_pair(tokens, g_qkv, offsets, qkv, pair)
 
-        attend_pair(qkv, bias, context, logs, core, row, pair)
-
+        for at, moves in (
+            (0, ((1, 3), (2, 2), (4, 1), (6, 0))),
+            (4, ((4, 2), (6, 1), (8, 0))),
+            (8, ((5, 2), (8, 1))),
+        ):
+            @pl.when(item == at)
+            def _():
+                spread(groups, *moves)
+
+        def probs_copy(number):
+            return pltpu.make_async_copy(
+                probs.at[number % 2], probs_out.at[number], local.at[28 + number % 2])
+
+        @pl.when(item >= 2)
+        def _():
+            probs_copy(item - 2).wait()
+
+        attend_pair(qkv, bias, probs.at[item % 2], flip_context, core, row, pair)
+        probs_copy(item).start()
+
+    spread(groups, (7, 2))
     for core in range(2):
         for pair in range(3):
             cols = slice(pair * PAIR, (pair + 1) * PAIR)
             keep(g_qkv.at[core, :, :, :, :, cols],
                  qkv_full.at[pair, :, :, :, :, core * PAIR:(core + 1) * PAIR])
     keep(qkv, qkv_out)
+    keep(flip_context, context_flip)
+    context[...] = flip_context[...].T
     context_kept = keep(context, context_out)
-    for row in range(2):
-        lse[row] = logs[row].T[0:16, :]
-    done(flip_kept)
-    flip[...] = context[...].T
-    flip_kept = keep(flip, context_flip)
+    for slot in range(2):
+        unwaited.append(
+            pltpu.make_async_copy(probs.at[slot], probs_out.at[10 + slot], local.at[28 + slot]))
     ready(3)
     rows_out = w_out.shape[0]
     for core in range(2):
         value = g_out[core].reshape(16, g_out.shape[4], D).astype(F32)[:, :rows_out]
         out_full[core * HALF:(core + 1) * HALF, :] = value.reshape(HALF, D).astype(BF)
     halves = [slice(row * LEN, (row + 1) * LEN) for row in range(2)]
-    for rows in halves:
+    for number, rows in enumerate(halves):
         attended = dot(context[rows, :], out_full[...]) + norm_out[0:1, :]
         normed, scale = norm_parts(tokens[rows, :].astype(F32) + attended)
         normed_one[rows, :] = normed
         hidden_scale[rows, :] = jnp.broadcast_to(scale, (LEN, 128))
         hidden_b[rows, :] = (normed * norm_out[2:3, :] + norm_out[3:4, :]).astype(BF)
+        spread(groups, *(((), ((5, 3),)))[number])
     cotangent_loaded = keep(cotangent_any, tokens)
     keep(normed_one, normed_out)
-    spread_tick(groups, 8)
     waiting = [[], []]
     for third in range(3):
         ready(4 + third)
@@ -954,7 +1015,7 @@
             ]
             for copy in waiting[core]:
                 copy.start()
-        spread_tick(groups, 9 + third)
+            spread(groups, *FEED_MOVES[2 * third + core])
     done(flip_kept)
     flip[...] = hidden_b[...].T
     keep(flip, hidden_flip)
@@ -966,6 +1027,7 @@
         down = g_down[:, :, :, :, :, cols].reshape(FF, DOWN_CHUNK)
         for rows in halves:
             branch[rows, cols] = dot(act[rows, :], down)
+        spread(groups, *(((), ((9, 3),), ()))[third])
     for core in range(2):
         keep(g_down.at[core], down_full.at[core])
     norm_sums[...] = jnp.zeros(norm_sums.shape, F32)
@@ -1009,7 +1071,7 @@
     rows = count // LEN
     flipped = shape((D, count), BF)
     small_outs = [
-        shape((8, 128), F32), shape((8, D), F32), shape((1, FF), F32), shape((rows, 16, LEN), F32),
+        shape((8, 128), F32), shape((8, D), F32), shape((1, FF), F32),
         shape((count, 128), F32), shape((D, D), BF), shape((rows, SEGS, D), F32), shape((8, D), F32),
     ]
     large_outs = [
@@ -1017,8 +1079,9 @@
         shape(grid + down.shape, BF), shape((3, count, D), BF), flipped, flipped, flipped,
         shape((count, D), F32), shape((count, D), BF), shape((FF, count), BF),
         shape((count, FF), BF), shape((count, D), BF), shape((count, D), BF), shape((count, D), F32),
+        shape((6 * rows, 2, LEN, LEN), BF),
     ]
-    slots = 11 * Spread.COUNT
+    slots = 88
     some = pl.BlockSpec(memory_space=pl.ANY)
     return pl.pallas_call(
         forward_gather_kernel,
@@ -1041,9 +1104,10 @@
             pltpu.VMEM((2, count, UP_CHUNK), BF),
             pltpu.VMEM((2, UP_CHUNK, count), BF),
             pltpu.VMEM((2, LEN, LEN), F32),
-            pltpu.VMEM((2, LEN, 128), F32),
+            pltpu.VMEM((2, 2, LEN, LEN), BF),
             pltpu.VMEM((2, 1, QKV_HALF), F32),
             pltpu.VMEM((count, D), F32),
+            pltpu.VMEM((D, count), BF),
             pltpu.SemaphoreType.DMA((slots,)),
             pltpu.SemaphoreType.DMA((slots,)),
             pltpu.SemaphoreType.DMA((30,)),
@@ -1055,10 +1119,12 @@
 
 
 class Collect:
-    COUNT = 8
-
-    def __init__(self, place, held, slots, result, start, width, flip, sems, base):
+    COUNT = 7
+
+    def __init__(self, place, held, slots, result, start, width, flip, sems, base, layer=None,
+                 stages=(0, 2)):
         self.place, self.held, self.slots, self.result = place, held, slots, result
+        self.layer, self.stages = layer, stages
         self.cols = pl.ds(start, width)
         tiles = width // 128
         cut = (tiles // 2 if flip else tiles - tiles // 2) * 128
@@ -1089,10 +1155,11 @@
             if stage == 1:
                 spot[order[0]] = getattr(place, order[0])
             spot[axis] = place.at(axis, 1)[axis]
-            land = (EVERY,) * (2 - stage) + (EVERY, cols)
+            layer = EVERY if self.layer is None else self.layer
+            land = (layer,) + (EVERY,) * (1 - stage) + (EVERY, cols)
             out.append(self.copy(
-                3 + 2 * stage + number, axis, 1, self.held.at[:, spot["y"], spot["x"], :, cols],
-                self.slots[stage].at[land]))
+                2 * stage + number + (0 if self.layer is not None else 3), axis, 1,
+                self.held.at[layer, spot["y"], spot["x"], :, cols], self.slots[stage].at[land]))
         return out
 
     def start(self, stage):
@@ -1111,58 +1178,67 @@
             return
         for order, cols in self.halves:
 
-            @pl.loop(0, 8 if stage == 0 else 4)
+            layers = 4 if self.layer is None else 1
+
+            @pl.loop(0, layers * (2 - stage))
             def _(index):
                 spot = {"y": place.y, "x": place.x}
                 if stage == 0:
-                    layer = index // 2
+                    layer = index // 2 if self.layer is None else self.layer
                     spot[order[1]] = index % 2
                     arrived = slots[layer, index % 2, :, cols]
                 else:
-                    layer = index
+                    layer = index if self.layer is None else self.layer
                     arrived = slots[layer, :, cols]
                 at = (layer, spot["y"], spot["x"], EVERY, cols)
                 held[at] = (held[at].astype(F32) + arrived.astype(F32)).astype(held.dtype)
 
     def finish(self):
-        for stage in range(3):
+        for stage in range(self.stages[0], self.stages[1] + 1):
             for sent in self.copies(stage):
                 sent.wait_send()
 
 
-def collect_tick(groups, tick):
-    for stage in range(4):
-        if 0 <= tick - stage < len(groups):
-            for chunk in groups[tick - stage]:
-                if stage:
-                    chunk.add(stage - 1)
-                if stage < 3:
-                    chunk.start(stage)
-
-
-def pack_small(target, core, norm_sums, grad_head, ffn_sums):
-    iota = lambda shape, axis: lax.broadcasted_iota(jnp.int32, shape, axis)
-    pick = (iota((D, 128), 0) % 24 == iota((D, 128), 1)).astype(F32).astype(BF)
-    pick_ffn = (iota((FF, 128), 0) % 96 == iota((FF, 128), 1)).astype(F32).astype(BF)
-
-    def split_dot(value, other):
-        high = value.astype(BF)
-        return dot(high, other) + dot((value - high.astype(F32)).astype(BF), other)
-
-    rows = jnp.concatenate(
-        [norm_sums[0:6, :], grad_head[0:2, :], jnp.zeros((8, D), F32)], axis=0)
-    rows = jnp.broadcast_to(rows[None], (16, 16, D)).reshape(256, D)
-    line = iota((256, D), 0)
-    device, kind = line // 16, line % 16
-    right = jnp.where(kind < 6, 2 * device + core, 16 * core + device)
-    rows = jnp.where(iota((256, D), 1) // 24 == right, rows, 0.0)
-    target[...] = split_dot(rows, pick).reshape(4, 2, 2, 16, 128)
-    right = iota((16, FF), 1) // 96 == iota((16, FF), 0) + 16 * core
-    ffn = split_dot(jnp.where(right, ffn_sums[...], 0.0), pick_ffn)
-    target[:, :, :, 8, :] = ffn.reshape(4, 2, 2, 128)
-
-
-def attend_back_pair(qkv, grad_context, lse, delta, bias, grad_head, core, row, pair):
+def advance(groups, *moves):
+    for group, stage in moves:
+        for chunk in groups[group]:
+            if stage > chunk.stages[0]:
+                chunk.add(stage - 1)
+            if stage <= chunk.stages[1]:
+                chunk.start(stage)
+
+
+def split_dot(value, other):
+    high = value.astype(BF)
+    return dot(high, other) + dot((value - high.astype(F32)).astype(BF), other)
+
+
+def picks(count, width):
+    shape = (count, 128)
+    lane = lax.broadcasted_iota(jnp.int32, shape, 0) % width
+    return (lane == lax.broadcasted_iota(jnp.int32, shape, 1)).astype(F32).astype(BF)
+
+
+def pack_rows(rows, right):
+    rows = jnp.broadcast_to(rows[None], (16, 8, D)).reshape(128, D)
+    iota = lambda axis: lax.broadcasted_iota(jnp.int32, (128, D), axis)
+    rows = jnp.where(iota(1) // 24 == right(iota(0) // 8), rows, 0.0)
+    return split_dot(rows, picks(D, 24)).reshape(4, 2, 2, 8, 128)
+
+
+def pack_small(target, core, norm_sums, ffn_sums):
+    target[:, :, :, 0:8, :] = pack_rows(norm_sums[...], lambda device: 2 * device + core)
+    iota = lambda axis: lax.broadcasted_iota(jnp.int32, (16, FF), axis)
+    ffn = jnp.where(iota(1) // 96 == iota(0) + 16 * core, ffn_sums[...], 0.0)
+    target[:, :, :, 8:16, :] = jnp.zeros((4, 2, 2, 8, 128), F32)
+    target[:, :, :, 8, :] = split_dot(ffn, picks(FF, 96)).reshape(4, 2, 2, 128)
+
+
+def pack_heads(core, grad_head):
+    return pack_rows(grad_head[...], lambda device: 16 * core + device)
+
+
+def attend_back_pair(qkv, grad_context, probs, delta, grad_head, core, row, pair):
     lane = lax.broadcasted_iota(jnp.int32, (LEN, 128), 1)
     item = core * 3 + pair
     queries, keys, values = (trio(qkv, core, row, part, pair) for part in range(3))
@@ -1172,12 +1248,10 @@
     flipped = keys.T
     grads_k, grads_v, grads_q = [], [], []
     for half, mask in enumerate(half_masks()):
-        head = item * 2 + half
-        scores = dot_last(keys * mask, queries) + bias[row] - lse[row, pl.ds(head, 1), :]
-        probs = jnp.exp(scores)
-        grad_probs = dot_last(values * mask, grad)
-        grad_scores = (probs * (grad_probs - delta[row, pl.ds(head, 1), :])).astype(BF)
-        grads_v.append(dot(probs.astype(BF), grad))
+        share = probs[half]
+        grad_probs = dot_last(values * mask, grad) - delta[row, pl.ds(item * 2 + half, 1), :]
+        grad_scores = (share.astype(F32) * grad_probs).astype(BF)
+        grads_v.append(dot(share, grad))
         grads_k.append(dot(grad_scores, queries))
         grads_q.append(dot(flipped[half * HD:(half + 1) * HD, :], grad_scores))
     grad_q = (jnp.concatenate(grads_q, axis=0).T * HD ** -0.5).astype(BF)
@@ -1192,20 +1266,23 @@
 def backward_scatter_kernel(*refs):
     refs = list(refs)
     take = lambda number: [refs.pop(0) for _ in range(number)]
-    lengths, lse, norm_given, norm, scale_one, w_out = take(6)
+    norm_given, norm, scale_one, w_out = take(4)
     rows_old, cols_old = take(4), take(4)
     head_sq, ffn_sq, norm_sq, weight_sums = take(4)
     (act_any, branch_any, down_any, slope_any, up_any, two_any, normed_any, hidden_any, context_any,
-     flip_any, token_any, qkv_any, weight_any) = take(13)
+     flip_any, token_any, qkv_any, weight_any, probs_any) = take(14)
     results = take(5)
     lines, totals, input_any = take(3)
-    held, other = take(5), take(5)
-    slots = [take(3) for _ in range(5)]
-    (wide, flip, flip_context, context, attended, qkv, weight, one, two, act, inner, bias, delta,
+    held, other = take(6), take(6)
+    slots = [take(3) for _ in range(6)]
+    heads_sum = refs.pop(0)
+    (wide, flip, flip_context, context, attended, qkv, weight, one, two, act, inner, probs, delta,
      grad_head, norm_sums, ffn_sums) = take(16)
-    mine_one, land_one, mine_two, land_two, old_small = take(5)
+    (mine_early, plane_early, line_early, mine_one, plane_one, line_one, mine_two, plane_two,
+     line_two, old_small) = take(10)
     send, recv, local = refs
     place = Place()
+    greet(place, True)
     sems = (send, recv)
     partner = place.device(place.at("m", 1))
     mine, theirs = place.m, 1 - place.m
@@ -1220,8 +1297,8 @@
     act_slots, chunk_slots = 16, 18
 
     def act_load(index):
-        core = jnp.where(index < 4, theirs, mine)
-        start = pl.multiple_of(core * (FF // 2) + (index % 4) * tile_rows, tile_rows)
+        core = jnp.where(index % 2 == 0, theirs, mine)
+        start = pl.multiple_of(core * (FF // 2) + (index // 2) * tile_rows, tile_rows)
         return pltpu.make_async_copy(
             act_any.at[pl.ds(start, tile_rows)], act.at[index % 2], local.at[act_slots + index % 2])
 
@@ -1249,18 +1326,10 @@
     load("branch", branch_any, wide)
     for index in range(2):
         act_load(index).start()
-    load("hidden", hidden_any, flip)
-    load("two", two_any, two)
-    for index in range(2):
-        for copy in chunk_loads(index):
-            copy.start()
-    load("normed", normed_any, one)
-    load("context", context_any, context)
-    load("flip", flip_any, flip_context)
-
-    small, qkv_held, out_held, up_held, down_held = held
-    small_other, qkv_other, out_other, up_other, down_other = other
-    base = 12
+
+    small, qkv_held, out_held, up_held, down_held, heads = held
+    small_other, qkv_other, out_other, up_other, down_other, heads_other = other
+    base = 13
 
     def swap(slot, source, target):
         return pltpu.make_async_remote_copy(
@@ -1281,41 +1350,68 @@
 
     out_swap = swap(7, out_held, out_other)
     small_swap = swap(11, small, small_other)
-    widths = (128, PAIR, D, UP_CHUNK, DOWN_CHUNK)
-    chunks = [[] for _ in range(5)]
-    for index in (4, 3, 2, 1, 0):
+    heads_swap = swap(12, heads, heads_other)
+    widths = (128, PAIR, D, UP_CHUNK, DOWN_CHUNK, 128)
+    chunks = [[] for _ in range(6)]
+    targets = results + [heads_sum]
+
+    def collect(index, start, width, flip=False, layer=None, stages=(0, 2), count=Collect.COUNT):
+        nonlocal base
+        made = Collect(place, held[index], slots[index], targets[index], start, width, flip, sems,
+                       base, layer, stages)
+        base += count
+        return made
+
+    groups = [[collect(4, 0, D, layer=z, stages=(0, 1), count=4)] for z in range(4)]
+    groups += [[collect(4, 0, D, stages=(2, 2), count=3)]]
+    for index in (3, 2, 1):
         for start in range(0, held[index].shape[4], widths[index]):
-            chunks[index].append(Collect(
-                place, held[index], slots[index], results[index], start, widths[index],
-                index == 1 and start == PAIR, sems, base))
-            base += Collect.COUNT
-    groups = [[c] for index in (4, 3, 2, 1) for c in chunks[index]]
-    groups[-1] += chunks[0]
-
-    greet(place)
+            groups.append([collect(index, start, widths[index], index == 1 and start == PAIR)])
+    groups[8].append(collect(0, 0, 128))
+    groups[11].append(collect(5, 0, 128))
     norm_sums[...] = norm_given[...]
     loaded["branch"].wait()
+    meet(place, True)
+
+    def down_tile_of(index):
+        act_load(index).wait()
+        value = dot(act[index % 2], wide[...]).reshape(2, 2, tile_rows // 4, D)
+
+        @pl.when(index < 6)
+        def _():
+            act_load(index + 2).start()
+
+        return value
+
+    def down_theirs(layer):
+        down_held[layer] = down_tile_of(2 * layer).astype(BF)
+        down_swap(layer).start()
+
+    down_theirs(0)
+    load("hidden", hidden_any, flip)
+    for index in range(2):
+        for copy in chunk_loads(index):
+            copy.start()
+    load("two", two_any, two)
+    load("normed", normed_any, one)
+    load("context", context_any, context)
+    load("flip", flip_any, flip_context)
 
     @pl.loop(0, 4)
     def _(layer):
-        act_load(layer).wait()
-        value = dot(act[layer % 2], wide[...])
-        down_held[layer] = value.reshape(2, 2, tile_rows // 4, D).astype(BF)
-        down_swap(layer).start()
-        act_load(layer + 2).start()
-
-    @pl.loop(0, 4)
-    def _(layer):
-        act_load(layer + 4).wait()
-        value = dot(act[layer % 2], wide[...]).reshape(2, 2, tile_rows // 4, D)
+        value = down_tile_of(2 * layer + 1)
+
+        @pl.when(layer < 3)
+        def _():
+            down_theirs(layer + 1)
+
         down_swap(layer).wait()
         down_held[layer] = (value + down_other[layer].astype(F32)).astype(BF)
-
-        @pl.when(layer < 2)
-        def _():
-            act_load(layer + 6).start()
-
-    collect_tick(groups, 0)
+        for z in range(4):
+            @pl.when(layer == z)
+            def _():
+                advance(groups, (z, 0))
+
     loaded["hidden"].wait()
     loaded["two"].wait()
 
@@ -1340,9 +1436,14 @@
         for copy in chunk_loads(third + 2):
             copy.start()
 
-        @pl.when(third == 1)
-        def _():
-            collect_tick(groups, 1)
+        for at, moves in (
+            (0, ((0, 1),)),
+            (1, ((1, 1),)),
+            (2, ((2, 1),)),
+        ):
+            @pl.when(third == at)
+            def _():
+                advance(groups, *moves)
 
     @pl.loop(0, 3)
     def _(third):
@@ -1356,14 +1457,29 @@
         def _():
             for copy in chunk_loads(5):
                 copy.start()
-            collect_tick(groups, 2)
-
+
+        for spot, moves in (
+            (0, ((3, 1), (5, 0))),
+            (1, ((0, 2), (1, 2), (6, 0))),
+            (2, ((2, 2), (3, 2), (4, 2), (7, 0))),
+        ):
+            @pl.when(third == spot)
+            def _():
+                advance(groups, *moves)
+
+    def probs_load(item):
+        pair, row = item // 4, item % 2
+        core = jnp.where(item % 4 < 2, theirs, mine)
+        return pltpu.make_async_copy(
+            probs_any.at[pair * 4 + row * 2 + core], probs.at[item % 2], local.at[24 + item % 2])
+
+    for item in range(2):
+        probs_load(item).start()
     load("token", token_any, flip)
     load("qkv", qkv_any, qkv)
     load("weight", weight_any, weight)
     loaded["normed"].wait()
     loaded["context"].wait()
-    collect_tick(groups, 3)
     for row in range(2):
         rows = slice(row * LEN, (row + 1) * LEN)
         back, gain, shift = norm_back(
@@ -1383,6 +1499,7 @@
         member = (lax.broadcasted_iota(jnp.int32, (16, D), 1) // HD == head).astype(F32).astype(BF)
         delta[row] = dot_last(member, high) + dot_last(member, low)
     loaded["flip"].wait()
+    advance(groups, (5, 1))
     spare = out_held.shape[3] - D // 32
 
     def out_half(core):
@@ -1393,12 +1510,15 @@
 
     out_held[...] = out_half(theirs).astype(BF)
     out_swap.start()
+    pack_small(small, theirs, norm_sums, ffn_sums)
+    small_swap.start()
     value = out_half(mine)
     out_swap.wait()
     out_held[...] = (value + out_other[...].astype(F32)).astype(BF)
-    collect_tick(groups, 4)
-    for row in range(2):
-        set_bias(bias.at[row], lengths, place.m * 2 + row)
+    small_swap.wait()
+    pack_small(small, mine, norm_sums, ffn_sums)
+    small[...] += small_other[...]
+    advance(groups, (8, 0))
     grad_head[...] = jnp.zeros(grad_head.shape, F32)
     for name in ("qkv", "token"):
         loaded[name].wait()
@@ -1418,26 +1538,40 @@
 
     @pl.loop(0, 12)
     def _(item):
-        pair, row, core = item // 4, (item % 4) // 2, item % 2
+        pair, row = item // 4, item % 2
+        core = jnp.where(item % 4 < 2, theirs, mine)
+
+        @pl.when(item % 4 == 2)
+        def _():
+            qkv_theirs(pair)
 
         @pl.when((item == 4) | (item == 8))
         def _():
-            qkv_theirs(pair - 1)
-
-        @pl.when((item == 5) | (item == 9))
-        def _():
             qkv_mine(pair - 1)
 
-        for number, at in enumerate((1, 4, 7, 10)):
+        for at, moves in (
+            (1, ((6, 1),)),
+            (3, ((7, 1),)),
+            (4, ((5, 2), (9, 0))),
+            (6, ((4, 3),)),
+            (7, ((8, 1),)),
+            (8, ((5, 3), (6, 2), (10, 0))),
+            (9, ((7, 2),)),
+            (10, ((9, 1),)),
+        ):
             @pl.when(item == at)
             def _():
-                collect_tick(groups, 5 + number)
-
-        attend_back_pair(qkv, wide, lse, delta, bias, grad_head, core, row, pair)
-
-    qkv_theirs(2)
-    pack_small(small, theirs, norm_sums, grad_head, ffn_sums)
-    small_swap.start()
+                advance(groups, *moves)
+
+        probs_load(item).wait()
+        attend_back_pair(qkv, wide, probs.at[item % 2], delta, grad_head, core, row, pair)
+
+        @pl.when(item < 10)
+        def _():
+            probs_load(item + 2).start()
+
+    heads[...] = pack_heads(theirs, grad_head)
+    heads_swap.start()
     loaded["weight"].wait()
 
     def input_rows(row):
@@ -1446,78 +1580,100 @@
                          + dot_last(qkv[2, rows, :], weight[2]))
 
     qkv_mine(2)
-    small_swap.wait()
-    pack_small(small, mine, norm_sums, grad_head, ffn_sums)
-    small[...] += small_other[...]
-    collect_tick(groups, 9)
+    heads_swap.wait()
+    heads[...] = pack_heads(mine, grad_head) + heads_other[...]
+    advance(groups, (6, 3), (8, 2), (11, 0))
     input_rows(0)
-    collect_tick(groups, 10)
+    advance(groups, (10, 1))
     input_rows(1)
     input_done = pltpu.make_async_copy(one, input_any, local.at[12])
     input_done.start()
-    collect_tick(groups, 11)
-    collect_tick(groups, 12)
+    advance(groups, (7, 3), (9, 2), (11, 1), (10, 2), (8, 3))
     small_sum, grads = results[0], results[1:]
     lines[...] = jnp.zeros(lines.shape, F32)
-    for index in range(4):
+
+    def put_sums(index):
         grad = grads[index][...]
         square = grad * grad + EPS_SQUARE
         put_line(lines, COL_LINES[index], jnp.sum(square, axis=0, keepdims=True))
         if index in (0, 2):
-            line = ROW_LINE + index // 2
+            line = UP_ROWS if index else QKV_ROWS
             lines[line:line + 1, 0:grad.shape[0]] = to_row(jnp.sum(square, axis=1, keepdims=True))
-    first = Exchange(place, mine_one, land_one, sems, base)
-    line = lax.broadcasted_iota(jnp.int32, lines.shape, 0)
-    value = lines[...]
-    first.mine[0] = value
-    paired = jnp.where(line >= OUT_LINE, first.swap(0, "m"), value)
-    total = paired
-    for stage, axis in ((1, "x"), (2, "y"), (3, "z")):
-        first.mine[stage] = total
-        total = first.swap(stage, axis)
-    lines[...] = jnp.where(line >= ROW_LINE, paired, total)
-    rows_new, cols_new = new_rows_cols(grads, rows_old, cols_old, lines)
-    ratios, row_totals = [], []
-    for index in range(4):
+
+    def ratio_of(index):
+        (row,), (col,) = new_rows_cols(grads, rows_old, cols_old, lines, (index,))
         grad = grads[index][...]
-        scaled = jnp.sum(grad * grad * (1.0 / cols_new[index]), axis=1, keepdims=True)
-        ratios.append(jnp.sum(scaled / rows_new[index], axis=0, keepdims=True))
+        scaled = jnp.sum(grad * grad * (1.0 / col), axis=1, keepdims=True)
         share = 0.5 if index in (0, 2) else 1.0
-        row_totals.append(jnp.sum(rows_new[index], axis=0, keepdims=True) * share)
+        return (jnp.sum(scaled / row, axis=0, keepdims=True),
+                jnp.sum(row, axis=0, keepdims=True) * share)
+
+    for index in (1, 2, 3):
+        put_sums(index)
+    early = Exchange(place, mine_early, plane_early, line_early, sems, base)
+    late = Exchange(place, mine_one, plane_one, line_one, sems, base + Exchange.COUNT)
+    second = Exchange(place, mine_two, plane_two, line_two, sems, base + 2 * Exchange.COUNT)
+    value = lines[LATE:, :]
+    early.start_plane(value)
+    advance(groups, (9, 3), (11, 2))
+    line = lax.broadcasted_iota(jnp.int32, value.shape, 0) + LATE
+    same, cross = early.end_plane()
+    paired = value + plane_early[theirs, place.y, place.x]
+    early.start_line(jnp.where((line >= OUT_LINE) & (line < UP_ROWS), same + cross, same))
+    advance(groups, (10, 3))
+    lines[LATE:, :] = jnp.where(line >= UP_ROWS, paired, early.end_line())
+    sums = {index: ratio_of(index) for index in (1, 2, 3)}
     place_small(old_small, norm_sq[...], head_sq[...], as_row(ffn_sq), 1.0)
+    advance(groups, (11, 3))
+    put_sums(0)
+    value = lines[0:LATE, :]
+    late.start_plane(value)
+    small_sum[6:8, :] = heads_sum[0:2, :]
     _, update = small_update(small_sum[...], old_small[...])
-    second = Exchange(place, mine_two, land_two, sems, base + 16)
-    totals[...] = add_up(
-        second, scalars(ratios + row_totals + small_sums(update)) + weight_sums[...])
+    others = small_sums(update)
+    line = lax.broadcasted_iota(jnp.int32, value.shape, 0)
+    same, _ = late.end_plane()
+    paired = value + plane_one[theirs, place.y, place.x]
+    late.start_line(same)
+    lines[0:LATE, :] = jnp.where(line >= QKV_ROWS, paired, late.end_line())
+    sums[0] = ratio_of(0)
+    second.start_plane(
+        scalars([sums[index][0] for index in range(4)] + [sums[index][1] for index in range(4)]
+                + others) + weight_sums[...])
+    same, cross = second.end_plane()
+    second.start_line(same + cross)
+    totals[...] = second.end_line()
     input_done.wait()
     for group in groups:
         for chunk in group:
             chunk.finish()
-    first.finish()
-    second.finish()
-
-
-def backward_scatter(lengths, lse, norm_sums, norm, scale_one, w_out, rows_old, cols_old, squares,
+    for exchange in (early, late, second):
+        exchange.finish()
+
+
+def backward_scatter(norm_sums, norm, scale_one, w_out, rows_old, cols_old, squares,
                      weight_sums, large, rows, widths):
     count = scale_one.shape[0]
     shape = jax.ShapeDtypeStruct
     some = pl.BlockSpec(memory_space=pl.ANY)
-    kinds = [F32, BF, BF, BF, BF]
-    padded = [16, rows[1], 32, rows[3], rows[4]]
-    held = [pltpu.VMEM((4, 2, 2, r, w), k) for r, w, k in zip(padded, widths, kinds)]
+    kinds = [F32, BF, BF, BF, BF, F32]
+    padded = [16, rows[1], 32, rows[3], rows[4], 8]
+    wide = widths + [128]
+    held = [pltpu.VMEM((4, 2, 2, r, w), k) for r, w, k in zip(padded, wide, kinds)]
     slots = []
-    for r, w, k in zip(padded, widths, kinds):
+    for r, w, k in zip(padded, wide, kinds):
         slots += [pltpu.VMEM((4, 2, r, w), k), pltpu.VMEM((4, r, w), k), pltpu.VMEM((3, r, w), k)]
-    sems = 12 + 11 * Collect.COUNT + 32
+    sems = 13 + 19 + 9 * Collect.COUNT + 3 * Exchange.COUNT
     outs = [shape((r, w), F32) for r, w in zip(rows, widths)]
     outs += [shape((LINES, 128), F32), shape((8, 128), F32), shape((count, D), F32)]
-    small = [lse, norm_sums, norm, scale_one, w_out, *rows_old, *cols_old, *squares, weight_sums]
+    small = [norm_sums, norm, scale_one, w_out, *rows_old, *cols_old, *squares, weight_sums]
     return pl.pallas_call(
         backward_scatter_kernel,
         out_shape=outs,
-        in_specs=[SMEM] + [VMEM] * len(small) + [some] * len(large),
+        in_specs=[VMEM] * len(small) + [some] * len(large),
         out_specs=[VMEM] * 7 + [some],
         scratch_shapes=held + held + slots + [
+            pltpu.VMEM((8, 128), F32),
             pltpu.VMEM((count, D), BF),
             pltpu.VMEM((D, count), BF),
             pltpu.VMEM((D, count), BF),
@@ -1529,24 +1685,24 @@
             pltpu.VMEM((count, D), F32),
             pltpu.VMEM((2, FF // 8, count), BF),
             pltpu.VMEM((count, UP_CHUNK), BF),
-            pltpu.VMEM((2, LEN, LEN), F32),
+            pltpu.VMEM((2, 2, LEN, LEN), BF),
             pltpu.VMEM((2, 16, LEN), F32),
             pltpu.VMEM((8, D), F32),
             pltpu.VMEM((8, D), F32),
             pltpu.VMEM((1, FF), F32),
-            pltpu.VMEM((4, LINES, 128), F32),
-            pltpu.VMEM((4, 4, LINES, 128), F32),
-            pltpu.VMEM((4, 8, 128), F32),
-            pltpu.VMEM((4, 4, 8, 128), F32),
+        ] + [
+            pltpu.VMEM(lead + (count, 128), F32)
+            for count in (LINES - LATE, LATE, 8) for lead in ((2,), (2, 2, 2), (4,))
+        ] + [
             pltpu.VMEM((16, 128), F32),
             pltpu.SemaphoreType.DMA((sems,)),
             pltpu.SemaphoreType.DMA((sems,)),
-            pltpu.SemaphoreType.DMA((24,)),
+            pltpu.SemaphoreType.DMA((26,)),
         ],
         compiler_params=pltpu.CompilerParams(
             collective_id=1, has_side_effects=True, vmem_limit_bytes=62 << 20),
         name="backward_scatter",
-    )(lengths, *small, *large)
+    )(*small, *large)
 
 
 def small_block(norm, head, ffn):
@@ -1590,19 +1746,18 @@
     vectors = [head_bias, ffn_bias if fast else ffn_bias.reshape(1, -1), norm_bias]
     rows_out = w_out.shape[0]
     if fast:
-        (weight_sums, norm_full, ffn_full, lse, scale_one, out_full, pooled, norm_sums, qkv_full,
+        (weight_sums, norm_full, ffn_full, scale_one, out_full, pooled, norm_sums, qkv_full,
          up_full, down_full, qkv, context_flip, token_flip, hidden_flip, normed_one, context,
-         act_flip, slope, layer_out, grad_branch, grad_two
+         act_flip, slope, layer_out, grad_branch, grad_two, probs
          ) = forward_gather(weights, vectors, seg_lengths, tokens, cotangent)
         rows_old = [qkv_rows, out_rows, up_rows, down_rows]
         cols_old = [qkv_cols, out_cols, up_cols, down_cols]
         old = [head_bias_sq, ffn_bias_sq, norm_sq]
         *reduced, lines, totals, input_grad = backward_scatter(
-            seg_lengths, lse, norm_sums, norm_full, scale_one, out_full, rows_old, cols_old, old,
-            weight_sums,
+            norm_sums, norm_full, scale_one, out_full, rows_old, cols_old, old, weight_sums,
             [act_flip, grad_branch, down_full.reshape(FF, D), slope,
              up_full.reshape(2, D, FF // 2), grad_two, normed_one, hidden_flip, context,
-             context_flip, token_flip, qkv, qkv_full.reshape(3, D, D)],
+             context_flip, token_flip, qkv, qkv_full.reshape(3, D, D), probs],
             [16, rows_qkv, rows_out, rows_qkv, w_down.shape[0]],
             [128, QKV_HALF, D, w_up.shape[1], D])
         new = step(reduced, lines, totals, weights, rows_old, cols_old, vectors, old,

time: 231 us -> 207 us (0.90)
  Pallas kernels: 227 us -> 204 us
    pallas_call x1, Pallas kernels: 124 us -> 107 us  [backward_scatter(): pl.pallas_call(backward_scatter_kernel, out_shape=outs, in_specs=[VMEM] *...]
    pallas_call x1, Pallas kernels: 95.4 us -> 89.9 us  [forward_gather(): pl.pallas_call(forward_gather_kernel, out_shape=small_outs + large_outs,...]
where the time goes in v7:
time: 207 us; the launch traced here: 205 us
  Pallas kernels  204 us (99%)
    pallas_call x1, Pallas kernels, backward_scatter(): pl.pallas_call(backward_scatter_kernel, out_shape=outs, in_specs=[VMEM] *...  107 us
    pallas_call x1, Pallas kernels, forward_gather(): pl.pallas_call(forward_gather_kernel, out_shape=small_outs + large_outs,...  89.9 us
    pallas_call x1, Pallas kernels, step(): pl.pallas_call(step_kernel, out_shape=outs + [jax.ShapeDtypeStruct(v.shap...  6.94 us

profile of v7, /device:TPU:0, one launch (start us, length us, event | category | flops | bytes accessed | tf_op | source)
XLA Modules:
  0.0 204.9 jit_solution(10934153485608479993)
XLA Ops:
  0.7 89.9 %forward_gather.1 = (f32[8,128]{1,0:T(8,128)}, f32[8,768]{1,0:T(8,128)}, f32[1,3072]{1,0:T(1,128)}, f32[1024,128]{1,0:T(8,128)}, bf16[768,768]{1,0:T(8,128)(2,1)...) custom-call(f32[3,48,384]{2,1,0:T(8,128)} %bitcast.9, ...), custom_call_target="tpu_custom_call" | custom-call | tf_op jit(solution)/shard_map/forward_gather/pallas_call | solution.py:1086
  90.6 107.1 %backward_scatter.1 = (f32[16,128]{1,0:T(8,128)}, f32[48,1152]{1,0:T(8,128)}, f32[24,768]{1,0:T(8,128)}, f32[48,1536]{1,0:T(8,128)}, f32[96,768]{1,0:T(8,128)}, ...) custom-call(f32[8,768]{1,0:T(8,128)} %get-tuple-element.85.refs_0_, f32[8,768]{1,0:T(8,128)} %get-tuple-element.86.refs_1_, ...), custom_call_target="tpu_custom_call" | custom-call | tf_op jit(solution)/shard_map/backward_scatter/pallas_call | solution.py:1670
  197.7 6.9 %adafactor_step.1 = (f32[3,48,384]{2,1,0:T(8,128)}, f32[24,768]{1,0:T(8,128)}, f32[48,1536]{1,0:T(8,128)}, f32[96,768]{1,0:T(8,128)}, f32[2,24]{1,0:T(2,128)}, /...) custom-call(f32[48,1152]{1,0:T(8,128)} %get-tuple-element.104.refs_0, ...), custom_call_target="tpu_custom_call" | custom-call | tf_op jit(solution)/shard_map/adafactor_step/pallas_call | solution.py:343

commit v8 on v7

--- a/solution.py
+++ b/solution.py
@@ -53,22 +53,35 @@
     return (1, 2, 3) if axis == "z" else (1,)
 
 
-def near(place, wide):
-    spots = [place.at("z", step) for step in (1, 2, 3)]
-    for steps in PLANE:
-        if wide or sum(steps) == 1:
-            spots.append(place.across(steps))
-    return [place.device(spot) for spot in spots]
-
-
-def greet(place, wide=False):
+def other_device(step):
+    count = lax.axis_size("dp") * lax.axis_size("mp")
+    number = (lax.axis_index("dp") * 2 + lax.axis_index("mp") + step) % count
+    return (number // 2, number % 2)
+
+
+def greet(place):
     barrier = pltpu.get_barrier_semaphore()
-    for device in near(place, wide):
-        pl.semaphore_signal(barrier, inc=1, device_id=device, device_id_type=MESH)
-
-
-def meet(place, wide=False):
-    pl.semaphore_wait(pltpu.get_barrier_semaphore(), len(near(place, wide)))
+    for axis in "zyxm":
+        for step in steps_of(axis):
+            pl.semaphore_signal(
+                barrier, inc=1, device_id=place.device(place.at(axis, step)), device_id_type=MESH)
+
+
+def meet():
+    pl.semaphore_wait(pltpu.get_barrier_semaphore(), 6)
+
+
+def greet_all():
+    barrier = pltpu.get_barrier_semaphore()
+
+    @pl.loop(1, 32)
+    def _(step):
+        pl.semaphore_signal(
+            barrier, inc=1, device_id=other_device(step), device_id_type=MESH)
+
+
+def meet_all():
+    pl.semaphore_wait(pltpu.get_barrier_semaphore(), 31)
 
 
 def weight_sums_of(weights, small):
@@ -126,15 +139,16 @@
 class Exchange:
     COUNT = 10
 
-    def __init__(self, place, mine, plane, line, sems, base):
+    def __init__(self, place, mine, plane, line, sems, base, peers=PLANE):
         self.place, self.mine, self.plane, self.line = place, mine, plane, line
+        self.peers = peers
         self.sems, self.base = sems, base
 
     def plane_copies(self):
         place = self.place
         send, recv = self.sems
         out = []
-        for number, steps in enumerate(PLANE):
+        for number, steps in enumerate(self.peers):
             spot = place.across(steps)
             slot = self.base + number
             device = place.device(spot)
@@ -172,8 +186,9 @@
         plane, core = self.plane, self.place.m
         for _, arrives in self.plane_copies():
             arrives.wait_recv()
+        cores = (core, 1 - core) if self.peers is PLANE else (core,)
         return [(plane[c, 0, 0] + plane[c, 0, 1]) + (plane[c, 1, 0] + plane[c, 1, 1])
-                for c in (core, 1 - core)]
+                for c in cores]
 
     def start_line(self, value):
         self.mine[1] = value
@@ -190,6 +205,44 @@
     def finish(self):
         for sent, _ in self.plane_copies() + self.line_copies():
             sent.wait_send()
+
+
+class Broadcast:
+    def __init__(self, mine, land, sems, slot, core_only):
+        self.mine, self.land, self.core_only = mine, land, core_only
+        self.send, self.recv = (sem.at[slot] for sem in sems)
+        self.number = lax.axis_index("dp") * 2 + lax.axis_index("mp")
+
+    def copy(self, device):
+        return pltpu.make_async_remote_copy(
+            self.mine, self.land.at[self.number], self.send, self.recv,
+            device_id=device, device_id_type=MESH)
+
+    def start(self, value):
+        self.mine[...] = value
+        if self.core_only:
+            @pl.loop(2, 32, step=2)
+            def _(step):
+                self.copy(other_device(step)).start()
+
+            self.copy((self.number // 2, 1 - self.number % 2)).start()
+        else:
+            @pl.loop(1, 32)
+            def _(step):
+                self.copy(other_device(step)).start()
+
+        self.land[self.number] = value
+
+    def all_of_it(self):
+        ref = self.land.at[pl.ds(0, 16 if self.core_only else 31)]
+        return pltpu.make_async_remote_copy(
+            ref, ref, self.send, self.recv, device_id=(0, 0), device_id_type=MESH)
+
+    def end(self):
+        self.all_of_it().wait_recv()
+
+    def finish(self):
+        self.all_of_it().wait_send()
 
 
 QKV_LINE, QKV_ROWS, UP_LINE, OUT_LINE, DOWN_LINE, UP_ROWS = 0, 9, 16, 28, 34, 40
@@ -899,7 +952,7 @@
         for made in groups[index]:
             made.arrived(3)
 
-    meet(place)
+    meet()
     spread(groups, (0, 0), (1, 0))
     sums[...] = weight_sums_of([w_qkv, w_out, w_up, w_down], g_small[here])
     for row in range(2):
@@ -924,7 +977,8 @@
             (4, ((2, 3),)),
             (6, ((7, 1), (9, 0))),
             (7, ((3, 3),)),
-            (10, ((4, 3), (9, 1))),
+            (9, ((9, 1),)),
+            (10, ((4, 3),)),
             (11, ((6, 2),)),
         ):
             @pl.when(item == at)
@@ -1022,12 +1076,13 @@
     for core in range(2):
         keep(g_up.at[core], up_full.at[core])
     for third in range(3):
+        if third == 1:
+            spread(groups, (9, 3))
         ready(7 + third)
         cols = slice(third * DOWN_CHUNK, (third + 1) * DOWN_CHUNK)
         down = g_down[:, :, :, :, :, cols].reshape(FF, DOWN_CHUNK)
         for rows in halves:
             branch[rows, cols] = dot(act[rows, :], down)
-        spread(groups, *(((), ((9, 3),), ()))[third])
     for core in range(2):
         keep(g_down.at[core], down_full.at[core])
     norm_sums[...] = jnp.zeros(norm_sums.shape, F32)
@@ -1266,23 +1321,22 @@
 def backward_scatter_kernel(*refs):
     refs = list(refs)
     take = lambda number: [refs.pop(0) for _ in range(number)]
-    norm_given, norm, scale_one, w_out = take(4)
+    norm_given, norm = take(2)
     rows_old, cols_old = take(4), take(4)
     head_sq, ffn_sq, norm_sq, weight_sums = take(4)
     (act_any, branch_any, down_any, slope_any, up_any, two_any, normed_any, hidden_any, context_any,
-     flip_any, token_any, qkv_any, weight_any, probs_any) = take(14)
+     flip_any, token_any, qkv_any, weight_any, probs_any, scale_any, out_any) = take(16)
     results = take(5)
     lines, totals, input_any = take(3)
     held, other = take(6), take(6)
     slots = [take(3) for _ in range(6)]
     heads_sum = refs.pop(0)
     (wide, flip, flip_context, context, attended, qkv, weight, one, two, act, inner, probs, delta,
-     grad_head, norm_sums, ffn_sums) = take(16)
-    (mine_early, plane_early, line_early, mine_one, plane_one, line_one, mine_two, plane_two,
-     line_two, old_small) = take(10)
+     grad_head, norm_sums, ffn_sums, scale_one, w_out) = take(18)
+    (mine_early, plane_early, line_early, mine_one, land_one, mine_two, land_two, old_small) = take(8)
     send, recv, local = refs
     place = Place()
-    greet(place, True)
+    greet_all()
     sems = (send, recv)
     partner = place.device(place.at("m", 1))
     mine, theirs = place.m, 1 - place.m
@@ -1297,8 +1351,8 @@
     act_slots, chunk_slots = 16, 18
 
     def act_load(index):
-        core = jnp.where(index % 2 == 0, theirs, mine)
-        start = pl.multiple_of(core * (FF // 2) + (index // 2) * tile_rows, tile_rows)
+        core = jnp.where(index < 4, theirs, mine)
+        start = pl.multiple_of(core * (FF // 2) + (index % 4) * tile_rows, tile_rows)
         return pltpu.make_async_copy(
             act_any.at[pl.ds(start, tile_rows)], act.at[index % 2], local.at[act_slots + index % 2])
 
@@ -1368,10 +1422,10 @@
         for start in range(0, held[index].shape[4], widths[index]):
             groups.append([collect(index, start, widths[index], index == 1 and start == PAIR)])
     groups[8].append(collect(0, 0, 128))
-    groups[11].append(collect(5, 0, 128))
+    groups.append([collect(5, 0, 128)])
     norm_sums[...] = norm_given[...]
     loaded["branch"].wait()
-    meet(place, True)
+    meet_all()
 
     def down_tile_of(index):
         act_load(index).wait()
@@ -1383,11 +1437,11 @@
 
         return value
 
-    def down_theirs(layer):
-        down_held[layer] = down_tile_of(2 * layer).astype(BF)
+    @pl.loop(0, 4)
+    def _(layer):
+        down_held[layer] = down_tile_of(layer).astype(BF)
         down_swap(layer).start()
 
-    down_theirs(0)
     load("hidden", hidden_any, flip)
     for index in range(2):
         for copy in chunk_loads(index):
@@ -1396,21 +1450,18 @@
     load("normed", normed_any, one)
     load("context", context_any, context)
     load("flip", flip_any, flip_context)
+    load("scale", scale_any, scale_one)
+    load("out", out_any, w_out)
 
     @pl.loop(0, 4)
     def _(layer):
-        value = down_tile_of(2 * layer + 1)
-
-        @pl.when(layer < 3)
-        def _():
-            down_theirs(layer + 1)
-
+        value = down_tile_of(layer + 4)
         down_swap(layer).wait()
         down_held[layer] = (value + down_other[layer].astype(F32)).astype(BF)
-        for z in range(4):
-            @pl.when(layer == z)
+        for at, moves in ((0, ((0, 0),)), (2, ((1, 0),))):
+            @pl.when(layer == at)
             def _():
-                advance(groups, (z, 0))
+                advance(groups, *moves)
 
     loaded["hidden"].wait()
     loaded["two"].wait()
@@ -1437,9 +1488,9 @@
             copy.start()
 
         for at, moves in (
-            (0, ((0, 1),)),
-            (1, ((1, 1),)),
-            (2, ((2, 1),)),
+            (0, ((2, 0),)),
+            (1, ((0, 1), (3, 0))),
+            (2, ((1, 1),)),
         ):
             @pl.when(third == at)
             def _():
@@ -1459,9 +1510,9 @@
                 copy.start()
 
         for spot, moves in (
-            (0, ((3, 1), (5, 0))),
-            (1, ((0, 2), (1, 2), (6, 0))),
-            (2, ((2, 2), (3, 2), (4, 2), (7, 0))),
+            (0, ((0, 2), (2, 1), (5, 0))),
+            (1, ((3, 1),)),
+            (2, ((1, 2), (2, 2), (6, 0))),
         ):
             @pl.when(third == spot)
             def _():
@@ -1479,7 +1530,8 @@
     load("qkv", qkv_any, qkv)
     load("weight", weight_any, weight)
     loaded["normed"].wait()
-    loaded["context"].wait()
+    for name in ("context", "scale", "out"):
+        loaded[name].wait()
     for row in range(2):
         rows = slice(row * LEN, (row + 1) * LEN)
         back, gain, shift = norm_back(
@@ -1512,13 +1564,16 @@
     out_swap.start()
     pack_small(small, theirs, norm_sums, ffn_sums)
     small_swap.start()
-    value = out_half(mine)
-    out_swap.wait()
-    out_held[...] = (value + out_other[...].astype(F32)).astype(BF)
-    small_swap.wait()
-    pack_small(small, mine, norm_sums, ffn_sums)
-    small[...] += small_other[...]
-    advance(groups, (8, 0))
+    advance(groups, (3, 2), (4, 2))
+
+    def out_mine():
+        value = out_half(mine)
+        out_swap.wait()
+        out_held[...] = (value + out_other[...].astype(F32)).astype(BF)
+        small_swap.wait()
+        pack_small(small, mine, norm_sums, ffn_sums)
+        small[...] += small_other[...]
+
     grad_head[...] = jnp.zeros(grad_head.shape, F32)
     for name in ("qkv", "token"):
         loaded[name].wait()
@@ -1541,6 +1596,10 @@
         pair, row = item // 4, item % 2
         core = jnp.where(item % 4 < 2, theirs, mine)
 
+        @pl.when(item == 2)
+        def _():
+            out_mine()
+
         @pl.when(item % 4 == 2)
         def _():
             qkv_theirs(pair)
@@ -1550,14 +1609,15 @@
             qkv_mine(pair - 1)
 
         for at, moves in (
-            (1, ((6, 1),)),
-            (3, ((7, 1),)),
-            (4, ((5, 2), (9, 0))),
-            (6, ((4, 3),)),
-            (7, ((8, 1),)),
-            (8, ((5, 3), (6, 2), (10, 0))),
-            (9, ((7, 2),)),
-            (10, ((9, 1),)),
+            (1, ((7, 0),)),
+            (2, ((5, 2), (6, 1))),
+            (3, ((8, 0),)),
+            (5, ((7, 1),)),
+            (6, ((6, 2),)),
+            (7, ((9, 0),)),
+            (8, ((4, 3), (8, 1))),
+            (10, ((5, 3), (7, 2), (10, 0))),
+            (11, ((9, 1),)),
         ):
             @pl.when(item == at)
             def _():
@@ -1570,8 +1630,6 @@
         def _():
             probs_load(item + 2).start()
 
-    heads[...] = pack_heads(theirs, grad_head)
-    heads_swap.start()
     loaded["weight"].wait()
 
     def input_rows(row):
@@ -1580,15 +1638,17 @@
                          + dot_last(qkv[2, rows, :], weight[2]))
 
     qkv_mine(2)
+    advance(groups, (6, 3), (8, 2), (11, 0))
+    heads[...] = pack_heads(theirs, grad_head)
+    heads_swap.start()
+    input_rows(0)
     heads_swap.wait()
     heads[...] = pack_heads(mine, grad_head) + heads_other[...]
-    advance(groups, (6, 3), (8, 2), (11, 0))
-    input_rows(0)
-    advance(groups, (10, 1))
+    advance(groups, (12, 0))
     input_rows(1)
     input_done = pltpu.make_async_copy(one, input_any, local.at[12])
     input_done.start()
-    advance(groups, (7, 3), (9, 2), (11, 1), (10, 2), (8, 3))
+    advance(groups, (7, 3), (9, 2), (10, 1), (11, 1), (12, 1), (8, 3), (10, 2))
     small_sum, grads = results[0], results[1:]
     lines[...] = jnp.zeros(lines.shape, F32)
 
@@ -1611,11 +1671,11 @@
     for index in (1, 2, 3):
         put_sums(index)
     early = Exchange(place, mine_early, plane_early, line_early, sems, base)
-    late = Exchange(place, mine_one, plane_one, line_one, sems, base + Exchange.COUNT)
-    second = Exchange(place, mine_two, plane_two, line_two, sems, base + 2 * Exchange.COUNT)
+    late = Broadcast(mine_one, land_one, sems, base + Exchange.COUNT, True)
+    second = Broadcast(mine_two, land_two, sems, base + Exchange.COUNT + 1, False)
     value = lines[LATE:, :]
     early.start_plane(value)
-    advance(groups, (9, 3), (11, 2))
+    advance(groups, (9, 3), (11, 2), (12, 2))
     line = lax.broadcasted_iota(jnp.int32, value.shape, 0) + LATE
     same, cross = early.end_plane()
     paired = value + plane_early[theirs, place.y, place.x]
@@ -1624,25 +1684,24 @@
     lines[LATE:, :] = jnp.where(line >= UP_ROWS, paired, early.end_line())
     sums = {index: ratio_of(index) for index in (1, 2, 3)}
     place_small(old_small, norm_sq[...], head_sq[...], as_row(ffn_sq), 1.0)
-    advance(groups, (11, 3))
+    advance(groups, (11, 3), (12, 3))
     put_sums(0)
     value = lines[0:LATE, :]
-    late.start_plane(value)
+    late.start(value)
     small_sum[6:8, :] = heads_sum[0:2, :]
     _, update = small_update(small_sum[...], old_small[...])
     others = small_sums(update)
     line = lax.broadcasted_iota(jnp.int32, value.shape, 0)
-    same, _ = late.end_plane()
-    paired = value + plane_one[theirs, place.y, place.x]
-    late.start_line(same)
-    lines[0:LATE, :] = jnp.where(line >= QKV_ROWS, paired, late.end_line())
+    late.end()
+    paired = value + land_one[lax.axis_index("dp") * 2 + theirs]
+    total = sum(land_one[2 * number + mine] for number in range(16))
+    lines[0:LATE, :] = jnp.where(line >= QKV_ROWS, paired, total)
     sums[0] = ratio_of(0)
-    second.start_plane(
+    second.start((
         scalars([sums[index][0] for index in range(4)] + [sums[index][1] for index in range(4)]
-                + others) + weight_sums[...])
-    same, cross = second.end_plane()
-    second.start_line(same + cross)
-    totals[...] = second.end_line()
+                + others) + weight_sums[...])[0:1])
+    second.end()
+    totals[...] = jnp.broadcast_to(jnp.sum(land_two[...], axis=0), totals.shape)
     input_done.wait()
     for group in groups:
         for chunk in group:
@@ -1651,9 +1710,9 @@
         exchange.finish()
 
 
-def backward_scatter(norm_sums, norm, scale_one, w_out, rows_old, cols_old, squares,
+def backward_scatter(norm_sums, norm, rows_old, cols_old, squares,
                      weight_sums, large, rows, widths):
-    count = scale_one.shape[0]
+    count = large[1].shape[0]
     shape = jax.ShapeDtypeStruct
     some = pl.BlockSpec(memory_space=pl.ANY)
     kinds = [F32, BF, BF, BF, BF, F32]
@@ -1663,10 +1722,10 @@
     slots = []
     for r, w, k in zip(padded, wide, kinds):
         slots += [pltpu.VMEM((4, 2, r, w), k), pltpu.VMEM((4, r, w), k), pltpu.VMEM((3, r, w), k)]
-    sems = 13 + 19 + 9 * Collect.COUNT + 3 * Exchange.COUNT
+    sems = 13 + 19 + 9 * Collect.COUNT + Exchange.COUNT + 2
     outs = [shape((r, w), F32) for r, w in zip(rows, widths)]
     outs += [shape((LINES, 128), F32), shape((8, 128), F32), shape((count, D), F32)]
-    small = [norm_sums, norm, scale_one, w_out, *rows_old, *cols_old, *squares, weight_sums]
+    small = [norm_sums, norm, *rows_old, *cols_old, *squares, weight_sums]
     return pl.pallas_call(
         backward_scatter_kernel,
         out_shape=outs,
@@ -1690,10 +1749,16 @@
             pltpu.VMEM((8, D), F32),
             pltpu.VMEM((8, D), F32),
             pltpu.VMEM((1, FF), F32),
+            pltpu.VMEM((count, 128), F32),
+            pltpu.VMEM((D, D), BF),
         ] + [
             pltpu.VMEM(lead + (count, 128), F32)
-            for count in (LINES - LATE, LATE, 8) for lead in ((2,), (2, 2, 2), (4,))
+            for count in (LINES - LATE,) for lead in ((2,), (2, 2, 2), (4,))
         ] + [
+            pltpu.VMEM((LATE, 128), F32),
+            pltpu.VMEM((32, LATE, 128), F32),
+            pltpu.VMEM((1, 128), F32),
+            pltpu.VMEM((32, 1, 128), F32),
             pltpu.VMEM((16, 128), F32),
             pltpu.SemaphoreType.DMA((sems,)),
             pltpu.SemaphoreType.DMA((sems,)),
@@ -1754,10 +1819,11 @@
         cols_old = [qkv_cols, out_cols, up_cols, down_cols]
         old = [head_bias_sq, ffn_bias_sq, norm_sq]
         *reduced, lines, totals, input_grad = backward_scatter(
-            norm_sums, norm_full, scale_one, out_full, rows_old, cols_old, old, weight_sums,
+            norm_sums, norm_full, rows_old, cols_old, old, weight_sums,
             [act_flip, grad_branch, down_full.reshape(FF, D), slope,
              up_full.reshape(2, D, FF // 2), grad_two, normed_one, hidden_flip, context,
-             context_flip, token_flip, qkv, qkv_full.reshape(3, D, D), probs],
+             context_flip, token_flip, qkv, qkv_full.reshape(3, D, D), probs,
+             scale_one, out_full],
             [16, rows_qkv, rows_out, rows_qkv, w_down.shape[0]],
             [128, QKV_HALF, D, w_up.shape[1], D])
         new = step(reduced, lines, totals, weights, rows_old, cols_old, vectors, old,

time: 207 us -> 203 us (0.981)
  Pallas kernels: 204 us -> 199 us
    pallas_call x1, Pallas kernels: 107 us -> 104 us  [backward_scatter(): pl.pallas_call(backward_scatter_kernel, out_shape=outs, in_specs=[VMEM] *...]
where the time goes in v8:
time: 203 us; the launch traced here: 200 us
  Pallas kernels  199 us (98%)
    pallas_call x1, Pallas kernels, backward_scatter(): pl.pallas_call(backward_scatter_kernel, out_shape=outs, in_specs=[VMEM] *...  104 us
    pallas_call x1, Pallas kernels, forward_gather(): pl.pallas_call(forward_gather_kernel, out_shape=small_outs + large_outs,...  88 us
    pallas_call x1, Pallas kernels, step(): pl.pallas_call(step_kernel, out_shape=outs + [jax.ShapeDtypeStruct(v.shap...  6.94 us

profile of v8, /device:TPU:0, one launch (start us, length us, event | category | flops | bytes accessed | tf_op | source)
XLA Modules:
  0.0 200.3 jit_solution(16275396720070566044)
XLA Ops:
  0.7 88.0 %forward_gather.1 = (f32[8,128]{1,0:T(8,128)}, f32[8,768]{1,0:T(8,128)}, f32[1,3072]{1,0:T(1,128)}, f32[1024,128]{1,0:T(8,128)}, bf16[768,768]{1,0:T(8,128)(2,1)...) custom-call(f32[3,48,384]{2,1,0:T(8,128)} %bitcast.9, ...), custom_call_target="tpu_custom_call" | custom-call | tf_op jit(solution)/shard_map/forward_gather/pallas_call | solution.py:1141
  88.7 104.4 %backward_scatter.1 = (f32[16,128]{1,0:T(8,128)}, f32[48,1152]{1,0:T(8,128)}, f32[24,768]{1,0:T(8,128)}, f32[48,1536]{1,0:T(8,128)}, f32[96,768]{1,0:T(8,128)}, ...) custom-call(f32[8,768]{1,0:T(8,128)} %get-tuple-element.85.refs_0_, f32[8,768]{1,0:T(8,128)} %get-tuple-element.86.refs_1_, ...), custom_call_target="tpu_custom_call" | custom-call | tf_op jit(solution)/shard_map/backward_scatter/pallas_call | solution.py:1729
  193.1 6.9 %adafactor_step.1 = (f32[3,48,384]{2,1,0:T(8,128)}, f32[24,768]{1,0:T(8,128)}, f32[48,1536]{1,0:T(8,128)}, f32[96,768]{1,0:T(8,128)}, f32[2,24]{1,0:T(2,128)}, /...) custom-call(f32[48,1152]{1,0:T(8,128)} %get-tuple-element.104.refs_0, ...), custom_call_target="tpu_custom_call" | custom-call | tf_op jit(solution)/shard_map/adafactor_step/pallas_call | solution.py:396

commit v9 on v8

--- a/solution.py
+++ b/solution.py
@@ -930,30 +930,30 @@
             start = pair * PAIR + part * 128
             g_qkv[here + (EVERY, slice(start, start + 128))] = w_qkv[
                 part, :, pair * 128:(pair + 1) * 128].astype(BF)
+    sems, base = (send, recv), [0]
+
+    def chunk(full, start, width, flip=False, orders=("zxy", "zyx")):
+        made = Spread(place, full, start, width, flip, orders, sems, base[0])
+        base[0] += made.count
+        return made
+
+    groups = [[chunk(g_small, 0, 128), chunk(g_qkv, 0, PAIR)]]
+    groups += [[chunk(g_qkv, pair * PAIR, PAIR, pair == 1)] for pair in (1, 2)]
+    groups += [[chunk(g_out, 0, D)]]
+    groups += [[chunk(g_up, at, UP_CHUNK)] for at in range(0, FF // 2, UP_CHUNK)]
+    groups += [[chunk(g_down, at, DOWN_CHUNK)] for at in range(0, D, DOWN_CHUNK)]
+
+    def ready(index):
+        for made in groups[index]:
+            made.arrived(3)
+
+    meet()
+    spread(groups, (0, 0), (1, 0))
     value = w_out[...]
     spare = g_out.shape[4] - value.shape[0]
     g_out[here] = jnp.concatenate([value, jnp.zeros((spare, D), F32)], axis=0).astype(BF)
     g_up[here] = w_up[...].astype(BF)
     g_down[here] = w_down[...].astype(BF)
-    sems, base = (send, recv), [0]
-
-    def chunk(full, start, width, flip=False, orders=("zxy", "zyx")):
-        made = Spread(place, full, start, width, flip, orders, sems, base[0])
-        base[0] += made.count
-        return made
-
-    groups = [[chunk(g_small, 0, 128), chunk(g_qkv, 0, PAIR)]]
-    groups += [[chunk(g_qkv, pair * PAIR, PAIR, pair == 1)] for pair in (1, 2)]
-    groups += [[chunk(g_out, 0, D)]]
-    groups += [[chunk(g_up, at, UP_CHUNK)] for at in range(0, FF // 2, UP_CHUNK)]
-    groups += [[chunk(g_down, at, DOWN_CHUNK)] for at in range(0, D, DOWN_CHUNK)]
-
-    def ready(index):
-        for made in groups[index]:
-            made.arrived(3)
-
-    meet()
-    spread(groups, (0, 0), (1, 0))
     sums[...] = weight_sums_of([w_qkv, w_out, w_up, w_down], g_small[here])
     for row in range(2):
         set_bias(bias.at[row], lengths, place.m * 2 + row)
@@ -1604,7 +1604,7 @@
         def _():
             qkv_theirs(pair)
 
-        @pl.when((item == 4) | (item == 8))
+        @pl.when((item == 5) | (item == 9))
         def _():
             qkv_mine(pair - 1)
 
@@ -1642,13 +1642,13 @@
     heads[...] = pack_heads(theirs, grad_head)
     heads_swap.start()
     input_rows(0)
+    input_rows(1)
     heads_swap.wait()
     heads[...] = pack_heads(mine, grad_head) + heads_other[...]
     advance(groups, (12, 0))
-    input_rows(1)
     input_done = pltpu.make_async_copy(one, input_any, local.at[12])
     input_done.start()
-    advance(groups, (7, 3), (9, 2), (10, 1), (11, 1), (12, 1), (8, 3), (10, 2))
+    advance(groups, (7, 3), (9, 2), (10, 1), (11, 1), (8, 3), (10, 2), (12, 1))
     small_sum, grads = results[0], results[1:]
     lines[...] = jnp.zeros(lines.shape, F32)
 

time: 203 us -> 201 us (level)
    pallas_call x1, Pallas kernels: 104 us -> 102 us  [backward_scatter(): pl.pallas_call(backward_scatter_kernel, out_shape=outs, in_specs=[VMEM] *...]
where the time goes in v9:
time: 201 us; the launch traced here: 198 us
  Pallas kernels  197 us (98%)
    pallas_call x1, Pallas kernels, backward_scatter(): pl.pallas_call(backward_scatter_kernel, out_shape=outs, in_specs=[VMEM] *...  102 us
    pallas_call x1, Pallas kernels, forward_gather(): pl.pallas_call(forward_gather_kernel, out_shape=small_outs + large_outs,...  88 us
    pallas_call x1, Pallas kernels, step(): pl.pallas_call(step_kernel, out_shape=outs + [jax.ShapeDtypeStruct(v.shap...  6.94 us

profile of v9, /device:TPU:0, one launch (start us, length us, event | category | flops | bytes accessed | tf_op | source)
XLA Modules:
  0.0 198.3 jit_solution(5384475238370391584)
XLA Ops:
  0.7 88.0 %forward_gather.1 = (f32[8,128]{1,0:T(8,128)}, f32[8,768]{1,0:T(8,128)}, f32[1,3072]{1,0:T(1,128)}, f32[1024,128]{1,0:T(8,128)}, bf16[768,768]{1,0:T(8,128)(2,1)...) custom-call(f32[3,48,384]{2,1,0:T(8,128)} %bitcast.9, ...), custom_call_target="tpu_custom_call" | custom-call | tf_op jit(solution)/shard_map/forward_gather/pallas_call | solution.py:1141
  88.7 102.4 %backward_scatter.1 = (f32[16,128]{1,0:T(8,128)}, f32[48,1152]{1,0:T(8,128)}, f32[24,768]{1,0:T(8,128)}, f32[48,1536]{1,0:T(8,128)}, f32[96,768]{1,0:T(8,128)}, ...) custom-call(f32[8,768]{1,0:T(8,128)} %get-tuple-element.85.refs_0_, f32[8,768]{1,0:T(8,128)} %get-tuple-element.86.refs_1_, ...), custom_call_target="tpu_custom_call" | custom-call | tf_op jit(solution)/shard_map/backward_scatter/pallas_call | solution.py:1729
  191.1 6.9 %adafactor_step.1 = (f32[3,48,384]{2,1,0:T(8,128)}, f32[24,768]{1,0:T(8,128)}, f32[48,1536]{1,0:T(8,128)}, f32[96,768]{1,0:T(8,128)}, f32[2,24]{1,0:T(2,128)}, /...) custom-call(f32[48,1152]{1,0:T(8,128)} %get-tuple-element.104.refs_0, ...), custom_call_target="tpu_custom_call" | custom-call | tf_op jit(solution)/shard_map/adafactor_step/pallas_call | solution.py:396
